TPU v7x, 32 devices: a whole 2x2x4 slice. The times are simulated.
32 devices in a mesh: gx: 8 (over z, y), gz: 4 (over x, core).
Axes of the slice: x: 2, y: 2, z: 4, core: 2. Of those that a mesh axis runs over, the one named last changes fastest.
Arguments:
- temp: float32 [64, 512, 256], P('gz', 'gx'), may hold values from -6 to 6
- u_vel: float32 [64, 512, 256], P('gz', 'gx'), may hold values from -1.8 to 1.8
- v_vel: float32 [64, 512, 256], P('gz', 'gx'), may hold values from -1.8 to 1.8
- w_vel: float32 [64, 512, 256], P('gz', 'gx'), may hold values from -1.8 to 1.8
- temp_prev_tend: float32 [64, 512, 256], P('gz', 'gx'), may hold values from -6 to 6
- w_prev_tend: float32 [64, 512, 256], P('gz', 'gx'), may hold values from -6 to 6
- lower_coupling: float32 [64], P('gz'), may hold values from 256 to 4096
- upper_coupling: float32 [64], P('gz'), may hold values from 256 to 4096, as said below
- vertical_metric: float32 [64], P('gz'), may hold values from 0.25 to 2
Outputs:
- temp_next: float32 [64, 512, 256], P('gz', 'gx')
- w_next: float32 [64, 512, 256], P('gz', 'gx')
- temp_tend: float32 [64, 512, 256], P('gz', 'gx')
- w_tend: float32 [64, 512, 256], P('gz', 'gx')
Inputs may be any that keep to these rules, and one draw needn't show every extreme that they name: upper_coupling[k] equals lower_coupling[k + 1] for k < 63: the face shared by two levels.
All inputs are finite; a program needn't handle non-finite values.
Results may differ from a plain program's by a relative error of at most 0.0003.
Values sent between devices are 32-bit elements; how exact they have to be, the bound alone decides.
No kernel may reach another device: no remote copies, remote signals or barrier semaphores. Data moves between devices by JAX's collectives and lax.ppermute only.
A program may use at most 128 MiB of HBM per device.

v0:
```python
import jax
import jax.numpy as jnp
from jax import lax
from jax.sharding import PartitionSpec as P

NEW_WEIGHT = 5.0 / 12.0
OLD_WEIGHT = -17.0 / 60.0
HORIZ_DIFF = 0.1


def padded(cells, sides, width, closed):
    for axis, dim in sides:
        count = lax.axis_size(axis)
        ends = count if closed else count - 1
        head = lax.slice_in_dim(cells, 0, width, axis=dim)
        tail = lax.slice_in_dim(cells, cells.shape[dim] - width, cells.shape[dim], axis=dim)
        cells = jnp.concatenate(
            [
                lax.ppermute(tail, axis, [(i, (i + 1) % count) for i in range(ends)]),
                cells,
                lax.ppermute(head, axis, [((i + 1) % count, i) for i in range(ends)]),
            ],
            axis=dim,
        )
    return cells


def shifted(array, axis, by):
    devices = lax.axis_size(axis)
    pairs = [(i, i + by) for i in range(devices) if 0 <= i + by < devices]
    return lax.ppermute(array, axis, pairs)


def sweep_solve(low_band, main_band, high_band, right_side):

    def forward(carry, row):
        ratio_prev, value_prev = carry
        low_val, main_val, high_val, rhs_row = row
        pivot_val = main_val - low_val * ratio_prev
        ratio_new = high_val / pivot_val
        value_new = (rhs_row - low_val * value_prev) / pivot_val
        return ((ratio_new, value_new), (ratio_new, value_new))

    start = (jnp.zeros((), jnp.float32), jnp.zeros(right_side.shape[1:], jnp.float32))
    _, (ratios, values) = lax.scan(
        forward, start, (low_band, main_band, high_band, right_side), unroll=True
    )

    def backward(next_value, row):
        ratio_row, value_row = row
        solved_row = value_row - ratio_row * next_value
        return (solved_row, solved_row)

    _, solved = lax.scan(
        backward,
        jnp.zeros(right_side.shape[1:], jnp.float32),
        (ratios, values),
        reverse=True,
        unroll=True,
    )
    return solved


def local(
    temp,
    u_vel,
    v_vel,
    w_vel,
    temp_prev_tend,
    w_prev_tend,
    lower_coupling,
    upper_coupling,
    vertical_metric,
):
    levels = temp.shape[0]
    inner_rows = levels - 1
    fields = jnp.stack((temp, w_vel))
    side_rim = padded(jnp.stack((temp, w_vel, u_vel)), (("gx", 2),), 1, True)
    wall_rim = padded(fields, (("gz", 1),), 1, False)
    flux_x = side_rim[:2] * side_rim[2:3]
    advect = 0.5 * (flux_x[:, :, 2:] - flux_x[:, :, :-2])
    flux_y = fields * v_vel
    advect = advect + 0.5 * (jnp.roll(flux_y, -1, 3) - jnp.roll(flux_y, 1, 3))
    flux_z = wall_rim * wall_rim[1:2]
    advect = advect + vertical_metric[:, None, None] * (flux_z[:, 2:] - flux_z[:, :-2])
    spread = (
        side_rim[:2, :, 2:]
        + side_rim[:2, :, :-2]
        + jnp.roll(fields, -1, 3)
        + jnp.roll(fields, 1, 3)
        - 4.0 * fields
    )
    tendency = -advect + HORIZ_DIFF * spread + jnp.stack((w_vel, temp))
    upper_face = upper_coupling[:, None, None]
    lower_face = lower_coupling[:, None, None]
    vertical = upper_face * (wall_rim[:, 2:] - fields) - lower_face * (fields - wall_rim[:, :-2])
    right_side = (
        fields
        + vertical
        + NEW_WEIGHT * tendency
        + OLD_WEIGHT * jnp.stack((temp_prev_tend, w_prev_tend))
    )
    inverse = sweep_solve(
        -lower_coupling[:inner_rows],
        1.0 + lower_coupling[:inner_rows] + upper_coupling[:inner_rows],
        -upper_coupling[:inner_rows],
        jnp.eye(inner_rows, dtype=jnp.float32),
    )
    partial_value = jnp.einsum(
        "kj,fjxy->fkxy", inverse, right_side[:, :inner_rows], precision=lax.Precision.HIGHEST
    )
    low_spike = lower_coupling[0] * inverse[:, 0]
    top_spike = upper_coupling[inner_rows - 1] * inverse[:, inner_rows - 1]
    head_above, low_above, top_above = shifted(
        (partial_value[:, 0], low_spike[0], top_spike[0]), "gz", -1
    )
    face_below = lower_coupling[levels - 1]
    face_above = upper_coupling[levels - 1]
    sub_here = -face_below * low_spike[inner_rows - 1]
    diag_here = (
        1.0
        + face_below
        + face_above
        - face_below * top_spike[inner_rows - 1]
        - face_above * low_above
    )
    sup_here = -face_above * top_above
    reduced = (
        right_side[:, levels - 1]
        + face_below * partial_value[:, inner_rows - 1]
        + face_above * head_above
    )
    position = lax.axis_index("gz")
    all_sub, all_diag, all_sup, all_rhs = (
        lax.all_gather(sub_here[None], "gz", axis=0, tiled=True),
        lax.all_gather(diag_here[None], "gz", axis=0, tiled=True),
        lax.all_gather(sup_here[None], "gz", axis=0, tiled=True),
        lax.all_gather(reduced[None], "gz", axis=0, tiled=True),
    )
    separators = sweep_solve(all_sub, all_diag, all_sup, all_rhs)
    own_value = lax.dynamic_index_in_dim(separators, position, 0, keepdims=False)
    below_value = lax.dynamic_index_in_dim(
        separators, jnp.maximum(position - 1, 0), 0, keepdims=False
    )
    below_value = jnp.where(position > 0, below_value, jnp.zeros_like(below_value))
    interior = (
        partial_value
        + low_spike[None, :, None, None] * below_value[:, None]
        + top_spike[None, :, None, None] * own_value[:, None]
    )
    solved = jnp.concatenate((interior, own_value[:, None]), axis=1)
    return (solved[0], solved[1], tendency[0], tendency[1])


def solution(mesh):
    return jax.shard_map(
        local,
        mesh=mesh,
        in_specs=(
            P("gz", "gx", None),
            P("gz", "gx", None),
            P("gz", "gx", None),
            P("gz", "gx", None),
            P("gz", "gx", None),
            P("gz", "gx", None),
            P("gz"),
            P("gz"),
            P("gz"),
        ),
        out_specs=(
            P("gz", "gx", None),
            P("gz", "gx", None),
            P("gz", "gx", None),
            P("gz", "gx", None),
        ),
        check_vma=False,
    )
```

profile of v0, /device:TPU:0, one launch (start us, length us, event | category | flops | bytes accessed | tf_op | source)
XLA Modules:
  0.0 140.4 jit_solution(16928255410111450933)
XLA Ops:
  0.6 1.4 fusion.85
  2.7 1.3 fusion.86
  31.7 8.0 %fusion.45 = (f32[1,15]{1,0:T(1,128)S(1)}, f32[1,15]{1,0:T(1,128)S(1)}, f32[1,15]{1,0:T(1,128)S(1)}, f32[1,15]{1,0:T(1,128)S(1)}, f32[1,15]{1,0:T(1,128)S(1)}, /...) fusion(f32[15,15]{1,0:T(8,128)S(1)} %fusion.43, ...), kind=kLoop, calls=%fused_computation.113 | loop fusion | flops 615 | bytes 1792 | tf_op jit(solution)/shard_map/eval_jaxpr/div | solution.py:41
  43.1 1.5 %fusion.60 = (f32[15]{0:T(128)S(1)}, f32[15,1]{1,0:T(8,128)S(1)}, f32[15]{0:T(128)S(1)}, f32[15,1]{1,0:T(8,128)S(1)}) fusion(f32[15,15]{1,0:T(8,128)S(1)} %concatenate.51, f32[]{:T(128)} %bitcast.55, f32[]{:T(128)} %bitcast.63), kind=kLoop, calls=%fused_computation.158 | loop fusion | flops 30 | bytes 368 | tf_op jit(solution)/shard_map/mul | solution.py:112
  46.5 1.3 collective-permute-start.5
  47.8 1.8 %copy.56 = f32[16,64,256]{2,0,1:T(8,128)S(1)} copy(f32[16,64,256]{2,1,0:T(8,128)} %param.10) | data formatting | bytes 2097152 | tf_op args[1]
  51.5 3.0 %collective-permute-start.2 = (f32[3,16,1,256]{3,1,2,0:T(8,128)}, f32[3,16,1,256]{3,1,2,0:T(8,128)S(1)}, u32[]{:S(2)}, u32[]{:S(2)}) collective-permute-start(f32[3,16,1,256]{3,1,2,0:T(8,128)} %get-tuple-element.59), channel_id=1, source_target_pairs={{0,4},{4,8},{8,12},{12,16},{16,20},{20,24},{24,28},{28,0},{1,5},{5... | collective-permute-start | bytes 147464 | tf_op jit(solution)/shard_map/ppermute | solution.py:19
  54.5 3.0 %collective-permute-start.3 = (f32[3,16,1,256]{3,1,2,0:T(8,128)}, f32[3,16,1,256]{3,1,2,0:T(8,128)S(1)}, u32[]{:S(2)}, u32[]{:S(2)}) collective-permute-start(f32[3,16,1,256]{3,1,2,0:T(8,128)} %get-tuple-element.58), channel_id=1, source_target_pairs={{4,0},{8,4},{12,8},{16,12},{20,16},{24,20},{28,24},{0,28},{5,1},{9... | collective-permute-start | bytes 147464 | tf_op jit(solution)/shard_map/ppermute | solution.py:21
  60.7 2.8 %fusion.78 = (f32[2,16,64,255]{3,1,2,0:T(8,128)}, f32[2,16,64,255]{3,1,2,0:T(8,128)}) fusion(f32[2,16,64,256]{3,1,2,0:T(8,128)S(1)} %fusion.25), kind=kLoop, calls=%fused_computation.160 | loop fusion | bytes 8355840 | tf_op jit(solution)/shard_map/jit(_roll_static)/slice | solution.py:83
  63.5 1.6 %fusion.79 = (f32[2,16,64,1]{3,1,2,0:T(8,128)}, f32[2,16,64,1]{3,1,2,0:T(8,128)}) fusion(f32[2,16,64,256]{3,1,2,0:T(8,128)S(1)} %fusion.25), kind=kLoop, calls=%fused_computation.161 | loop fusion | bytes 32768 | tf_op jit(solution)/shard_map/jit(_roll_static)/slice | solution.py:83
  65.2 2.7 %fusion = (f32[2,16,64,255]{3,1,2,0:T(8,128)}, f32[2,16,64,255]{3,1,2,0:T(8,128)}) fusion(f32[1,16,64,256]{3,1,2,0:T(8,128)S(1)} %get-tuple-element.152, f32[1,16,64,256]{3,1,2,0:T(8,128)S(1)} %get-tuple-element.151), kind=kLoop, calls=%fused_computation.16 | loop fusion | flops 1044480 | bytes 6275072 | tf_op jit(solution)/shard_map/stack | solution.py:77
  67.9 1.7 %fusion.28 = (f32[2,16,64,1]{3,1,2,0:T(8,128)}, f32[2,16,64,1]{3,1,2,0:T(8,128)}) fusion(f32[1,16,64,256]{3,1,2,0:T(8,128)S(1)} %get-tuple-element.152, f32[1,16,64,256]{3,1,2,0:T(8,128)S(1)} %get-tuple-element.151), kind=kLoop, calls=%fused_computation.65 | loop fusion | flops 4096 | bytes 2113536 | tf_op jit(solution)/shard_map/stack | solution.py:77
  74.5 4.1 %copy_bitcast_fusion.1 = (f32[1,16,64,256]{3,1,2,0:T(8,128)}, f32[1,16,64,256]{3,1,2,0:T(8,128)}) fusion(f32[16,64,256]{2,1,0:T(8,128)} %param.14, f32[16,64,256]{2,1,0:T(8,128)} %param.13), kind=kLoop, calls=%fused_computation.71 | loop fusion | bytes 4194304 | tf_op jit(solution)/shard_map/stack | solution.py:101
  79.3 4.0 %collective-permute-start.1 = (f32[2,1,64,256]{3,1,2,0:T(1,128)}, f32[2,1,64,256]{3,1,2,0:T(1,128)S(1)}, u32[]{:S(2)}, u32[]{:S(2)}) collective-permute-start(f32[2,1,64,256]{3,1,2,0:T(1,128)} %get-tuple-element.73), channel_id=1, source_target_pairs={{0,1},{1,2},{2,3},{4,5},{5,6},{6,7},{8,9},{9,10},{10,11},{12,13},{... | collective-permute-start | bytes 393224 | tf_op jit(solution)/shard_map/ppermute | solution.py:19
  86.7 7.9 %all-reduce.3 = (f32[4]{0:T(128)S(1)}, f32[4]{0:T(128)S(1)}, f32[4]{0:T(128)S(1)}) all-reduce(f32[4]{0:T(128)S(1)} %dynamic-update-slice.1, f32[4]{0:T(128)S(1)} %dynamic-update-slice, f32[4]{0:T(128)S(1)} %dynamic-update-slice.2), channel_id=1, replica_groups=mesh['gx'=8,'gz'=4] {'gz'}, use_global_device_ids=true, to_apply=%add.1 | all-reduce | flops 12 | bytes 96
  106.6 8.9 %fusion.21 = (f32[2,16,64,256]{3,1,2,0:T(8,128)}, f32[2,16,64,256]{3,1,2,0:T(8,128)}) fusion(f32[2,1,64,256]{3,1,2,0:T(1,128)S(1)} %collective-permute-done.1, f32[1,16,64,256]{3,1,2,0:T(8,128)S(1)} %get-tuple-element.151, f32[1,16,64,256]{3,1,2,0:T(8,128)S(1)} %get-tuple-element.152, f32[2,1,64,256]{3,1,2,0:T(1,128)S(1)} %collective-permute-done, ...), kind=kLoop, calls=%fused_computation.46 | loop fusion | flops 22544384 | bytes 26575040 | tf_op jit(solution)/shard_map/add | solution.py:98
  115.5 3.5 %fusion.2 = f32[2,64,256,15]{2,3,1,0:T(8,128)S(1)} fusion(f32[2,16,64,256]{3,1,2,0:T(8,128)} %get-tuple-element.56, f32[15,15]{1,0:T(8,128)S(1)} %concatenate.51), kind=kOutput, calls=%fused_computation.18 | convolution fusion | flops 88473600 | bytes 4064132 | tf_op jit(solution)/shard_map/kj,fjxy->fkxy/dot_general | solution.py:109
  120.8 1.3 collective-permute-start.4
  122.3 1.6 %copy.41 = f32[16,64,256]{2,1,0:T(8,128)} copy(f32[16,64,256]{2,0,1:T(8,128)S(1)} %get-tuple-element.61) | data formatting | bytes 2097152
  123.9 1.6 %copy.42 = f32[16,64,256]{2,1,0:T(8,128)} copy(f32[16,64,256]{2,0,1:T(8,128)S(1)} %get-tuple-element.60) | data formatting | bytes 2097152
  125.5 1.4 %slice_add_fusion = f32[2,1,64,256]{3,1,2,0:T(1,128)S(1)} fusion(f32[2,16,64,256]{3,1,2,0:T(8,128)} %get-tuple-element.56, f32[2,1,64,256]{3,2,0,1:T(8,128)S(1)} %get-tuple-element.75), kind=kLoop, calls=%fused_computation.94 | loop fusion | flops 32768 | bytes 393216 | tf_op jit(solution)/shard_map/add | solution.py:129
  127.5 8.1 %all-gather = f32[8,64,256]{2,1,0:T(8,128)S(1)} all-gather(f32[2,64,256]{2,1,0:T(8,128)S(1)} %bitcast_add_fusion), channel_id=2, replica_groups=mesh['gx'=8,'gz'=4] {'gz'}, dimensions={0}, use_global_device_ids=true | all-gather | bytes 655360 | tf_op jit(solution)/shard_map/all_gather | solution.py:138
  135.6 2.1 %multiply_subtract_fusion = (f32[1,2,64,256]{3,2,1,0:T(8,128)S(1)}, f32[1,2,64,256]{3,2,1,0:T(8,128)S(1)}, f32[1,2,64,256]{3,2,1,0:T(8,128)S(1)}, f32[1,2,64,256]{3,2,1,0:T(8,128)S(1)}) fusion(f32[8,64,256]{2,1,0:T(8,128)S(1)} %all-gather, f32[]{:T(128)S(6)} %sub.627, f32[]{:T(128)} %bitcast.62, f32[]{:T(128)S(6)} %div.459, f32[]{:T(128)S(6)} %div.462, ...), kind=kLoop, calls=%fused_computation.97 | loop fusion | flops 589824 | bytes 1048624 | tf_op jit(solution)/shard_map/eval_jaxpr/sub | solution.py:51
  138.9 1.5 %fusion.30 = (f32[16,64,256]{2,1,0:T(8,128)}, f32[16,64,256]{2,1,0:T(8,128)}) fusion(f32[2,1,64,256]{3,2,0,1:T(8,128)S(1)} %get-tuple-element.76, f32[2,15,64,256]{3,2,0,1:T(8,128)S(1)} %multiply_add_fusion), kind=kLoop, calls=%fused_computation.70 | loop fusion | flops 524288 | bytes 4194304 | tf_op jit(solution)/shard_map/squeeze | solution.py:152
  (61 shorter events, 21.3 us)
Async XLA Ops:
  43.1 6.5 %copy-start.2 = (f32[16,64,256]{2,1,0:T(8,128)S(1)}, f32[16,64,256]{2,1,0:T(8,128)}, u32[]{:S(2)}) copy-start(f32[16,64,256]{2,1,0:T(8,128)} %param.12) | copy-start | bytes 3145732
  43.1 6.5 %copy-start.3 = (f32[16,64,256]{2,1,0:T(8,128)S(1)}, f32[16,64,256]{2,1,0:T(8,128)}, u32[]{:S(2)}) copy-start(f32[16,64,256]{2,1,0:T(8,128)} %param.9) | copy-start | bytes 3145732
  45.2 34.1 %collective-permute-start.6 = (f32[]{:T(128)}, f32[]{:T(128)}, u32[]{:S(2)}, u32[]{:S(2)}) collective-permute-start(f32[]{:T(128)} %bitcast.69), channel_id=1, source_target_pairs={{1,0},{2,1},{3,2},{5,4},{6,5},{7,6},{9,8},{10,9},{11,10},{13,12},{... | collective-permute-start | bytes 20 | tf_op jit(solution)/shard_map/ppermute | solution.py:31
  46.5 38.3 %collective-permute-start.5 = (f32[]{:T(128)}, f32[]{:T(128)}, u32[]{:S(2)}, u32[]{:S(2)}) collective-permute-start(f32[]{:T(128)} %bitcast.65), channel_id=1, source_target_pairs={{1,0},{2,1},{3,2},{5,4},{6,5},{7,6},{9,8},{10,9},{11,10},{13,12},{... | collective-permute-start | bytes 20 | tf_op jit(solution)/shard_map/ppermute | solution.py:31
  50.9 8.9 %copy-start.1 = (f32[16,64,256]{2,1,0:T(8,128)S(1)}, f32[16,64,256]{2,1,0:T(8,128)}, u32[]{:S(2)}) copy-start(f32[16,64,256]{2,1,0:T(8,128)} %param.11) | copy-start | bytes 3145732
  51.5 52.9 %collective-permute-start.2 = (f32[3,16,1,256]{3,1,2,0:T(8,128)}, f32[3,16,1,256]{3,1,2,0:T(8,128)S(1)}, u32[]{:S(2)}, u32[]{:S(2)}) collective-permute-start(f32[3,16,1,256]{3,1,2,0:T(8,128)} %get-tuple-element.59), channel_id=1, source_target_pairs={{0,4},{4,8},{8,12},{12,16},{16,20},{20,24},{24,28},{28,0},{1,5},{5... | collective-permute-start | bytes 147464 | tf_op jit(solution)/shard_map/ppermute | solution.py:19
  54.5 50.0 %collective-permute-start.3 = (f32[3,16,1,256]{3,1,2,0:T(8,128)}, f32[3,16,1,256]{3,1,2,0:T(8,128)S(1)}, u32[]{:S(2)}, u32[]{:S(2)}) collective-permute-start(f32[3,16,1,256]{3,1,2,0:T(8,128)} %get-tuple-element.58), channel_id=1, source_target_pairs={{4,0},{8,4},{12,8},{16,12},{20,16},{24,20},{28,24},{0,28},{5,1},{9... | collective-permute-start | bytes 147464 | tf_op jit(solution)/shard_map/ppermute | solution.py:21
  58.5 46.8 %collective-permute-start = (f32[2,1,64,256]{3,1,2,0:T(1,128)}, f32[2,1,64,256]{3,1,2,0:T(1,128)S(1)}, u32[]{:S(2)}, u32[]{:S(2)}) collective-permute-start(f32[2,1,64,256]{3,1,2,0:T(1,128)} %get-tuple-element.72), channel_id=1, source_target_pairs={{1,0},{2,1},{3,2},{5,4},{6,5},{7,6},{9,8},{10,9},{11,10},{13,12},{... | collective-permute-start | bytes 393224 | tf_op jit(solution)/shard_map/ppermute | solution.py:21
  67.9 5.3 %copy-start.7 = (u32[32]{0:T(128)S(1)}, u32[32]{0:T(128)}, u32[]{:S(2)}) copy-start(u32[32]{0:T(128)} %constant.39) | copy-start | bytes 388
  79.3 25.9 %collective-permute-start.1 = (f32[2,1,64,256]{3,1,2,0:T(1,128)}, f32[2,1,64,256]{3,1,2,0:T(1,128)S(1)}, u32[]{:S(2)}, u32[]{:S(2)}) collective-permute-start(f32[2,1,64,256]{3,1,2,0:T(1,128)} %get-tuple-element.73), channel_id=1, source_target_pairs={{0,1},{1,2},{2,3},{4,5},{5,6},{6,7},{8,9},{9,10},{10,11},{12,13},{... | collective-permute-start | bytes 393224 | tf_op jit(solution)/shard_map/ppermute | solution.py:19
  105.9 0.7 copy-start.4
  105.9 0.7 copy-start.5
  105.9 0.7 copy-start.6
  119.0 3.1 %copy-start = (f32[2,16,64,256]{3,1,2,0:T(8,128)S(1)}, f32[2,16,64,256]{3,1,2,0:T(8,128)}, u32[]{:S(2)}) copy-start(f32[2,16,64,256]{3,1,2,0:T(8,128)} %get-tuple-element.57) | copy-start | bytes 6291460
  120.8 6.1 %collective-permute-start.4 = (f32[2,64,256]{2,1,0:T(8,128)S(1)}, f32[2,64,256]{2,1,0:T(8,128)S(1)}, u32[]{:S(2)}, u32[]{:S(2)}) collective-permute-start(f32[2,64,256]{2,1,0:T(8,128)S(1)} %get-tuple-element.74), channel_id=1, source_target_pairs={{1,0},{2,1},{3,2},{5,4},{6,5},{7,6},{9,8},{10,9},{11,10},{13,12},{... | collective-permute-start | bytes 393224 | tf_op jit(solution)/shard_map/ppermute | solution.py:31
where the time goes:
time: 142 us; the launch traced here: 140 us
  between operations  43.1 us (30%)
  other arithmetic  35.3 us (25%)
  local copies, waits for them, and re-layouts  27.3 us (19%)
  blocking collectives  16 us (11%)
  starting transfers between devices  15.2 us (11%)
  matrix products  3.5 us (2%)
    add x1, other arithmetic, local(): fields + vertical + NEW_WEIGHT * tendency  8.9 us
    unnamed x27, local copies, waits for them, and re-layouts  8.69 us
    all_gather x1, blocking collectives, local(): lax.all_gather(reduced[None], 'gz', axis=0, tiled=True)  8.07 us
    div x1, other arithmetic, forward(): value_new = (rhs_row - low_val * value_prev) / pivot_val  8.02 us
    unnamed x1, blocking collectives  7.93 us
    ppermute x2, starting transfers between devices, padded(): lax.ppermute(tail, axis, [(i, (i + 1) % count) for i in range(ends)])  6.97 us
    another operation x3, other arithmetic, local(): fields = jnp.stack((temp, w_vel))  5.25 us
    slice x2, local copies, waits for them, and re-layouts, local(): advect = advect + 0.5 * (jnp.roll(flux_y, -1, 3) - jnp.roll(flux_y, 1, 3))  4.42 us
  transfers between devices with their start and end apart: 7, of which 0 were waited for; matrix products, arithmetic and copies ran while one was open for 21% of the time, Pallas kernels for 0%

commit v1 on v0

v1 whole, which is shorter than its diff:
```python
import functools

import jax
import jax.numpy as jnp
from jax import lax
from jax.experimental import pallas as pl
from jax.experimental.pallas import tpu as pltpu
from jax.sharding import PartitionSpec as P

NEW_WEIGHT = 5.0 / 12.0
HORIZ_DIFF = 0.1
FIELD_WEIGHT = 2.0 / NEW_WEIGHT
PREV_WEIGHT = (17.0 / 60.0) / NEW_WEIGHT
TILE = 8
MIB = 1024 * 1024

PIVOT_NEW, LOWER_PIVOT, UPPER_PIVOT, FIRST_GREEN, BELOW_FORWARD, PIVOT = range(6)
FIRST, CORNER, LAST, BELOW, ABOVE, METRIC_BELOW, METRIC_ABOVE = range(7)
FROM_ABOVE, FROM_BELOW = range(2)

VMEM = pltpu.VMEM
F32 = jnp.float32


def whole(space):
    return pl.BlockSpec(memory_space=space)


def held(*shape):
    return pltpu.VMEM(shape, F32)


def in_vmem(array):
    return pltpu.with_memory_space_constraint(array, pltpu.VMEM)


def in_hbm(*arrays):
    return [pltpu.with_memory_space_constraint(array, pltpu.HBM) for array in arrays]


def bit_of(axis, bit):
    return (lax.axis_index(axis) >> bit) & 1


def edges_kernel(temp, u_vel, w_vel, to_left, to_right, outer, inner, strips, layers, sems):
    levels, rows, _ = temp.shape
    copies = []
    for at, array in enumerate((temp, w_vel, u_vel)):
        for side, first in enumerate((0, rows - TILE)):
            copies.append((array.at[:, pl.ds(first, TILE), :], strips.at[at, side]))
    for at, array in enumerate((temp, w_vel)):
        for side, level in enumerate((0, levels - 1)):
            copies.append((array.at[level], layers.at[at, side]))
    copies = [pltpu.make_async_copy(src, dst, sems.at[i]) for i, (src, dst) in enumerate(copies)]
    for copy in copies:
        copy.start()
    for copy in copies:
        copy.wait()
    for field in range(2):
        at = pl.ds(field * levels, levels)
        to_left[at, :] = (HORIZ_DIFF - 0.5 * strips[2, 0, :, 0, :]) * strips[field, 0, :, 0, :]
        last = TILE - 1
        to_right[at, :] = (HORIZ_DIFF + 0.5 * strips[2, 1, :, last, :]) * strips[
            field, 1, :, last, :
        ]
    upper = bit_of("gz", 0) == 1
    for field in range(2):
        at = pl.ds(field * rows, rows)
        bottom = layers[1, 0] * layers[field, 0]
        top = layers[1, 1] * layers[field, 1]
        outer[at, :] = jnp.where(upper, top, bottom)
        inner[at, :] = jnp.where(upper, bottom, top)


def edges(temp, u_vel, w_vel):
    levels, rows, cols = temp.shape
    return pl.pallas_call(
        edges_kernel,
        out_shape=(
            held(2 * levels, cols),
            held(2 * levels, cols),
            held(2 * rows, cols),
            held(2 * rows, cols),
        ),
        in_specs=[whole(pl.ANY)] * 3,
        out_specs=[whole(VMEM)] * 4,
        scratch_shapes=[
            pltpu.VMEM((3, 2, levels, TILE, cols), F32),
            pltpu.VMEM((2, 2, rows, cols), F32),
            pltpu.SemaphoreType.DMA((10,)),
        ],
        compiler_params=pltpu.CompilerParams(vmem_limit_bytes=8 * MIB),
        name="edges",
    )(*in_hbm(temp, u_vel, w_vel))


def coefficients(lower, upper, metric, table, scalars):
    levels, _, cols = table.shape

    def row(value):
        return jnp.full((1, cols), value, F32)

    ratio = jnp.zeros((1, cols), F32)
    forward = jnp.ones((1, cols), F32)
    for level in range(levels):
        low, high = row(lower[level]), row(upper[level])
        pivot = 1.0 / (1.0 + low + high - low * ratio)
        ratio = high * pivot
        lower_pivot = low * pivot
        forward = pivot if level == 0 else lower_pivot * forward
        table[level, pl.ds(PIVOT_NEW, 1), :] = NEW_WEIGHT * pivot
        table[level, pl.ds(LOWER_PIVOT, 1), :] = lower_pivot
        table[level, pl.ds(UPPER_PIVOT, 1), :] = ratio
        table[level, pl.ds(BELOW_FORWARD, 1), :] = forward
        table[level, pl.ds(PIVOT, 1), :] = pivot
    green = forward
    table[levels - 1, pl.ds(FIRST_GREEN, 1), :] = NEW_WEIGHT * green
    for level in range(levels - 2, -1, -1):
        green = (
            table[level, pl.ds(BELOW_FORWARD, 1), :]
            + table[level, pl.ds(UPPER_PIVOT, 1), :] * green
        )
        table[level, pl.ds(FIRST_GREEN, 1), :] = NEW_WEIGHT * green
    scalars[pl.ds(FIRST, 1), :] = green
    scalars[pl.ds(CORNER, 1), :] = forward
    scalars[pl.ds(LAST, 1), :] = pivot
    scalars[pl.ds(BELOW, 1), :] = row(lower[0])
    scalars[pl.ds(ABOVE, 1), :] = row(upper[levels - 1])
    scalars[pl.ds(METRIC_BELOW, 1), :] = row(NEW_WEIGHT * metric[0])
    scalars[pl.ds(METRIC_ABOVE, 1), :] = row(NEW_WEIGHT * metric[levels - 1])
    scalars[pl.ds(7, 1), :] = row(0.0)


def bulk_kernel(
    chunks,
    lower,
    upper,
    metric,
    temp,
    u_vel,
    v_vel,
    w_vel,
    temp_prev,
    w_prev,
    temp_pad,
    w_pad,
    forward,
    tend,
    first,
    table,
    scalars,
    u_buf,
    v_buf,
    tp_buf,
    wp_buf,
    sems,
):
    levels, rows, cols = temp.shape
    depth = levels // chunks
    moves = (
        (temp, temp_pad, 1),
        (w_vel, w_pad, 1),
        (u_vel, u_buf, 0),
        (v_vel, v_buf, 0),
        (temp_prev, tp_buf, 0),
        (w_prev, wp_buf, 0),
    )

    def copies(chunk):
        return [
            pltpu.make_async_copy(
                src.at[pl.ds(chunk * depth, depth)],
                dst.at[pl.ds(chunk * depth + shift, depth)],
                sems.at[i, chunk],
            )
            for i, (src, dst, shift) in enumerate(moves)
        ]

    for chunk in range(chunks):
        for copy in copies(chunk):
            copy.start()

    zeros = jnp.zeros((rows, cols), F32)
    for pad in (temp_pad, w_pad):
        pad[0] = zeros
        pad[levels + 1] = zeros
    for field in range(2):
        forward[field, 0] = zeros
        first[field] = zeros
    coefficients(lower, upper, metric, table, scalars)

    def level_step(level, carry):
        half_u = 0.5 * u_buf[level]
        half_v = 0.5 * v_buf[level]
        u_next, u_last = HORIZ_DIFF - half_u, HORIZ_DIFF + half_u
        v_next, v_last = HORIZ_DIFF - half_v, HORIZ_DIFF + half_v
        pivot = table[level, pl.ds(PIVOT_NEW, 1), :]
        lower_pivot = table[level, pl.ds(LOWER_PIVOT, 1), :]
        green = table[level, pl.ds(FIRST_GREEN, 1), :]
        slope = metric[level]
        cells = (temp_pad[level + 1], w_pad[level + 1])
        for field, (pad, prev) in enumerate(((temp_pad, tp_buf), (w_pad, wp_buf))):
            here, other = cells[field], cells[1 - field]
            sides = (
                pltpu.roll(u_next * here, rows - 1, 0)
                + pltpu.roll(u_last * here, 1, 0)
                + pltpu.roll(v_next * here, cols - 1, 1)
                + pltpu.roll(v_last * here, 1, 1)
            )
            rise = w_pad[level + 2] * pad[level + 2] - w_pad[level] * pad[level]
            change = sides - slope * rise + (other - (4.0 * HORIZ_DIFF) * here)
            tend[field, level] = change
            right = change + (FIELD_WEIGHT * here - PREV_WEIGHT * prev[level])
            forward[field, level + 1] = pivot * right + lower_pivot * forward[field, level]
            first[field] = first[field] + green * right
        return carry

    for copy in copies(0):
        copy.wait()
    for chunk in range(chunks):
        begin, end = chunk * depth, (chunk + 1) * depth
        if chunk + 1 < chunks:
            for copy in copies(chunk + 1):
                copy.wait()
        lax.fori_loop(begin, end, level_step, 0)


def bulk(lower, upper, metric, temp, u_vel, v_vel, w_vel, temp_prev, w_prev):
    levels, rows, cols = temp.shape
    chunks = 4
    block = pltpu.VMEM((levels, rows, cols), F32)
    return pl.pallas_call(
        functools.partial(bulk_kernel, chunks),
        out_shape=(
            held(levels + 2, rows, cols),
            held(levels + 2, rows, cols),
            held(2, levels + 1, rows, cols),
            held(2, levels, rows, cols),
            held(2, rows, cols),
            held(levels, TILE, cols),
            held(TILE, cols),
        ),
        in_specs=[whole(pltpu.SMEM)] * 3 + [whole(pl.ANY)] * 6,
        out_specs=[whole(VMEM)] * 7,
        scratch_shapes=[block] * 4 + [pltpu.SemaphoreType.DMA((6, chunks))],
        compiler_params=pltpu.CompilerParams(vmem_limit_bytes=24 * MIB),
        cost_estimate=pl.CostEstimate(
            flops=70 * levels * rows * cols,
            bytes_accessed=24 * levels * rows * cols,
            transcendentals=0,
        ),
        name="bulk",
    )(lower, upper, metric, *in_hbm(temp, u_vel, v_vel, w_vel, temp_prev, w_prev))


def side_changes(to_left, to_right, from_left, from_right):
    return from_left[...] - to_right[...], from_right[...] - to_left[...]


def ends(rows, cols, head, tail):
    at = lax.broadcasted_iota(jnp.int32, (rows, cols), 0)
    return jnp.where(at == 0, head, jnp.where(at == rows - 1, tail, 0.0))


def fix_kernel(
    levels, to_left, to_right, from_left, from_right, outer, inner, forward, first, table, scalars,
    message, changes,
):
    _, rows, cols = first.shape
    diffs = side_changes(to_left, to_right, from_left, from_right)
    upper = bit_of("gz", 0) == 1

    def scalar(at):
        return scalars[pl.ds(at, 1), :]

    below, above = scalar(METRIC_BELOW), scalar(METRIC_ABOVE)
    first_gain = jnp.where(upper, -above * scalar(CORNER), below * scalar(FIRST))
    last_gain = jnp.where(upper, -above * scalar(LAST), below * scalar(CORNER))
    for field in range(2):
        firsts, lasts = [], []
        for side in range(2):
            value = jnp.zeros((1, cols), F32)
            total = jnp.zeros((1, cols), F32)
            for level in range(levels):
                right = diffs[side][field * levels + level : field * levels + level + 1, :]
                value = (
                    table[level, pl.ds(PIVOT_NEW, 1), :] * right
                    + table[level, pl.ds(LOWER_PIVOT, 1), :] * value
                )
                total = total + table[level, pl.ds(FIRST_GREEN, 1), :] * right
                changes[pl.ds((side * 2 + field) * levels + level, 1), :] = value
            firsts.append(total)
            lasts.append(value)
        flux = outer[pl.ds(field * rows, rows), :]
        message[pl.ds(field * rows, rows), :] = (
            first[field] + first_gain * flux + ends(rows, cols, *firsts)
        )
        message[pl.ds((2 + field) * rows, rows), :] = (
            forward[field, levels] + last_gain * flux + ends(rows, cols, *lasts)
        )
    message[pl.ds(4 * rows, 2 * rows), :] = inner[...]
    message[pl.ds(6 * rows, TILE), :] = scalars[...]


def fix(to_left, to_right, from_left, from_right, outer, inner, forward, first, table, scalars):
    levels = table.shape[0]
    _, rows, cols = first.shape
    return pl.pallas_call(
        functools.partial(fix_kernel, levels),
        out_shape=(held(6 * rows + TILE, cols), held(4 * levels, cols)),
        in_specs=[whole(VMEM)] * 10,
        out_specs=[whole(VMEM)] * 2,
        compiler_params=pltpu.CompilerParams(vmem_limit_bytes=8 * MIB),
        name="fix",
    )(
        to_left, to_right, from_left, from_right, outer, inner,
        in_vmem(forward), in_vmem(first), in_vmem(table), scalars,
    )


def tends_kernel(
    metric, tend, to_left, to_right, from_left, from_right, outer, other,
    temp_tend, w_tend, layers, strips, sems,
):
    _, levels, rows, cols = tend.shape
    inside = pl.ds(1, levels - 2)
    outs = (temp_tend, w_tend)
    copies = [
        pltpu.make_async_copy(
            tend.at[field, inside, pl.ds(TILE, rows - 2 * TILE), :],
            outs[field].at[inside, pl.ds(TILE, rows - 2 * TILE), :],
            sems.at[field],
        )
        for field in range(2)
    ]
    for copy in copies:
        copy.start()
    upper = bit_of("gz", 0) == 1
    diffs = side_changes(to_left, to_right, from_left, from_right)
    tile_at = lax.broadcasted_iota(jnp.int32, (TILE, cols), 0)
    for field in range(2):
        out = outs[field]
        near = other[pl.ds((4 + field) * rows, rows), :]
        far = outer[pl.ds(field * rows, rows), :]
        below = jnp.where(upper, near, far)
        above = jnp.where(upper, far, near)
        for side, level, change in (
            (0, 0, metric[0] * below),
            (1, levels - 1, -metric[levels - 1] * above),
        ):
            at = field * levels + level
            rim = ends(rows, cols, diffs[0][at : at + 1, :], diffs[1][at : at + 1, :])
            layers[field, side] = tend[field, level] + change + rim
            copies.append(
                pltpu.make_async_copy(
                    layers.at[field, side], out.at[level], sems.at[2 + 2 * field + side]
                )
            )
            copies[-1].start()
        for side, begin, row in ((0, 0, 0), (1, rows - TILE, TILE - 1)):
            for level in range(1, levels - 1):
                at = field * levels + level
                strips[field, side, level] = tend[field, level, pl.ds(begin, TILE), :] + jnp.where(
                    tile_at == row, diffs[side][at : at + 1, :], 0.0
                )
            copies.append(
                pltpu.make_async_copy(
                    strips.at[field, side, inside],
                    out.at[inside, pl.ds(begin, TILE), :],
                    sems.at[6 + 2 * field + side],
                )
            )
            copies[-1].start()
    for copy in copies:
        copy.wait()


def tends(metric, tend, to_left, to_right, from_left, from_right, outer, other):
    _, levels, rows, cols = tend.shape
    return pl.pallas_call(
        tends_kernel,
        out_shape=(jax.ShapeDtypeStruct((levels, rows, cols), F32),) * 2,
        in_specs=[whole(pltpu.SMEM)] + [whole(VMEM)] * 7,
        out_specs=[whole(pl.ANY)] * 2,
        scratch_shapes=[
            pltpu.VMEM((2, 2, rows, cols), F32),
            pltpu.VMEM((2, 2, levels, TILE, cols), F32),
            pltpu.SemaphoreType.DMA((10,)),
        ],
        compiler_params=pltpu.CompilerParams(vmem_limit_bytes=8 * MIB),
        cost_estimate=pl.CostEstimate(
            flops=levels * rows * cols,
            bytes_accessed=8 * levels * rows * cols,
            transcendentals=0,
        ),
        name="tends",
    )(metric, in_vmem(tend), to_left, to_right, from_left, from_right, outer, other)


def interface(low, high):
    coupling = low[ABOVE]
    return coupling, 1.0 / (1.0 - coupling * coupling * low[LAST] * high[FIRST])


def scalar_rows(ref, begin):
    return [ref[pl.ds(begin + at, 1), :] for at in range(7)]


def merge_kernel(bit, with_flux, halves, mine, theirs, message, base, gains):
    _, rows, cols = base.shape
    upper = bit_of("gz", bit) == 1
    parts = 6 if with_flux else 4
    own, far = scalar_rows(mine, parts * rows), scalar_rows(theirs, parts * rows)
    low = [jnp.where(upper, b, a) for a, b in zip(own, far)]
    high = [jnp.where(upper, a, b) for a, b in zip(own, far)]
    coupling, inverse = interface(low, high)
    to_high, to_low = high[FIRST] * coupling, low[LAST] * coupling
    low_out, high_out = low[CORNER] * coupling, high[CORNER] * coupling
    if halves:
        sends_last = bit_of("gz", bit + 1) == 0
    for field in range(2):

        def part(at):
            a = mine[pl.ds((at + field) * rows, rows), :]
            b = theirs[pl.ds((at + field) * rows, rows), :]
            return jnp.where(upper, b, a), jnp.where(upper, a, b)

        (low_first, high_first), (low_last, high_last) = part(0), part(2)
        if with_flux:
            low_flux, high_flux = part(4)
            low_first = low_first - (low[CORNER] * low[METRIC_ABOVE]) * high_flux
            low_last = low_last - (low[LAST] * low[METRIC_ABOVE]) * high_flux
            high_first = high_first + (high[FIRST] * high[METRIC_BELOW]) * low_flux
            high_last = high_last + (high[CORNER] * high[METRIC_BELOW]) * low_flux
        above = inverse * (high_first + to_high * low_last)
        below = inverse * (low_last + to_low * high_first)
        into = coupling * jnp.where(upper, below, above)
        if with_flux:
            into = into + jnp.where(
                upper, high[METRIC_BELOW] * low_flux, -low[METRIC_ABOVE] * high_flux
            )
        base[field] = into
        all_first = low_first + low_out * above
        all_last = high_last + high_out * below
        if halves:
            message[pl.ds(field * rows, rows), :] = jnp.where(sends_last, all_last, all_first)
        else:
            message[pl.ds(field * rows, rows), :] = all_first
            message[pl.ds((2 + field) * rows, rows), :] = all_last
    scalars = [
        low[FIRST] + low_out * inverse * to_high * low[CORNER],
        low_out * inverse * high[CORNER],
        high[LAST] + high_out * inverse * to_low * high[CORNER],
        low[BELOW],
        high[ABOVE],
        low[METRIC_BELOW],
        high[METRIC_ABOVE],
    ]
    begin = (2 if halves else 4) * rows
    for at, value in enumerate(scalars):
        message[pl.ds(begin + at, 1), :] = value
    message[pl.ds(begin + 7, 1), :] = jnp.zeros((1, cols), F32)
    scale = coupling * inverse
    gains[...] = jnp.zeros(gains.shape, F32)
    gains[pl.ds(FROM_ABOVE, 1), :] = (
        scale * high[CORNER] * jnp.where(upper, to_low, 1.0)
    )
    gains[pl.ds(FROM_BELOW, 1), :] = (
        scale * low[CORNER] * jnp.where(upper, 1.0, to_high)
    )


def merge(bit, with_flux, halves, rows, mine, theirs):
    cols = mine.shape[1]
    return pl.pallas_call(
        functools.partial(merge_kernel, bit, with_flux, halves),
        out_shape=(
            held((2 if halves else 4) * rows + TILE, cols),
            held(2, rows, cols),
            held(TILE, cols),
        ),
        in_specs=[whole(VMEM)] * 2,
        out_specs=[whole(VMEM)] * 3,
        compiler_params=pltpu.CompilerParams(vmem_limit_bytes=8 * MIB),
        name="merge",
    )(mine, theirs)


def finish_kernel(
    rounds, strips, temp_pad, w_pad, forward, table, changes, scalars, outer, mine, theirs, *rest
):
    bases, gains = rest[: rounds - 1], rest[rounds - 1 : 2 * rounds - 2]
    temp_next, w_next, result, below_in, above_in, sems = rest[2 * rounds - 2 :]
    levels = table.shape[0]
    _, _, rows, cols = forward.shape
    upper = bit_of("gz", rounds - 1) == 1
    own, far = scalar_rows(mine, 2 * rows), scalar_rows(theirs, 2 * rows)
    low = [jnp.where(upper, b, a) for a, b in zip(own, far)]
    high = [jnp.where(upper, a, b) for a, b in zip(own, far)]
    coupling, inverse = interface(low, high)
    to_other = coupling * jnp.where(upper, low[LAST], high[FIRST])
    scale = coupling * inverse
    for field in range(2):
        at = pl.ds(field * rows, rows)
        into = scale * (theirs[at, :] + to_other * mine[at, :])
        zero = jnp.zeros((rows, cols), F32)
        below, above = jnp.where(upper, into, zero), jnp.where(upper, zero, into)
        for step in range(rounds - 2, -1, -1):
            side = bit_of("gz", step) == 1
            into = (
                bases[step][field]
                + gains[step][pl.ds(FROM_ABOVE, 1), :] * above
                + gains[step][pl.ds(FROM_BELOW, 1), :] * below
            )
            below, above = jnp.where(side, into, below), jnp.where(side, above, into)
        side = bit_of("gz", 0) == 1
        flux = outer[at, :]
        gain_below = jnp.where(side, 0.0, scalars[pl.ds(METRIC_BELOW, 1), :])
        gain_above = jnp.where(side, -scalars[pl.ds(METRIC_ABOVE, 1), :], 0.0)
        below_in[field] = below + gain_below * flux
        above_in[field] = above + gain_above * flux

    size = rows // strips
    row_at = lax.broadcasted_iota(jnp.int32, (TILE, cols), 0)
    copies = []
    for field, (pad, out) in enumerate(((temp_pad, temp_next), (w_pad, w_next))):
        for strip in range(strips):
            at = pl.ds(strip * size, size)
            below = below_in[field, at, :]

            def solve(level, carry, factor, field=field, strip=strip, at=at, below=below, pad=pad):
                value = (
                    forward[field, level + 1, at, :]
                    + table[level, pl.ds(BELOW_FORWARD, 1), :] * below
                    + factor * carry
                )
                if strip == 0:
                    change = changes[pl.ds(field * levels + level, 1), :]
                    value = jnp.concatenate(
                        [value[:TILE] + jnp.where(row_at == 0, change, 0.0), value[TILE:]]
                    )
                if strip == strips - 1:
                    change = changes[pl.ds((2 + field) * levels + level, 1), :]
                    value = jnp.concatenate(
                        [value[:-TILE], value[-TILE:] + jnp.where(row_at == TILE - 1, change, 0.0)]
                    )
                result[field, level, at, :] = value - pad[level + 1, at, :]
                return value

            carry = solve(levels - 1, above_in[field, at, :], table[levels - 1, pl.ds(PIVOT, 1), :])

            def step(back, carry, solve=solve):
                level = levels - 2 - back
                return solve(level, carry, table[level, pl.ds(UPPER_PIVOT, 1), :])

            lax.fori_loop(0, levels - 1, step, carry)
            copies.append(
                pltpu.make_async_copy(
                    result.at[field, :, at, :], out.at[:, at, :], sems.at[field, strip]
                )
            )
            copies[-1].start()
    for copy in copies:
        copy.wait()


def finish(rounds, temp_pad, w_pad, forward, table, changes, scalars, outer, mine, theirs, bases, gains):
    levels = table.shape[0]
    _, _, rows, cols = forward.shape
    strips = 2
    return pl.pallas_call(
        functools.partial(finish_kernel, rounds, strips),
        out_shape=(jax.ShapeDtypeStruct((levels, rows, cols), F32),) * 2,
        in_specs=[whole(VMEM)] * (7 + 2 + 2 * (rounds - 1)),
        out_specs=[whole(pl.ANY)] * 2,
        scratch_shapes=[
            pltpu.VMEM((2, levels, rows, cols), F32),
            pltpu.VMEM((2, rows, cols), F32),
            pltpu.VMEM((2, rows, cols), F32),
            pltpu.SemaphoreType.DMA((2, strips)),
        ],
        compiler_params=pltpu.CompilerParams(vmem_limit_bytes=16 * MIB),
        name="finish",
    )(
        in_vmem(temp_pad), in_vmem(w_pad), in_vmem(forward), in_vmem(table), changes, scalars,
        outer, mine, theirs, *bases, *gains,
    )


def local(temp, u_vel, v_vel, w_vel, temp_prev, w_prev, lower, upper, metric):
    _, rows, _ = temp.shape
    across, stacked = lax.axis_size("gx"), lax.axis_size("gz")
    rounds = stacked.bit_length() - 1
    to_left, to_right, outer, inner = edges(temp, u_vel, w_vel)
    from_right = lax.ppermute(to_left, "gx", [((i + 1) % across, i) for i in range(across)])
    from_left = lax.ppermute(to_right, "gx", [(i, (i + 1) % across) for i in range(across)])
    seams = [(i, i + 1) for i in range(1, stacked - 1, 2)]
    outer = lax.ppermute(outer, "gz", seams + [(b, a) for a, b in seams])
    temp_pad, w_pad, forward, tend, first, table, scalars = bulk(
        lower, upper, metric, temp, u_vel, v_vel, w_vel, temp_prev, w_prev
    )
    mine, changes = fix(
        to_left, to_right, from_left, from_right, outer, inner, forward, first, table, scalars
    )
    bases, gains = [], []
    for step in range(rounds):
        theirs = lax.ppermute(mine, "gz", [(i, i ^ (1 << step)) for i in range(stacked)])
        if step == 0:
            temp_tend, w_tend = tends(
                metric, tend, to_left, to_right, from_left, from_right, outer, theirs
            )
        if step + 1 < rounds:
            mine, base, gain = merge(step, step == 0, step + 2 == rounds, rows, mine, theirs)
            bases.append(base)
            gains.append(gain)
    temp_next, w_next = finish(
        rounds, temp_pad, w_pad, forward, table, changes, scalars, outer, mine, theirs, bases, gains
    )
    return temp_next, w_next, temp_tend, w_tend


def solution(mesh):
    field = P("gz", "gx", None)
    return jax.shard_map(
        local,
        mesh=mesh,
        in_specs=(field,) * 6 + (P("gz"),) * 3,
        out_specs=(field,) * 4,
        check_vma=False,
    )
```

time: 142 us -> 26.6 us (0.19); the launches traced: 140 us -> 26.5 us
  between operations: 43.1 us -> 0.72 us
  other arithmetic: 35.3 us -> 0 us
  local copies, waits for them, and re-layouts: 27.3 us -> 0.01 us
  blocking collectives: 16 us -> 0 us
  Pallas kernels: 0 us -> 10.9 us
  starting transfers between devices: 15.2 us -> 9.98 us
  waiting for transfers between devices: 0.02 us -> 4.85 us
  matrix products: 3.5 us -> 0 us
    add x4 -> x0, other arithmetic: 12.1 us -> none  [the longest x1 8.9 us: local(): fields + vertical + NEW_WEIGHT * tendency]
    slice x11 -> x0, local copies, waits for them, and re-layouts: 11.8 us -> none  [the longest x2 4.42 us: local(): advect = advect + 0.5 * (jnp.roll(flux_y, -1, 3) - jnp.roll(flux_y, 1, 3))]
    pallas_call x0 -> x6, Pallas kernels: none -> 10.9 us  [the longest x1 5.68 us: bulk(): pl.pallas_call(functools.partial(bulk_kernel, chunks), out_shape=(held(le...]
    unnamed x27 -> x6, local copies, waits for them, and re-layouts: 8.69 us -> 0.01 us
    all_gather x1 -> x0, blocking collectives: 8.07 us -> none  [local(): lax.all_gather(reduced[None], 'gz', axis=0, tiled=True)]
    div x1 -> x0, other arithmetic: 8.02 us -> none  [forward(): value_new = (rhs_row - low_val * value_prev) / pivot_val]
    unnamed x1 -> x0, blocking collectives: 7.93 us -> none
    another operation x4 -> x0, other arithmetic: 5.91 us -> none  [the longest x3 5.25 us: local(): fields = jnp.stack((temp, w_vel))]
  transfers between devices with their start and end apart: 7 -> 5, of which waited for: 0 -> 3; matrix products, arithmetic and copies ran while one was open for 21% -> 0% of each run, Pallas kernels for 0% -> 29%
where the time goes in v1:
time: 26.6 us; the launch traced here: 26.5 us
  Pallas kernels  10.9 us (41%)
  starting transfers between devices  9.98 us (38%)
  waiting for transfers between devices  4.85 us (18%)
  between operations  0.72 us (3%)
    ppermute x1, starting transfers between devices, local(): lax.ppermute(to_left, 'gx', [((i + 1) % across, i) for i in range(across)])  6.06 us
    pallas_call x1, Pallas kernels, bulk(): pl.pallas_call(functools.partial(bulk_kernel, chunks), out_shape=(held(le...  5.68 us
    ppermute x2, waiting for transfers between devices, local(): lax.ppermute(mine, 'gz', [(i, i ^ 1 << step) for i in range(stacked)])  3.95 us
    ppermute x2, starting transfers between devices, local(): lax.ppermute(mine, 'gz', [(i, i ^ 1 << step) for i in range(stacked)])  3.25 us
    pallas_call x1, Pallas kernels, tends(): pl.pallas_call(tends_kernel, out_shape=(jax.ShapeDtypeStruct((levels, row...  1.92 us
    pallas_call x1, Pallas kernels, finish(): pl.pallas_call(functools.partial(finish_kernel, rounds, strips), out_shap...  1.62 us
    pallas_call x1, Pallas kernels, edges(): pl.pallas_call(edges_kernel, out_shape=(held(2 * levels, cols), held(2 *...  1.41 us
    ppermute x1, waiting for transfers between devices, local(): lax.ppermute(to_right, 'gx', [(i, (i + 1) % across) for i in range(across)])  0.89 us
  transfers between devices with their start and end apart: 5, of which 3 were waited for; matrix products, arithmetic and copies ran while one was open for 0% of the time, Pallas kernels for 29%

profile of v1, /device:TPU:0, one launch (start us, length us, event | category | flops | bytes accessed | tf_op | source)
XLA Modules:
  0.0 26.5 jit_solution(5834796237767696766)
XLA Ops:
  0.6 0.0 copy-start
  0.6 0.0 copy-start.2
  0.7 0.0 copy-start.1
  0.7 1.4 %edges.1 = (f32[32,256]{1,0:T(8,128)S(1)}, f32[32,256]{1,0:T(8,128)S(1)}, f32[128,256]{1,0:T(8,128)S(1)}, f32[128,256]{1,0:T(8,128)S(1)}) custom-call(f32[16,64,256]{2,1,0:T(8,128)} %temp.3, f32[16,64,256]{2,1,0:T(8,128)} %u_vel.3, f32[16,64,256]{2,1,0:T(8,128)} %w_vel.3), custom_call_target="tpu_custom_call" | custom-call | tf_op jit(solution)/shard_map/edges/pallas_call | solution.py:77
  2.1 0.7 %collective-permute-start.2 = (f32[128,256]{1,0:T(8,128)S(1)}, f32[128,256]{1,0:T(8,128)S(1)}, u32[]{:S(2)}, u32[]{:S(2)}) collective-permute-start(f32[128,256]{1,0:T(8,128)S(1)} %get-tuple-element.30), channel_id=1, source_target_pairs={{1,2},{2,1},{5,6},{6,5},{9,10},{10,9},{13,14},{14,13},{17,18},{18,... | collective-permute-start | bytes 393224 | tf_op jit(solution)/shard_map/ppermute | solution.py:598
  2.8 6.1 %collective-permute-start.1 = (f32[32,256]{1,0:T(8,128)S(1)}, f32[32,256]{1,0:T(8,128)S(1)}, u32[]{:S(2)}, u32[]{:S(2)}) collective-permute-start(f32[32,256]{1,0:T(8,128)S(1)} %get-tuple-element.28.to_left), channel_id=1, source_target_pairs={{4,0},{8,4},{12,8},{16,12},{20,16},{24,20},{28,24},{0,28},{5,1},{9... | collective-permute-start | bytes 98312 | tf_op jit(solution)/shard_map/ppermute | solution.py:595
  8.8 0.0 collective-permute-start
  8.8 0.0 copy-done
  8.8 0.0 copy-done.2
  8.8 0.0 copy-done.1
  8.8 5.7 %bulk.1 = (f32[18,64,256]{2,1,0:T(8,128)S(1)}, f32[18,64,256]{2,1,0:T(8,128)S(1)}, f32[2,17,64,256]{3,2,1,0:T(8,128)S(1)}, f32[2,16,64,256]{3,2,1,0:T(8,128)S(1)...) custom-call(f32[16]{0:T(128)S(1)} %copy-done.1, f32[16]{0:T(128)S(1)} %copy-done.2, ...), custom_call_target="tpu_custom_call" | custom-call | flops 18350080 | bytes 6291456 | tf_op jit(solution)/shard_map/bulk/pallas_call | solution.py:232
  14.5 0.0 collective-permute-done.1.from_right
  14.5 0.9 %collective-permute-done.from_left = f32[32,256]{1,0:T(8,128)S(1)} collective-permute-done((f32[32,256]{1,0:T(8,128)S(1)}, f32[32,256]{1,0:T(8,128)S(1)}, u32[]{:S(2)}, u32[]{:S(2)}) %collective-permute-start) | collective-permute-done | bytes 32800 | tf_op jit(solution)/shard_map/ppermute | solution.py:596
  15.4 0.0 collective-permute-done.2.outer
  15.4 0.1 fix.1
  15.6 1.8 %collective-permute-start.3 = (f32[392,256]{1,0:T(8,128)S(1)}, f32[392,256]{1,0:T(8,128)S(1)}, u32[]{:S(2)}, u32[]{:S(2)}) collective-permute-start(f32[392,256]{1,0:T(8,128)S(1)} %get-tuple-element.35.mine), channel_id=1, source_target_pairs={{0,1},{1,0},{2,3},{3,2},{4,5},{5,4},{6,7},{7,6},{8,9},{9,8},{10,11... | collective-permute-start | bytes 1204232 | tf_op jit(solution)/shard_map/ppermute | solution.py:607
  17.3 1.4 %collective-permute-done.3.theirs.other = f32[392,256]{1,0:T(8,128)S(1)} collective-permute-done((f32[392,256]{1,0:T(8,128)S(1)}, f32[392,256]{1,0:T(8,128)S(1)}, u32[]{:S(2)}, u32[]{:S(2)}) %collective-permute-start.3) | collective-permute-done | bytes 401440 | tf_op jit(solution)/shard_map/ppermute | solution.py:607
  18.7 0.2 merge.1
  18.8 1.5 %collective-permute-start.4 = (f32[136,256]{1,0:T(8,128)S(1)}, f32[136,256]{1,0:T(8,128)S(1)}, u32[]{:S(2)}, u32[]{:S(2)}) collective-permute-start(f32[136,256]{1,0:T(8,128)S(1)} %get-tuple-element.36.mine), channel_id=1, source_target_pairs={{0,2},{1,3},{2,0},{3,1},{4,6},{5,7},{6,4},{7,5},{8,10},{9,11},{10,... | collective-permute-start | bytes 417800 | tf_op jit(solution)/shard_map/ppermute | solution.py:607
  20.3 1.9 %tends.1 = (f32[16,64,256]{2,1,0:T(8,128)}, f32[16,64,256]{2,1,0:T(8,128)}) custom-call(f32[16]{0:T(128)S(1)} %copy-done, f32[2,16,64,256]{3,2,1,0:T(8,128)S(1)} %get-tuple-element.41.tend, f32[32,256]{1,0:T(8,128)S(1)} %get-tuple-element.28.to_left, f32[32,256]{1,0:T(8,128)S(1)} %get-tuple-element.29.to_right, ...), custom_call_target="tpu_custom_call" | custom-call | flops 262144 | bytes 2097152 | tf_op jit(solution)/shard_map/tends/pallas_call | solution.py:380
  22.3 2.6 %collective-permute-done.4.theirs = f32[136,256]{1,0:T(8,128)S(1)} collective-permute-done((f32[136,256]{1,0:T(8,128)S(1)}, f32[136,256]{1,0:T(8,128)S(1)}, u32[]{:S(2)}, u32[]{:S(2)}) %collective-permute-start.4) | collective-permute-done | bytes 139296 | tf_op jit(solution)/shard_map/ppermute | solution.py:607
  24.9 1.6 %finish.1 = (f32[16,64,256]{2,1,0:T(8,128)}, f32[16,64,256]{2,1,0:T(8,128)}) custom-call(f32[18,64,256]{2,1,0:T(8,128)S(1)} %get-tuple-element.24.temp_pad, f32[18,64,256]{2,1,0:T(8,128)S(1)} %get-tuple-element.25.w_pad, f32[2,17,64,256]{3,2,1,0:T(8,128)S(1)} %get-tuple-element.26.forward, f32[16,8,256]{2,1,0:T(8,128)S(1)} %get-tuple-element.27.table, ...), custom_call_target="tpu_custom_call" | custom-call | tf_op jit(solution)/shard_map/finish/pallas_call | solution.py:571
Async XLA Ops:
  0.6 8.2 %copy-start = (f32[16]{0:T(128)S(1)}, f32[16]{0:T(128)}, u32[]{:S(2)}) copy-start(f32[16]{0:T(128)} %metric.3) | copy-start | bytes 196
  0.6 8.2 %copy-start.2 = (f32[16]{0:T(128)S(1)}, f32[16]{0:T(128)}, u32[]{:S(2)}) copy-start(f32[16]{0:T(128)} %upper.1) | copy-start | bytes 196
  0.7 8.2 %copy-start.1 = (f32[16]{0:T(128)S(1)}, f32[16]{0:T(128)}, u32[]{:S(2)}) copy-start(f32[16]{0:T(128)} %lower.1) | copy-start | bytes 196
  2.1 13.3 %collective-permute-start.2 = (f32[128,256]{1,0:T(8,128)S(1)}, f32[128,256]{1,0:T(8,128)S(1)}, u32[]{:S(2)}, u32[]{:S(2)}) collective-permute-start(f32[128,256]{1,0:T(8,128)S(1)} %get-tuple-element.30), channel_id=1, source_target_pairs={{1,2},{2,1},{5,6},{6,5},{9,10},{10,9},{13,14},{14,13},{17,18},{18,... | collective-permute-start | bytes 393224 | tf_op jit(solution)/shard_map/ppermute | solution.py:598
  2.8 11.8 %collective-permute-start.1 = (f32[32,256]{1,0:T(8,128)S(1)}, f32[32,256]{1,0:T(8,128)S(1)}, u32[]{:S(2)}, u32[]{:S(2)}) collective-permute-start(f32[32,256]{1,0:T(8,128)S(1)} %get-tuple-element.28.to_left), channel_id=1, source_target_pairs={{4,0},{8,4},{12,8},{16,12},{20,16},{24,20},{28,24},{0,28},{5,1},{9... | collective-permute-start | bytes 98312 | tf_op jit(solution)/shard_map/ppermute | solution.py:595
  8.8 6.6 %collective-permute-start = (f32[32,256]{1,0:T(8,128)S(1)}, f32[32,256]{1,0:T(8,128)S(1)}, u32[]{:S(2)}, u32[]{:S(2)}) collective-permute-start(f32[32,256]{1,0:T(8,128)S(1)} %get-tuple-element.29.to_right), channel_id=1, source_target_pairs={{0,4},{4,8},{8,12},{12,16},{16,20},{20,24},{24,28},{28,0},{1,5},{5... | collective-permute-start | bytes 98312 | tf_op jit(solution)/shard_map/ppermute | solution.py:596
  15.6 3.1 %collective-permute-start.3 = (f32[392,256]{1,0:T(8,128)S(1)}, f32[392,256]{1,0:T(8,128)S(1)}, u32[]{:S(2)}, u32[]{:S(2)}) collective-permute-start(f32[392,256]{1,0:T(8,128)S(1)} %get-tuple-element.35.mine), channel_id=1, source_target_pairs={{0,1},{1,0},{2,3},{3,2},{4,5},{5,4},{6,7},{7,6},{8,9},{9,8},{10,11... | collective-permute-start | bytes 1204232 | tf_op jit(solution)/shard_map/ppermute | solution.py:607
  18.8 6.0 %collective-permute-start.4 = (f32[136,256]{1,0:T(8,128)S(1)}, f32[136,256]{1,0:T(8,128)S(1)}, u32[]{:S(2)}, u32[]{:S(2)}) collective-permute-start(f32[136,256]{1,0:T(8,128)S(1)} %get-tuple-element.36.mine), channel_id=1, source_target_pairs={{0,2},{1,3},{2,0},{3,1},{4,6},{5,7},{6,4},{7,5},{8,10},{9,11},{10,... | collective-permute-start | bytes 417800 | tf_op jit(solution)/shard_map/ppermute | solution.py:607

commit v2 on v1

--- a/solution.py
+++ b/solution.py
@@ -42,7 +42,7 @@
     return (lax.axis_index(axis) >> bit) & 1
 
 
-def edges_kernel(temp, u_vel, w_vel, to_left, to_right, outer, inner, strips, layers, sems):
+def edges_kernel(temp, u_vel, w_vel, v_vel, temp_prev, w_prev, near, far, outer, inner, strips, layers, sems):
     levels, rows, _ = temp.shape
     copies = []
     for at, array in enumerate((temp, w_vel, u_vel)):
@@ -56,13 +56,14 @@
         copy.start()
     for copy in copies:
         copy.wait()
+    odd = bit_of("gx", 0) == 1
+    last = TILE - 1
     for field in range(2):
         at = pl.ds(field * levels, levels)
-        to_left[at, :] = (HORIZ_DIFF - 0.5 * strips[2, 0, :, 0, :]) * strips[field, 0, :, 0, :]
-        last = TILE - 1
-        to_right[at, :] = (HORIZ_DIFF + 0.5 * strips[2, 1, :, last, :]) * strips[
-            field, 1, :, last, :
-        ]
+        to_left = (HORIZ_DIFF - 0.5 * strips[2, 0, :, 0, :]) * strips[field, 0, :, 0, :]
+        to_right = (HORIZ_DIFF + 0.5 * strips[2, 1, :, last, :]) * strips[field, 1, :, last, :]
+        near[at, :] = jnp.where(odd, to_left, to_right)
+        far[at, :] = jnp.where(odd, to_right, to_left)
     upper = bit_of("gz", 0) == 1
     for field in range(2):
         at = pl.ds(field * rows, rows)
@@ -72,7 +73,7 @@
         inner[at, :] = jnp.where(upper, bottom, top)
 
 
-def edges(temp, u_vel, w_vel):
+def edges(temp, u_vel, w_vel, *later):
     levels, rows, cols = temp.shape
     return pl.pallas_call(
         edges_kernel,
@@ -82,7 +83,7 @@
             held(2 * rows, cols),
             held(2 * rows, cols),
         ),
-        in_specs=[whole(pl.ANY)] * 3,
+        in_specs=[whole(pl.ANY)] * 6,
         out_specs=[whole(VMEM)] * 4,
         scratch_shapes=[
             pltpu.VMEM((3, 2, levels, TILE, cols), F32),
@@ -91,7 +92,7 @@
         ],
         compiler_params=pltpu.CompilerParams(vmem_limit_bytes=8 * MIB),
         name="edges",
-    )(*in_hbm(temp, u_vel, w_vel))
+    )(*in_hbm(temp, u_vel, w_vel, *later))
 
 
 def coefficients(lower, upper, metric, table, scalars):
@@ -132,7 +133,6 @@
 
 
 def bulk_kernel(
-    chunks,
     lower,
     upper,
     metric,
@@ -142,119 +142,100 @@
     w_vel,
     temp_prev,
     w_prev,
-    temp_pad,
-    w_pad,
     forward,
     tend,
     first,
     table,
     scalars,
-    u_buf,
-    v_buf,
-    tp_buf,
-    wp_buf,
-    sems,
 ):
     levels, rows, cols = temp.shape
-    depth = levels // chunks
-    moves = (
-        (temp, temp_pad, 1),
-        (w_vel, w_pad, 1),
-        (u_vel, u_buf, 0),
-        (v_vel, v_buf, 0),
-        (temp_prev, tp_buf, 0),
-        (w_prev, wp_buf, 0),
-    )
-
-    def copies(chunk):
-        return [
-            pltpu.make_async_copy(
-                src.at[pl.ds(chunk * depth, depth)],
-                dst.at[pl.ds(chunk * depth + shift, depth)],
-                sems.at[i, chunk],
+    strips = rows // TILE
+    fields, prevs = (temp, w_vel), (temp_prev, w_prev)
+    coefficients(lower, upper, metric, table, scalars)
+    for field in range(2):
+        forward[field, 0] = jnp.zeros((rows, cols), F32)
+        first[field] = jnp.zeros((rows, cols), F32)
+    row_at = lax.broadcasted_iota(jnp.int32, (TILE, cols), 0)
+    zero = jnp.zeros((TILE, cols), F32)
+
+    def level_step(level, carry):
+        pivot = jnp.broadcast_to(table[level, pl.ds(PIVOT_NEW, 1), :], (TILE, cols))
+        lower_pivot = jnp.broadcast_to(table[level, pl.ds(LOWER_PIVOT, 1), :], (TILE, cols))
+        green = jnp.broadcast_to(table[level, pl.ds(FIRST_GREEN, 1), :], (TILE, cols))
+        slope = metric[level]
+        rise = jnp.where(level < levels - 1, slope, 0.0)
+        fall = jnp.where(level > 0, slope, 0.0)
+        over = jnp.minimum(level + 1, levels - 1)
+        under = jnp.maximum(level - 1, 0)
+
+        def sides(strip):
+            at = pl.ds(strip * TILE, TILE)
+            half = 0.5 * u_vel[level, at, :]
+            back, ahead = HORIZ_DIFF - half, HORIZ_DIFF + half
+            here = [values[level, at, :] for values in fields]
+            return (
+                here,
+                [pltpu.roll(back * value, TILE - 1, 0) for value in here],
+                [pltpu.roll(ahead * value, 1, 0) for value in here],
             )
-            for i, (src, dst, shift) in enumerate(moves)
-        ]
-
-    for chunk in range(chunks):
-        for copy in copies(chunk):
-            copy.start()
-
-    zeros = jnp.zeros((rows, cols), F32)
-    for pad in (temp_pad, w_pad):
-        pad[0] = zeros
-        pad[levels + 1] = zeros
-    for field in range(2):
-        forward[field, 0] = zeros
-        first[field] = zeros
-    coefficients(lower, upper, metric, table, scalars)
-
-    def level_step(level, carry):
-        half_u = 0.5 * u_buf[level]
-        half_v = 0.5 * v_buf[level]
-        u_next, u_last = HORIZ_DIFF - half_u, HORIZ_DIFF + half_u
-        v_next, v_last = HORIZ_DIFF - half_v, HORIZ_DIFF + half_v
-        pivot = table[level, pl.ds(PIVOT_NEW, 1), :]
-        lower_pivot = table[level, pl.ds(LOWER_PIVOT, 1), :]
-        green = table[level, pl.ds(FIRST_GREEN, 1), :]
-        slope = metric[level]
-        cells = (temp_pad[level + 1], w_pad[level + 1])
-        for field, (pad, prev) in enumerate(((temp_pad, tp_buf), (w_pad, wp_buf))):
-            here, other = cells[field], cells[1 - field]
-            sides = (
-                pltpu.roll(u_next * here, rows - 1, 0)
-                + pltpu.roll(u_last * here, 1, 0)
-                + pltpu.roll(v_next * here, cols - 1, 1)
-                + pltpu.roll(v_last * here, 1, 1)
-            )
-            rise = w_pad[level + 2] * pad[level + 2] - w_pad[level] * pad[level]
-            change = sides - slope * rise + (other - (4.0 * HORIZ_DIFF) * here)
-            tend[field, level] = change
-            right = change + (FIELD_WEIGHT * here - PREV_WEIGHT * prev[level])
-            forward[field, level + 1] = pivot * right + lower_pivot * forward[field, level]
-            first[field] = first[field] + green * right
+
+        before = [zero, zero]
+        here, back, ahead = sides(0)
+        for strip in range(strips):
+            after = sides(strip + 1) if strip + 1 < strips else (None, [zero, zero], None)
+            at = pl.ds(strip * TILE, TILE)
+            half = 0.5 * v_vel[level, at, :]
+            v_back, v_ahead = HORIZ_DIFF - half, HORIZ_DIFF + half
+            w_over = rise * w_vel[over, at, :]
+            w_under = fall * w_vel[under, at, :]
+            for field in range(2):
+                value = here[field]
+                change = jnp.where(row_at == TILE - 1, after[1][field], back[field])
+                change = change + jnp.where(row_at == 0, before[field], ahead[field])
+                change = change + pltpu.roll(v_back * value, cols - 1, 1)
+                change = change + pltpu.roll(v_ahead * value, 1, 1)
+                change = change - w_over * fields[field][over, at, :]
+                change = change + w_under * fields[field][under, at, :]
+                change = change + (here[1 - field] - (4.0 * HORIZ_DIFF) * value)
+                tend[field, level, at, :] = change
+                right = change + (FIELD_WEIGHT * value - PREV_WEIGHT * prevs[field][level, at, :])
+                forward[field, level + 1, at, :] = (
+                    pivot * right + lower_pivot * forward[field, level, at, :]
+                )
+                first[field, at, :] = first[field, at, :] + green * right
+            before = ahead
+            here, back, ahead = after
         return carry
 
-    for copy in copies(0):
-        copy.wait()
-    for chunk in range(chunks):
-        begin, end = chunk * depth, (chunk + 1) * depth
-        if chunk + 1 < chunks:
-            for copy in copies(chunk + 1):
-                copy.wait()
-        lax.fori_loop(begin, end, level_step, 0)
-
-
-def bulk(lower, upper, metric, temp, u_vel, v_vel, w_vel, temp_prev, w_prev):
-    levels, rows, cols = temp.shape
-    chunks = 4
-    block = pltpu.VMEM((levels, rows, cols), F32)
+    lax.fori_loop(0, levels, level_step, 0)
+
+
+def bulk(lower, upper, metric, *arrays):
+    levels, rows, cols = arrays[0].shape
     return pl.pallas_call(
-        functools.partial(bulk_kernel, chunks),
+        bulk_kernel,
         out_shape=(
-            held(levels + 2, rows, cols),
-            held(levels + 2, rows, cols),
             held(2, levels + 1, rows, cols),
             held(2, levels, rows, cols),
             held(2, rows, cols),
             held(levels, TILE, cols),
             held(TILE, cols),
         ),
-        in_specs=[whole(pltpu.SMEM)] * 3 + [whole(pl.ANY)] * 6,
-        out_specs=[whole(VMEM)] * 7,
-        scratch_shapes=[block] * 4 + [pltpu.SemaphoreType.DMA((6, chunks))],
-        compiler_params=pltpu.CompilerParams(vmem_limit_bytes=24 * MIB),
+        in_specs=[whole(pltpu.SMEM)] * 3 + [whole(VMEM)] * 6,
+        out_specs=[whole(VMEM)] * 5,
+        compiler_params=pltpu.CompilerParams(vmem_limit_bytes=8 * MIB),
         cost_estimate=pl.CostEstimate(
             flops=70 * levels * rows * cols,
             bytes_accessed=24 * levels * rows * cols,
             transcendentals=0,
         ),
         name="bulk",
-    )(lower, upper, metric, *in_hbm(temp, u_vel, v_vel, w_vel, temp_prev, w_prev))
-
-
-def side_changes(to_left, to_right, from_left, from_right):
-    return from_left[...] - to_right[...], from_right[...] - to_left[...]
+    )(lower, upper, metric, *map(in_vmem, arrays))
+
+
+def side_changes(near, far):
+    odd = bit_of("gx", 0) == 1
+    return jnp.where(odd, near[...], far[...]), jnp.where(odd, far[...], near[...])
 
 
 def ends(rows, cols, head, tail):
@@ -263,11 +244,11 @@
 
 
 def fix_kernel(
-    levels, to_left, to_right, from_left, from_right, outer, inner, forward, first, table, scalars,
+    levels, near, far, outer, inner, forward, first, table, scalars,
     message, changes,
 ):
     _, rows, cols = first.shape
-    diffs = side_changes(to_left, to_right, from_left, from_right)
+    diffs = side_changes(near, far)
     upper = bit_of("gz", 0) == 1
 
     def scalar(at):
@@ -302,24 +283,24 @@
     message[pl.ds(6 * rows, TILE), :] = scalars[...]
 
 
-def fix(to_left, to_right, from_left, from_right, outer, inner, forward, first, table, scalars):
+def fix(near, far, outer, inner, forward, first, table, scalars):
     levels = table.shape[0]
     _, rows, cols = first.shape
     return pl.pallas_call(
         functools.partial(fix_kernel, levels),
         out_shape=(held(6 * rows + TILE, cols), held(4 * levels, cols)),
-        in_specs=[whole(VMEM)] * 10,
+        in_specs=[whole(VMEM)] * 8,
         out_specs=[whole(VMEM)] * 2,
         compiler_params=pltpu.CompilerParams(vmem_limit_bytes=8 * MIB),
         name="fix",
     )(
-        to_left, to_right, from_left, from_right, outer, inner,
+        near, far, outer, inner,
         in_vmem(forward), in_vmem(first), in_vmem(table), scalars,
     )
 
 
 def tends_kernel(
-    metric, tend, to_left, to_right, from_left, from_right, outer, other,
+    metric, tend, near, far, outer, other,
     temp_tend, w_tend, layers, strips, sems,
 ):
     _, levels, rows, cols = tend.shape
@@ -336,7 +317,7 @@
     for copy in copies:
         copy.start()
     upper = bit_of("gz", 0) == 1
-    diffs = side_changes(to_left, to_right, from_left, from_right)
+    diffs = side_changes(near, far)
     tile_at = lax.broadcasted_iota(jnp.int32, (TILE, cols), 0)
     for field in range(2):
         out = outs[field]
@@ -375,12 +356,12 @@
         copy.wait()
 
 
-def tends(metric, tend, to_left, to_right, from_left, from_right, outer, other):
+def tends(metric, tend, near, far, outer, other):
     _, levels, rows, cols = tend.shape
     return pl.pallas_call(
         tends_kernel,
         out_shape=(jax.ShapeDtypeStruct((levels, rows, cols), F32),) * 2,
-        in_specs=[whole(pltpu.SMEM)] + [whole(VMEM)] * 7,
+        in_specs=[whole(pltpu.SMEM)] + [whole(VMEM)] * 5,
         out_specs=[whole(pl.ANY)] * 2,
         scratch_shapes=[
             pltpu.VMEM((2, 2, rows, cols), F32),
@@ -394,7 +375,7 @@
             transcendentals=0,
         ),
         name="tends",
-    )(metric, in_vmem(tend), to_left, to_right, from_left, from_right, outer, other)
+    )(metric, in_vmem(tend), near, far, outer, other)
 
 
 def interface(low, high):
@@ -486,77 +467,133 @@
     )(mine, theirs)
 
 
-def finish_kernel(
-    rounds, strips, temp_pad, w_pad, forward, table, changes, scalars, outer, mine, theirs, *rest
+def prepare_kernel(
+    rounds, temp, w_vel, forward, table, changes, scalars, outer, *rest
 ):
     bases, gains = rest[: rounds - 1], rest[rounds - 1 : 2 * rounds - 2]
-    temp_next, w_next, result, below_in, above_in, sems = rest[2 * rounds - 2 :]
-    levels = table.shape[0]
-    _, _, rows, cols = forward.shape
+    known, response, below_in, above_in = rest[2 * rounds - 2 :]
+    levels, rows, cols = temp.shape
+    upper = bit_of("gz", rounds - 1) == 1
+    one, none = jnp.ones((1, cols), F32), jnp.zeros((1, cols), F32)
+    below_gain, above_gain = jnp.where(upper, one, none), jnp.where(upper, none, one)
+    below = above = None
+    for step in range(rounds - 2, -1, -1):
+        side = bit_of("gz", step) == 1
+        from_above = gains[step][pl.ds(FROM_ABOVE, 1), :]
+        from_below = gains[step][pl.ds(FROM_BELOW, 1), :]
+        gain = from_above * above_gain + from_below * below_gain
+        below_gain = jnp.where(side, gain, below_gain)
+        above_gain = jnp.where(side, above_gain, gain)
+        into = [bases[step][field] for field in range(2)]
+        if below is None:
+            below = above = [jnp.zeros((rows, cols), F32)] * 2
+        else:
+            into = [
+                into[field] + from_above * above[field] + from_below * below[field]
+                for field in range(2)
+            ]
+        below = [jnp.where(side, into[field], below[field]) for field in range(2)]
+        above = [jnp.where(side, above[field], into[field]) for field in range(2)]
+    side = bit_of("gz", 0) == 1
+    flux_below = jnp.where(side, none, scalars[pl.ds(METRIC_BELOW, 1), :])
+    flux_above = jnp.where(side, -scalars[pl.ds(METRIC_ABOVE, 1), :], none)
+    for field in range(2):
+        flux = outer[pl.ds(field * rows, rows), :]
+        below_in[field] = below[field] + flux_below * flux
+        above_in[field] = above[field] + flux_above * flux
+
+    gain = above_gain * table[levels - 1, pl.ds(PIVOT, 1), :]
+    for level in range(levels - 1, -1, -1):
+        if level < levels - 1:
+            gain = gain * table[level, pl.ds(UPPER_PIVOT, 1), :]
+        gain = gain + below_gain * table[level, pl.ds(BELOW_FORWARD, 1), :]
+        response[level] = jnp.broadcast_to(gain, (TILE, cols))
+
+    row_at = lax.broadcasted_iota(jnp.int32, (TILE, cols), 0)
+    width = 2 * TILE
+    for field, cells in enumerate((temp, w_vel)):
+        for begin in range(0, rows, width):
+            at = pl.ds(begin, width)
+            below = below_in[field, at, :]
+
+            def solve(level, carry, factor, field=field, begin=begin, at=at, below=below, cells=cells):
+                value = (
+                    forward[field, level + 1, at, :]
+                    + table[level, pl.ds(BELOW_FORWARD, 1), :] * below
+                    + factor * carry
+                )
+                if begin == 0:
+                    change = changes[pl.ds(field * levels + level, 1), :]
+                    head = value[:TILE] + jnp.where(row_at == 0, change, 0.0)
+                    value = jnp.concatenate([head, value[TILE:]])
+                if begin == rows - width:
+                    change = changes[pl.ds((2 + field) * levels + level, 1), :]
+                    tail = value[-TILE:] + jnp.where(row_at == TILE - 1, change, 0.0)
+                    value = jnp.concatenate([value[:-TILE], tail])
+                known[field, level, at, :] = value - cells[level, at, :]
+                return value
+
+            carry = solve(levels - 1, above_in[field, at, :], table[levels - 1, pl.ds(PIVOT, 1), :])
+
+            def step(back, carry, solve=solve):
+                level = levels - 2 - back
+                return solve(level, carry, table[level, pl.ds(UPPER_PIVOT, 1), :])
+
+            lax.fori_loop(0, levels - 1, step, carry)
+
+
+def prepare(rounds, temp, w_vel, forward, table, changes, scalars, outer, bases, gains):
+    levels, rows, cols = temp.shape
+    return pl.pallas_call(
+        functools.partial(prepare_kernel, rounds),
+        out_shape=(held(2, levels, rows, cols), held(levels, TILE, cols)),
+        in_specs=[whole(VMEM)] * (7 + 2 * (rounds - 1)),
+        out_specs=[whole(VMEM)] * 2,
+        scratch_shapes=[pltpu.VMEM((2, rows, cols), F32)] * 2,
+        compiler_params=pltpu.CompilerParams(vmem_limit_bytes=8 * MIB),
+        cost_estimate=pl.CostEstimate(
+            flops=12 * levels * rows * cols,
+            bytes_accessed=24 * levels * rows * cols,
+            transcendentals=0,
+        ),
+        name="prepare",
+    )(
+        in_vmem(temp), in_vmem(w_vel), in_vmem(forward), in_vmem(table), changes, scalars,
+        outer, *bases, *gains,
+    )
+
+
+def finish_kernel(rounds, known, response, mine, theirs, temp_next, w_next, result, sems):
+    _, levels, rows, cols = known.shape
     upper = bit_of("gz", rounds - 1) == 1
     own, far = scalar_rows(mine, 2 * rows), scalar_rows(theirs, 2 * rows)
     low = [jnp.where(upper, b, a) for a, b in zip(own, far)]
     high = [jnp.where(upper, a, b) for a, b in zip(own, far)]
     coupling, inverse = interface(low, high)
-    to_other = coupling * jnp.where(upper, low[LAST], high[FIRST])
     scale = coupling * inverse
-    for field in range(2):
-        at = pl.ds(field * rows, rows)
-        into = scale * (theirs[at, :] + to_other * mine[at, :])
-        zero = jnp.zeros((rows, cols), F32)
-        below, above = jnp.where(upper, into, zero), jnp.where(upper, zero, into)
-        for step in range(rounds - 2, -1, -1):
-            side = bit_of("gz", step) == 1
-            into = (
-                bases[step][field]
-                + gains[step][pl.ds(FROM_ABOVE, 1), :] * above
-                + gains[step][pl.ds(FROM_BELOW, 1), :] * below
-            )
-            below, above = jnp.where(side, into, below), jnp.where(side, above, into)
-        side = bit_of("gz", 0) == 1
-        flux = outer[at, :]
-        gain_below = jnp.where(side, 0.0, scalars[pl.ds(METRIC_BELOW, 1), :])
-        gain_above = jnp.where(side, -scalars[pl.ds(METRIC_ABOVE, 1), :], 0.0)
-        below_in[field] = below + gain_below * flux
-        above_in[field] = above + gain_above * flux
-
-    size = rows // strips
-    row_at = lax.broadcasted_iota(jnp.int32, (TILE, cols), 0)
+    to_other = scale * coupling * jnp.where(upper, low[LAST], high[FIRST])
+    width, half = 2 * TILE, rows // 2
     copies = []
-    for field, (pad, out) in enumerate(((temp_pad, temp_next), (w_pad, w_next))):
-        for strip in range(strips):
-            at = pl.ds(strip * size, size)
-            below = below_in[field, at, :]
-
-            def solve(level, carry, factor, field=field, strip=strip, at=at, below=below, pad=pad):
-                value = (
-                    forward[field, level + 1, at, :]
-                    + table[level, pl.ds(BELOW_FORWARD, 1), :] * below
-                    + factor * carry
-                )
-                if strip == 0:
-                    change = changes[pl.ds(field * levels + level, 1), :]
-                    value = jnp.concatenate(
-                        [value[:TILE] + jnp.where(row_at == 0, change, 0.0), value[TILE:]]
-                    )
-                if strip == strips - 1:
-                    change = changes[pl.ds((2 + field) * levels + level, 1), :]
-                    value = jnp.concatenate(
-                        [value[:-TILE], value[-TILE:] + jnp.where(row_at == TILE - 1, change, 0.0)]
-                    )
-                result[field, level, at, :] = value - pad[level + 1, at, :]
-                return value
-
-            carry = solve(levels - 1, above_in[field, at, :], table[levels - 1, pl.ds(PIVOT, 1), :])
-
-            def step(back, carry, solve=solve):
-                level = levels - 2 - back
-                return solve(level, carry, table[level, pl.ds(UPPER_PIVOT, 1), :])
-
-            lax.fori_loop(0, levels - 1, step, carry)
+    for field, out in enumerate((temp_next, w_next)):
+        for part in range(2):
+            for begin in range(part * half, (part + 1) * half, width):
+                at = pl.ds(begin, width)
+                here = pl.ds(field * rows + begin, width)
+                into = scale * theirs[here, :] + to_other * mine[here, :]
+                tiles = [into[i : i + TILE] for i in range(0, width, TILE)]
+
+                def step(level, carry, field=field, begin=begin, tiles=tiles):
+                    gain = response[level]
+                    for i, tile in enumerate(tiles):
+                        at = pl.ds(begin + i * TILE, TILE)
+                        result[field, level, at, :] = known[field, level, at, :] + gain * tile
+                    return carry
+
+                lax.fori_loop(0, levels, step, 0, unroll=4)
+            at = pl.ds(part * half, half)
             copies.append(
                 pltpu.make_async_copy(
-                    result.at[field, :, at, :], out.at[:, at, :], sems.at[field, strip]
+                    result.at[field, :, at, :], out.at[:, at, :], sems.at[field, part]
                 )
             )
             copies[-1].start()
@@ -564,58 +601,50 @@
         copy.wait()
 
 
-def finish(rounds, temp_pad, w_pad, forward, table, changes, scalars, outer, mine, theirs, bases, gains):
-    levels = table.shape[0]
-    _, _, rows, cols = forward.shape
-    strips = 2
+def finish(rounds, known, response, mine, theirs):
+    _, levels, rows, cols = known.shape
     return pl.pallas_call(
-        functools.partial(finish_kernel, rounds, strips),
+        functools.partial(finish_kernel, rounds),
         out_shape=(jax.ShapeDtypeStruct((levels, rows, cols), F32),) * 2,
-        in_specs=[whole(VMEM)] * (7 + 2 + 2 * (rounds - 1)),
+        in_specs=[whole(VMEM)] * 4,
         out_specs=[whole(pl.ANY)] * 2,
         scratch_shapes=[
             pltpu.VMEM((2, levels, rows, cols), F32),
-            pltpu.VMEM((2, rows, cols), F32),
-            pltpu.VMEM((2, rows, cols), F32),
-            pltpu.SemaphoreType.DMA((2, strips)),
+            pltpu.SemaphoreType.DMA((2, 2)),
         ],
-        compiler_params=pltpu.CompilerParams(vmem_limit_bytes=16 * MIB),
+        compiler_params=pltpu.CompilerParams(vmem_limit_bytes=8 * MIB),
         name="finish",
-    )(
-        in_vmem(temp_pad), in_vmem(w_pad), in_vmem(forward), in_vmem(table), changes, scalars,
-        outer, mine, theirs, *bases, *gains,
-    )
+    )(in_vmem(known), response, mine, theirs)
 
 
 def local(temp, u_vel, v_vel, w_vel, temp_prev, w_prev, lower, upper, metric):
-    _, rows, _ = temp.shape
+    rows = temp.shape[1]
     across, stacked = lax.axis_size("gx"), lax.axis_size("gz")
     rounds = stacked.bit_length() - 1
-    to_left, to_right, outer, inner = edges(temp, u_vel, w_vel)
-    from_right = lax.ppermute(to_left, "gx", [((i + 1) % across, i) for i in range(across)])
-    from_left = lax.ppermute(to_right, "gx", [(i, (i + 1) % across) for i in range(across)])
-    seams = [(i, i + 1) for i in range(1, stacked - 1, 2)]
-    outer = lax.ppermute(outer, "gz", seams + [(b, a) for a, b in seams])
-    temp_pad, w_pad, forward, tend, first, table, scalars = bulk(
+    near, far, outer, inner = edges(temp, u_vel, w_vel, v_vel, temp_prev, w_prev)
+    pairs = [(i, (i + 1) % across) for i in range(1, across, 2)]
+    far = lax.ppermute(far, "gx", pairs + [(b, a) for a, b in pairs])
+    pairs = [(i, i + 1) for i in range(0, across, 2)]
+    near = lax.ppermute(near, "gx", pairs + [(b, a) for a, b in pairs])
+    pairs = [(i, i + 1) for i in range(1, stacked - 1, 2)]
+    outer = lax.ppermute(outer, "gz", pairs + [(b, a) for a, b in pairs])
+    forward, tend, first, table, scalars = bulk(
         lower, upper, metric, temp, u_vel, v_vel, w_vel, temp_prev, w_prev
     )
-    mine, changes = fix(
-        to_left, to_right, from_left, from_right, outer, inner, forward, first, table, scalars
-    )
+    mine, changes = fix(near, far, outer, inner, forward, first, table, scalars)
     bases, gains = [], []
     for step in range(rounds):
         theirs = lax.ppermute(mine, "gz", [(i, i ^ (1 << step)) for i in range(stacked)])
         if step == 0:
-            temp_tend, w_tend = tends(
-                metric, tend, to_left, to_right, from_left, from_right, outer, theirs
-            )
+            temp_tend, w_tend = tends(metric, tend, near, far, outer, theirs)
         if step + 1 < rounds:
             mine, base, gain = merge(step, step == 0, step + 2 == rounds, rows, mine, theirs)
             bases.append(base)
             gains.append(gain)
-    temp_next, w_next = finish(
-        rounds, temp_pad, w_pad, forward, table, changes, scalars, outer, mine, theirs, bases, gains
+    known, response = prepare(
+        rounds, temp, w_vel, forward, table, changes, scalars, outer, bases, gains
     )
+    temp_next, w_next = finish(rounds, known, response, mine, theirs)
     return temp_next, w_next, temp_tend, w_tend
 
 

time: 26.6 us -> 25 us (0.940)
  waiting for transfers between devices: 4.85 us -> 3.38 us
  Pallas kernels: 10.9 us -> 10 us
  starting transfers between devices: 9.98 us -> 10.6 us
    pallas_call x2 -> x3, Pallas kernels: 7.3 us -> 6.25 us  [the longest x1 3.65 us: bulk(): pl.pallas_call(bulk_kernel, out_shape=(held(2, levels + 1, rows, cols), h...]
    ppermute x3, waiting for transfers between devices: 0.9 us -> 0.01 us  [the longest x1 0.01 us: local(): near = lax.ppermute(near, 'gx', pairs + [(b, a) for a, b in pairs])]
    ppermute x3, starting transfers between devices: 6.73 us -> 7.38 us  [the longest x1 3.54 us: local(): far = lax.ppermute(far, 'gx', pairs + [(b, a) for a, b in pairs])]
    ppermute x2, waiting for transfers between devices: 3.95 us -> 3.38 us  [local(): lax.ppermute(mine, 'gz', [(i, i ^ 1 << step) for i in range(stacked)])]
  transfers between devices with their start and end apart: 5 -> 5, of which waited for: 3 -> 2; matrix products, arithmetic and copies ran while one was open for 0% -> 0% of each run, Pallas kernels for 29% -> 27%
where the time goes in v2:
time: 25 us; the launch traced here: 24.9 us
  starting transfers between devices  10.6 us (42%)
  Pallas kernels  10 us (40%)
  waiting for transfers between devices  3.38 us (14%)
  between operations  0.82 us (3%)
    pallas_call x1, Pallas kernels, bulk(): pl.pallas_call(bulk_kernel, out_shape=(held(2, levels + 1, rows, cols), h...  3.65 us
    ppermute x1, starting transfers between devices, local(): far = lax.ppermute(far, 'gx', pairs + [(b, a) for a, b in pairs])  3.54 us
    ppermute x2, waiting for transfers between devices, local(): lax.ppermute(mine, 'gz', [(i, i ^ 1 << step) for i in range(stacked)])  3.38 us
    ppermute x2, starting transfers between devices, local(): lax.ppermute(mine, 'gz', [(i, i ^ 1 << step) for i in range(stacked)])  3.25 us
    ppermute x1, starting transfers between devices, local(): near = lax.ppermute(near, 'gx', pairs + [(b, a) for a, b in pairs])  3.03 us
    pallas_call x1, Pallas kernels, tends(): pl.pallas_call(tends_kernel, out_shape=(jax.ShapeDtypeStruct((levels, row...  1.92 us
    pallas_call x1, Pallas kernels, edges(): pl.pallas_call(edges_kernel, out_shape=(held(2 * levels, cols), held(2 *...  1.56 us
    pallas_call x1, Pallas kernels, finish(): pl.pallas_call(functools.partial(finish_kernel, rounds), out_shape=(jax.S...  1.44 us
  transfers between devices with their start and end apart: 5, of which 2 were waited for; matrix products, arithmetic and copies ran while one was open for 0% of the time, Pallas kernels for 27%

profile of v2, /device:TPU:0, one launch (start us, length us, event | category | flops | bytes accessed | tf_op | source)
XLA Modules:
  0.0 24.9 jit_solution(9810048487891003040)
XLA Ops:
  0.6 0.0 copy-start.1
  0.6 0.0 copy-start
  0.7 0.0 copy-start.5
  0.7 0.0 copy-start.4
  0.7 0.0 copy-start.3
  0.7 0.0 copy-start.2
  0.7 1.6 %edges.1 = (f32[32,256]{1,0:T(8,128)S(1)}, f32[32,256]{1,0:T(8,128)S(1)}, f32[128,256]{1,0:T(8,128)S(1)}, f32[128,256]{1,0:T(8,128)S(1)}) custom-call(f32[16,64,256]{2,1,0:T(8,128)} %temp.5, f32[16,64,256]{2,1,0:T(8,128)} %u_vel.3, f32[16,64,256]{2,1,0:T(8,128)} %w_vel.5, f32[16,64,256]{2,1,0:T(8,128)} %v_vel.3, f32[16,64,256]{2,1,0:T(8,128)} %temp_prev.3, ...), custom_call_target="tpu_custom_call" | custom-call | tf_op jit(solution)/shard_map/edges/pallas_call | solution.py:78
  2.3 0.8 %collective-permute-start.2 = (f32[128,256]{1,0:T(8,128)S(1)}, f32[128,256]{1,0:T(8,128)S(1)}, u32[]{:S(2)}, u32[]{:S(2)}) collective-permute-start(f32[128,256]{1,0:T(8,128)S(1)} %get-tuple-element.28), channel_id=1, source_target_pairs={{1,2},{2,1},{5,6},{6,5},{9,10},{10,9},{13,14},{14,13},{17,18},{18,... | collective-permute-start | bytes 393224 | tf_op jit(solution)/shard_map/ppermute | solution.py:630
  3.1 3.0 %collective-permute-start = (f32[32,256]{1,0:T(8,128)S(1)}, f32[32,256]{1,0:T(8,128)S(1)}, u32[]{:S(2)}, u32[]{:S(2)}) collective-permute-start(f32[32,256]{1,0:T(8,128)S(1)} %get-tuple-element.26), channel_id=1, source_target_pairs={{0,4},{8,12},{16,20},{24,28},{4,0},{12,8},{20,16},{28,24},{1,5},{9... | collective-permute-start | bytes 98312 | tf_op jit(solution)/shard_map/ppermute | solution.py:628
  6.1 3.5 %collective-permute-start.1 = (f32[32,256]{1,0:T(8,128)S(1)}, f32[32,256]{1,0:T(8,128)S(1)}, u32[]{:S(2)}, u32[]{:S(2)}) collective-permute-start(f32[32,256]{1,0:T(8,128)S(1)} %get-tuple-element.27), channel_id=1, source_target_pairs={{4,8},{12,16},{20,24},{28,0},{8,4},{16,12},{24,20},{0,28},{5,9},{1... | collective-permute-start | bytes 98312 | tf_op jit(solution)/shard_map/ppermute | solution.py:626
  9.7 0.0 copy-done
  9.7 3.6 %bulk.1 = (f32[2,17,64,256]{3,2,1,0:T(8,128)S(1)}, f32[2,16,64,256]{3,2,1,0:T(8,128)S(1)}, f32[2,64,256]{2,1,0:T(8,128)S(1)}, f32[16,8,256]{2,1,0:T(8,128)S(1)}, f32[8,256]{1,0:T(8,128)S(1)}) custom-call(f32[16]{0:T(128)S(1)} %copy-done.7, f32[16]{0:T(128)S(1)} %copy-done.8, f32[16]{0:T(128)S(1)} %copy-done.6, f32[16,64,256]{2,1,0:T(8,128)S(1)} %copy-done, ...), custom_call_target="tpu_custom_call" | custom-call | flops 18350080 | bytes 6291456 | tf_op jit(solution)/shard_map/bulk/pallas_call | solution.py:215
  13.4 0.0 collective-permute-done.near
  13.4 0.0 collective-permute-done.1.far
  13.4 0.0 collective-permute-done.2.outer
  13.4 0.1 fix.1
  13.6 2.4 %collective-permute-start.3 = (f32[392,256]{1,0:T(8,128)S(1)}, f32[392,256]{1,0:T(8,128)S(1)}, u32[]{:S(2)}, u32[]{:S(2)}) collective-permute-start(f32[392,256]{1,0:T(8,128)S(1)} %get-tuple-element.33.mine), channel_id=1, source_target_pairs={{0,1},{1,0},{2,3},{3,2},{4,5},{5,4},{6,7},{7,6},{8,9},{9,8},{10,11... | collective-permute-start | bytes 1204232 | tf_op jit(solution)/shard_map/ppermute | solution.py:637
  15.9 1.4 %collective-permute-done.3.theirs.other = f32[392,256]{1,0:T(8,128)S(1)} collective-permute-done((f32[392,256]{1,0:T(8,128)S(1)}, f32[392,256]{1,0:T(8,128)S(1)}, u32[]{:S(2)}, u32[]{:S(2)}) %collective-permute-start.3) | collective-permute-done | bytes 401440 | tf_op jit(solution)/shard_map/ppermute | solution.py:637
  17.3 0.2 merge.1
  17.4 0.9 %collective-permute-start.4 = (f32[136,256]{1,0:T(8,128)S(1)}, f32[136,256]{1,0:T(8,128)S(1)}, u32[]{:S(2)}, u32[]{:S(2)}) collective-permute-start(f32[136,256]{1,0:T(8,128)S(1)} %get-tuple-element.38.mine), channel_id=1, source_target_pairs={{0,2},{1,3},{2,0},{3,1},{4,6},{5,7},{6,4},{7,5},{8,10},{9,11},{10,... | collective-permute-start | bytes 417800 | tf_op jit(solution)/shard_map/ppermute | solution.py:637
  18.3 1.9 %tends.1 = (f32[16,64,256]{2,1,0:T(8,128)}, f32[16,64,256]{2,1,0:T(8,128)}) custom-call(f32[16]{0:T(128)S(1)} %copy-done.6, f32[2,16,64,256]{3,2,1,0:T(8,128)S(1)} %get-tuple-element.41.tend, f32[32,256]{1,0:T(8,128)S(1)} %collective-permute-done.near, f32[32,256]{1,0:T(8,128)S(1)} %collective-permute-done.1.far, ...), custom_call_target="tpu_custom_call" | custom-call | flops 262144 | bytes 2097152 | tf_op jit(solution)/shard_map/tends/pallas_call | solution.py:361
  20.3 1.2 %prepare.1 = (f32[2,16,64,256]{3,2,1,0:T(8,128)S(1)}, f32[16,8,256]{2,1,0:T(8,128)S(1)}) custom-call(f32[16,64,256]{2,1,0:T(8,128)S(1)} %copy-done, f32[16,64,256]{2,1,0:T(8,128)S(1)} %copy-done.1, f32[2,17,64,256]{3,2,1,0:T(8,128)S(1)} %get-tuple-element.24.forward, f32[16,8,256]{2,1,0:T(8,128)S(1)} %get-tuple-element.25.table, ...), custom_call_target="tpu_custom_call" | custom-call | flops 3145728 | bytes 6291456 | tf_op jit(solution)/shard_map/prepare/pallas_call | solution.py:547
  21.4 2.0 %collective-permute-done.4.theirs = f32[136,256]{1,0:T(8,128)S(1)} collective-permute-done((f32[136,256]{1,0:T(8,128)S(1)}, f32[136,256]{1,0:T(8,128)S(1)}, u32[]{:S(2)}, u32[]{:S(2)}) %collective-permute-start.4) | collective-permute-done | bytes 139296 | tf_op jit(solution)/shard_map/ppermute | solution.py:637
  23.5 1.4 %finish.1 = (f32[16,64,256]{2,1,0:T(8,128)}, f32[16,64,256]{2,1,0:T(8,128)}) custom-call(f32[2,16,64,256]{3,2,1,0:T(8,128)S(1)} %get-tuple-element.36.known, f32[16,8,256]{2,1,0:T(8,128)S(1)} %get-tuple-element.37.response, f32[136,256]{1,0:T(8,128)S(1)} %get-tuple-element.38.mine, f32[136,256]{1,0:T(8,128)S(1)} %collective-permute-done.4.theirs), custom_call_target="tpu_custom_call" | custom-call | tf_op jit(solution)/shard_map/finish/pallas_call | solution.py:606
  (11 shorter events, 0.0 us)
Async XLA Ops:
  0.6 9.0 %copy-start.1 = (f32[16,64,256]{2,1,0:T(8,128)S(1)}, f32[16,64,256]{2,1,0:T(8,128)}, u32[]{:S(2)}) copy-start(f32[16,64,256]{2,1,0:T(8,128)} %w_vel.5) | copy-start | bytes 3145732
  0.6 9.0 %copy-start = (f32[16,64,256]{2,1,0:T(8,128)S(1)}, f32[16,64,256]{2,1,0:T(8,128)}, u32[]{:S(2)}) copy-start(f32[16,64,256]{2,1,0:T(8,128)} %temp.5) | copy-start | bytes 3145732
  0.7 9.0 %copy-start.5 = (f32[16,64,256]{2,1,0:T(8,128)S(1)}, f32[16,64,256]{2,1,0:T(8,128)}, u32[]{:S(2)}) copy-start(f32[16,64,256]{2,1,0:T(8,128)} %w_prev.3) | copy-start | bytes 3145732
  0.7 9.0 %copy-start.4 = (f32[16,64,256]{2,1,0:T(8,128)S(1)}, f32[16,64,256]{2,1,0:T(8,128)}, u32[]{:S(2)}) copy-start(f32[16,64,256]{2,1,0:T(8,128)} %temp_prev.3) | copy-start | bytes 3145732
  0.7 9.0 %copy-start.3 = (f32[16,64,256]{2,1,0:T(8,128)S(1)}, f32[16,64,256]{2,1,0:T(8,128)}, u32[]{:S(2)}) copy-start(f32[16,64,256]{2,1,0:T(8,128)} %v_vel.3) | copy-start | bytes 3145732
  0.7 9.0 %copy-start.2 = (f32[16,64,256]{2,1,0:T(8,128)S(1)}, f32[16,64,256]{2,1,0:T(8,128)}, u32[]{:S(2)}) copy-start(f32[16,64,256]{2,1,0:T(8,128)} %u_vel.3) | copy-start | bytes 3145732
  0.7 9.0 %copy-start.6 = (f32[16]{0:T(128)S(1)}, f32[16]{0:T(128)}, u32[]{:S(2)}) copy-start(f32[16]{0:T(128)} %metric.3) | copy-start | bytes 196
  0.7 9.0 %copy-start.8 = (f32[16]{0:T(128)S(1)}, f32[16]{0:T(128)}, u32[]{:S(2)}) copy-start(f32[16]{0:T(128)} %upper.1) | copy-start | bytes 196
  0.7 9.0 %copy-start.7 = (f32[16]{0:T(128)S(1)}, f32[16]{0:T(128)}, u32[]{:S(2)}) copy-start(f32[16]{0:T(128)} %lower.1) | copy-start | bytes 196
  2.3 11.1 %collective-permute-start.2 = (f32[128,256]{1,0:T(8,128)S(1)}, f32[128,256]{1,0:T(8,128)S(1)}, u32[]{:S(2)}, u32[]{:S(2)}) collective-permute-start(f32[128,256]{1,0:T(8,128)S(1)} %get-tuple-element.28), channel_id=1, source_target_pairs={{1,2},{2,1},{5,6},{6,5},{9,10},{10,9},{13,14},{14,13},{17,18},{18,... | collective-permute-start | bytes 393224 | tf_op jit(solution)/shard_map/ppermute | solution.py:630
  3.1 10.3 %collective-permute-start = (f32[32,256]{1,0:T(8,128)S(1)}, f32[32,256]{1,0:T(8,128)S(1)}, u32[]{:S(2)}, u32[]{:S(2)}) collective-permute-start(f32[32,256]{1,0:T(8,128)S(1)} %get-tuple-element.26), channel_id=1, source_target_pairs={{0,4},{8,12},{16,20},{24,28},{4,0},{12,8},{20,16},{28,24},{1,5},{9... | collective-permute-start | bytes 98312 | tf_op jit(solution)/shard_map/ppermute | solution.py:628
  6.1 7.3 %collective-permute-start.1 = (f32[32,256]{1,0:T(8,128)S(1)}, f32[32,256]{1,0:T(8,128)S(1)}, u32[]{:S(2)}, u32[]{:S(2)}) collective-permute-start(f32[32,256]{1,0:T(8,128)S(1)} %get-tuple-element.27), channel_id=1, source_target_pairs={{4,8},{12,16},{20,24},{28,0},{8,4},{16,12},{24,20},{0,28},{5,9},{1... | collective-permute-start | bytes 98312 | tf_op jit(solution)/shard_map/ppermute | solution.py:626
  13.6 3.7 %collective-permute-start.3 = (f32[392,256]{1,0:T(8,128)S(1)}, f32[392,256]{1,0:T(8,128)S(1)}, u32[]{:S(2)}, u32[]{:S(2)}) collective-permute-start(f32[392,256]{1,0:T(8,128)S(1)} %get-tuple-element.33.mine), channel_id=1, source_target_pairs={{0,1},{1,0},{2,3},{3,2},{4,5},{5,4},{6,7},{7,6},{8,9},{9,8},{10,11... | collective-permute-start | bytes 1204232 | tf_op jit(solution)/shard_map/ppermute | solution.py:637
  17.4 6.0 %collective-permute-start.4 = (f32[136,256]{1,0:T(8,128)S(1)}, f32[136,256]{1,0:T(8,128)S(1)}, u32[]{:S(2)}, u32[]{:S(2)}) collective-permute-start(f32[136,256]{1,0:T(8,128)S(1)} %get-tuple-element.38.mine), channel_id=1, source_target_pairs={{0,2},{1,3},{2,0},{3,1},{4,6},{5,7},{6,4},{7,5},{8,10},{9,11},{10,... | collective-permute-start | bytes 417800 | tf_op jit(solution)/shard_map/ppermute | solution.py:637

commit v3 on v2

v3 whole, which is shorter than its diff:
```python
import functools

import jax
import jax.numpy as jnp
from jax import lax
from jax.experimental import pallas as pl
from jax.experimental.pallas import tpu as pltpu
from jax.sharding import PartitionSpec as P

NEW_WEIGHT = 5.0 / 12.0
HORIZ_DIFF = 0.1
FIELD_WEIGHT = 2.0 / NEW_WEIGHT
PREV_WEIGHT = (17.0 / 60.0) / NEW_WEIGHT
TILE = 8
MIB = 1024 * 1024

PIVOT_NEW, LOWER_PIVOT, UPPER_PIVOT, FIRST_GREEN, BELOW_FORWARD, PIVOT, RISE, FALL = range(8)
FIRST, CORNER, LAST, BELOW, ABOVE, METRIC_BELOW, METRIC_ABOVE = range(7)
FROM_ABOVE, FROM_BELOW = range(2)

VMEM = pltpu.VMEM
F32 = jnp.float32


def whole(space):
    return pl.BlockSpec(memory_space=space)


def held(*shape):
    return pltpu.VMEM(shape, F32)


def in_vmem(array):
    return pltpu.with_memory_space_constraint(array, pltpu.VMEM)


def in_hbm(*arrays):
    return [pltpu.with_memory_space_constraint(array, pltpu.HBM) for array in arrays]


def bit_of(axis, bit):
    return (lax.axis_index(axis) >> bit) & 1


def edges_kernel(
    temp,
    u_vel,
    w_vel,
    v_vel,
    temp_prev,
    w_prev,
    lower,
    upper,
    metric,
    far,
    near,
    outer,
    inner,
    table,
    scalars,
    strips,
    layers,
    lower_at,
    upper_at,
    metric_at,
    sems,
):
    levels, rows, cols = temp.shape
    copies = [(lower, lower_at), (upper, upper_at), (metric, metric_at)]
    for at, array in enumerate((temp, w_vel, u_vel)):
        for side, first in enumerate((0, rows - TILE)):
            copies.append((array.at[:, pl.ds(first, TILE), :], strips.at[at, side]))
    for at, array in enumerate((temp, w_vel)):
        for side, level in enumerate((0, levels - 1)):
            copies.append((array.at[level], layers.at[at, side]))
    copies = [pltpu.make_async_copy(src, dst, sems.at[i]) for i, (src, dst) in enumerate(copies)]
    for copy in copies:
        copy.start()
    for copy in copies[:3]:
        copy.wait()
    coefficients(lower_at, upper_at, metric_at, table, scalars)
    for copy in copies[3:]:
        copy.wait()
    odd = bit_of("gx", 0) == 1
    last = TILE - 1
    for field in range(2):
        at = pl.ds(field * levels, levels)
        to_left = (HORIZ_DIFF - 0.5 * strips[2, 0, :, 0, :]) * strips[field, 0, :, 0, :]
        to_right = (HORIZ_DIFF + 0.5 * strips[2, 1, :, last, :]) * strips[field, 1, :, last, :]
        near[at, :] = jnp.where(odd, to_left, to_right)
        far[at, :] = jnp.where(odd, to_right, to_left)
    position = lax.axis_index("gz")
    upper_core = bit_of("gz", 0) == 1
    wall = (position == 0) | (position == lax.axis_size("gz") - 1)
    zero = jnp.zeros((rows, cols), F32)
    for field in range(2):
        at = pl.ds(field * rows, rows)
        bottom = layers[1, 0] * layers[field, 0]
        top = layers[1, 1] * layers[field, 1]
        outer[at, :] = jnp.where(wall, zero, jnp.where(upper_core, top, bottom))
        inner[at, :] = jnp.where(upper_core, bottom, top)


def edges(temp, u_vel, w_vel, v_vel, temp_prev, w_prev, lower, upper, metric):
    levels, rows, cols = temp.shape
    return pl.pallas_call(
        edges_kernel,
        out_shape=(
            held(2 * levels, cols),
            held(2 * levels, cols),
            held(2 * rows, cols),
            held(2 * rows, cols),
            held(levels, TILE, cols),
            held(TILE, cols),
        ),
        in_specs=[whole(pl.ANY)] * 9,
        out_specs=[whole(VMEM)] * 6,
        scratch_shapes=[
            pltpu.VMEM((3, 2, levels, TILE, cols), F32),
            pltpu.VMEM((2, 2, rows, cols), F32),
            pltpu.SMEM((levels,), F32),
            pltpu.SMEM((levels,), F32),
            pltpu.SMEM((levels,), F32),
            pltpu.SemaphoreType.DMA((13,)),
        ],
        compiler_params=pltpu.CompilerParams(vmem_limit_bytes=8 * MIB),
        name="edges",
    )(*in_hbm(temp, u_vel, w_vel, v_vel, temp_prev, w_prev, lower, upper, metric))


def coefficients(lower, upper, metric, table, scalars):
    levels, _, cols = table.shape

    def row(value):
        return jnp.full((1, cols), value, F32)

    ratio = jnp.zeros((1, cols), F32)
    forward = jnp.ones((1, cols), F32)
    for level in range(levels):
        low, high = row(lower[level]), row(upper[level])
        pivot = 1.0 / (1.0 + low + high - low * ratio)
        ratio = high * pivot
        lower_pivot = low * pivot
        forward = pivot if level == 0 else lower_pivot * forward
        table[level, pl.ds(PIVOT_NEW, 1), :] = NEW_WEIGHT * pivot
        table[level, pl.ds(LOWER_PIVOT, 1), :] = lower_pivot
        table[level, pl.ds(UPPER_PIVOT, 1), :] = ratio
        table[level, pl.ds(BELOW_FORWARD, 1), :] = forward
        table[level, pl.ds(PIVOT, 1), :] = pivot
        table[level, pl.ds(RISE, 1), :] = row(metric[level] if level < levels - 1 else 0.0)
        table[level, pl.ds(FALL, 1), :] = row(metric[level] if level > 0 else 0.0)
    green = forward
    table[levels - 1, pl.ds(FIRST_GREEN, 1), :] = NEW_WEIGHT * green
    for level in range(levels - 2, -1, -1):
        green = (
            table[level, pl.ds(BELOW_FORWARD, 1), :]
            + table[level, pl.ds(UPPER_PIVOT, 1), :] * green
        )
        table[level, pl.ds(FIRST_GREEN, 1), :] = NEW_WEIGHT * green
    scalars[pl.ds(FIRST, 1), :] = green
    scalars[pl.ds(CORNER, 1), :] = forward
    scalars[pl.ds(LAST, 1), :] = pivot
    scalars[pl.ds(BELOW, 1), :] = row(lower[0])
    scalars[pl.ds(ABOVE, 1), :] = row(upper[levels - 1])
    scalars[pl.ds(METRIC_BELOW, 1), :] = row(NEW_WEIGHT * metric[0])
    scalars[pl.ds(METRIC_ABOVE, 1), :] = row(NEW_WEIGHT * metric[levels - 1])
    scalars[pl.ds(7, 1), :] = row(0.0)


def bulk_kernel(
    table,
    temp,
    u_vel,
    v_vel,
    w_vel,
    temp_prev,
    w_prev,
    forward,
    tend,
    first,
):
    levels, rows, cols = temp.shape
    strips = rows // TILE
    fields, prevs = (temp, w_vel), (temp_prev, w_prev)
    for field in range(2):
        forward[field, 0] = jnp.zeros((rows, cols), F32)
        first[field] = jnp.zeros((rows, cols), F32)
    row_at = lax.broadcasted_iota(jnp.int32, (TILE, cols), 0)
    zero = jnp.zeros((TILE, cols), F32)

    def level_step(level, carry):
        def spread(at):
            return jnp.broadcast_to(table[level, pl.ds(at, 1), :], (TILE, cols))

        pivot, lower_pivot, green = spread(PIVOT_NEW), spread(LOWER_PIVOT), spread(FIRST_GREEN)
        rise, fall = spread(RISE), spread(FALL)
        over = jnp.minimum(level + 1, levels - 1)
        under = jnp.maximum(level - 1, 0)

        def sides(strip):
            at = pl.ds(strip * TILE, TILE)
            half = 0.5 * u_vel[level, at, :]
            back, ahead = HORIZ_DIFF - half, HORIZ_DIFF + half
            here = [values[level, at, :] for values in fields]
            return (
                here,
                [pltpu.roll(back * value, TILE - 1, 0) for value in here],
                [pltpu.roll(ahead * value, 1, 0) for value in here],
            )

        before = [zero, zero]
        here, back, ahead = sides(0)
        for strip in range(strips):
            after = sides(strip + 1) if strip + 1 < strips else (None, [zero, zero], None)
            at = pl.ds(strip * TILE, TILE)
            half = 0.5 * v_vel[level, at, :]
            v_back, v_ahead = HORIZ_DIFF - half, HORIZ_DIFF + half
            w_over = rise * w_vel[over, at, :]
            w_under = fall * w_vel[under, at, :]
            for field in range(2):
                value = here[field]
                change = jnp.where(row_at == TILE - 1, after[1][field], back[field])
                change = change + jnp.where(row_at == 0, before[field], ahead[field])
                change = change + pltpu.roll(v_back * value, cols - 1, 1)
                change = change + pltpu.roll(v_ahead * value, 1, 1)
                change = change - w_over * fields[field][over, at, :]
                change = change + w_under * fields[field][under, at, :]
                change = change + (here[1 - field] - (4.0 * HORIZ_DIFF) * value)
                tend[field, level, at, :] = change
                right = change + (FIELD_WEIGHT * value - PREV_WEIGHT * prevs[field][level, at, :])
                forward[field, level + 1, at, :] = (
                    pivot * right + lower_pivot * forward[field, level, at, :]
                )
                first[field, at, :] = first[field, at, :] + green * right
            before = ahead
            here, back, ahead = after
        return carry

    lax.fori_loop(0, levels, level_step, 0)


def bulk(table, *arrays):
    levels, rows, cols = arrays[0].shape
    return pl.pallas_call(
        bulk_kernel,
        out_shape=(
            held(2, levels + 1, rows, cols),
            held(2, levels, rows, cols),
            held(2, rows, cols),
        ),
        in_specs=[whole(VMEM)] * 7,
        out_specs=[whole(VMEM)] * 3,
        compiler_params=pltpu.CompilerParams(vmem_limit_bytes=8 * MIB),
        cost_estimate=pl.CostEstimate(
            flops=7000 * levels * rows * cols,
            bytes_accessed=24 * levels * rows * cols,
            transcendentals=0,
        ),
        name="bulk",
    )(*map(in_vmem, (table, *arrays)))


def side_changes(far, near):
    odd = bit_of("gx", 0) == 1
    return jnp.where(odd, near[...], far[...]), jnp.where(odd, far[...], near[...])


def level_fluxes(outer, inner, at):
    upper = bit_of("gz", 0) == 1
    return jnp.where(upper, inner[at, :], outer[at, :]), jnp.where(upper, outer[at, :], inner[at, :])


def ends(rows, cols, head, tail):
    at = lax.broadcasted_iota(jnp.int32, (rows, cols), 0)
    return jnp.where(at == 0, head, jnp.where(at == rows - 1, tail, 0.0))


def fix_kernel(
    levels, far, near, outer, inner, forward, first, table, scalars, message, changes
):
    _, rows, cols = first.shape
    diffs = side_changes(far, near)

    def scalar(at):
        return scalars[pl.ds(at, 1), :]

    below, above = scalar(METRIC_BELOW), -scalar(METRIC_ABOVE)
    for field in range(2):
        firsts, lasts = [], []
        for side in range(2):
            value = jnp.zeros((1, cols), F32)
            total = jnp.zeros((1, cols), F32)
            for level in range(levels):
                right = diffs[side][field * levels + level : field * levels + level + 1, :]
                value = (
                    table[level, pl.ds(PIVOT_NEW, 1), :] * right
                    + table[level, pl.ds(LOWER_PIVOT, 1), :] * value
                )
                total = total + table[level, pl.ds(FIRST_GREEN, 1), :] * right
                changes[pl.ds((side * 2 + field) * levels + level, 1), :] = value
            firsts.append(total)
            lasts.append(value)
        flux_below, flux_above = level_fluxes(outer, inner, pl.ds(field * rows, rows))
        message[pl.ds(field * rows, rows), :] = (
            first[field]
            + (below * scalar(FIRST)) * flux_below
            + (above * scalar(CORNER)) * flux_above
            + ends(rows, cols, *firsts)
        )
        message[pl.ds((2 + field) * rows, rows), :] = (
            forward[field, levels]
            + (below * scalar(CORNER)) * flux_below
            + (above * scalar(LAST)) * flux_above
            + ends(rows, cols, *lasts)
        )
    message[pl.ds(4 * rows, TILE), :] = scalars[...]


def fix(far, near, outer, inner, forward, first, table, scalars):
    levels = table.shape[0]
    _, rows, cols = first.shape
    return pl.pallas_call(
        functools.partial(fix_kernel, levels),
        out_shape=(held(4 * rows + TILE, cols), held(4 * levels, cols)),
        in_specs=[whole(VMEM)] * 8,
        out_specs=[whole(VMEM)] * 2,
        compiler_params=pltpu.CompilerParams(vmem_limit_bytes=8 * MIB),
        name="fix",
    )(far, near, outer, inner, in_vmem(forward), in_vmem(first), in_vmem(table), scalars)


def tends_kernel(field, table, tend, far, near, outer, inner, out, layers, strips, sems):
    _, levels, rows, cols = tend.shape
    inside = pl.ds(1, levels - 2)
    copies = [
        pltpu.make_async_copy(
            tend.at[field, inside, pl.ds(TILE, rows - 2 * TILE), :],
            out.at[inside, pl.ds(TILE, rows - 2 * TILE), :],
            sems.at[0],
        )
    ]
    copies[0].start()
    diffs = side_changes(far, near)
    tile_at = lax.broadcasted_iota(jnp.int32, (TILE, cols), 0)
    below, above = level_fluxes(outer, inner, pl.ds(field * rows, rows))
    for side, level, change in (
        (0, 0, table[0, pl.ds(RISE, 1), :] * below),
        (1, levels - 1, -table[levels - 1, pl.ds(FALL, 1), :] * above),
    ):
        at = field * levels + level
        rim = ends(rows, cols, diffs[0][at : at + 1, :], diffs[1][at : at + 1, :])
        layers[side] = tend[field, level] + change + rim
        copies.append(pltpu.make_async_copy(layers.at[side], out.at[level], sems.at[1 + side]))
        copies[-1].start()
    for side, begin, row in ((0, 0, 0), (1, rows - TILE, TILE - 1)):
        for level in range(1, levels - 1):
            at = field * levels + level
            strips[side, level] = tend[field, level, pl.ds(begin, TILE), :] + jnp.where(
                tile_at == row, diffs[side][at : at + 1, :], 0.0
            )
        copies.append(
            pltpu.make_async_copy(
                strips.at[side, inside], out.at[inside, pl.ds(begin, TILE), :], sems.at[3 + side]
            )
        )
        copies[-1].start()
    for copy in copies:
        copy.wait()


def tends(field, table, tend, far, near, outer, inner):
    _, levels, rows, cols = tend.shape
    return pl.pallas_call(
        functools.partial(tends_kernel, field),
        out_shape=jax.ShapeDtypeStruct((levels, rows, cols), F32),
        in_specs=[whole(VMEM)] * 6,
        out_specs=whole(pl.ANY),
        scratch_shapes=[
            pltpu.VMEM((2, rows, cols), F32),
            pltpu.VMEM((2, levels, TILE, cols), F32),
            pltpu.SemaphoreType.DMA((5,)),
        ],
        compiler_params=pltpu.CompilerParams(vmem_limit_bytes=8 * MIB),
        cost_estimate=pl.CostEstimate(
            flops=2000 * levels * rows * cols,
            bytes_accessed=4 * levels * rows * cols,
            transcendentals=0,
        ),
        name="tends",
    )(in_vmem(table), in_vmem(tend), far, near, outer, inner)


def interface(low, high):
    coupling = low[ABOVE]
    return coupling, 1.0 / (1.0 - coupling * coupling * low[LAST] * high[FIRST])


def scalar_rows(ref, begin):
    return [ref[pl.ds(begin + at, 1), :] for at in range(7)]


def merge_kernel(bit, final, beside, mine, theirs, *rest):
    base, gains, merged, *half = rest[beside:]
    _, rows, cols = base.shape
    upper = bit_of("gz", bit) == 1
    own, far = scalar_rows(mine, 4 * rows), scalar_rows(theirs, 4 * rows)
    low = [jnp.where(upper, b, a) for a, b in zip(own, far)]
    high = [jnp.where(upper, a, b) for a, b in zip(own, far)]
    coupling, inverse = interface(low, high)
    to_high, to_low = high[FIRST] * coupling, low[LAST] * coupling
    low_out, high_out = low[CORNER] * coupling, high[CORNER] * coupling
    core = bit_of("gz", 0) == 1
    sends_last = bit_of("gz", bit + 1) == 0
    for field in range(2):

        def part(at):
            a = mine[pl.ds((at + field) * rows, rows), :]
            b = theirs[pl.ds((at + field) * rows, rows), :]
            return jnp.where(upper, b, a), jnp.where(upper, a, b)

        (low_first, high_first), (low_last, high_last) = part(0), part(2)
        above = inverse * (high_first + to_high * low_last)
        below = inverse * (low_last + to_low * high_first)
        base[field] = coupling * jnp.where(upper, below, above)
        all_first = low_first + low_out * above
        all_last = high_last + high_out * below
        if final:
            entry = jnp.where(sends_last, all_last, all_first)
            merged[pl.ds(field * rows, rows), :] = entry
            size = rows // 2
            half[0][pl.ds(field * size, size), :] = jnp.where(core, entry[size:], entry[:size])
        else:
            merged[pl.ds(field * rows, rows), :] = all_first
            merged[pl.ds((2 + field) * rows, rows), :] = all_last
    scalars = [
        low[FIRST] + low_out * inverse * to_high * low[CORNER],
        low_out * inverse * high[CORNER],
        high[LAST] + high_out * inverse * to_low * high[CORNER],
        low[BELOW],
        high[ABOVE],
        low[METRIC_BELOW],
        high[METRIC_ABOVE],
        jnp.zeros((1, cols), F32),
    ]
    for at, value in enumerate(scalars):
        merged[pl.ds((2 if final else 4) * rows + at, 1), :] = value
        if final:
            half[0][pl.ds(rows + at, 1), :] = value
    scale = coupling * inverse
    gains[...] = jnp.zeros(gains.shape, F32)
    gains[pl.ds(FROM_ABOVE, 1), :] = scale * high[CORNER] * jnp.where(upper, to_low, 1.0)
    gains[pl.ds(FROM_BELOW, 1), :] = scale * low[CORNER] * jnp.where(upper, 1.0, to_high)


def merge(bit, final, rows, mine, theirs, *beside):
    cols = mine.shape[1]
    shapes = [held(2, rows, cols), held(TILE, cols), held((2 if final else 4) * rows + TILE, cols)]
    if final:
        shapes.append(held(rows + TILE, cols))
    return pl.pallas_call(
        functools.partial(merge_kernel, bit, final, len(beside)),
        out_shape=tuple(shapes),
        in_specs=[whole(VMEM)] * 2 + [whole(pl.ANY)] * len(beside),
        out_specs=[whole(VMEM)] * len(shapes),
        compiler_params=pltpu.CompilerParams(vmem_limit_bytes=8 * MIB),
        name="merge",
    )(mine, theirs, *in_hbm(*beside))


def prepare_kernel(
    rounds, temp, w_vel, forward, table, changes, scalars, outer, inner, *rest
):
    bases, gains = rest[: rounds - 1], rest[rounds - 1 : 2 * rounds - 2]
    known, response, below_in, above_in = rest[2 * rounds - 2 :]
    levels, rows, cols = temp.shape
    upper = bit_of("gz", rounds - 1) == 1
    one, none = jnp.ones((1, cols), F32), jnp.zeros((1, cols), F32)
    below_gain, above_gain = jnp.where(upper, one, none), jnp.where(upper, none, one)
    below = above = None
    for step in range(rounds - 2, -1, -1):
        side = bit_of("gz", step) == 1
        from_above = gains[step][pl.ds(FROM_ABOVE, 1), :]
        from_below = gains[step][pl.ds(FROM_BELOW, 1), :]
        gain = from_above * above_gain + from_below * below_gain
        below_gain = jnp.where(side, gain, below_gain)
        above_gain = jnp.where(side, above_gain, gain)
        into = [bases[step][field] for field in range(2)]
        if below is None:
            below = above = [jnp.zeros((rows, cols), F32)] * 2
        else:
            into = [
                into[field] + from_above * above[field] + from_below * below[field]
                for field in range(2)
            ]
        below = [jnp.where(side, into[field], below[field]) for field in range(2)]
        above = [jnp.where(side, above[field], into[field]) for field in range(2)]
    for field in range(2):
        flux_below, flux_above = level_fluxes(outer, inner, pl.ds(field * rows, rows))
        below_in[field] = below[field] + scalars[pl.ds(METRIC_BELOW, 1), :] * flux_below
        above_in[field] = above[field] - scalars[pl.ds(METRIC_ABOVE, 1), :] * flux_above

    gain = above_gain * table[levels - 1, pl.ds(PIVOT, 1), :]
    for level in range(levels - 1, -1, -1):
        if level < levels - 1:
            gain = gain * table[level, pl.ds(UPPER_PIVOT, 1), :]
        gain = gain + below_gain * table[level, pl.ds(BELOW_FORWARD, 1), :]
        response[level] = jnp.broadcast_to(gain, (TILE, cols))

    row_at = lax.broadcasted_iota(jnp.int32, (TILE, cols), 0)
    width = 2 * TILE
    for field, cells in enumerate((temp, w_vel)):
        for begin in range(0, rows, width):
            at = pl.ds(begin, width)
            below = below_in[field, at, :]

            def solve(level, carry, factor, field=field, begin=begin, at=at, below=below, cells=cells):
                value = (
                    forward[field, level + 1, at, :]
                    + table[level, pl.ds(BELOW_FORWARD, 1), :] * below
                    + factor * carry
                )
                if begin == 0:
                    change = changes[pl.ds(field * levels + level, 1), :]
                    head = value[:TILE] + jnp.where(row_at == 0, change, 0.0)
                    value = jnp.concatenate([head, value[TILE:]])
                if begin == rows - width:
                    change = changes[pl.ds((2 + field) * levels + level, 1), :]
                    tail = value[-TILE:] + jnp.where(row_at == TILE - 1, change, 0.0)
                    value = jnp.concatenate([value[:-TILE], tail])
                known[field, level, at, :] = value - cells[level, at, :]
                return value

            carry = solve(levels - 1, above_in[field, at, :], table[levels - 1, pl.ds(PIVOT, 1), :])

            def step(back, carry, solve=solve):
                level = levels - 2 - back
                return solve(level, carry, table[level, pl.ds(UPPER_PIVOT, 1), :])

            lax.fori_loop(0, levels - 1, step, carry)


def prepare(rounds, temp, w_vel, forward, table, changes, scalars, outer, inner, bases, gains):
    levels, rows, cols = temp.shape
    return pl.pallas_call(
        functools.partial(prepare_kernel, rounds),
        out_shape=(held(2, levels, rows, cols), held(levels, TILE, cols)),
        in_specs=[whole(VMEM)] * (8 + 2 * (rounds - 1)),
        out_specs=[whole(VMEM)] * 2,
        scratch_shapes=[pltpu.VMEM((2, rows, cols), F32)] * 2,
        compiler_params=pltpu.CompilerParams(vmem_limit_bytes=8 * MIB),
        cost_estimate=pl.CostEstimate(
            flops=2000 * levels * rows * cols,
            bytes_accessed=24 * levels * rows * cols,
            transcendentals=0,
        ),
        name="prepare",
    )(
        in_vmem(temp), in_vmem(w_vel), in_vmem(forward), in_vmem(table), changes, scalars,
        outer, inner, *bases, *gains,
    )


def finish_kernel(rounds, swapped, known, response, mine, theirs, *rest):
    temp_next, w_next, result, sems = rest[2 if swapped else 0 :]
    _, levels, rows, cols = known.shape
    upper = bit_of("gz", rounds - 1) == 1
    own, far = scalar_rows(mine, 2 * rows), scalar_rows(theirs, rows)
    low = [jnp.where(upper, b, a) for a, b in zip(own, far)]
    high = [jnp.where(upper, a, b) for a, b in zip(own, far)]
    coupling, inverse = interface(low, high)
    scale = coupling * inverse
    to_other = scale * coupling * jnp.where(upper, low[LAST], high[FIRST])
    width, half = 2 * TILE, rows // 2
    core = bit_of("gz", 0)
    start = pl.multiple_of((1 - core if swapped else core) * half, half)
    copies = []
    for field, out in enumerate((temp_next, w_next)):
        for begin in range(0, half, width):
            here = pl.ds(field * rows + start + begin, width)
            into = scale * theirs[pl.ds(field * half + begin, width), :] + to_other * mine[here, :]
            tiles = [into[i : i + TILE] for i in range(0, width, TILE)]

            def step(level, carry, field=field, begin=begin, tiles=tiles):
                gain = response[level]
                for i, tile in enumerate(tiles):
                    at = begin + i * TILE
                    value = known[field, level, pl.ds(start + at, TILE), :] + gain * tile
                    result[field, level, pl.ds(at, TILE), :] = value
                return carry

            lax.fori_loop(0, levels, step, 0, unroll=4)
        copies.append(
            pltpu.make_async_copy(
                result.at[field], out.at[:, pl.ds(start, half), :], sems.at[field]
            )
        )
        copies[-1].start()
    for copy in copies:
        copy.wait()


def finish(rounds, known, response, mine, theirs, written=()):
    _, levels, rows, cols = known.shape
    return pl.pallas_call(
        functools.partial(finish_kernel, rounds, bool(written)),
        out_shape=(jax.ShapeDtypeStruct((levels, rows, cols), F32),) * 2,
        in_specs=[whole(VMEM)] * 4 + [whole(pl.ANY)] * len(written),
        out_specs=[whole(pl.ANY)] * 2,
        scratch_shapes=[
            pltpu.VMEM((2, levels, rows // 2, cols), F32),
            pltpu.SemaphoreType.DMA((2,)),
        ],
        input_output_aliases={4: 0, 5: 1} if written else {},
        compiler_params=pltpu.CompilerParams(vmem_limit_bytes=8 * MIB),
        cost_estimate=pl.CostEstimate(
            flops=20000 * levels * rows * cols,
            bytes_accessed=8 * levels * rows * cols,
            transcendentals=0,
        ),
        name="finish",
    )(in_vmem(known), response, mine, theirs, *written)


def both_ways(pairs):
    return pairs + [(b, a) for a, b in pairs]


def local(temp, u_vel, v_vel, w_vel, temp_prev, w_prev, lower, upper, metric):
    rows = temp.shape[1]
    across, stacked = lax.axis_size("gx"), lax.axis_size("gz")
    rounds = stacked.bit_length() - 1
    cores = both_ways([(i, i + 1) for i in range(0, stacked, 2)])
    seams = both_ways([(i, i + 1) for i in range(1, stacked - 1, 2)])
    seams = seams + [(i, i) for i in (0, stacked - 1)]
    far, near, outer, inner, table, scalars = edges(
        temp, u_vel, w_vel, v_vel, temp_prev, w_prev, lower, upper, metric
    )
    far = lax.ppermute(far, "gx", both_ways([(i, (i + 1) % across) for i in range(1, across, 2)]))
    near = lax.ppermute(near, "gx", both_ways([(i, i + 1) for i in range(0, across, 2)]))
    outer = lax.ppermute(outer, "gz", seams)
    inner = lax.ppermute(inner, "gz", cores)
    forward, tend, first = bulk(table, temp, u_vel, v_vel, w_vel, temp_prev, w_prev)
    mine, changes = fix(far, near, outer, inner, forward, first, table, scalars)
    temp_tend = tends(0, table, tend, far, near, outer, inner)
    bases, gains = [], []
    for step in range(rounds - 1):
        theirs = lax.ppermute(mine, "gz", [(i, i ^ (1 << step)) for i in range(stacked)])
        base, gain, mine, *half = merge(step, step + 2 == rounds, rows, mine, theirs, temp_tend)
        bases.append(base)
        gains.append(gain)
    (half,) = half
    theirs = lax.ppermute(half, "gz", [(i, i ^ (stacked // 2)) for i in range(stacked)])
    swapped = lax.ppermute(theirs, "gz", cores)
    w_tend = tends(1, table, tend, far, near, outer, inner)
    known, response = prepare(
        rounds, temp, w_vel, forward, table, changes, scalars, outer, inner, bases, gains
    )
    written = finish(rounds, known, response, mine, theirs)
    temp_next, w_next = finish(rounds, known, response, mine, swapped, written)
    return temp_next, w_next, temp_tend, w_tend


def solution(mesh):
    field = P("gz", "gx", None)
    return jax.shard_map(
        local,
        mesh=mesh,
        in_specs=(field,) * 6 + (P("gz"),) * 3,
        out_specs=(field,) * 4,
        check_vma=False,
    )
```

time: 25 us -> 23.6 us (0.944)
  waiting for transfers between devices: 3.38 us -> 1.54 us
  starting transfers between devices: 10.6 us -> 11.1 us
    ppermute x3 -> x6, starting transfers between devices: 7.38 us -> 11 us  [the longest x1 6.07 us: local(): lax.ppermute(far, 'gx', both_ways([(i, (i + 1) % across) for i in range(1...]
    ppermute x2 -> x1, starting transfers between devices: 3.25 us -> 0.11 us  [local(): lax.ppermute(mine, 'gz', [(i, i ^ 1 << step) for i in range(stacked)])]
    ppermute x2 -> x1, waiting for transfers between devices: 3.38 us -> 0.5 us  [local(): lax.ppermute(mine, 'gz', [(i, i ^ 1 << step) for i in range(stacked)])]
    ppermute x3 -> x6, waiting for transfers between devices: 0.01 us -> 1.04 us  [the longest x1 0.84 us: local(): lax.ppermute(half, 'gz', [(i, i ^ stacked // 2) for i in range(stacked)])]
    pallas_call x1, Pallas kernels: 3.65 us -> 2.79 us  [bulk(): pl.pallas_call(bulk_kernel, out_shape=(held(2, levels + 1, rows, cols), h...]
    pallas_call x4 -> x6, Pallas kernels: 3.65 us -> 4.38 us  [the longest x2 2.15 us: finish(): pl.pallas_call(functools.partial(finish_kernel, rounds, bool(written)), o...]
  transfers between devices with their start and end apart: 5 -> 7, of which waited for: 2 -> 3; matrix products, arithmetic and copies ran while one was open for 0% -> 0% of each run, Pallas kernels for 27% -> 30%
where the time goes in v3:
time: 23.6 us; the launch traced here: 23.4 us
  starting transfers between devices  11.1 us (47%)
  Pallas kernels  9.93 us (42%)
  waiting for transfers between devices  1.54 us (7%)
  between operations  0.8 us (3%)
    ppermute x1, starting transfers between devices, local(): lax.ppermute(far, 'gx', both_ways([(i, (i + 1) % across) for i in range(1...  6.07 us
    ppermute x1, starting transfers between devices, local(): inner = lax.ppermute(inner, 'gz', cores)  2.91 us
    pallas_call x1, Pallas kernels, bulk(): pl.pallas_call(bulk_kernel, out_shape=(held(2, levels + 1, rows, cols), h...  2.79 us
    pallas_call x2, Pallas kernels, finish(): pl.pallas_call(functools.partial(finish_kernel, rounds, bool(written)), o...  2.15 us
    pallas_call x2, Pallas kernels, tends(): pl.pallas_call(functools.partial(tends_kernel, field), out_shape=jax.Shap...  1.99 us
    pallas_call x1, Pallas kernels, edges(): pl.pallas_call(edges_kernel, out_shape=(held(2 * levels, cols), held(2 *...  1.59 us
    ppermute x1, starting transfers between devices, local(): lax.ppermute(half, 'gz', [(i, i ^ stacked // 2) for i in range(stacked)])  1.39 us
    pallas_call x1, Pallas kernels, prepare(): pl.pallas_call(functools.partial(prepare_kernel, rounds), out_shape=(held...  1.17 us
  transfers between devices with their start and end apart: 7, of which 3 were waited for; matrix products, arithmetic and copies ran while one was open for 0% of the time, Pallas kernels for 30%

profile of v3, /device:TPU:0, one launch (start us, length us, event | category | flops | bytes accessed | tf_op | source)
XLA Modules:
  0.0 23.4 jit_solution(18280350106243732903)
XLA Ops:
  0.7 1.6 %edges.1 = (f32[32,256]{1,0:T(8,128)S(1)}, f32[32,256]{1,0:T(8,128)S(1)}, f32[128,256]{1,0:T(8,128)S(1)}, f32[128,256]{1,0:T(8,128)S(1)}, f32[16,8,256]{2,1,0:T(8,128)S(1)}, /*index=5*/f32[8,256]{1,0:T(8,128)S(1)}) custom-call(f32[16,64,256]{2,1,0:T(8,128)} %temp.5, f32[16,64,256]{2,1,0:T(8,128)} %u_vel.3, f32[16,64,256]{2,1,0:T(8,128)} %w_vel.5, ...), custom_call_target="tpu_custom_call" | custom-call | tf_op jit(solution)/shard_map/edges/pallas_call | solution.py:106
  2.3 6.1 %collective-permute-start = (f32[32,256]{1,0:T(8,128)S(1)}, f32[32,256]{1,0:T(8,128)S(1)}, u32[]{:S(2)}, u32[]{:S(2)}) collective-permute-start(f32[32,256]{1,0:T(8,128)S(1)} %get-tuple-element.27), channel_id=1, source_target_pairs={{4,8},{12,16},{20,24},{28,0},{8,4},{16,12},{24,20},{0,28},{5,9},{1... | collective-permute-start | bytes 98312 | tf_op jit(solution)/shard_map/ppermute | solution.py:638
  8.4 0.0 collective-permute-start.1
  8.4 0.7 %collective-permute-start.2 = (f32[128,256]{1,0:T(8,128)S(1)}, f32[128,256]{1,0:T(8,128)S(1)}, u32[]{:S(2)}, u32[]{:S(2)}) collective-permute-start(f32[128,256]{1,0:T(8,128)S(1)} %get-tuple-element.29), channel_id=1, source_target_pairs={{1,2},{2,1},{0,0},{3,3},{5,6},{6,5},{4,4},{7,7},{9,10},{10,9},{8,8... | collective-permute-start | bytes 393224 | tf_op jit(solution)/shard_map/ppermute | solution.py:640
  9.0 2.9 %collective-permute-start.3 = (f32[128,256]{1,0:T(8,128)S(1)}, f32[128,256]{1,0:T(8,128)S(1)}, u32[]{:S(2)}, u32[]{:S(2)}) collective-permute-start(f32[128,256]{1,0:T(8,128)S(1)} %get-tuple-element.30), channel_id=1, source_target_pairs={{0,1},{2,3},{1,0},{3,2},{4,5},{6,7},{5,4},{7,6},{8,9},{10,11},{9,8... | collective-permute-start | bytes 393224 | tf_op jit(solution)/shard_map/ppermute | solution.py:641
  11.9 0.0 copy-done.1
  12.0 2.8 %bulk.1 = (f32[2,17,64,256]{3,2,1,0:T(8,128)S(1)}, f32[2,16,64,256]{3,2,1,0:T(8,128)S(1)}, f32[2,64,256]{2,1,0:T(8,128)S(1)}) custom-call(f32[16,8,256]{2,1,0:T(8,128)S(1)} %get-tuple-element.25.table, f32[16,64,256]{2,1,0:T(8,128)S(1)} %copy-done, f32[16,64,256]{2,1,0:T(8,128)S(1)} %copy-done.2, f32[16,64,256]{2,1,0:T(8,128)S(1)} %copy-done.3, ...), custom_call_target="tpu_custom_call" | custom-call | flops 1835008000 | bytes 6291456 | tf_op jit(solution)/shard_map/bulk/pallas_call | solution.py:244
  14.8 0.0 collective-permute-done.far
  14.8 0.0 collective-permute-done.1.near
  14.8 0.0 collective-permute-done.2.outer
  14.8 0.0 collective-permute-done.3.inner
  14.8 0.1 fix.1
  14.9 0.1 collective-permute-start.4
  15.1 1.0 %tends.2.rest_0_ = f32[16,64,256]{2,1,0:T(8,128)} custom-call(f32[16,8,256]{2,1,0:T(8,128)S(1)} %get-tuple-element.25.table, f32[2,16,64,256]{3,2,1,0:T(8,128)S(1)} %get-tuple-element.35.tend, f32[32,256]{1,0:T(8,128)S(1)} %collective-permute-done.far, f32[32,256]{1,0:T(8,128)S(1)} %collective-permute-done.1.near, ...), custom_call_target="tpu_custom_call" | custom-call | flops 524288000 | bytes 1048576 | tf_op jit(solution)/shard_map/tends/pallas_call | solution.py:373
  16.1 0.5 %collective-permute-done.4.theirs = f32[264,256]{1,0:T(8,128)S(1)} collective-permute-done((f32[264,256]{1,0:T(8,128)S(1)}, f32[264,256]{1,0:T(8,128)S(1)}, u32[]{:S(2)}, u32[]{:S(2)}) %collective-permute-start.4) | collective-permute-done | bytes 270368 | tf_op jit(solution)/shard_map/ppermute | solution.py:647
  16.6 0.1 merge.1
  16.7 1.4 %collective-permute-start.5 = (f32[72,256]{1,0:T(8,128)S(1)}, f32[72,256]{1,0:T(8,128)S(1)}, u32[]{:S(2)}, u32[]{:S(2)}) collective-permute-start(f32[72,256]{1,0:T(8,128)S(1)} %get-tuple-element.41), channel_id=1, source_target_pairs={{0,2},{1,3},{2,0},{3,1},{4,6},{5,7},{6,4},{7,5},{8,10},{9,11},{10,... | collective-permute-start | bytes 221192 | tf_op jit(solution)/shard_map/ppermute | solution.py:652
  18.1 1.0 %tends.3 = f32[16,64,256]{2,1,0:T(8,128)} custom-call(f32[16,8,256]{2,1,0:T(8,128)S(1)} %get-tuple-element.25.table, f32[2,16,64,256]{3,2,1,0:T(8,128)S(1)} %get-tuple-element.35.tend, f32[32,256]{1,0:T(8,128)S(1)} %collective-permute-done.far, f32[32,256]{1,0:T(8,128)S(1)} %collective-permute-done.1.near, f32[128,256]{1,0:T(8,128)S(1)} %collective-permute-done.2.outer, ...), custom_call_target="tpu_custom_call" | custom-call | flops 524288000 | bytes 1048576 | tf_op jit(solution)/shard_map/tends/pallas_call | solution.py:373
  19.1 1.2 %prepare.1 = (f32[2,16,64,256]{3,2,1,0:T(8,128)S(1)}, f32[16,8,256]{2,1,0:T(8,128)S(1)}) custom-call(f32[16,64,256]{2,1,0:T(8,128)S(1)} %copy-done, f32[16,64,256]{2,1,0:T(8,128)S(1)} %copy-done.1, f32[2,17,64,256]{3,2,1,0:T(8,128)S(1)} %get-tuple-element.26.forward, f32[16,8,256]{2,1,0:T(8,128)S(1)} %get-tuple-element.25.table, ...), custom_call_target="tpu_custom_call" | custom-call | flops 524288000 | bytes 6291456 | tf_op jit(solution)/shard_map/prepare/pallas_call | solution.py:544
  20.2 0.8 %collective-permute-done.5.theirs = f32[72,256]{1,0:T(8,128)S(1)} collective-permute-done((f32[72,256]{1,0:T(8,128)S(1)}, f32[72,256]{1,0:T(8,128)S(1)}, u32[]{:S(2)}, u32[]{:S(2)}) %collective-permute-start.5) | collective-permute-done | bytes 73760 | tf_op jit(solution)/shard_map/ppermute | solution.py:652
  21.1 0.0 collective-permute-start.6
  21.1 1.1 %finish.2 = (f32[16,64,256]{2,1,0:T(8,128)}, f32[16,64,256]{2,1,0:T(8,128)}) custom-call(f32[2,16,64,256]{3,2,1,0:T(8,128)S(1)} %get-tuple-element.38.known, f32[16,8,256]{2,1,0:T(8,128)S(1)} %get-tuple-element.39.response, f32[136,256]{1,0:T(8,128)S(1)} %get-tuple-element.40.mine, f32[72,256]{1,0:T(8,128)S(1)} %collective-permute-done.5.theirs), custom_call_target="tpu_custom_call" | custom-call | flops 5242880000 | bytes 2097152 | tf_op jit(solution)/shard_map/finish/pallas_call | solution.py:604
  22.2 0.2 collective-permute-done.6.theirs
  22.4 1.1 %finish.3 = (f32[16,64,256]{2,1,0:T(8,128)}, f32[16,64,256]{2,1,0:T(8,128)}) custom-call(f32[2,16,64,256]{3,2,1,0:T(8,128)S(1)} %get-tuple-element.38.known, f32[16,8,256]{2,1,0:T(8,128)S(1)} %get-tuple-element.39.response, f32[136,256]{1,0:T(8,128)S(1)} %get-tuple-element.40.mine, ...), custom_call_target="tpu_custom_call", output_to_operand_aliasing={{0}: (4, {}), {1}: (5, {})} | custom-call | flops 5242880000 | bytes 2097152 | tf_op jit(solution)/shard_map/finish/pallas_call | solution.py:604
  (11 shorter events, 0.0 us)
Async XLA Ops:
  0.6 11.3 %copy-start.1 = (f32[16,64,256]{2,1,0:T(8,128)S(1)}, f32[16,64,256]{2,1,0:T(8,128)}, u32[]{:S(2)}) copy-start(f32[16,64,256]{2,1,0:T(8,128)} %w_vel.5) | copy-start | bytes 3145732
  0.6 11.3 %copy-start = (f32[16,64,256]{2,1,0:T(8,128)S(1)}, f32[16,64,256]{2,1,0:T(8,128)}, u32[]{:S(2)}) copy-start(f32[16,64,256]{2,1,0:T(8,128)} %temp.5) | copy-start | bytes 3145732
  0.7 11.3 %copy-start.5 = (f32[16,64,256]{2,1,0:T(8,128)S(1)}, f32[16,64,256]{2,1,0:T(8,128)}, u32[]{:S(2)}) copy-start(f32[16,64,256]{2,1,0:T(8,128)} %w_prev.3) | copy-start | bytes 3145732
  0.7 11.3 %copy-start.4 = (f32[16,64,256]{2,1,0:T(8,128)S(1)}, f32[16,64,256]{2,1,0:T(8,128)}, u32[]{:S(2)}) copy-start(f32[16,64,256]{2,1,0:T(8,128)} %temp_prev.3) | copy-start | bytes 3145732
  0.7 11.3 %copy-start.3 = (f32[16,64,256]{2,1,0:T(8,128)S(1)}, f32[16,64,256]{2,1,0:T(8,128)}, u32[]{:S(2)}) copy-start(f32[16,64,256]{2,1,0:T(8,128)} %v_vel.3) | copy-start | bytes 3145732
  0.7 11.3 %copy-start.2 = (f32[16,64,256]{2,1,0:T(8,128)S(1)}, f32[16,64,256]{2,1,0:T(8,128)}, u32[]{:S(2)}) copy-start(f32[16,64,256]{2,1,0:T(8,128)} %u_vel.3) | copy-start | bytes 3145732
  2.3 12.5 %collective-permute-start = (f32[32,256]{1,0:T(8,128)S(1)}, f32[32,256]{1,0:T(8,128)S(1)}, u32[]{:S(2)}, u32[]{:S(2)}) collective-permute-start(f32[32,256]{1,0:T(8,128)S(1)} %get-tuple-element.27), channel_id=1, source_target_pairs={{4,8},{12,16},{20,24},{28,0},{8,4},{16,12},{24,20},{0,28},{5,9},{1... | collective-permute-start | bytes 98312 | tf_op jit(solution)/shard_map/ppermute | solution.py:638
  8.4 6.4 %collective-permute-start.1 = (f32[32,256]{1,0:T(8,128)S(1)}, f32[32,256]{1,0:T(8,128)S(1)}, u32[]{:S(2)}, u32[]{:S(2)}) collective-permute-start(f32[32,256]{1,0:T(8,128)S(1)} %get-tuple-element.28), channel_id=1, source_target_pairs={{0,4},{8,12},{16,20},{24,28},{4,0},{12,8},{20,16},{28,24},{1,5},{9... | collective-permute-start | bytes 98312 | tf_op jit(solution)/shard_map/ppermute | solution.py:639
  8.4 6.4 %collective-permute-start.2 = (f32[128,256]{1,0:T(8,128)S(1)}, f32[128,256]{1,0:T(8,128)S(1)}, u32[]{:S(2)}, u32[]{:S(2)}) collective-permute-start(f32[128,256]{1,0:T(8,128)S(1)} %get-tuple-element.29), channel_id=1, source_target_pairs={{1,2},{2,1},{0,0},{3,3},{5,6},{6,5},{4,4},{7,7},{9,10},{10,9},{8,8... | collective-permute-start | bytes 393224 | tf_op jit(solution)/shard_map/ppermute | solution.py:640
  9.0 5.8 %collective-permute-start.3 = (f32[128,256]{1,0:T(8,128)S(1)}, f32[128,256]{1,0:T(8,128)S(1)}, u32[]{:S(2)}, u32[]{:S(2)}) collective-permute-start(f32[128,256]{1,0:T(8,128)S(1)} %get-tuple-element.30), channel_id=1, source_target_pairs={{0,1},{2,3},{1,0},{3,2},{4,5},{6,7},{5,4},{7,6},{8,9},{10,11},{9,8... | collective-permute-start | bytes 393224 | tf_op jit(solution)/shard_map/ppermute | solution.py:641
  14.9 1.6 %collective-permute-start.4 = (f32[264,256]{1,0:T(8,128)S(1)}, f32[264,256]{1,0:T(8,128)S(1)}, u32[]{:S(2)}, u32[]{:S(2)}) collective-permute-start(f32[264,256]{1,0:T(8,128)S(1)} %get-tuple-element.34.mine), channel_id=1, source_target_pairs={{0,1},{1,0},{2,3},{3,2},{4,5},{5,4},{6,7},{7,6},{8,9},{9,8},{10,11... | collective-permute-start | bytes 811016 | tf_op jit(solution)/shard_map/ppermute | solution.py:647
  16.7 4.4 %collective-permute-start.5 = (f32[72,256]{1,0:T(8,128)S(1)}, f32[72,256]{1,0:T(8,128)S(1)}, u32[]{:S(2)}, u32[]{:S(2)}) collective-permute-start(f32[72,256]{1,0:T(8,128)S(1)} %get-tuple-element.41), channel_id=1, source_target_pairs={{0,2},{1,3},{2,0},{3,1},{4,6},{5,7},{6,4},{7,5},{8,10},{9,11},{10,... | collective-permute-start | bytes 221192 | tf_op jit(solution)/shard_map/ppermute | solution.py:652
  21.1 1.3 %collective-permute-start.6 = (f32[72,256]{1,0:T(8,128)S(1)}, f32[72,256]{1,0:T(8,128)S(1)}, u32[]{:S(2)}, u32[]{:S(2)}) collective-permute-start(f32[72,256]{1,0:T(8,128)S(1)} %collective-permute-done.5.theirs), channel_id=1, source_target_pairs={{0,1},{2,3},{1,0},{3,2},{4,5},{6,7},{5,4},{7,6},{8,9},{10,11},{9,8... | collective-permute-start | bytes 221192 | tf_op jit(solution)/shard_map/ppermute | solution.py:653

commit v4 on v3

--- a/solution.py
+++ b/solution.py
@@ -52,12 +52,10 @@
     lower,
     upper,
     metric,
+    near,
     far,
-    near,
-    outer,
-    inner,
+    fluxes,
     table,
-    scalars,
     strips,
     layers,
     lower_at,
@@ -78,7 +76,7 @@
         copy.start()
     for copy in copies[:3]:
         copy.wait()
-    coefficients(lower_at, upper_at, metric_at, table, scalars)
+    coefficients(lower_at, upper_at, metric_at, table, fluxes.at[pl.ds(4 * rows, TILE)])
     for copy in copies[3:]:
         copy.wait()
     odd = bit_of("gx", 0) == 1
@@ -94,11 +92,11 @@
     wall = (position == 0) | (position == lax.axis_size("gz") - 1)
     zero = jnp.zeros((rows, cols), F32)
     for field in range(2):
-        at = pl.ds(field * rows, rows)
         bottom = layers[1, 0] * layers[field, 0]
         top = layers[1, 1] * layers[field, 1]
-        outer[at, :] = jnp.where(wall, zero, jnp.where(upper_core, top, bottom))
-        inner[at, :] = jnp.where(upper_core, bottom, top)
+        fluxes[pl.ds(field * rows, rows), :] = jnp.where(upper_core, bottom, top)
+        outward = jnp.where(wall, zero, jnp.where(upper_core, top, bottom))
+        fluxes[pl.ds((2 + field) * rows, rows), :] = outward
 
 
 def edges(temp, u_vel, w_vel, v_vel, temp_prev, w_prev, lower, upper, metric):
@@ -108,13 +106,11 @@
         out_shape=(
             held(2 * levels, cols),
             held(2 * levels, cols),
-            held(2 * rows, cols),
-            held(2 * rows, cols),
+            held(4 * rows + TILE, cols),
             held(levels, TILE, cols),
-            held(TILE, cols),
         ),
         in_specs=[whole(pl.ANY)] * 9,
-        out_specs=[whole(VMEM)] * 6,
+        out_specs=[whole(VMEM)] * 4,
         scratch_shapes=[
             pltpu.VMEM((3, 2, levels, TILE, cols), F32),
             pltpu.VMEM((2, 2, rows, cols), F32),
@@ -252,7 +248,7 @@
         out_specs=[whole(VMEM)] * 3,
         compiler_params=pltpu.CompilerParams(vmem_limit_bytes=8 * MIB),
         cost_estimate=pl.CostEstimate(
-            flops=7000 * levels * rows * cols,
+            flops=100000 * levels * rows * cols,
             bytes_accessed=24 * levels * rows * cols,
             transcendentals=0,
         ),
@@ -260,14 +256,18 @@
     )(*map(in_vmem, (table, *arrays)))
 
 
-def side_changes(far, near):
+def side_changes(near, far):
     odd = bit_of("gx", 0) == 1
     return jnp.where(odd, near[...], far[...]), jnp.where(odd, far[...], near[...])
 
 
-def level_fluxes(outer, inner, at):
+def level_fluxes(inner, outer):
     upper = bit_of("gz", 0) == 1
-    return jnp.where(upper, inner[at, :], outer[at, :]), jnp.where(upper, outer[at, :], inner[at, :])
+    return jnp.where(upper, inner, outer), jnp.where(upper, outer, inner)
+
+
+def beside_seam(rounds):
+    return bit_of("gz", 0) != bit_of("gz", rounds - 1)
 
 
 def ends(rows, cols, head, tail):
@@ -275,16 +275,43 @@
     return jnp.where(at == 0, head, jnp.where(at == rows - 1, tail, 0.0))
 
 
-def fix_kernel(
-    levels, far, near, outer, inner, forward, first, table, scalars, message, changes
-):
+def scalar_rows(ref, begin=0):
+    return [ref[pl.ds(begin + at, 1), :] for at in range(7)]
+
+
+def in_order(upper, own, other):
+    low = [jnp.where(upper, b, a) for a, b in zip(own, other)]
+    high = [jnp.where(upper, a, b) for a, b in zip(own, other)]
+    return low, high
+
+
+def interface(low, high):
+    coupling = low[ABOVE]
+    return coupling, 1.0 / (1.0 - coupling * coupling * low[LAST] * high[FIRST])
+
+
+def joint_scalars(low, high):
+    coupling, inverse = interface(low, high)
+    low_out, high_out = low[CORNER] * coupling, high[CORNER] * coupling
+    return [
+        low[FIRST] + low_out * low_out * inverse * high[FIRST],
+        low_out * inverse * high[CORNER],
+        high[LAST] + high_out * high_out * inverse * low[LAST],
+        low[BELOW],
+        high[ABOVE],
+        low[METRIC_BELOW],
+        high[METRIC_ABOVE],
+        jnp.zeros_like(coupling),
+    ]
+
+
+def fix_kernel(rounds, levels, near, far, fluxes, other, forward, first, table, *rest):
+    outer, rest = (rest[0], rest[1:]) if rounds > 2 else (None, rest)
+    message, changes, *late = rest
     _, rows, cols = first.shape
-    diffs = side_changes(far, near)
-
-    def scalar(at):
-        return scalars[pl.ds(at, 1), :]
-
-    below, above = scalar(METRIC_BELOW), -scalar(METRIC_ABOVE)
+    diffs = side_changes(near, far)
+    scalars = scalar_rows(fluxes, 4 * rows)
+    below, above = scalars[METRIC_BELOW], -scalars[METRIC_ABOVE]
     for field in range(2):
         firsts, lasts = [], []
         for side in range(2):
@@ -300,36 +327,53 @@
                 changes[pl.ds((side * 2 + field) * levels + level, 1), :] = value
             firsts.append(total)
             lasts.append(value)
-        flux_below, flux_above = level_fluxes(outer, inner, pl.ds(field * rows, rows))
-        message[pl.ds(field * rows, rows), :] = (
+        at = pl.ds(field * rows, rows)
+        flux_below, flux_above = level_fluxes(other[at, :], 0.0 if outer is None else outer[at, :])
+        message[at, :] = (
             first[field]
-            + (below * scalar(FIRST)) * flux_below
-            + (above * scalar(CORNER)) * flux_above
+            + (below * scalars[FIRST]) * flux_below
+            + (above * scalars[CORNER]) * flux_above
             + ends(rows, cols, *firsts)
         )
         message[pl.ds((2 + field) * rows, rows), :] = (
             forward[field, levels]
-            + (below * scalar(CORNER)) * flux_below
-            + (above * scalar(LAST)) * flux_above
+            + (below * scalars[CORNER]) * flux_below
+            + (above * scalars[LAST]) * flux_above
             + ends(rows, cols, *lasts)
         )
-    message[pl.ds(4 * rows, TILE), :] = scalars[...]
-
-
-def fix(far, near, outer, inner, forward, first, table, scalars):
+    if not late:
+        return
+    seam, half = late
+    core, size = bit_of("gz", 0) == 1, rows // 2
+    for field in range(2):
+        outward = pl.ds((2 + field) * rows, rows)
+        value = jnp.where(beside_seam(rounds), fluxes[outward, :], other[outward, :])
+        seam[pl.ds(field * rows, rows), :] = value
+        half[pl.ds(field * size, size), :] = jnp.where(core, value[size:], value[:size])
+    for at, value in enumerate(
+        joint_scalars(*in_order(core, scalars, scalar_rows(other, 4 * rows)))
+    ):
+        half[pl.ds(rows + at, 1), :] = value
+
+
+def fix(rounds, near, far, fluxes, other, forward, first, table, outer):
     levels = table.shape[0]
     _, rows, cols = first.shape
+    shapes = [held(4 * rows, cols), held(4 * levels, cols)]
+    if rounds == 2:
+        shapes += [held(2 * rows, cols), held(rows + TILE, cols)]
     return pl.pallas_call(
-        functools.partial(fix_kernel, levels),
-        out_shape=(held(4 * rows + TILE, cols), held(4 * levels, cols)),
-        in_specs=[whole(VMEM)] * 8,
-        out_specs=[whole(VMEM)] * 2,
+        functools.partial(fix_kernel, rounds, levels),
+        out_shape=tuple(shapes),
+        in_specs=[whole(VMEM)] * (7 + len(outer)),
+        out_specs=[whole(VMEM)] * len(shapes),
         compiler_params=pltpu.CompilerParams(vmem_limit_bytes=8 * MIB),
         name="fix",
-    )(far, near, outer, inner, in_vmem(forward), in_vmem(first), in_vmem(table), scalars)
-
-
-def tends_kernel(field, table, tend, far, near, outer, inner, out, layers, strips, sems):
+    )(near, far, fluxes, other, in_vmem(forward), in_vmem(first), in_vmem(table), *outer)
+
+
+def tends_kernel(rounds, field, table, tend, near, far, other, *rest):
+    *outer, out, layers, strips, sems = rest
     _, levels, rows, cols = tend.shape
     inside = pl.ds(1, levels - 2)
     copies = [
@@ -340,9 +384,10 @@
         )
     ]
     copies[0].start()
-    diffs = side_changes(far, near)
+    diffs = side_changes(near, far)
     tile_at = lax.broadcasted_iota(jnp.int32, (TILE, cols), 0)
-    below, above = level_fluxes(outer, inner, pl.ds(field * rows, rows))
+    at = pl.ds(field * rows, rows)
+    below, above = level_fluxes(other[at, :], outer[0][at, :] if outer else 0.0)
     for side, level, change in (
         (0, 0, table[0, pl.ds(RISE, 1), :] * below),
         (1, levels - 1, -table[levels - 1, pl.ds(FALL, 1), :] * above),
@@ -368,12 +413,12 @@
         copy.wait()
 
 
-def tends(field, table, tend, far, near, outer, inner):
+def tends(rounds, field, table, tend, near, far, other, outer):
     _, levels, rows, cols = tend.shape
     return pl.pallas_call(
-        functools.partial(tends_kernel, field),
+        functools.partial(tends_kernel, rounds, field),
         out_shape=jax.ShapeDtypeStruct((levels, rows, cols), F32),
-        in_specs=[whole(VMEM)] * 6,
+        in_specs=[whole(VMEM)] * (5 + len(outer)),
         out_specs=whole(pl.ANY),
         scratch_shapes=[
             pltpu.VMEM((2, rows, cols), F32),
@@ -382,30 +427,18 @@
         ],
         compiler_params=pltpu.CompilerParams(vmem_limit_bytes=8 * MIB),
         cost_estimate=pl.CostEstimate(
-            flops=2000 * levels * rows * cols,
+            flops=levels * rows * cols,
             bytes_accessed=4 * levels * rows * cols,
             transcendentals=0,
         ),
         name="tends",
-    )(in_vmem(table), in_vmem(tend), far, near, outer, inner)
-
-
-def interface(low, high):
-    coupling = low[ABOVE]
-    return coupling, 1.0 / (1.0 - coupling * coupling * low[LAST] * high[FIRST])
-
-
-def scalar_rows(ref, begin):
-    return [ref[pl.ds(begin + at, 1), :] for at in range(7)]
-
-
-def merge_kernel(bit, final, beside, mine, theirs, *rest):
-    base, gains, merged, *half = rest[beside:]
+    )(in_vmem(table), in_vmem(tend), near, far, other, *outer)
+
+
+def merge_kernel(bit, final, own_at, other_at, mine, theirs, own, other, base, gains, scalars, merged, *half):
     _, rows, cols = base.shape
     upper = bit_of("gz", bit) == 1
-    own, far = scalar_rows(mine, 4 * rows), scalar_rows(theirs, 4 * rows)
-    low = [jnp.where(upper, b, a) for a, b in zip(own, far)]
-    high = [jnp.where(upper, a, b) for a, b in zip(own, far)]
+    low, high = in_order(upper, scalar_rows(own, own_at), scalar_rows(other, other_at))
     coupling, inverse = interface(low, high)
     to_high, to_low = high[FIRST] * coupling, low[LAST] * coupling
     low_out, high_out = low[CORNER] * coupling, high[CORNER] * coupling
@@ -432,44 +465,38 @@
         else:
             merged[pl.ds(field * rows, rows), :] = all_first
             merged[pl.ds((2 + field) * rows, rows), :] = all_last
-    scalars = [
-        low[FIRST] + low_out * inverse * to_high * low[CORNER],
-        low_out * inverse * high[CORNER],
-        high[LAST] + high_out * inverse * to_low * high[CORNER],
-        low[BELOW],
-        high[ABOVE],
-        low[METRIC_BELOW],
-        high[METRIC_ABOVE],
-        jnp.zeros((1, cols), F32),
-    ]
-    for at, value in enumerate(scalars):
-        merged[pl.ds((2 if final else 4) * rows + at, 1), :] = value
-        if final:
-            half[0][pl.ds(rows + at, 1), :] = value
+    for at, value in enumerate(joint_scalars(low, high)):
+        scalars[pl.ds(at, 1), :] = value
     scale = coupling * inverse
     gains[...] = jnp.zeros(gains.shape, F32)
     gains[pl.ds(FROM_ABOVE, 1), :] = scale * high[CORNER] * jnp.where(upper, to_low, 1.0)
     gains[pl.ds(FROM_BELOW, 1), :] = scale * low[CORNER] * jnp.where(upper, 1.0, to_high)
 
 
-def merge(bit, final, rows, mine, theirs, *beside):
+def merge(bit, final, rows, mine, theirs, own, other):
     cols = mine.shape[1]
-    shapes = [held(2, rows, cols), held(TILE, cols), held((2 if final else 4) * rows + TILE, cols)]
-    if final:
-        shapes.append(held(rows + TILE, cols))
     return pl.pallas_call(
-        functools.partial(merge_kernel, bit, final, len(beside)),
-        out_shape=tuple(shapes),
-        in_specs=[whole(VMEM)] * 2 + [whole(pl.ANY)] * len(beside),
-        out_specs=[whole(VMEM)] * len(shapes),
+        functools.partial(
+            merge_kernel, bit, final, own.shape[0] - TILE, other.shape[0] - TILE
+        ),
+        out_shape=(
+            held(2, rows, cols),
+            held(TILE, cols),
+            held(TILE, cols),
+            held((2 if final else 4) * rows, cols),
+        )
+        + (held(rows, cols),) * final,
+        in_specs=[whole(VMEM)] * 4,
+        out_specs=[whole(VMEM)] * (4 + final),
         compiler_params=pltpu.CompilerParams(vmem_limit_bytes=8 * MIB),
         name="merge",
-    )(mine, theirs, *in_hbm(*beside))
+    )(mine, theirs, own, other)
 
 
 def prepare_kernel(
-    rounds, temp, w_vel, forward, table, changes, scalars, outer, inner, *rest
+    rounds, temp, w_vel, forward, table, changes, fluxes, other, *rest
 ):
+    outer, rest = (rest[0], rest[1:]) if rounds > 2 else (None, rest)
     bases, gains = rest[: rounds - 1], rest[rounds - 1 : 2 * rounds - 2]
     known, response, below_in, above_in = rest[2 * rounds - 2 :]
     levels, rows, cols = temp.shape
@@ -494,10 +521,12 @@
             ]
         below = [jnp.where(side, into[field], below[field]) for field in range(2)]
         above = [jnp.where(side, above[field], into[field]) for field in range(2)]
-    for field in range(2):
-        flux_below, flux_above = level_fluxes(outer, inner, pl.ds(field * rows, rows))
-        below_in[field] = below[field] + scalars[pl.ds(METRIC_BELOW, 1), :] * flux_below
-        above_in[field] = above[field] - scalars[pl.ds(METRIC_ABOVE, 1), :] * flux_above
+    scalars = scalar_rows(fluxes, 4 * rows)
+    for field in range(2):
+        at = pl.ds(field * rows, rows)
+        flux_below, flux_above = level_fluxes(other[at, :], 0.0 if outer is None else outer[at, :])
+        below_in[field] = below[field] + scalars[METRIC_BELOW] * flux_below
+        above_in[field] = above[field] - scalars[METRIC_ABOVE] * flux_above
 
     gain = above_gain * table[levels - 1, pl.ds(PIVOT, 1), :]
     for level in range(levels - 1, -1, -1):
@@ -539,45 +568,75 @@
             lax.fori_loop(0, levels - 1, step, carry)
 
 
-def prepare(rounds, temp, w_vel, forward, table, changes, scalars, outer, inner, bases, gains):
+def prepare(rounds, temp, w_vel, forward, table, changes, fluxes, other, outer, bases, gains):
     levels, rows, cols = temp.shape
     return pl.pallas_call(
         functools.partial(prepare_kernel, rounds),
         out_shape=(held(2, levels, rows, cols), held(levels, TILE, cols)),
-        in_specs=[whole(VMEM)] * (8 + 2 * (rounds - 1)),
+        in_specs=[whole(VMEM)] * (7 + len(outer) + 2 * (rounds - 1)),
         out_specs=[whole(VMEM)] * 2,
         scratch_shapes=[pltpu.VMEM((2, rows, cols), F32)] * 2,
         compiler_params=pltpu.CompilerParams(vmem_limit_bytes=8 * MIB),
         cost_estimate=pl.CostEstimate(
-            flops=2000 * levels * rows * cols,
+            flops=levels * rows * cols,
             bytes_accessed=24 * levels * rows * cols,
             transcendentals=0,
         ),
         name="prepare",
     )(
-        in_vmem(temp), in_vmem(w_vel), in_vmem(forward), in_vmem(table), changes, scalars,
-        outer, inner, *bases, *gains,
+        in_vmem(temp), in_vmem(w_vel), in_vmem(forward), in_vmem(table), changes, fluxes, other,
+        *outer, *bases, *gains,
     )
 
 
-def finish_kernel(rounds, swapped, known, response, mine, theirs, *rest):
-    temp_next, w_next, result, sems = rest[2 if swapped else 0 :]
-    _, levels, rows, cols = known.shape
+def join_kernel(rounds, own_at, other_at, mine, theirs, own, other, *rest):
+    *seam, joined = rest
+    size = theirs.shape[0] // 2
+    rows = 2 * size
     upper = bit_of("gz", rounds - 1) == 1
-    own, far = scalar_rows(mine, 2 * rows), scalar_rows(theirs, rows)
-    low = [jnp.where(upper, b, a) for a, b in zip(own, far)]
-    high = [jnp.where(upper, a, b) for a, b in zip(own, far)]
+    low, high = in_order(upper, scalar_rows(own, own_at), scalar_rows(other, other_at))
     coupling, inverse = interface(low, high)
     scale = coupling * inverse
     to_other = scale * coupling * jnp.where(upper, low[LAST], high[FIRST])
+    up, down = high[METRIC_BELOW] * inverse, -low[METRIC_ABOVE] * inverse
+    own_gain = coupling * jnp.where(upper, down * low[LAST], up * high[FIRST])
+    other_gain = jnp.where(upper, up, down)
+    start = pl.multiple_of(bit_of("gz", 0) * size, size)
+    for field in range(2):
+        here, there = pl.ds(field * rows + start, size), pl.ds(field * size, size)
+        into = scale * theirs[there, :] + to_other * mine[here, :]
+        if seam:
+            flux = other[there, :]
+            into = into + (own_gain * seam[0][here, :] + other_gain * flux)
+            joined[pl.ds((2 + field) * size, size), :] = flux
+        joined[there, :] = into
+
+
+def join(rounds, mine, theirs, own, other, seam):
+    size, cols = theirs.shape
+    return pl.pallas_call(
+        functools.partial(join_kernel, rounds, own.shape[0] - TILE, other.shape[0] - TILE),
+        out_shape=held(size * (1 + len(seam)), cols),
+        in_specs=[whole(VMEM)] * (4 + len(seam)),
+        out_specs=whole(VMEM),
+        compiler_params=pltpu.CompilerParams(vmem_limit_bytes=8 * MIB),
+        name="join",
+    )(mine, theirs, own, other, *seam)
+
+
+def finish_kernel(rounds, swapped, known, response, joined, *rest):
+    late, results = rounds == 2, 4 if rounds == 2 else 2
+    table, tend, near, far = rest[:4] if late else (None,) * 4
+    rest = rest[(4 if late else 0) + (results if swapped else results - 2) :]
+    outs, (result, rim, sems) = rest[:results], rest[results:]
+    _, levels, rows, cols = known.shape
     width, half = 2 * TILE, rows // 2
     core = bit_of("gz", 0)
     start = pl.multiple_of((1 - core if swapped else core) * half, half)
     copies = []
-    for field, out in enumerate((temp_next, w_next)):
+    for field in range(2):
         for begin in range(0, half, width):
-            here = pl.ds(field * rows + start + begin, width)
-            into = scale * theirs[pl.ds(field * half + begin, width), :] + to_other * mine[here, :]
+            into = joined[pl.ds(field * half + begin, width), :]
             tiles = [into[i : i + TILE] for i in range(0, width, TILE)]
 
             def step(level, carry, field=field, begin=begin, tiles=tiles):
@@ -591,26 +650,60 @@
             lax.fori_loop(0, levels, step, 0, unroll=4)
         copies.append(
             pltpu.make_async_copy(
-                result.at[field], out.at[:, pl.ds(start, half), :], sems.at[field]
+                result.at[field], outs[field].at[:, pl.ds(start, half), :], sems.at[field]
             )
         )
         copies[-1].start()
+    if late:
+        diffs = side_changes(near, far)
+        level = core * (levels - 1)
+        gain = jnp.where(
+            core == 1, -table[levels - 1, pl.ds(FALL, 1), :], table[0, pl.ds(RISE, 1), :]
+        )
+        gain = jnp.where(beside_seam(rounds), gain, 0.0)
+        row_at = start + lax.broadcasted_iota(jnp.int32, (half, cols), 0)
+        for field in range(2):
+            head, tail = (
+                jnp.where(
+                    core == 1,
+                    diff[(field + 1) * levels - 1 : (field + 1) * levels, :],
+                    diff[field * levels : field * levels + 1, :],
+                )
+                for diff in diffs
+            )
+            edge = jnp.where(row_at == 0, head, jnp.where(row_at == rows - 1, tail, 0.0))
+            flux = joined[pl.ds((2 + field) * half, half), :]
+            rim[field] = tend[field, level, pl.ds(start, half), :] + gain * flux + edge
+            copies.append(
+                pltpu.make_async_copy(
+                    rim.at[field],
+                    outs[2 + field].at[level, pl.ds(start, half), :],
+                    sems.at[2 + field],
+                )
+            )
+            copies[-1].start()
     for copy in copies:
         copy.wait()
 
 
-def finish(rounds, known, response, mine, theirs, written=()):
+def finish(rounds, known, response, joined, late, written):
     _, levels, rows, cols = known.shape
+    results = 4 if rounds == 2 else 2
+    inputs = 3 + len(late)
+    swapped = len(written) == results
     return pl.pallas_call(
-        functools.partial(finish_kernel, rounds, bool(written)),
-        out_shape=(jax.ShapeDtypeStruct((levels, rows, cols), F32),) * 2,
-        in_specs=[whole(VMEM)] * 4 + [whole(pl.ANY)] * len(written),
-        out_specs=[whole(pl.ANY)] * 2,
+        functools.partial(finish_kernel, rounds, swapped),
+        out_shape=(jax.ShapeDtypeStruct((levels, rows, cols), F32),) * results,
+        in_specs=[whole(VMEM)] * inputs + [whole(pl.ANY)] * len(written),
+        out_specs=[whole(pl.ANY)] * results,
         scratch_shapes=[
             pltpu.VMEM((2, levels, rows // 2, cols), F32),
-            pltpu.SemaphoreType.DMA((2,)),
+            pltpu.VMEM((2, rows // 2, cols), F32),
+            pltpu.SemaphoreType.DMA((4,)),
         ],
-        input_output_aliases={4: 0, 5: 1} if written else {},
+        input_output_aliases={
+            inputs + i: results - len(written) + i for i in range(len(written))
+        },
         compiler_params=pltpu.CompilerParams(vmem_limit_bytes=8 * MIB),
         cost_estimate=pl.CostEstimate(
             flops=20000 * levels * rows * cols,
@@ -618,7 +711,7 @@
             transcendentals=0,
         ),
         name="finish",
-    )(in_vmem(known), response, mine, theirs, *written)
+    )(in_vmem(known), response, joined, *map(in_vmem, late), *written)
 
 
 def both_ways(pairs):
@@ -630,34 +723,47 @@
     across, stacked = lax.axis_size("gx"), lax.axis_size("gz")
     rounds = stacked.bit_length() - 1
     cores = both_ways([(i, i + 1) for i in range(0, stacked, 2)])
-    seams = both_ways([(i, i + 1) for i in range(1, stacked - 1, 2)])
-    seams = seams + [(i, i) for i in (0, stacked - 1)]
-    far, near, outer, inner, table, scalars = edges(
+    near, far, fluxes, table = edges(
         temp, u_vel, w_vel, v_vel, temp_prev, w_prev, lower, upper, metric
     )
+    near = lax.ppermute(near, "gx", both_ways([(i, i + 1) for i in range(0, across, 2)]))
     far = lax.ppermute(far, "gx", both_ways([(i, (i + 1) % across) for i in range(1, across, 2)]))
-    near = lax.ppermute(near, "gx", both_ways([(i, i + 1) for i in range(0, across, 2)]))
-    outer = lax.ppermute(outer, "gz", seams)
-    inner = lax.ppermute(inner, "gz", cores)
+    other = lax.ppermute(fluxes, "gz", cores)
+    outer = ()
+    if rounds > 2:
+        seams = both_ways([(i, i + 1) for i in range(1, stacked - 1, 2)])
+        outer = (lax.ppermute(fluxes[2 * rows : 4 * rows], "gz", seams),)
     forward, tend, first = bulk(table, temp, u_vel, v_vel, w_vel, temp_prev, w_prev)
-    mine, changes = fix(far, near, outer, inner, forward, first, table, scalars)
-    temp_tend = tends(0, table, tend, far, near, outer, inner)
-    bases, gains = [], []
+    mine, changes, *late = fix(rounds, near, far, fluxes, other, forward, first, table, outer)
+    bases, gains, own, other_own = [], [], fluxes, other
     for step in range(rounds - 1):
-        theirs = lax.ppermute(mine, "gz", [(i, i ^ (1 << step)) for i in range(stacked)])
-        base, gain, mine, *half = merge(step, step + 2 == rounds, rows, mine, theirs, temp_tend)
+        partners = [(i, i ^ (1 << step)) for i in range(stacked)]
+        theirs = lax.ppermute(mine, "gz", partners)
+        if step > 0:
+            other_own = lax.ppermute(own, "gz", partners)
+        base, gain, own, mine, *half = merge(
+            step, step + 2 == rounds, rows, mine, theirs, own, other_own
+        )
         bases.append(base)
         gains.append(gain)
-    (half,) = half
-    theirs = lax.ppermute(half, "gz", [(i, i ^ (stacked // 2)) for i in range(stacked)])
-    swapped = lax.ppermute(theirs, "gz", cores)
-    w_tend = tends(1, table, tend, far, near, outer, inner)
+    partners = [(i, i ^ (stacked // 2)) for i in range(stacked)]
+    theirs = lax.ppermute(half[0], "gz", partners)
+    seam = ()
+    if late:
+        *seam, own = late
+        late = (table, tend, near, far)
+    other_own = lax.ppermute(own, "gz", partners)
     known, response = prepare(
-        rounds, temp, w_vel, forward, table, changes, scalars, outer, inner, bases, gains
+        rounds, temp, w_vel, forward, table, changes, fluxes, other, outer, bases, gains
     )
-    written = finish(rounds, known, response, mine, theirs)
-    temp_next, w_next = finish(rounds, known, response, mine, swapped, written)
-    return temp_next, w_next, temp_tend, w_tend
+    tendencies = tuple(
+        tends(rounds, field, table, tend, near, far, other, outer) for field in range(2)
+    )
+    joined = join(rounds, mine, theirs, own, other_own, seam)
+    swapped = lax.ppermute(joined, "gz", cores)
+    written = finish(rounds, known, response, joined, late, tendencies if late else ())
+    written = finish(rounds, known, response, swapped, late, written)
+    return tuple(written) if late else (*written, *tendencies)
 
 
 def solution(mesh):

time: 23.6 us -> 21.7 us (0.919)
  starting transfers between devices: 11.1 us -> 9.74 us
  waiting for transfers between devices: 1.54 us -> 0.56 us
  Pallas kernels: 9.93 us -> 10.4 us
    ppermute x1, starting transfers between devices: 0.01 us -> 3.03 us  [local(): lax.ppermute(near, 'gx', both_ways([(i, i + 1) for i in range(0, across,...]
    ppermute x1, starting transfers between devices: 6.07 us -> 3.54 us  [local(): lax.ppermute(far, 'gx', both_ways([(i, (i + 1) % across) for i in range(1...]
    ppermute x5, starting transfers between devices: 5.06 us -> 3.16 us  [the longest x1 1.49 us: local(): other_own = lax.ppermute(own, 'gz', partners)]
    ppermute x5, waiting for transfers between devices: 1.53 us -> 0.24 us  [the longest x1 0.23 us: local(): swapped = lax.ppermute(joined, 'gz', cores)]
    pallas_call x6 -> x7, Pallas kernels: 4.38 us -> 4.98 us  [the longest x2 2.17 us: finish(): pl.pallas_call(functools.partial(finish_kernel, rounds, swapped), out_sha...]
    ppermute x1, waiting for transfers between devices: 0.01 us -> 0.31 us  [local(): lax.ppermute(far, 'gx', both_ways([(i, (i + 1) % across) for i in range(1...]
  transfers between devices with their start and end apart: 7 -> 7, of which waited for: 3 -> 2; matrix products, arithmetic and copies ran while one was open for 0% -> 0% of each run, Pallas kernels for 30% -> 35%
where the time goes in v4:
time: 21.7 us; the launch traced here: 21.6 us
  Pallas kernels  10.4 us (48%)
  starting transfers between devices  9.74 us (45%)
  between operations  0.81 us (4%)
  waiting for transfers between devices  0.56 us (3%)
    ppermute x1, starting transfers between devices, local(): lax.ppermute(far, 'gx', both_ways([(i, (i + 1) % across) for i in range(1...  3.54 us
    ppermute x1, starting transfers between devices, local(): lax.ppermute(near, 'gx', both_ways([(i, i + 1) for i in range(0, across,...  3.03 us
    pallas_call x1, Pallas kernels, bulk(): pl.pallas_call(bulk_kernel, out_shape=(held(2, levels + 1, rows, cols), h...  2.69 us
    pallas_call x2, Pallas kernels, finish(): pl.pallas_call(functools.partial(finish_kernel, rounds, swapped), out_sha...  2.17 us
    pallas_call x2, Pallas kernels, tends(): pl.pallas_call(functools.partial(tends_kernel, rounds, field), out_shape=...  2 us
    pallas_call x1, Pallas kernels, edges(): pl.pallas_call(edges_kernel, out_shape=(held(2 * levels, cols), held(2 *...  1.59 us
    ppermute x1, starting transfers between devices, local(): other_own = lax.ppermute(own, 'gz', partners)  1.49 us
    ppermute x1, starting transfers between devices, local(): theirs = lax.ppermute(half[0], 'gz', partners)  1.33 us
  transfers between devices with their start and end apart: 7, of which 2 were waited for; matrix products, arithmetic and copies ran while one was open for 0% of the time, Pallas kernels for 35%

profile of v4, /device:TPU:0, one launch (start us, length us, event | category | flops | bytes accessed | tf_op | source)
XLA Modules:
  0.0 21.6 jit_solution(15608982835428460561)
XLA Ops:
  0.7 1.6 %edges.1 = (f32[32,256]{1,0:T(8,128)S(1)}, f32[32,256]{1,0:T(8,128)S(1)}, f32[264,256]{1,0:T(8,128)S(1)}, f32[16,8,256]{2,1,0:T(8,128)S(1)}) custom-call(f32[16,64,256]{2,1,0:T(8,128)} %temp.5, f32[16,64,256]{2,1,0:T(8,128)} %u_vel.3, f32[16,64,256]{2,1,0:T(8,128)} %w_vel.5, f32[16,64,256]{2,1,0:T(8,128)} %v_vel.3, f32[16,64,256]{2,1,0:T(8,128)} %temp_prev.3, ...), custom_call_target="tpu_custom_call" | custom-call | tf_op jit(solution)/shard_map/edges/pallas_call | solution.py:104
  2.3 3.0 %collective-permute-start = (f32[32,256]{1,0:T(8,128)S(1)}, f32[32,256]{1,0:T(8,128)S(1)}, u32[]{:S(2)}, u32[]{:S(2)}) collective-permute-start(f32[32,256]{1,0:T(8,128)S(1)} %get-tuple-element.27), channel_id=1, source_target_pairs={{0,4},{8,12},{16,20},{24,28},{4,0},{12,8},{20,16},{28,24},{1,5},{9... | collective-permute-start | bytes 98312 | tf_op jit(solution)/shard_map/ppermute | solution.py:729
  5.3 3.5 %collective-permute-start.1 = (f32[32,256]{1,0:T(8,128)S(1)}, f32[32,256]{1,0:T(8,128)S(1)}, u32[]{:S(2)}, u32[]{:S(2)}) collective-permute-start(f32[32,256]{1,0:T(8,128)S(1)} %get-tuple-element.28), channel_id=1, source_target_pairs={{4,8},{12,16},{20,24},{28,0},{8,4},{16,12},{24,20},{0,28},{5,9},{1... | collective-permute-start | bytes 98312 | tf_op jit(solution)/shard_map/ppermute | solution.py:730
  8.9 0.0 collective-permute-start.2
  8.9 0.0 copy-done.5
  8.9 2.7 %bulk.1 = (f32[2,17,64,256]{3,2,1,0:T(8,128)S(1)}, f32[2,16,64,256]{3,2,1,0:T(8,128)S(1)}, f32[2,64,256]{2,1,0:T(8,128)S(1)}) custom-call(f32[16,8,256]{2,1,0:T(8,128)S(1)} %get-tuple-element.25.table.rest_0_, f32[16,64,256]{2,1,0:T(8,128)S(1)} %copy-done, f32[16,64,256]{2,1,0:T(8,128)S(1)} %copy-done.2, f32[16,64,256]{2,1,0:T(8,128)S(1)} %copy-done.3, ...), custom_call_target="tpu_custom_call" | custom-call | flops 26214400000 | bytes 6291456 | tf_op jit(solution)/shard_map/bulk/pallas_call | solution.py:240
  11.6 0.0 collective-permute-done.near.rest_2_
  11.6 0.3 %collective-permute-done.1.far.rest_3_ = f32[32,256]{1,0:T(8,128)S(1)} collective-permute-done((f32[32,256]{1,0:T(8,128)S(1)}, f32[32,256]{1,0:T(8,128)S(1)}, u32[]{:S(2)}, u32[]{:S(2)}) %collective-permute-start.1) | collective-permute-done | bytes 32800 | tf_op jit(solution)/shard_map/ppermute | solution.py:730
  11.9 0.0 collective-permute-done.2.other
  11.9 0.1 fix.1
  12.1 0.3 %collective-permute-start.3 = (f32[256,256]{1,0:T(8,128)S(1)}, f32[256,256]{1,0:T(8,128)S(1)}, u32[]{:S(2)}, u32[]{:S(2)}) collective-permute-start(f32[256,256]{1,0:T(8,128)S(1)} %get-tuple-element.32.mine), channel_id=1, source_target_pairs={{0,1},{1,0},{2,3},{3,2},{4,5},{5,4},{6,7},{7,6},{8,9},{9,8},{10,11... | collective-permute-start | bytes 786440 | tf_op jit(solution)/shard_map/ppermute | solution.py:741
  12.4 1.5 %collective-permute-start.5 = (f32[72,256]{1,0:T(8,128)S(1)}, f32[72,256]{1,0:T(8,128)S(1)}, u32[]{:S(2)}, u32[]{:S(2)}) collective-permute-start(f32[72,256]{1,0:T(8,128)S(1)} %get-tuple-element.39.own), channel_id=1, source_target_pairs={{0,2},{1,3},{2,0},{3,1},{4,6},{5,7},{6,4},{7,5},{8,10},{9,11},{10,... | collective-permute-start | bytes 221192 | tf_op jit(solution)/shard_map/ppermute | solution.py:755
  13.8 0.0 collective-permute-done.3.theirs
  13.9 0.6 %merge.1 = (f32[2,64,256]{2,1,0:T(8,128)S(1)}, f32[8,256]{1,0:T(8,128)S(1)}, f32[8,256]{1,0:T(8,128)}, f32[128,256]{1,0:T(8,128)S(1)}, f32[64,256]{1,0:T(8,128)S(1)}) custom-call(f32[256,256]{1,0:T(8,128)S(1)} %get-tuple-element.32.mine, f32[256,256]{1,0:T(8,128)S(1)} %collective-permute-done.3.theirs, f32[264,256]{1,0:T(8,128)S(1)} %get-tuple-element.29.fluxes.own, ...), custom_call_target="tpu_custom_call" | custom-call | tf_op jit(solution)/shard_map/merge/pallas_call | solution.py:478
  14.5 1.3 %collective-permute-start.4 = (f32[64,256]{1,0:T(8,128)S(1)}, f32[64,256]{1,0:T(8,128)S(1)}, u32[]{:S(2)}, u32[]{:S(2)}) collective-permute-start(f32[64,256]{1,0:T(8,128)S(1)} %get-tuple-element.38), channel_id=1, source_target_pairs={{0,2},{1,3},{2,0},{3,1},{4,6},{5,7},{6,4},{7,5},{8,10},{9,11},{10,... | collective-permute-start | bytes 196616 | tf_op jit(solution)/shard_map/ppermute | solution.py:750
  15.8 1.0 %tends.3.rest_5_ = f32[16,64,256]{2,1,0:T(8,128)} custom-call(f32[16,8,256]{2,1,0:T(8,128)S(1)} %get-tuple-element.25.table.rest_0_, f32[2,16,64,256]{3,2,1,0:T(8,128)S(1)} %get-tuple-element.41.tend.rest_1_, f32[32,256]{1,0:T(8,128)S(1)} %collective-permute-done.near.rest_2_, f32[32,256]{1,0:T(8,128)S(1)} %collective-permute-done.1.far.rest_3_, ...), custom_call_target="tpu_custom_call" | custom-call | flops 262144 | bytes 1048576 | tf_op jit(solution)/shard_map/tends/pallas_call | solution.py:418
  16.8 1.0 %tends.2.rest_4_ = f32[16,64,256]{2,1,0:T(8,128)} custom-call(f32[16,8,256]{2,1,0:T(8,128)S(1)} %get-tuple-element.25.table.rest_0_, f32[2,16,64,256]{3,2,1,0:T(8,128)S(1)} %get-tuple-element.41.tend.rest_1_, f32[32,256]{1,0:T(8,128)S(1)} %collective-permute-done.near.rest_2_, f32[32,256]{1,0:T(8,128)S(1)} %collective-permute-done.1.far.rest_3_, ...), custom_call_target="tpu_custom_call" | custom-call | flops 262144 | bytes 1048576 | tf_op jit(solution)/shard_map/tends/pallas_call | solution.py:418
  17.8 1.2 %prepare.1 = (f32[2,16,64,256]{3,2,1,0:T(8,128)S(1)}, f32[16,8,256]{2,1,0:T(8,128)S(1)}) custom-call(f32[16,64,256]{2,1,0:T(8,128)S(1)} %copy-done, f32[16,64,256]{2,1,0:T(8,128)S(1)} %copy-done.1, f32[2,17,64,256]{3,2,1,0:T(8,128)S(1)} %get-tuple-element.26.forward, f32[16,8,256]{2,1,0:T(8,128)S(1)} %get-tuple-element.25.table.rest_0_, ...), custom_call_target="tpu_custom_call" | custom-call | flops 262144 | bytes 6291456 | tf_op jit(solution)/shard_map/prepare/pallas_call | solution.py:573
  19.0 0.0 collective-permute-done.5.other
  19.0 0.0 collective-permute-done.4.theirs
  19.1 0.1 collective-permute-start.6
  19.2 1.1 %finish.2 = (f32[16,64,256]{2,1,0:T(8,128)}, f32[16,64,256]{2,1,0:T(8,128)}, f32[16,64,256]{2,1,0:T(8,128)}, f32[16,64,256]{2,1,0:T(8,128)}) custom-call(f32[2,16,64,256]{3,2,1,0:T(8,128)S(1)} %get-tuple-element.35.known, f32[16,8,256]{2,1,0:T(8,128)S(1)} %get-tuple-element.36.response, ...), custom_call_target="tpu_custom_call", output_to_operand_aliasing={{2}: (7, {}), {3}: (8, {})} | custom-call | flops 5242880000 | bytes 2097152 | tf_op jit(solution)/shard_map/finish/pallas_call | solution.py:694
  20.3 0.2 %collective-permute-done.6.joined = f32[128,256]{1,0:T(8,128)S(1)} collective-permute-done((f32[128,256]{1,0:T(8,128)S(1)}, f32[128,256]{1,0:T(8,128)S(1)}, u32[]{:S(2)}, u32[]{:S(2)}) %collective-permute-start.6) | collective-permute-done | bytes 131104 | tf_op jit(solution)/shard_map/ppermute | solution.py:763
  20.5 1.1 %finish.3 = (f32[16,64,256]{2,1,0:T(8,128)}, f32[16,64,256]{2,1,0:T(8,128)}, f32[16,64,256]{2,1,0:T(8,128)}, f32[16,64,256]{2,1,0:T(8,128)}) custom-call(f32[2,16,64,256]{3,2,1,0:T(8,128)S(1)} %get-tuple-element.35.known, f32[16,8,256]{2,1,0:T(8,128)S(1)} %get-tuple-element.36.response, ...), custom_call_target="tpu_custom_call", output_to_operand_aliasing={{0}: (7, {}), {1}: (8, {}), {2}: (9, {}), {3}: (10, {})} | custom-call | flops 5242880000 | bytes 2097152 | tf_op jit(solution)/shard_map/finish/pallas_call | solution.py:694
  (12 shorter events, 0.1 us)
Async XLA Ops:
  0.6 8.2 %copy-start.1 = (f32[16,64,256]{2,1,0:T(8,128)S(1)}, f32[16,64,256]{2,1,0:T(8,128)}, u32[]{:S(2)}) copy-start(f32[16,64,256]{2,1,0:T(8,128)} %w_vel.5) | copy-start | bytes 3145732
  0.6 8.2 %copy-start = (f32[16,64,256]{2,1,0:T(8,128)S(1)}, f32[16,64,256]{2,1,0:T(8,128)}, u32[]{:S(2)}) copy-start(f32[16,64,256]{2,1,0:T(8,128)} %temp.5) | copy-start | bytes 3145732
  0.7 8.2 %copy-start.5 = (f32[16,64,256]{2,1,0:T(8,128)S(1)}, f32[16,64,256]{2,1,0:T(8,128)}, u32[]{:S(2)}) copy-start(f32[16,64,256]{2,1,0:T(8,128)} %w_prev.3) | copy-start | bytes 3145732
  0.7 8.2 %copy-start.4 = (f32[16,64,256]{2,1,0:T(8,128)S(1)}, f32[16,64,256]{2,1,0:T(8,128)}, u32[]{:S(2)}) copy-start(f32[16,64,256]{2,1,0:T(8,128)} %temp_prev.3) | copy-start | bytes 3145732
  0.7 8.2 %copy-start.3 = (f32[16,64,256]{2,1,0:T(8,128)S(1)}, f32[16,64,256]{2,1,0:T(8,128)}, u32[]{:S(2)}) copy-start(f32[16,64,256]{2,1,0:T(8,128)} %v_vel.3) | copy-start | bytes 3145732
  0.7 8.2 %copy-start.2 = (f32[16,64,256]{2,1,0:T(8,128)S(1)}, f32[16,64,256]{2,1,0:T(8,128)}, u32[]{:S(2)}) copy-start(f32[16,64,256]{2,1,0:T(8,128)} %u_vel.3) | copy-start | bytes 3145732
  2.3 9.3 %collective-permute-start = (f32[32,256]{1,0:T(8,128)S(1)}, f32[32,256]{1,0:T(8,128)S(1)}, u32[]{:S(2)}, u32[]{:S(2)}) collective-permute-start(f32[32,256]{1,0:T(8,128)S(1)} %get-tuple-element.27), channel_id=1, source_target_pairs={{0,4},{8,12},{16,20},{24,28},{4,0},{12,8},{20,16},{28,24},{1,5},{9... | collective-permute-start | bytes 98312 | tf_op jit(solution)/shard_map/ppermute | solution.py:729
  5.3 6.6 %collective-permute-start.1 = (f32[32,256]{1,0:T(8,128)S(1)}, f32[32,256]{1,0:T(8,128)S(1)}, u32[]{:S(2)}, u32[]{:S(2)}) collective-permute-start(f32[32,256]{1,0:T(8,128)S(1)} %get-tuple-element.28), channel_id=1, source_target_pairs={{4,8},{12,16},{20,24},{28,0},{8,4},{16,12},{24,20},{0,28},{5,9},{1... | collective-permute-start | bytes 98312 | tf_op jit(solution)/shard_map/ppermute | solution.py:730
  8.9 3.1 %collective-permute-start.2 = (f32[264,256]{1,0:T(8,128)S(1)}, f32[264,256]{1,0:T(8,128)S(1)}, u32[]{:S(2)}, u32[]{:S(2)}) collective-permute-start(f32[264,256]{1,0:T(8,128)S(1)} %get-tuple-element.29.fluxes.own), channel_id=1, source_target_pairs={{0,1},{2,3},{1,0},{3,2},{4,5},{6,7},{5,4},{7,6},{8,9},{10,11},{9,8... | collective-permute-start | bytes 811016 | tf_op jit(solution)/shard_map/ppermute | solution.py:731
  12.1 1.8 %collective-permute-start.3 = (f32[256,256]{1,0:T(8,128)S(1)}, f32[256,256]{1,0:T(8,128)S(1)}, u32[]{:S(2)}, u32[]{:S(2)}) collective-permute-start(f32[256,256]{1,0:T(8,128)S(1)} %get-tuple-element.32.mine), channel_id=1, source_target_pairs={{0,1},{1,0},{2,3},{3,2},{4,5},{5,4},{6,7},{7,6},{8,9},{9,8},{10,11... | collective-permute-start | bytes 786440 | tf_op jit(solution)/shard_map/ppermute | solution.py:741
  12.4 6.7 %collective-permute-start.5 = (f32[72,256]{1,0:T(8,128)S(1)}, f32[72,256]{1,0:T(8,128)S(1)}, u32[]{:S(2)}, u32[]{:S(2)}) collective-permute-start(f32[72,256]{1,0:T(8,128)S(1)} %get-tuple-element.39.own), channel_id=1, source_target_pairs={{0,2},{1,3},{2,0},{3,1},{4,6},{5,7},{6,4},{7,5},{8,10},{9,11},{10,... | collective-permute-start | bytes 221192 | tf_op jit(solution)/shard_map/ppermute | solution.py:755
  14.5 4.5 %collective-permute-start.4 = (f32[64,256]{1,0:T(8,128)S(1)}, f32[64,256]{1,0:T(8,128)S(1)}, u32[]{:S(2)}, u32[]{:S(2)}) collective-permute-start(f32[64,256]{1,0:T(8,128)S(1)} %get-tuple-element.38), channel_id=1, source_target_pairs={{0,2},{1,3},{2,0},{3,1},{4,6},{5,7},{6,4},{7,5},{8,10},{9,11},{10,... | collective-permute-start | bytes 196616 | tf_op jit(solution)/shard_map/ppermute | solution.py:750
  19.1 1.4 %collective-permute-start.6 = (f32[128,256]{1,0:T(8,128)S(1)}, f32[128,256]{1,0:T(8,128)S(1)}, u32[]{:S(2)}, u32[]{:S(2)}) collective-permute-start(f32[128,256]{1,0:T(8,128)S(1)} %join.1.joined), channel_id=1, source_target_pairs={{0,1},{2,3},{1,0},{3,2},{4,5},{6,7},{5,4},{7,6},{8,9},{10,11},{9,8... | collective-permute-start | bytes 393224 | tf_op jit(solution)/shard_map/ppermute | solution.py:763

commit v5 on v4

--- a/solution.py
+++ b/solution.py
@@ -12,6 +12,7 @@
 FIELD_WEIGHT = 2.0 / NEW_WEIGHT
 PREV_WEIGHT = (17.0 / 60.0) / NEW_WEIGHT
 TILE = 8
+CHUNK = 4
 MIB = 1024 * 1024
 
 PIVOT_NEW, LOWER_PIVOT, UPPER_PIVOT, FIRST_GREEN, BELOW_FORWARD, PIVOT, RISE, FALL = range(8)
@@ -52,9 +53,10 @@
     lower,
     upper,
     metric,
+    far,
     near,
-    far,
     fluxes,
+    outward,
     table,
     strips,
     layers,
@@ -76,7 +78,7 @@
         copy.start()
     for copy in copies[:3]:
         copy.wait()
-    coefficients(lower_at, upper_at, metric_at, table, fluxes.at[pl.ds(4 * rows, TILE)])
+    coefficients(lower_at, upper_at, metric_at, table, fluxes.at[pl.ds(3 * rows, TILE)])
     for copy in copies[3:]:
         copy.wait()
     odd = bit_of("gx", 0) == 1
@@ -90,13 +92,16 @@
     position = lax.axis_index("gz")
     upper_core = bit_of("gz", 0) == 1
     wall = (position == 0) | (position == lax.axis_size("gz") - 1)
-    zero = jnp.zeros((rows, cols), F32)
+    zero, size = jnp.zeros((rows, cols), F32), rows // 2
     for field in range(2):
         bottom = layers[1, 0] * layers[field, 0]
         top = layers[1, 1] * layers[field, 1]
         fluxes[pl.ds(field * rows, rows), :] = jnp.where(upper_core, bottom, top)
-        outward = jnp.where(wall, zero, jnp.where(upper_core, top, bottom))
-        fluxes[pl.ds((2 + field) * rows, rows), :] = outward
+        value = jnp.where(wall, zero, jnp.where(upper_core, top, bottom))
+        outward[pl.ds(field * rows, rows), :] = value
+        fluxes[pl.ds(2 * rows + field * size, size), :] = jnp.where(
+            upper_core, value[:size], value[size:]
+        )
 
 
 def edges(temp, u_vel, w_vel, v_vel, temp_prev, w_prev, lower, upper, metric):
@@ -106,11 +111,12 @@
         out_shape=(
             held(2 * levels, cols),
             held(2 * levels, cols),
-            held(4 * rows + TILE, cols),
+            held(3 * rows + TILE, cols),
+            held(2 * rows, cols),
             held(levels, TILE, cols),
         ),
         in_specs=[whole(pl.ANY)] * 9,
-        out_specs=[whole(VMEM)] * 4,
+        out_specs=[whole(VMEM)] * 5,
         scratch_shapes=[
             pltpu.VMEM((3, 2, levels, TILE, cols), F32),
             pltpu.VMEM((2, 2, rows, cols), F32),
@@ -174,6 +180,9 @@
     forward,
     tend,
     first,
+    temp_tend,
+    w_tend,
+    sems,
 ):
     levels, rows, cols = temp.shape
     strips = rows // TILE
@@ -183,6 +192,13 @@
         first[field] = jnp.zeros((rows, cols), F32)
     row_at = lax.broadcasted_iota(jnp.int32, (TILE, cols), 0)
     zero = jnp.zeros((TILE, cols), F32)
+
+    def chunk_copies(chunk):
+        at = pl.ds(chunk * CHUNK, CHUNK)
+        return [
+            pltpu.make_async_copy(tend.at[field, at], out.at[at], sems.at[field, chunk])
+            for field, out in enumerate((temp_tend, w_tend))
+        ]
 
     def level_step(level, carry):
         def spread(at):
@@ -230,9 +246,18 @@
                 first[field, at, :] = first[field, at, :] + green * right
             before = ahead
             here, back, ahead = after
+
+        @pl.when((level % CHUNK == CHUNK - 1) & (level < levels - CHUNK))
+        def _():
+            for copy in chunk_copies(level // CHUNK):
+                copy.start()
+
         return carry
 
     lax.fori_loop(0, levels, level_step, 0)
+    for chunk in range(levels // CHUNK - 1):
+        for copy in chunk_copies(chunk):
+            copy.wait()
 
 
 def bulk(table, *arrays):
@@ -243,9 +268,12 @@
             held(2, levels + 1, rows, cols),
             held(2, levels, rows, cols),
             held(2, rows, cols),
+            jax.ShapeDtypeStruct((levels, rows, cols), F32),
+            jax.ShapeDtypeStruct((levels, rows, cols), F32),
         ),
         in_specs=[whole(VMEM)] * 7,
-        out_specs=[whole(VMEM)] * 3,
+        out_specs=[whole(VMEM)] * 3 + [whole(pl.ANY)] * 2,
+        scratch_shapes=[pltpu.SemaphoreType.DMA((2, levels // CHUNK - 1))],
         compiler_params=pltpu.CompilerParams(vmem_limit_bytes=8 * MIB),
         cost_estimate=pl.CostEstimate(
             flops=100000 * levels * rows * cols,
@@ -256,7 +284,7 @@
     )(*map(in_vmem, (table, *arrays)))
 
 
-def side_changes(near, far):
+def side_changes(far, near):
     odd = bit_of("gx", 0) == 1
     return jnp.where(odd, near[...], far[...]), jnp.where(odd, far[...], near[...])
 
@@ -305,13 +333,16 @@
     ]
 
 
-def fix_kernel(rounds, levels, near, far, fluxes, other, forward, first, table, *rest):
+def fix_kernel(
+    rounds, levels, far, near, fluxes, outward, other, forward, first, table, *rest
+):
     outer, rest = (rest[0], rest[1:]) if rounds > 2 else (None, rest)
-    message, changes, *late = rest
+    entries, changes, *late = rest
     _, rows, cols = first.shape
-    diffs = side_changes(near, far)
-    scalars = scalar_rows(fluxes, 4 * rows)
+    diffs = side_changes(far, near)
+    scalars = scalar_rows(fluxes, 3 * rows)
     below, above = scalars[METRIC_BELOW], -scalars[METRIC_ABOVE]
+    core, size = bit_of("gz", 0) == 1, rows // 2
     for field in range(2):
         firsts, lasts = [], []
         for side in range(2):
@@ -329,165 +360,176 @@
             lasts.append(value)
         at = pl.ds(field * rows, rows)
         flux_below, flux_above = level_fluxes(other[at, :], 0.0 if outer is None else outer[at, :])
-        message[at, :] = (
+        first_entry = (
             first[field]
             + (below * scalars[FIRST]) * flux_below
             + (above * scalars[CORNER]) * flux_above
             + ends(rows, cols, *firsts)
         )
-        message[pl.ds((2 + field) * rows, rows), :] = (
+        last_entry = (
             forward[field, levels]
             + (below * scalars[CORNER]) * flux_below
             + (above * scalars[LAST]) * flux_above
             + ends(rows, cols, *lasts)
         )
-    if not late:
-        return
-    seam, half = late
-    core, size = bit_of("gz", 0) == 1, rows // 2
-    for field in range(2):
-        outward = pl.ds((2 + field) * rows, rows)
-        value = jnp.where(beside_seam(rounds), fluxes[outward, :], other[outward, :])
-        seam[pl.ds(field * rows, rows), :] = value
-        half[pl.ds(field * size, size), :] = jnp.where(core, value[size:], value[:size])
-    for at, value in enumerate(
-        joint_scalars(*in_order(core, scalars, scalar_rows(other, 4 * rows)))
-    ):
-        half[pl.ds(rows + at, 1), :] = value
-
-
-def fix(rounds, near, far, fluxes, other, forward, first, table, outer):
+        entries[at, :] = first_entry
+        entries[pl.ds((2 + field) * rows, rows), :] = last_entry
+        if late:
+            message, seam = late
+            message[at, :] = jnp.where(core, first_entry, last_entry)
+            there = pl.ds(2 * rows + field * size, size)
+            message[there, :] = jnp.where(core, last_entry[:size], first_entry[size:])
+            value = outward[at, :]
+            value = jnp.where(core, value[size:], value[:size])
+            seam[pl.ds(field * size, size), :] = jnp.where(
+                beside_seam(rounds), value, other[there, :]
+            )
+    if late:
+        far_scalars = scalar_rows(other, 3 * rows)
+        for at, value in enumerate(joint_scalars(*in_order(core, scalars, far_scalars))):
+            seam[pl.ds(rows + at, 1), :] = value
+
+
+def fix(rounds, far, near, fluxes, outward, other, forward, first, table, outer):
     levels = table.shape[0]
     _, rows, cols = first.shape
     shapes = [held(4 * rows, cols), held(4 * levels, cols)]
     if rounds == 2:
-        shapes += [held(2 * rows, cols), held(rows + TILE, cols)]
+        shapes += [held(3 * rows, cols), held(rows + TILE, cols)]
     return pl.pallas_call(
         functools.partial(fix_kernel, rounds, levels),
         out_shape=tuple(shapes),
-        in_specs=[whole(VMEM)] * (7 + len(outer)),
+        in_specs=[whole(VMEM)] * (8 + len(outer)),
         out_specs=[whole(VMEM)] * len(shapes),
         compiler_params=pltpu.CompilerParams(vmem_limit_bytes=8 * MIB),
         name="fix",
-    )(near, far, fluxes, other, in_vmem(forward), in_vmem(first), in_vmem(table), *outer)
-
-
-def tends_kernel(rounds, field, table, tend, near, far, other, *rest):
-    *outer, out, layers, strips, sems = rest
+    )(
+        far, near, fluxes, outward, other, in_vmem(forward), in_vmem(first), in_vmem(table), *outer
+    )
+
+
+def tends_kernel(rounds, table, tend, far, near, other, *rest):
+    outer, rest = (rest[0], rest[1:]) if rounds > 2 else (None, rest)
+    *outs, layers, strips, sems = rest[2:]
     _, levels, rows, cols = tend.shape
-    inside = pl.ds(1, levels - 2)
-    copies = [
-        pltpu.make_async_copy(
-            tend.at[field, inside, pl.ds(TILE, rows - 2 * TILE), :],
-            out.at[inside, pl.ds(TILE, rows - 2 * TILE), :],
-            sems.at[0],
-        )
-    ]
-    copies[0].start()
-    diffs = side_changes(near, far)
+    inside, middle = pl.ds(1, levels - 2), pl.ds(TILE, rows - 2 * TILE)
+    left = pl.ds(levels - CHUNK, CHUNK - 1)
+    copies = []
+
+    def send(field, at, src, dst):
+        copies.append(pltpu.make_async_copy(src, dst, sems.at[field, at]))
+        copies[-1].start()
+
+    for field, out in enumerate(outs):
+        send(field, 0, tend.at[field, left, middle, :], out.at[left, middle, :])
+    diffs = side_changes(far, near)
     tile_at = lax.broadcasted_iota(jnp.int32, (TILE, cols), 0)
-    at = pl.ds(field * rows, rows)
-    below, above = level_fluxes(other[at, :], outer[0][at, :] if outer else 0.0)
-    for side, level, change in (
-        (0, 0, table[0, pl.ds(RISE, 1), :] * below),
-        (1, levels - 1, -table[levels - 1, pl.ds(FALL, 1), :] * above),
-    ):
-        at = field * levels + level
-        rim = ends(rows, cols, diffs[0][at : at + 1, :], diffs[1][at : at + 1, :])
-        layers[side] = tend[field, level] + change + rim
-        copies.append(pltpu.make_async_copy(layers.at[side], out.at[level], sems.at[1 + side]))
-        copies[-1].start()
-    for side, begin, row in ((0, 0, 0), (1, rows - TILE, TILE - 1)):
-        for level in range(1, levels - 1):
+    for field, out in enumerate(outs):
+        at = pl.ds(field * rows, rows)
+        below, above = level_fluxes(other[at, :], 0.0 if outer is None else outer[at, :])
+        for side, level, change in (
+            (0, 0, table[0, pl.ds(RISE, 1), :] * below),
+            (1, levels - 1, -table[levels - 1, pl.ds(FALL, 1), :] * above),
+        ):
             at = field * levels + level
-            strips[side, level] = tend[field, level, pl.ds(begin, TILE), :] + jnp.where(
-                tile_at == row, diffs[side][at : at + 1, :], 0.0
-            )
-        copies.append(
-            pltpu.make_async_copy(
-                strips.at[side, inside], out.at[inside, pl.ds(begin, TILE), :], sems.at[3 + side]
-            )
-        )
-        copies[-1].start()
+            rim = ends(rows, cols, diffs[0][at : at + 1, :], diffs[1][at : at + 1, :])
+            layers[field, side] = tend[field, level] + change + rim
+            send(field, 1 + side, layers.at[field, side], out.at[level])
+        for side, begin, row in ((0, 0, 0), (1, rows - TILE, TILE - 1)):
+            for level in range(1, levels - 1):
+                at = field * levels + level
+                edge = jnp.where(tile_at == row, diffs[side][at : at + 1, :], 0.0)
+                strips[field, side, level] = tend[field, level, pl.ds(begin, TILE), :] + edge
+            there = out.at[inside, pl.ds(begin, TILE), :]
+            send(field, 3 + side, strips.at[field, side, inside], there)
     for copy in copies:
         copy.wait()
 
 
-def tends(rounds, field, table, tend, near, far, other, outer):
+def tends(rounds, table, tend, far, near, other, outer, written):
     _, levels, rows, cols = tend.shape
+    inputs = 5 + len(outer)
     return pl.pallas_call(
-        functools.partial(tends_kernel, rounds, field),
-        out_shape=jax.ShapeDtypeStruct((levels, rows, cols), F32),
-        in_specs=[whole(VMEM)] * (5 + len(outer)),
-        out_specs=whole(pl.ANY),
+        functools.partial(tends_kernel, rounds),
+        out_shape=(jax.ShapeDtypeStruct((levels, rows, cols), F32),) * 2,
+        in_specs=[whole(VMEM)] * inputs + [whole(pl.ANY)] * 2,
+        out_specs=[whole(pl.ANY)] * 2,
         scratch_shapes=[
-            pltpu.VMEM((2, rows, cols), F32),
-            pltpu.VMEM((2, levels, TILE, cols), F32),
-            pltpu.SemaphoreType.DMA((5,)),
+            pltpu.VMEM((2, 2, rows, cols), F32),
+            pltpu.VMEM((2, 2, levels, TILE, cols), F32),
+            pltpu.SemaphoreType.DMA((2, 5)),
         ],
+        input_output_aliases={inputs: 0, inputs + 1: 1},
         compiler_params=pltpu.CompilerParams(vmem_limit_bytes=8 * MIB),
         cost_estimate=pl.CostEstimate(
             flops=levels * rows * cols,
-            bytes_accessed=4 * levels * rows * cols,
+            bytes_accessed=8 * levels * rows * cols,
             transcendentals=0,
         ),
         name="tends",
-    )(in_vmem(table), in_vmem(tend), near, far, other, *outer)
-
-
-def merge_kernel(bit, final, own_at, other_at, mine, theirs, own, other, base, gains, scalars, merged, *half):
+    )(in_vmem(table), in_vmem(tend), far, near, other, *outer, *in_hbm(*written))
+
+
+def merge_kernel(bit, final, late, own_at, other_at, mine, theirs, own, other, base, gains, *rest):
     _, rows, cols = base.shape
     upper = bit_of("gz", bit) == 1
     low, high = in_order(upper, scalar_rows(own, own_at), scalar_rows(other, other_at))
     coupling, inverse = interface(low, high)
     to_high, to_low = high[FIRST] * coupling, low[LAST] * coupling
     low_out, high_out = low[CORNER] * coupling, high[CORNER] * coupling
-    core = bit_of("gz", 0) == 1
+    core, size = bit_of("gz", 0) == 1, rows // 2
     sends_last = bit_of("gz", bit + 1) == 0
     for field in range(2):
-
-        def part(at):
-            a = mine[pl.ds((at + field) * rows, rows), :]
-            b = theirs[pl.ds((at + field) * rows, rows), :]
-            return jnp.where(upper, b, a), jnp.where(upper, a, b)
-
-        (low_first, high_first), (low_last, high_last) = part(0), part(2)
+        here = pl.ds(field * rows, rows)
+        own_first, own_last = mine[here, :], mine[pl.ds((2 + field) * rows, rows), :]
+        if late:
+            low_last = jnp.where(upper, theirs[here, :], own_last)
+            high_first = jnp.where(upper, own_first, theirs[here, :])
+        else:
+            other_first, other_last = theirs[here, :], theirs[pl.ds((2 + field) * rows, rows), :]
+            low_last = jnp.where(upper, other_last, own_last)
+            high_first = jnp.where(upper, own_first, other_first)
+            low_first = jnp.where(upper, other_first, own_first)
+            high_last = jnp.where(upper, own_last, other_last)
         above = inverse * (high_first + to_high * low_last)
         below = inverse * (low_last + to_low * high_first)
         base[field] = coupling * jnp.where(upper, below, above)
-        all_first = low_first + low_out * above
-        all_last = high_last + high_out * below
+        more = jnp.where(sends_last, high_out * below, low_out * above)
+        if late:
+            outside = jnp.where(upper, own_last, own_first)
+            outside = jnp.where(core, outside[size:], outside[:size])
+            there = theirs[pl.ds(2 * rows + field * size, size), :]
+            outside = jnp.where(sends_last == upper, outside, there)
+        elif final:
+            outside = jnp.where(sends_last, high_last, low_first)
+            outside = jnp.where(core, outside[size:], outside[:size])
         if final:
-            entry = jnp.where(sends_last, all_last, all_first)
-            merged[pl.ds(field * rows, rows), :] = entry
-            size = rows // 2
-            half[0][pl.ds(field * size, size), :] = jnp.where(core, entry[size:], entry[:size])
+            value = outside + jnp.where(core, more[size:], more[:size])
+            rest[0][pl.ds(field * size, size), :] = value
         else:
-            merged[pl.ds(field * rows, rows), :] = all_first
-            merged[pl.ds((2 + field) * rows, rows), :] = all_last
-    for at, value in enumerate(joint_scalars(low, high)):
-        scalars[pl.ds(at, 1), :] = value
+            rest[0][here, :] = low_first + low_out * above
+            rest[0][pl.ds((2 + field) * rows, rows), :] = high_last + high_out * below
+    if not late:
+        for at, value in enumerate(joint_scalars(low, high)):
+            rest[1][pl.ds(at, 1), :] = value
     scale = coupling * inverse
     gains[...] = jnp.zeros(gains.shape, F32)
     gains[pl.ds(FROM_ABOVE, 1), :] = scale * high[CORNER] * jnp.where(upper, to_low, 1.0)
     gains[pl.ds(FROM_BELOW, 1), :] = scale * low[CORNER] * jnp.where(upper, 1.0, to_high)
 
 
-def merge(bit, final, rows, mine, theirs, own, other):
+def merge(bit, final, late, rows, mine, theirs, own, other):
     cols = mine.shape[1]
+    shapes = [held(2, rows, cols), held(TILE, cols), held((1 if final else 4) * rows, cols)]
+    if not late:
+        shapes.append(held(TILE, cols))
     return pl.pallas_call(
         functools.partial(
-            merge_kernel, bit, final, own.shape[0] - TILE, other.shape[0] - TILE
+            merge_kernel, bit, final, late, own.shape[0] - TILE, other.shape[0] - TILE
         ),
-        out_shape=(
-            held(2, rows, cols),
-            held(TILE, cols),
-            held(TILE, cols),
-            held((2 if final else 4) * rows, cols),
-        )
-        + (held(rows, cols),) * final,
+        out_shape=tuple(shapes),
         in_specs=[whole(VMEM)] * 4,
-        out_specs=[whole(VMEM)] * (4 + final),
+        out_specs=[whole(VMEM)] * len(shapes),
         compiler_params=pltpu.CompilerParams(vmem_limit_bytes=8 * MIB),
         name="merge",
     )(mine, theirs, own, other)
@@ -521,7 +563,7 @@
             ]
         below = [jnp.where(side, into[field], below[field]) for field in range(2)]
         above = [jnp.where(side, above[field], into[field]) for field in range(2)]
-    scalars = scalar_rows(fluxes, 4 * rows)
+    scalars = scalar_rows(fluxes, 3 * rows)
     for field in range(2):
         at = pl.ds(field * rows, rows)
         flux_below, flux_above = level_fluxes(other[at, :], 0.0 if outer is None else outer[at, :])
@@ -537,17 +579,15 @@
 
     row_at = lax.broadcasted_iota(jnp.int32, (TILE, cols), 0)
     width = 2 * TILE
-    for field, cells in enumerate((temp, w_vel)):
-        for begin in range(0, rows, width):
-            at = pl.ds(begin, width)
-            below = below_in[field, at, :]
-
-            def solve(level, carry, factor, field=field, begin=begin, at=at, below=below, cells=cells):
-                value = (
-                    forward[field, level + 1, at, :]
-                    + table[level, pl.ds(BELOW_FORWARD, 1), :] * below
-                    + factor * carry
-                )
+    for begin in range(0, rows, width):
+        at = pl.ds(begin, width)
+
+        def solve(level, carry, factor, begin=begin, at=at):
+            factor = table[level, pl.ds(factor, 1), :]
+            below_factor = table[level, pl.ds(BELOW_FORWARD, 1), :]
+            values = []
+            for field, cells in enumerate((temp, w_vel)):
+                value = forward[field, level + 1, at, :] + below_factor * below_in[field, at, :]
                 if begin == 0:
                     change = changes[pl.ds(field * levels + level, 1), :]
                     head = value[:TILE] + jnp.where(row_at == 0, change, 0.0)
@@ -556,16 +596,17 @@
                     change = changes[pl.ds((2 + field) * levels + level, 1), :]
                     tail = value[-TILE:] + jnp.where(row_at == TILE - 1, change, 0.0)
                     value = jnp.concatenate([value[:-TILE], tail])
+                value = value + factor * carry[field]
                 known[field, level, at, :] = value - cells[level, at, :]
-                return value
-
-            carry = solve(levels - 1, above_in[field, at, :], table[levels - 1, pl.ds(PIVOT, 1), :])
-
-            def step(back, carry, solve=solve):
-                level = levels - 2 - back
-                return solve(level, carry, table[level, pl.ds(UPPER_PIVOT, 1), :])
-
-            lax.fori_loop(0, levels - 1, step, carry)
+                values.append(value)
+            return tuple(values)
+
+        carry = solve(levels - 1, [above_in[field, at, :] for field in range(2)], PIVOT)
+
+        def step(back, carry, solve=solve):
+            return solve(levels - 2 - back, carry, UPPER_PIVOT)
+
+        lax.fori_loop(0, levels - 1, step, carry, unroll=3)
 
 
 def prepare(rounds, temp, w_vel, forward, table, changes, fluxes, other, outer, bases, gains):
@@ -589,10 +630,8 @@
     )
 
 
-def join_kernel(rounds, own_at, other_at, mine, theirs, own, other, *rest):
-    *seam, joined = rest
+def join_kernel(rounds, late, own_at, other_at, mine, theirs, own, other, joined):
     size = theirs.shape[0] // 2
-    rows = 2 * size
     upper = bit_of("gz", rounds - 1) == 1
     low, high = in_order(upper, scalar_rows(own, own_at), scalar_rows(other, other_at))
     coupling, inverse = interface(low, high)
@@ -601,32 +640,31 @@
     up, down = high[METRIC_BELOW] * inverse, -low[METRIC_ABOVE] * inverse
     own_gain = coupling * jnp.where(upper, down * low[LAST], up * high[FIRST])
     other_gain = jnp.where(upper, up, down)
-    start = pl.multiple_of(bit_of("gz", 0) * size, size)
     for field in range(2):
-        here, there = pl.ds(field * rows + start, size), pl.ds(field * size, size)
-        into = scale * theirs[there, :] + to_other * mine[here, :]
-        if seam:
-            flux = other[there, :]
-            into = into + (own_gain * seam[0][here, :] + other_gain * flux)
+        at = pl.ds(field * size, size)
+        into = scale * theirs[at, :] + to_other * mine[at, :]
+        if late:
+            flux = other[at, :]
+            into = into + (own_gain * own[at, :] + other_gain * flux)
             joined[pl.ds((2 + field) * size, size), :] = flux
-        joined[there, :] = into
-
-
-def join(rounds, mine, theirs, own, other, seam):
+        joined[at, :] = into
+
+
+def join(rounds, late, mine, theirs, own, other):
     size, cols = theirs.shape
     return pl.pallas_call(
-        functools.partial(join_kernel, rounds, own.shape[0] - TILE, other.shape[0] - TILE),
-        out_shape=held(size * (1 + len(seam)), cols),
-        in_specs=[whole(VMEM)] * (4 + len(seam)),
+        functools.partial(join_kernel, rounds, late, own.shape[0] - TILE, other.shape[0] - TILE),
+        out_shape=held(size * (2 if late else 1), cols),
+        in_specs=[whole(VMEM)] * 4,
         out_specs=whole(VMEM),
         compiler_params=pltpu.CompilerParams(vmem_limit_bytes=8 * MIB),
         name="join",
-    )(mine, theirs, own, other, *seam)
+    )(mine, theirs, own, other)
 
 
 def finish_kernel(rounds, swapped, known, response, joined, *rest):
     late, results = rounds == 2, 4 if rounds == 2 else 2
-    table, tend, near, far = rest[:4] if late else (None,) * 4
+    table, tend, far, near = rest[:4] if late else (None,) * 4
     rest = rest[(4 if late else 0) + (results if swapped else results - 2) :]
     outs, (result, rim, sems) = rest[:results], rest[results:]
     _, levels, rows, cols = known.shape
@@ -634,28 +672,8 @@
     core = bit_of("gz", 0)
     start = pl.multiple_of((1 - core if swapped else core) * half, half)
     copies = []
-    for field in range(2):
-        for begin in range(0, half, width):
-            into = joined[pl.ds(field * half + begin, width), :]
-            tiles = [into[i : i + TILE] for i in range(0, width, TILE)]
-
-            def step(level, carry, field=field, begin=begin, tiles=tiles):
-                gain = response[level]
-                for i, tile in enumerate(tiles):
-                    at = begin + i * TILE
-                    value = known[field, level, pl.ds(start + at, TILE), :] + gain * tile
-                    result[field, level, pl.ds(at, TILE), :] = value
-                return carry
-
-            lax.fori_loop(0, levels, step, 0, unroll=4)
-        copies.append(
-            pltpu.make_async_copy(
-                result.at[field], outs[field].at[:, pl.ds(start, half), :], sems.at[field]
-            )
-        )
-        copies[-1].start()
     if late:
-        diffs = side_changes(near, far)
+        diffs = side_changes(far, near)
         level = core * (levels - 1)
         gain = jnp.where(
             core == 1, -table[levels - 1, pl.ds(FALL, 1), :], table[0, pl.ds(RISE, 1), :]
@@ -678,7 +696,29 @@
                 pltpu.make_async_copy(
                     rim.at[field],
                     outs[2 + field].at[level, pl.ds(start, half), :],
-                    sems.at[2 + field],
+                    sems.at[field],
+                )
+            )
+            copies[-1].start()
+    for field in range(2):
+        for part, begin in enumerate(range(0, half, width)):
+            into = joined[pl.ds(field * half + begin, width), :]
+            tiles = [into[i : i + TILE] for i in range(0, width, TILE)]
+
+            def step(level, carry, field=field, begin=begin, tiles=tiles):
+                gain = response[level]
+                for i, tile in enumerate(tiles):
+                    at = begin + i * TILE
+                    value = known[field, level, pl.ds(start + at, TILE), :] + gain * tile
+                    result[field, level, pl.ds(at, TILE), :] = value
+                return carry
+
+            lax.fori_loop(0, levels, step, 0, unroll=4)
+            copies.append(
+                pltpu.make_async_copy(
+                    result.at[field, :, pl.ds(begin, width), :],
+                    outs[field].at[:, pl.ds(start + begin, width), :],
+                    sems.at[2 + 2 * field + part],
                 )
             )
             copies[-1].start()
@@ -699,7 +739,7 @@
         scratch_shapes=[
             pltpu.VMEM((2, levels, rows // 2, cols), F32),
             pltpu.VMEM((2, rows // 2, cols), F32),
-            pltpu.SemaphoreType.DMA((4,)),
+            pltpu.SemaphoreType.DMA((6,)),
         ],
         input_output_aliases={
             inputs + i: results - len(written) + i for i in range(len(written))
@@ -723,44 +763,43 @@
     across, stacked = lax.axis_size("gx"), lax.axis_size("gz")
     rounds = stacked.bit_length() - 1
     cores = both_ways([(i, i + 1) for i in range(0, stacked, 2)])
-    near, far, fluxes, table = edges(
+    far, near, fluxes, outward, table = edges(
         temp, u_vel, w_vel, v_vel, temp_prev, w_prev, lower, upper, metric
     )
+    far = lax.ppermute(far, "gx", both_ways([(i, (i + 1) % across) for i in range(1, across, 2)]))
     near = lax.ppermute(near, "gx", both_ways([(i, i + 1) for i in range(0, across, 2)]))
-    far = lax.ppermute(far, "gx", both_ways([(i, (i + 1) % across) for i in range(1, across, 2)]))
     other = lax.ppermute(fluxes, "gz", cores)
     outer = ()
     if rounds > 2:
         seams = both_ways([(i, i + 1) for i in range(1, stacked - 1, 2)])
-        outer = (lax.ppermute(fluxes[2 * rows : 4 * rows], "gz", seams),)
-    forward, tend, first = bulk(table, temp, u_vel, v_vel, w_vel, temp_prev, w_prev)
-    mine, changes, *late = fix(rounds, near, far, fluxes, other, forward, first, table, outer)
+        outer = (lax.ppermute(outward, "gz", seams),)
+    forward, tend, first, *written = bulk(table, temp, u_vel, v_vel, w_vel, temp_prev, w_prev)
+    entries, changes, *late = fix(
+        rounds, far, near, fluxes, outward, other, forward, first, table, outer
+    )
+    message, seam = late if late else (entries, fluxes)
     bases, gains, own, other_own = [], [], fluxes, other
     for step in range(rounds - 1):
         partners = [(i, i ^ (1 << step)) for i in range(stacked)]
-        theirs = lax.ppermute(mine, "gz", partners)
+        theirs = lax.ppermute(message, "gz", partners)
         if step > 0:
             other_own = lax.ppermute(own, "gz", partners)
-        base, gain, own, mine, *half = merge(
-            step, step + 2 == rounds, rows, mine, theirs, own, other_own
+        base, gain, message, *scalars = merge(
+            step, step + 2 == rounds, bool(late), rows, entries, theirs, own, other_own
         )
+        entries, own = message, scalars[0] if scalars else seam
         bases.append(base)
         gains.append(gain)
     partners = [(i, i ^ (stacked // 2)) for i in range(stacked)]
-    theirs = lax.ppermute(half[0], "gz", partners)
-    seam = ()
-    if late:
-        *seam, own = late
-        late = (table, tend, near, far)
+    theirs = lax.ppermute(message, "gz", partners)
     other_own = lax.ppermute(own, "gz", partners)
     known, response = prepare(
         rounds, temp, w_vel, forward, table, changes, fluxes, other, outer, bases, gains
     )
-    tendencies = tuple(
-        tends(rounds, field, table, tend, near, far, other, outer) for field in range(2)
-    )
-    joined = join(rounds, mine, theirs, own, other_own, seam)
+    tendencies = tends(rounds, table, tend, far, near, other, outer, written)
+    joined = join(rounds, bool(late), message, theirs, own, other_own)
     swapped = lax.ppermute(joined, "gz", cores)
+    late = (table, tend, far, near) if late else ()
     written = finish(rounds, known, response, joined, late, tendencies if late else ())
     written = finish(rounds, known, response, swapped, late, written)
     return tuple(written) if late else (*written, *tendencies)

time: 21.7 us -> 21.3 us (0.982)
  waiting for transfers between devices: 0.56 us -> 2.47 us
  Pallas kernels: 10.4 us -> 8.64 us
  starting transfers between devices: 9.74 us -> 9.2 us
    ppermute x1, starting transfers between devices: 3.03 us -> 0.01 us  [local(): lax.ppermute(near, 'gx', both_ways([(i, i + 1) for i in range(0, across,...]
    ppermute x1, starting transfers between devices: 3.54 us -> 6.07 us  [local(): lax.ppermute(far, 'gx', both_ways([(i, (i + 1) % across) for i in range(1...]
    pallas_call x4 -> x3, Pallas kernels: 2.67 us -> 1.15 us  [the longest x1 1.03 us: tends(): pl.pallas_call(functools.partial(tends_kernel, rounds), out_shape=(jax.Sh...]
    ppermute x2, waiting for transfers between devices: 0.01 us -> 1.18 us  [local(): theirs = lax.ppermute(message, 'gz', partners)]
    ppermute x1, waiting for transfers between devices: 0.01 us -> 0.88 us  [local(): lax.ppermute(near, 'gx', both_ways([(i, i + 1) for i in range(0, across,...]
    pallas_call x1, Pallas kernels: 1.17 us -> 0.63 us  [prepare(): pl.pallas_call(functools.partial(prepare_kernel, rounds), out_shape=(held...]
    ppermute x1, waiting for transfers between devices: 0.31 us -> 0.01 us  [local(): lax.ppermute(far, 'gx', both_ways([(i, (i + 1) % across) for i in range(1...]
    pallas_call x1, Pallas kernels: 2.69 us -> 2.95 us  [bulk(): pl.pallas_call(bulk_kernel, out_shape=(held(2, levels + 1, rows, cols), h...]
  transfers between devices with their start and end apart: 7 -> 7, of which waited for: 2 -> 4; matrix products, arithmetic and copies ran while one was open for 0% -> 0% of each run, Pallas kernels for 35% -> 27%
where the time goes in v5:
time: 21.3 us; the launch traced here: 21.1 us
  starting transfers between devices  9.2 us (43%)
  Pallas kernels  8.64 us (41%)
  waiting for transfers between devices  2.47 us (12%)
  between operations  0.8 us (4%)
    ppermute x1, starting transfers between devices, local(): lax.ppermute(far, 'gx', both_ways([(i, (i + 1) % across) for i in range(1...  6.07 us
    pallas_call x1, Pallas kernels, bulk(): pl.pallas_call(bulk_kernel, out_shape=(held(2, levels + 1, rows, cols), h...  2.95 us
    pallas_call x2, Pallas kernels, finish(): pl.pallas_call(functools.partial(finish_kernel, rounds, swapped), out_sha...  2.16 us
    pallas_call x1, Pallas kernels, edges(): pl.pallas_call(edges_kernel, out_shape=(held(2 * levels, cols), held(2 *...  1.59 us
    ppermute x1, starting transfers between devices, local(): other_own = lax.ppermute(own, 'gz', partners)  1.56 us
    ppermute x2, starting transfers between devices, local(): theirs = lax.ppermute(message, 'gz', partners)  1.5 us
    ppermute x2, waiting for transfers between devices, local(): theirs = lax.ppermute(message, 'gz', partners)  1.18 us
    pallas_call x1, Pallas kernels, tends(): pl.pallas_call(functools.partial(tends_kernel, rounds), out_shape=(jax.Sh...  1.03 us
  transfers between devices with their start and end apart: 7, of which 4 were waited for; matrix products, arithmetic and copies ran while one was open for 0% of the time, Pallas kernels for 27%

profile of v5, /device:TPU:0, one launch (start us, length us, event | category | flops | bytes accessed | tf_op | source)
XLA Modules:
  0.0 21.1 jit_solution(17059791656555700099)
XLA Ops:
  0.6 0.0 copy-start.1
  0.6 0.0 copy-start
  0.7 1.6 %edges.1 = (f32[32,256]{1,0:T(8,128)S(1)}, f32[32,256]{1,0:T(8,128)S(1)}, f32[200,256]{1,0:T(8,128)S(1)}, f32[128,256]{1,0:T(8,128)S(1)}, f32[16,8,256]{2,1,0:T(8,128)S(1)}) custom-call(f32[16,64,256]{2,1,0:T(8,128)} %temp.5, f32[16,64,256]{2,1,0:T(8,128)} %u_vel.3, f32[16,64,256]{2,1,0:T(8,128)} %w_vel.5, f32[16,64,256]{2,1,0:T(8,128)} %v_vel.3, ...), custom_call_target="tpu_custom_call" | custom-call | tf_op jit(solution)/shard_map/edges/pallas_call | solution.py:109
  2.3 6.1 %collective-permute-start = (f32[32,256]{1,0:T(8,128)S(1)}, f32[32,256]{1,0:T(8,128)S(1)}, u32[]{:S(2)}, u32[]{:S(2)}) collective-permute-start(f32[32,256]{1,0:T(8,128)S(1)} %get-tuple-element.31), channel_id=1, source_target_pairs={{4,8},{12,16},{20,24},{28,0},{8,4},{16,12},{24,20},{0,28},{5,9},{1... | collective-permute-start | bytes 98312 | tf_op jit(solution)/shard_map/ppermute | solution.py:769
  8.4 0.0 collective-permute-start.1
  8.4 0.0 collective-permute-start.2
  8.4 3.0 %bulk.1 = (f32[2,17,64,256]{3,2,1,0:T(8,128)S(1)}, f32[2,16,64,256]{3,2,1,0:T(8,128)S(1)}, f32[2,64,256]{2,1,0:T(8,128)S(1)}, f32[16,64,256]{2,1,0:T(8,128)}, f32[16,64,256]{2,1,0:T(8,128)}) custom-call(f32[16,8,256]{2,1,0:T(8,128)S(1)} %get-tuple-element.29.table.rest_0_, f32[16,64,256]{2,1,0:T(8,128)S(1)} %copy-done, f32[16,64,256]{2,1,0:T(8,128)S(1)} %copy-done.2, ...), custom_call_target="tpu_custom_call" | custom-call | flops 26214400000 | bytes 6291456 | tf_op jit(solution)/shard_map/bulk/pallas_call | solution.py:265
  11.4 0.0 collective-permute-done.far.rest_2_
  11.4 0.9 %collective-permute-done.1.near.rest_3_ = f32[32,256]{1,0:T(8,128)S(1)} collective-permute-done((f32[32,256]{1,0:T(8,128)S(1)}, f32[32,256]{1,0:T(8,128)S(1)}, u32[]{:S(2)}, u32[]{:S(2)}) %collective-permute-start.1) | collective-permute-done | bytes 32800 | tf_op jit(solution)/shard_map/ppermute | solution.py:770
  12.3 0.0 collective-permute-done.2.other
  12.3 0.2 fix.1
  12.4 0.1 collective-permute-start.3
  12.5 1.6 %collective-permute-start.5 = (f32[72,256]{1,0:T(8,128)S(1)}, f32[72,256]{1,0:T(8,128)S(1)}, u32[]{:S(2)}, u32[]{:S(2)}) collective-permute-start(f32[72,256]{1,0:T(8,128)S(1)} %get-tuple-element.44.own), channel_id=1, source_target_pairs={{0,2},{1,3},{2,0},{3,1},{4,6},{5,7},{6,4},{7,5},{8,10},{9,11},{10,... | collective-permute-start | bytes 221192 | tf_op jit(solution)/shard_map/ppermute | solution.py:795
  14.1 0.0 collective-permute-done.3.theirs
  14.1 0.1 merge.1
  14.2 1.4 %collective-permute-start.4 = (f32[64,256]{1,0:T(8,128)S(1)}, f32[64,256]{1,0:T(8,128)S(1)}, u32[]{:S(2)}, u32[]{:S(2)}) collective-permute-start(f32[64,256]{1,0:T(8,128)S(1)} %get-tuple-element.43.mine), channel_id=1, source_target_pairs={{0,2},{1,3},{2,0},{3,1},{4,6},{5,7},{6,4},{7,5},{8,10},{9,11},{10,... | collective-permute-start | bytes 196616 | tf_op jit(solution)/shard_map/ppermute | solution.py:794
  15.6 1.0 %tends.1 = (f32[16,64,256]{2,1,0:T(8,128)}, f32[16,64,256]{2,1,0:T(8,128)}) custom-call(f32[16,8,256]{2,1,0:T(8,128)S(1)} %get-tuple-element.29.table.rest_0_, f32[2,16,64,256]{3,2,1,0:T(8,128)S(1)} %get-tuple-element.45.tend.rest_1_, f32[32,256]{1,0:T(8,128)S(1)} %collective-permute-done.far.rest_2_, ...), custom_call_target="tpu_custom_call", output_to_operand_aliasing={{0}: (5, {}), {1}: (6, {})} | custom-call | flops 262144 | bytes 2097152 | tf_op jit(solution)/shard_map/tends/pallas_call | solution.py:452
  16.6 0.6 %prepare.1 = (f32[2,16,64,256]{3,2,1,0:T(8,128)S(1)}, f32[16,8,256]{2,1,0:T(8,128)S(1)}) custom-call(f32[16,64,256]{2,1,0:T(8,128)S(1)} %copy-done, f32[16,64,256]{2,1,0:T(8,128)S(1)} %copy-done.1, f32[2,17,64,256]{3,2,1,0:T(8,128)S(1)} %get-tuple-element.30.forward, f32[16,8,256]{2,1,0:T(8,128)S(1)} %get-tuple-element.29.table.rest_0_, ...), custom_call_target="tpu_custom_call" | custom-call | flops 262144 | bytes 6291456 | tf_op jit(solution)/shard_map/prepare/pallas_call | solution.py:614
  17.3 0.2 collective-permute-done.5.other
  17.4 1.2 %collective-permute-done.4.theirs = f32[64,256]{1,0:T(8,128)S(1)} collective-permute-done((f32[64,256]{1,0:T(8,128)S(1)}, f32[64,256]{1,0:T(8,128)S(1)}, u32[]{:S(2)}, u32[]{:S(2)}) %collective-permute-start.4) | collective-permute-done | bytes 65568 | tf_op jit(solution)/shard_map/ppermute | solution.py:794
  18.7 0.1 collective-permute-start.6
  18.7 1.1 %finish.2 = (f32[16,64,256]{2,1,0:T(8,128)}, f32[16,64,256]{2,1,0:T(8,128)}, f32[16,64,256]{2,1,0:T(8,128)}, f32[16,64,256]{2,1,0:T(8,128)}) custom-call(f32[2,16,64,256]{3,2,1,0:T(8,128)S(1)} %get-tuple-element.41.known, f32[16,8,256]{2,1,0:T(8,128)S(1)} %get-tuple-element.42.response, ...), custom_call_target="tpu_custom_call", output_to_operand_aliasing={{2}: (7, {}), {3}: (8, {})} | custom-call | flops 5242880000 | bytes 2097152 | tf_op jit(solution)/shard_map/finish/pallas_call | solution.py:734
  19.8 0.2 %collective-permute-done.6.joined = f32[128,256]{1,0:T(8,128)S(1)} collective-permute-done((f32[128,256]{1,0:T(8,128)S(1)}, f32[128,256]{1,0:T(8,128)S(1)}, u32[]{:S(2)}, u32[]{:S(2)}) %collective-permute-start.6) | collective-permute-done | bytes 131104 | tf_op jit(solution)/shard_map/ppermute | solution.py:801
  20.1 1.1 %finish.3 = (f32[16,64,256]{2,1,0:T(8,128)}, f32[16,64,256]{2,1,0:T(8,128)}, f32[16,64,256]{2,1,0:T(8,128)}, f32[16,64,256]{2,1,0:T(8,128)}) custom-call(f32[2,16,64,256]{3,2,1,0:T(8,128)S(1)} %get-tuple-element.41.known, f32[16,8,256]{2,1,0:T(8,128)S(1)} %get-tuple-element.42.response, ...), custom_call_target="tpu_custom_call", output_to_operand_aliasing={{0}: (7, {}), {1}: (8, {}), {2}: (9, {}), {3}: (10, {})} | custom-call | flops 5242880000 | bytes 2097152 | tf_op jit(solution)/shard_map/finish/pallas_call | solution.py:734
  (11 shorter events, 0.1 us)
Async XLA Ops:
  0.6 7.7 %copy-start.1 = (f32[16,64,256]{2,1,0:T(8,128)S(1)}, f32[16,64,256]{2,1,0:T(8,128)}, u32[]{:S(2)}) copy-start(f32[16,64,256]{2,1,0:T(8,128)} %w_vel.5) | copy-start | bytes 3145732
  0.6 7.7 %copy-start = (f32[16,64,256]{2,1,0:T(8,128)S(1)}, f32[16,64,256]{2,1,0:T(8,128)}, u32[]{:S(2)}) copy-start(f32[16,64,256]{2,1,0:T(8,128)} %temp.5) | copy-start | bytes 3145732
  0.7 7.7 %copy-start.5 = (f32[16,64,256]{2,1,0:T(8,128)S(1)}, f32[16,64,256]{2,1,0:T(8,128)}, u32[]{:S(2)}) copy-start(f32[16,64,256]{2,1,0:T(8,128)} %w_prev.3) | copy-start | bytes 3145732
  0.7 7.7 %copy-start.4 = (f32[16,64,256]{2,1,0:T(8,128)S(1)}, f32[16,64,256]{2,1,0:T(8,128)}, u32[]{:S(2)}) copy-start(f32[16,64,256]{2,1,0:T(8,128)} %temp_prev.3) | copy-start | bytes 3145732
  0.7 7.7 %copy-start.3 = (f32[16,64,256]{2,1,0:T(8,128)S(1)}, f32[16,64,256]{2,1,0:T(8,128)}, u32[]{:S(2)}) copy-start(f32[16,64,256]{2,1,0:T(8,128)} %v_vel.3) | copy-start | bytes 3145732
  0.7 7.7 %copy-start.2 = (f32[16,64,256]{2,1,0:T(8,128)S(1)}, f32[16,64,256]{2,1,0:T(8,128)}, u32[]{:S(2)}) copy-start(f32[16,64,256]{2,1,0:T(8,128)} %u_vel.3) | copy-start | bytes 3145732
  2.3 9.1 %collective-permute-start = (f32[32,256]{1,0:T(8,128)S(1)}, f32[32,256]{1,0:T(8,128)S(1)}, u32[]{:S(2)}, u32[]{:S(2)}) collective-permute-start(f32[32,256]{1,0:T(8,128)S(1)} %get-tuple-element.31), channel_id=1, source_target_pairs={{4,8},{12,16},{20,24},{28,0},{8,4},{16,12},{24,20},{0,28},{5,9},{1... | collective-permute-start | bytes 98312 | tf_op jit(solution)/shard_map/ppermute | solution.py:769
  8.4 3.9 %collective-permute-start.1 = (f32[32,256]{1,0:T(8,128)S(1)}, f32[32,256]{1,0:T(8,128)S(1)}, u32[]{:S(2)}, u32[]{:S(2)}) collective-permute-start(f32[32,256]{1,0:T(8,128)S(1)} %get-tuple-element.32), channel_id=1, source_target_pairs={{0,4},{8,12},{16,20},{24,28},{4,0},{12,8},{20,16},{28,24},{1,5},{9... | collective-permute-start | bytes 98312 | tf_op jit(solution)/shard_map/ppermute | solution.py:770
  8.4 3.9 %collective-permute-start.2 = (f32[200,256]{1,0:T(8,128)S(1)}, f32[200,256]{1,0:T(8,128)S(1)}, u32[]{:S(2)}, u32[]{:S(2)}) collective-permute-start(f32[200,256]{1,0:T(8,128)S(1)} %get-tuple-element.33.fluxes.own), channel_id=1, source_target_pairs={{0,1},{2,3},{1,0},{3,2},{4,5},{6,7},{5,4},{7,6},{8,9},{10,11},{9,8... | collective-permute-start | bytes 614408 | tf_op jit(solution)/shard_map/ppermute | solution.py:771
  12.4 1.6 %collective-permute-start.3 = (f32[192,256]{1,0:T(8,128)S(1)}, f32[192,256]{1,0:T(8,128)S(1)}, u32[]{:S(2)}, u32[]{:S(2)}) collective-permute-start(f32[192,256]{1,0:T(8,128)S(1)} %get-tuple-element.38), channel_id=1, source_target_pairs={{0,1},{1,0},{2,3},{3,2},{4,5},{5,4},{6,7},{7,6},{8,9},{9,8},{10,11... | collective-permute-start | bytes 589832 | tf_op jit(solution)/shard_map/ppermute | solution.py:784
  12.5 4.9 %collective-permute-start.5 = (f32[72,256]{1,0:T(8,128)S(1)}, f32[72,256]{1,0:T(8,128)S(1)}, u32[]{:S(2)}, u32[]{:S(2)}) collective-permute-start(f32[72,256]{1,0:T(8,128)S(1)} %get-tuple-element.44.own), channel_id=1, source_target_pairs={{0,2},{1,3},{2,0},{3,1},{4,6},{5,7},{6,4},{7,5},{8,10},{9,11},{10,... | collective-permute-start | bytes 221192 | tf_op jit(solution)/shard_map/ppermute | solution.py:795
  14.2 4.4 %collective-permute-start.4 = (f32[64,256]{1,0:T(8,128)S(1)}, f32[64,256]{1,0:T(8,128)S(1)}, u32[]{:S(2)}, u32[]{:S(2)}) collective-permute-start(f32[64,256]{1,0:T(8,128)S(1)} %get-tuple-element.43.mine), channel_id=1, source_target_pairs={{0,2},{1,3},{2,0},{3,1},{4,6},{5,7},{6,4},{7,5},{8,10},{9,11},{10,... | collective-permute-start | bytes 196616 | tf_op jit(solution)/shard_map/ppermute | solution.py:794
  18.7 1.4 %collective-permute-start.6 = (f32[128,256]{1,0:T(8,128)S(1)}, f32[128,256]{1,0:T(8,128)S(1)}, u32[]{:S(2)}, u32[]{:S(2)}) collective-permute-start(f32[128,256]{1,0:T(8,128)S(1)} %join.1.joined), channel_id=1, source_target_pairs={{0,1},{2,3},{1,0},{3,2},{4,5},{6,7},{5,4},{7,6},{8,9},{10,11},{9,8... | collective-permute-start | bytes 393224 | tf_op jit(solution)/shard_map/ppermute | solution.py:801

commit v6 on v5

--- a/solution.py
+++ b/solution.py
@@ -12,7 +12,6 @@
 FIELD_WEIGHT = 2.0 / NEW_WEIGHT
 PREV_WEIGHT = (17.0 / 60.0) / NEW_WEIGHT
 TILE = 8
-CHUNK = 4
 MIB = 1024 * 1024
 
 PIVOT_NEW, LOWER_PIVOT, UPPER_PIVOT, FIRST_GREEN, BELOW_FORWARD, PIVOT, RISE, FALL = range(8)
@@ -170,6 +169,7 @@
 
 
 def bulk_kernel(
+    arrived,
     table,
     temp,
     u_vel,
@@ -180,9 +180,6 @@
     forward,
     tend,
     first,
-    temp_tend,
-    w_tend,
-    sems,
 ):
     levels, rows, cols = temp.shape
     strips = rows // TILE
@@ -192,13 +189,6 @@
         first[field] = jnp.zeros((rows, cols), F32)
     row_at = lax.broadcasted_iota(jnp.int32, (TILE, cols), 0)
     zero = jnp.zeros((TILE, cols), F32)
-
-    def chunk_copies(chunk):
-        at = pl.ds(chunk * CHUNK, CHUNK)
-        return [
-            pltpu.make_async_copy(tend.at[field, at], out.at[at], sems.at[field, chunk])
-            for field, out in enumerate((temp_tend, w_tend))
-        ]
 
     def level_step(level, carry):
         def spread(at):
@@ -246,21 +236,12 @@
                 first[field, at, :] = first[field, at, :] + green * right
             before = ahead
             here, back, ahead = after
-
-        @pl.when((level % CHUNK == CHUNK - 1) & (level < levels - CHUNK))
-        def _():
-            for copy in chunk_copies(level // CHUNK):
-                copy.start()
-
         return carry
 
     lax.fori_loop(0, levels, level_step, 0)
-    for chunk in range(levels // CHUNK - 1):
-        for copy in chunk_copies(chunk):
-            copy.wait()
-
-
-def bulk(table, *arrays):
+
+
+def bulk(arrived, table, *arrays):
     levels, rows, cols = arrays[0].shape
     return pl.pallas_call(
         bulk_kernel,
@@ -268,12 +249,9 @@
             held(2, levels + 1, rows, cols),
             held(2, levels, rows, cols),
             held(2, rows, cols),
-            jax.ShapeDtypeStruct((levels, rows, cols), F32),
-            jax.ShapeDtypeStruct((levels, rows, cols), F32),
         ),
-        in_specs=[whole(VMEM)] * 7,
-        out_specs=[whole(VMEM)] * 3 + [whole(pl.ANY)] * 2,
-        scratch_shapes=[pltpu.SemaphoreType.DMA((2, levels // CHUNK - 1))],
+        in_specs=[whole(pl.ANY)] + [whole(VMEM)] * 7,
+        out_specs=[whole(VMEM)] * 3,
         compiler_params=pltpu.CompilerParams(vmem_limit_bytes=8 * MIB),
         cost_estimate=pl.CostEstimate(
             flops=100000 * levels * rows * cols,
@@ -281,7 +259,7 @@
             transcendentals=0,
         ),
         name="bulk",
-    )(*map(in_vmem, (table, *arrays)))
+    )(arrived, *map(in_vmem, (table, *arrays)))
 
 
 def side_changes(far, near):
@@ -334,7 +312,7 @@
 
 
 def fix_kernel(
-    rounds, levels, far, near, fluxes, outward, other, forward, first, table, *rest
+    rounds, levels, other, far, near, fluxes, outward, forward, first, table, *rest
 ):
     outer, rest = (rest[0], rest[1:]) if rounds > 2 else (None, rest)
     entries, changes, *late = rest
@@ -390,7 +368,7 @@
             seam[pl.ds(rows + at, 1), :] = value
 
 
-def fix(rounds, far, near, fluxes, outward, other, forward, first, table, outer):
+def fix(rounds, other, far, near, fluxes, outward, forward, first, table, outer):
     levels = table.shape[0]
     _, rows, cols = first.shape
     shapes = [held(4 * rows, cols), held(4 * levels, cols)]
@@ -404,16 +382,15 @@
         compiler_params=pltpu.CompilerParams(vmem_limit_bytes=8 * MIB),
         name="fix",
     )(
-        far, near, fluxes, outward, other, in_vmem(forward), in_vmem(first), in_vmem(table), *outer
+        other, far, near, fluxes, outward, in_vmem(forward), in_vmem(first), in_vmem(table), *outer
     )
 
 
 def tends_kernel(rounds, table, tend, far, near, other, *rest):
     outer, rest = (rest[0], rest[1:]) if rounds > 2 else (None, rest)
-    *outs, layers, strips, sems = rest[2:]
+    *outs, layers, strips, sems = rest
     _, levels, rows, cols = tend.shape
     inside, middle = pl.ds(1, levels - 2), pl.ds(TILE, rows - 2 * TILE)
-    left = pl.ds(levels - CHUNK, CHUNK - 1)
     copies = []
 
     def send(field, at, src, dst):
@@ -421,7 +398,7 @@
         copies[-1].start()
 
     for field, out in enumerate(outs):
-        send(field, 0, tend.at[field, left, middle, :], out.at[left, middle, :])
+        send(field, 0, tend.at[field, inside, middle, :], out.at[inside, middle, :])
     diffs = side_changes(far, near)
     tile_at = lax.broadcasted_iota(jnp.int32, (TILE, cols), 0)
     for field, out in enumerate(outs):
@@ -446,20 +423,18 @@
         copy.wait()
 
 
-def tends(rounds, table, tend, far, near, other, outer, written):
+def tends(rounds, table, tend, far, near, other, outer):
     _, levels, rows, cols = tend.shape
-    inputs = 5 + len(outer)
     return pl.pallas_call(
         functools.partial(tends_kernel, rounds),
         out_shape=(jax.ShapeDtypeStruct((levels, rows, cols), F32),) * 2,
-        in_specs=[whole(VMEM)] * inputs + [whole(pl.ANY)] * 2,
+        in_specs=[whole(VMEM)] * (5 + len(outer)),
         out_specs=[whole(pl.ANY)] * 2,
         scratch_shapes=[
             pltpu.VMEM((2, 2, rows, cols), F32),
             pltpu.VMEM((2, 2, levels, TILE, cols), F32),
             pltpu.SemaphoreType.DMA((2, 5)),
         ],
-        input_output_aliases={inputs: 0, inputs + 1: 1},
         compiler_params=pltpu.CompilerParams(vmem_limit_bytes=8 * MIB),
         cost_estimate=pl.CostEstimate(
             flops=levels * rows * cols,
@@ -467,7 +442,7 @@
             transcendentals=0,
         ),
         name="tends",
-    )(in_vmem(table), in_vmem(tend), far, near, other, *outer, *in_hbm(*written))
+    )(in_vmem(table), in_vmem(tend), far, near, other, *outer)
 
 
 def merge_kernel(bit, final, late, own_at, other_at, mine, theirs, own, other, base, gains, *rest):
@@ -766,16 +741,16 @@
     far, near, fluxes, outward, table = edges(
         temp, u_vel, w_vel, v_vel, temp_prev, w_prev, lower, upper, metric
     )
+    other = lax.ppermute(fluxes, "gz", cores)
     far = lax.ppermute(far, "gx", both_ways([(i, (i + 1) % across) for i in range(1, across, 2)]))
     near = lax.ppermute(near, "gx", both_ways([(i, i + 1) for i in range(0, across, 2)]))
-    other = lax.ppermute(fluxes, "gz", cores)
     outer = ()
     if rounds > 2:
         seams = both_ways([(i, i + 1) for i in range(1, stacked - 1, 2)])
         outer = (lax.ppermute(outward, "gz", seams),)
-    forward, tend, first, *written = bulk(table, temp, u_vel, v_vel, w_vel, temp_prev, w_prev)
+    forward, tend, first = bulk(other, table, temp, u_vel, v_vel, w_vel, temp_prev, w_prev)
     entries, changes, *late = fix(
-        rounds, far, near, fluxes, outward, other, forward, first, table, outer
+        rounds, other, far, near, fluxes, outward, forward, first, table, outer
     )
     message, seam = late if late else (entries, fluxes)
     bases, gains, own, other_own = [], [], fluxes, other
@@ -796,7 +771,7 @@
     known, response = prepare(
         rounds, temp, w_vel, forward, table, changes, fluxes, other, outer, bases, gains
     )
-    tendencies = tends(rounds, table, tend, far, near, other, outer, written)
+    tendencies = tends(rounds, table, tend, far, near, other, outer)
     joined = join(rounds, bool(late), message, theirs, own, other_own)
     swapped = lax.ppermute(joined, "gz", cores)
     late = (table, tend, far, near) if late else ()

time: 21.3 us -> 21.4 us (level)
  waiting for transfers between devices: 2.47 us -> 2.21 us
  Pallas kernels: 8.64 us -> 8.9 us
    ppermute x1, starting transfers between devices: 0.01 us -> 0.52 us  [local(): other = lax.ppermute(fluxes, 'gz', cores)]
    ppermute x1, starting transfers between devices: 6.07 us -> 5.63 us  [local(): lax.ppermute(far, 'gx', both_ways([(i, (i + 1) % across) for i in range(1...]
    pallas_call x1, Pallas kernels: 1.03 us -> 1.38 us  [tends(): pl.pallas_call(functools.partial(tends_kernel, rounds), out_shape=(jax.Sh...]
  transfers between devices with their start and end apart: 7 -> 7, of which waited for: 4 -> 3; matrix products, arithmetic and copies ran while one was open for 0% -> 0% of each run, Pallas kernels for 27% -> 28%
where the time goes in v6:
time: 21.4 us; the launch traced here: 21.2 us
  starting transfers between devices  9.27 us (43%)
  Pallas kernels  8.9 us (42%)
  waiting for transfers between devices  2.21 us (10%)
  between operations  0.81 us (4%)
    ppermute x1, starting transfers between devices, local(): lax.ppermute(far, 'gx', both_ways([(i, (i + 1) % across) for i in range(1...  5.63 us
    pallas_call x1, Pallas kernels, bulk(): pl.pallas_call(bulk_kernel, out_shape=(held(2, levels + 1, rows, cols), h...  2.88 us
    pallas_call x2, Pallas kernels, finish(): pl.pallas_call(functools.partial(finish_kernel, rounds, swapped), out_sha...  2.16 us
    pallas_call x1, Pallas kernels, edges(): pl.pallas_call(edges_kernel, out_shape=(held(2 * levels, cols), held(2 *...  1.59 us
    ppermute x1, starting transfers between devices, local(): other_own = lax.ppermute(own, 'gz', partners)  1.56 us
    ppermute x2, starting transfers between devices, local(): theirs = lax.ppermute(message, 'gz', partners)  1.5 us
    pallas_call x1, Pallas kernels, tends(): pl.pallas_call(functools.partial(tends_kernel, rounds), out_shape=(jax.Sh...  1.38 us
    ppermute x2, waiting for transfers between devices, local(): theirs = lax.ppermute(message, 'gz', partners)  1.01 us
  transfers between devices with their start and end apart: 7, of which 3 were waited for; matrix products, arithmetic and copies ran while one was open for 0% of the time, Pallas kernels for 28%

profile of v6, /device:TPU:0, one launch (start us, length us, event | category | flops | bytes accessed | tf_op | source)
XLA Modules:
  0.0 21.2 jit_solution(964785877240562493)
XLA Ops:
  0.6 0.0 copy-start.1
  0.6 0.0 copy-start
  0.7 1.6 %edges.1 = (f32[32,256]{1,0:T(8,128)S(1)}, f32[32,256]{1,0:T(8,128)S(1)}, f32[200,256]{1,0:T(8,128)S(1)}, f32[128,256]{1,0:T(8,128)S(1)}, f32[16,8,256]{2,1,0:T(8,128)S(1)}) custom-call(f32[16,64,256]{2,1,0:T(8,128)} %temp.5, f32[16,64,256]{2,1,0:T(8,128)} %u_vel.3, f32[16,64,256]{2,1,0:T(8,128)} %w_vel.5, f32[16,64,256]{2,1,0:T(8,128)} %v_vel.3, ...), custom_call_target="tpu_custom_call" | custom-call | tf_op jit(solution)/shard_map/edges/pallas_call | solution.py:108
  2.3 0.5 %collective-permute-start = (f32[200,256]{1,0:T(8,128)S(1)}, f32[200,256]{1,0:T(8,128)S(1)}, u32[]{:S(2)}, u32[]{:S(2)}) collective-permute-start(f32[200,256]{1,0:T(8,128)S(1)} %get-tuple-element.27.fluxes.own), channel_id=1, source_target_pairs={{0,1},{2,3},{1,0},{3,2},{4,5},{6,7},{5,4},{7,6},{8,9},{10,11},{9,8... | collective-permute-start | bytes 614408 | tf_op jit(solution)/shard_map/ppermute | solution.py:744
  2.8 5.6 %collective-permute-start.1 = (f32[32,256]{1,0:T(8,128)S(1)}, f32[32,256]{1,0:T(8,128)S(1)}, u32[]{:S(2)}, u32[]{:S(2)}) collective-permute-start(f32[32,256]{1,0:T(8,128)S(1)} %get-tuple-element.30), channel_id=1, source_target_pairs={{4,8},{12,16},{20,24},{28,0},{8,4},{16,12},{24,20},{0,28},{5,9},{1... | collective-permute-start | bytes 98312 | tf_op jit(solution)/shard_map/ppermute | solution.py:745
  8.4 0.0 collective-permute-start.2
  8.4 0.0 collective-permute-done.arrived.other
  8.5 2.9 %bulk.1 = (f32[2,17,64,256]{3,2,1,0:T(8,128)S(1)}, f32[2,16,64,256]{3,2,1,0:T(8,128)S(1)}, f32[2,64,256]{2,1,0:T(8,128)S(1)}) custom-call(f32[200,256]{1,0:T(8,128)S(1)} %collective-permute-done.arrived.other, f32[16,8,256]{2,1,0:T(8,128)S(1)} %get-tuple-element.28.table.rest_0_, f32[16,64,256]{2,1,0:T(8,128)S(1)} %copy-done, f32[16,64,256]{2,1,0:T(8,128)S(1)} %copy-done.2, ...), custom_call_target="tpu_custom_call" | custom-call | flops 26214400000 | bytes 6291456 | tf_op jit(solution)/shard_map/bulk/pallas_call | solution.py:246
  11.4 0.0 collective-permute-done.1.far.rest_2_
  11.4 1.0 %collective-permute-done.2.near.rest_3_ = f32[32,256]{1,0:T(8,128)S(1)} collective-permute-done((f32[32,256]{1,0:T(8,128)S(1)}, f32[32,256]{1,0:T(8,128)S(1)}, u32[]{:S(2)}, u32[]{:S(2)}) %collective-permute-start.2) | collective-permute-done | bytes 32800 | tf_op jit(solution)/shard_map/ppermute | solution.py:746
  12.4 0.2 fix.1
  12.5 0.1 collective-permute-start.3
  12.6 1.6 %collective-permute-start.5 = (f32[72,256]{1,0:T(8,128)S(1)}, f32[72,256]{1,0:T(8,128)S(1)}, u32[]{:S(2)}, u32[]{:S(2)}) collective-permute-start(f32[72,256]{1,0:T(8,128)S(1)} %get-tuple-element.42.own), channel_id=1, source_target_pairs={{0,2},{1,3},{2,0},{3,1},{4,6},{5,7},{6,4},{7,5},{8,10},{9,11},{10,... | collective-permute-start | bytes 221192 | tf_op jit(solution)/shard_map/ppermute | solution.py:770
  14.1 0.0 collective-permute-done.3.theirs
  14.1 0.1 merge.1
  14.2 1.4 %collective-permute-start.4 = (f32[64,256]{1,0:T(8,128)S(1)}, f32[64,256]{1,0:T(8,128)S(1)}, u32[]{:S(2)}, u32[]{:S(2)}) collective-permute-start(f32[64,256]{1,0:T(8,128)S(1)} %get-tuple-element.41.mine), channel_id=1, source_target_pairs={{0,2},{1,3},{2,0},{3,1},{4,6},{5,7},{6,4},{7,5},{8,10},{9,11},{10,... | collective-permute-start | bytes 196616 | tf_op jit(solution)/shard_map/ppermute | solution.py:769
  15.7 1.4 %tends.1 = (f32[16,64,256]{2,1,0:T(8,128)}, f32[16,64,256]{2,1,0:T(8,128)}) custom-call(f32[16,8,256]{2,1,0:T(8,128)S(1)} %get-tuple-element.28.table.rest_0_, f32[2,16,64,256]{3,2,1,0:T(8,128)S(1)} %get-tuple-element.43.tend.rest_1_, f32[32,256]{1,0:T(8,128)S(1)} %collective-permute-done.1.far.rest_2_, f32[32,256]{1,0:T(8,128)S(1)} %collective-permute-done.2.near.rest_3_, ...), custom_call_target="tpu_custom_call" | custom-call | flops 262144 | bytes 2097152 | tf_op jit(solution)/shard_map/tends/pallas_call | solution.py:428
  17.1 0.6 %prepare.1 = (f32[2,16,64,256]{3,2,1,0:T(8,128)S(1)}, f32[16,8,256]{2,1,0:T(8,128)S(1)}) custom-call(f32[16,64,256]{2,1,0:T(8,128)S(1)} %copy-done, f32[16,64,256]{2,1,0:T(8,128)S(1)} %copy-done.1, f32[2,17,64,256]{3,2,1,0:T(8,128)S(1)} %get-tuple-element.29.forward, f32[16,8,256]{2,1,0:T(8,128)S(1)} %get-tuple-element.28.table.rest_0_, ...), custom_call_target="tpu_custom_call" | custom-call | flops 262144 | bytes 6291456 | tf_op jit(solution)/shard_map/prepare/pallas_call | solution.py:589
  17.7 0.0 collective-permute-done.5.other
  17.7 1.0 %collective-permute-done.4.theirs = f32[64,256]{1,0:T(8,128)S(1)} collective-permute-done((f32[64,256]{1,0:T(8,128)S(1)}, f32[64,256]{1,0:T(8,128)S(1)}, u32[]{:S(2)}, u32[]{:S(2)}) %collective-permute-start.4) | collective-permute-done | bytes 65568 | tf_op jit(solution)/shard_map/ppermute | solution.py:769
  18.7 0.1 collective-permute-start.6
  18.8 1.1 %finish.2 = (f32[16,64,256]{2,1,0:T(8,128)}, f32[16,64,256]{2,1,0:T(8,128)}, f32[16,64,256]{2,1,0:T(8,128)}, f32[16,64,256]{2,1,0:T(8,128)}) custom-call(f32[2,16,64,256]{3,2,1,0:T(8,128)S(1)} %get-tuple-element.39.known, f32[16,8,256]{2,1,0:T(8,128)S(1)} %get-tuple-element.40.response, ...), custom_call_target="tpu_custom_call", output_to_operand_aliasing={{2}: (7, {}), {3}: (8, {})} | custom-call | flops 5242880000 | bytes 2097152 | tf_op jit(solution)/shard_map/finish/pallas_call | solution.py:709
  19.9 0.2 %collective-permute-done.6.joined = f32[128,256]{1,0:T(8,128)S(1)} collective-permute-done((f32[128,256]{1,0:T(8,128)S(1)}, f32[128,256]{1,0:T(8,128)S(1)}, u32[]{:S(2)}, u32[]{:S(2)}) %collective-permute-start.6) | collective-permute-done | bytes 131104 | tf_op jit(solution)/shard_map/ppermute | solution.py:776
  20.1 1.1 %finish.3 = (f32[16,64,256]{2,1,0:T(8,128)}, f32[16,64,256]{2,1,0:T(8,128)}, f32[16,64,256]{2,1,0:T(8,128)}, f32[16,64,256]{2,1,0:T(8,128)}) custom-call(f32[2,16,64,256]{3,2,1,0:T(8,128)S(1)} %get-tuple-element.39.known, f32[16,8,256]{2,1,0:T(8,128)S(1)} %get-tuple-element.40.response, ...), custom_call_target="tpu_custom_call", output_to_operand_aliasing={{0}: (7, {}), {1}: (8, {}), {2}: (9, {}), {3}: (10, {})} | custom-call | flops 5242880000 | bytes 2097152 | tf_op jit(solution)/shard_map/finish/pallas_call | solution.py:709
  (11 shorter events, 0.1 us)
Async XLA Ops:
  0.6 7.8 %copy-start.1 = (f32[16,64,256]{2,1,0:T(8,128)S(1)}, f32[16,64,256]{2,1,0:T(8,128)}, u32[]{:S(2)}) copy-start(f32[16,64,256]{2,1,0:T(8,128)} %w_vel.5) | copy-start | bytes 3145732
  0.6 7.8 %copy-start = (f32[16,64,256]{2,1,0:T(8,128)S(1)}, f32[16,64,256]{2,1,0:T(8,128)}, u32[]{:S(2)}) copy-start(f32[16,64,256]{2,1,0:T(8,128)} %temp.5) | copy-start | bytes 3145732
  0.7 7.8 %copy-start.5 = (f32[16,64,256]{2,1,0:T(8,128)S(1)}, f32[16,64,256]{2,1,0:T(8,128)}, u32[]{:S(2)}) copy-start(f32[16,64,256]{2,1,0:T(8,128)} %w_prev.3) | copy-start | bytes 3145732
  0.7 7.8 %copy-start.4 = (f32[16,64,256]{2,1,0:T(8,128)S(1)}, f32[16,64,256]{2,1,0:T(8,128)}, u32[]{:S(2)}) copy-start(f32[16,64,256]{2,1,0:T(8,128)} %temp_prev.3) | copy-start | bytes 3145732
  0.7 7.8 %copy-start.3 = (f32[16,64,256]{2,1,0:T(8,128)S(1)}, f32[16,64,256]{2,1,0:T(8,128)}, u32[]{:S(2)}) copy-start(f32[16,64,256]{2,1,0:T(8,128)} %v_vel.3) | copy-start | bytes 3145732
  0.7 7.8 %copy-start.2 = (f32[16,64,256]{2,1,0:T(8,128)S(1)}, f32[16,64,256]{2,1,0:T(8,128)}, u32[]{:S(2)}) copy-start(f32[16,64,256]{2,1,0:T(8,128)} %u_vel.3) | copy-start | bytes 3145732
  2.3 6.2 %collective-permute-start = (f32[200,256]{1,0:T(8,128)S(1)}, f32[200,256]{1,0:T(8,128)S(1)}, u32[]{:S(2)}, u32[]{:S(2)}) collective-permute-start(f32[200,256]{1,0:T(8,128)S(1)} %get-tuple-element.27.fluxes.own), channel_id=1, source_target_pairs={{0,1},{2,3},{1,0},{3,2},{4,5},{6,7},{5,4},{7,6},{8,9},{10,11},{9,8... | collective-permute-start | bytes 614408 | tf_op jit(solution)/shard_map/ppermute | solution.py:744
  2.8 8.6 %collective-permute-start.1 = (f32[32,256]{1,0:T(8,128)S(1)}, f32[32,256]{1,0:T(8,128)S(1)}, u32[]{:S(2)}, u32[]{:S(2)}) collective-permute-start(f32[32,256]{1,0:T(8,128)S(1)} %get-tuple-element.30), channel_id=1, source_target_pairs={{4,8},{12,16},{20,24},{28,0},{8,4},{16,12},{24,20},{0,28},{5,9},{1... | collective-permute-start | bytes 98312 | tf_op jit(solution)/shard_map/ppermute | solution.py:745
  8.4 3.9 %collective-permute-start.2 = (f32[32,256]{1,0:T(8,128)S(1)}, f32[32,256]{1,0:T(8,128)S(1)}, u32[]{:S(2)}, u32[]{:S(2)}) collective-permute-start(f32[32,256]{1,0:T(8,128)S(1)} %get-tuple-element.31), channel_id=1, source_target_pairs={{0,4},{8,12},{16,20},{24,28},{4,0},{12,8},{20,16},{28,24},{1,5},{9... | collective-permute-start | bytes 98312 | tf_op jit(solution)/shard_map/ppermute | solution.py:746
  12.5 1.6 %collective-permute-start.3 = (f32[192,256]{1,0:T(8,128)S(1)}, f32[192,256]{1,0:T(8,128)S(1)}, u32[]{:S(2)}, u32[]{:S(2)}) collective-permute-start(f32[192,256]{1,0:T(8,128)S(1)} %get-tuple-element.36), channel_id=1, source_target_pairs={{0,1},{1,0},{2,3},{3,2},{4,5},{5,4},{6,7},{7,6},{8,9},{9,8},{10,11... | collective-permute-start | bytes 589832 | tf_op jit(solution)/shard_map/ppermute | solution.py:759
  12.6 5.1 %collective-permute-start.5 = (f32[72,256]{1,0:T(8,128)S(1)}, f32[72,256]{1,0:T(8,128)S(1)}, u32[]{:S(2)}, u32[]{:S(2)}) collective-permute-start(f32[72,256]{1,0:T(8,128)S(1)} %get-tuple-element.42.own), channel_id=1, source_target_pairs={{0,2},{1,3},{2,0},{3,1},{4,6},{5,7},{6,4},{7,5},{8,10},{9,11},{10,... | collective-permute-start | bytes 221192 | tf_op jit(solution)/shard_map/ppermute | solution.py:770
  14.2 4.4 %collective-permute-start.4 = (f32[64,256]{1,0:T(8,128)S(1)}, f32[64,256]{1,0:T(8,128)S(1)}, u32[]{:S(2)}, u32[]{:S(2)}) collective-permute-start(f32[64,256]{1,0:T(8,128)S(1)} %get-tuple-element.41.mine), channel_id=1, source_target_pairs={{0,2},{1,3},{2,0},{3,1},{4,6},{5,7},{6,4},{7,5},{8,10},{9,11},{10,... | collective-permute-start | bytes 196616 | tf_op jit(solution)/shard_map/ppermute | solution.py:769
  18.7 1.4 %collective-permute-start.6 = (f32[128,256]{1,0:T(8,128)S(1)}, f32[128,256]{1,0:T(8,128)S(1)}, u32[]{:S(2)}, u32[]{:S(2)}) collective-permute-start(f32[128,256]{1,0:T(8,128)S(1)} %join.1.joined), channel_id=1, source_target_pairs={{0,1},{2,3},{1,0},{3,2},{4,5},{6,7},{5,4},{7,6},{8,9},{10,11},{9,8... | collective-permute-start | bytes 393224 | tf_op jit(solution)/shard_map/ppermute | solution.py:776

commit v7 on v6

--- a/solution.py
+++ b/solution.py
@@ -312,7 +312,7 @@
 
 
 def fix_kernel(
-    rounds, levels, other, far, near, fluxes, outward, forward, first, table, *rest
+    rounds, levels, other, near, far, fluxes, outward, forward, first, table, *rest
 ):
     outer, rest = (rest[0], rest[1:]) if rounds > 2 else (None, rest)
     entries, changes, *late = rest
@@ -368,7 +368,7 @@
             seam[pl.ds(rows + at, 1), :] = value
 
 
-def fix(rounds, other, far, near, fluxes, outward, forward, first, table, outer):
+def fix(rounds, other, near, far, fluxes, outward, forward, first, table, outer):
     levels = table.shape[0]
     _, rows, cols = first.shape
     shapes = [held(4 * rows, cols), held(4 * levels, cols)]
@@ -382,7 +382,7 @@
         compiler_params=pltpu.CompilerParams(vmem_limit_bytes=8 * MIB),
         name="fix",
     )(
-        other, far, near, fluxes, outward, in_vmem(forward), in_vmem(first), in_vmem(table), *outer
+        other, near, far, fluxes, outward, in_vmem(forward), in_vmem(first), in_vmem(table), *outer
     )
 
 
@@ -511,11 +511,13 @@
 
 
 def prepare_kernel(
-    rounds, temp, w_vel, forward, table, changes, fluxes, other, *rest
+    rounds, temp, w_vel, forward, table, changes, fluxes, other, crossing, *rest
 ):
-    outer, rest = (rest[0], rest[1:]) if rounds > 2 else (None, rest)
+    outer = crossing if rounds > 2 else None
     bases, gains = rest[: rounds - 1], rest[rounds - 1 : 2 * rounds - 2]
-    known, response, below_in, above_in = rest[2 * rounds - 2 :]
+    known, response, *passed, below_in, above_in = rest[2 * rounds - 2 :]
+    if passed:
+        passed[0][...] = crossing[pl.ds(0, passed[0].shape[0]), :]
     levels, rows, cols = temp.shape
     upper = bit_of("gz", rounds - 1) == 1
     one, none = jnp.ones((1, cols), F32), jnp.zeros((1, cols), F32)
@@ -584,13 +586,15 @@
         lax.fori_loop(0, levels - 1, step, carry, unroll=3)
 
 
-def prepare(rounds, temp, w_vel, forward, table, changes, fluxes, other, outer, bases, gains):
+def prepare(rounds, temp, w_vel, forward, table, changes, fluxes, other, crossing, bases, gains):
     levels, rows, cols = temp.shape
+    shapes = (held(2, levels, rows, cols), held(levels, TILE, cols))
+    shapes += (held(rows, cols),) * (rounds == 2)
     return pl.pallas_call(
         functools.partial(prepare_kernel, rounds),
-        out_shape=(held(2, levels, rows, cols), held(levels, TILE, cols)),
-        in_specs=[whole(VMEM)] * (7 + len(outer) + 2 * (rounds - 1)),
-        out_specs=[whole(VMEM)] * 2,
+        out_shape=shapes,
+        in_specs=[whole(VMEM)] * (8 + 2 * (rounds - 1)),
+        out_specs=[whole(VMEM)] * len(shapes),
         scratch_shapes=[pltpu.VMEM((2, rows, cols), F32)] * 2,
         compiler_params=pltpu.CompilerParams(vmem_limit_bytes=8 * MIB),
         cost_estimate=pl.CostEstimate(
@@ -601,7 +605,7 @@
         name="prepare",
     )(
         in_vmem(temp), in_vmem(w_vel), in_vmem(forward), in_vmem(table), changes, fluxes, other,
-        *outer, *bases, *gains,
+        crossing, *bases, *gains,
     )
 
 
@@ -619,9 +623,7 @@
         at = pl.ds(field * size, size)
         into = scale * theirs[at, :] + to_other * mine[at, :]
         if late:
-            flux = other[at, :]
-            into = into + (own_gain * own[at, :] + other_gain * flux)
-            joined[pl.ds((2 + field) * size, size), :] = flux
+            into = into + (own_gain * own[at, :] + other_gain * other[at, :])
         joined[at, :] = into
 
 
@@ -629,7 +631,7 @@
     size, cols = theirs.shape
     return pl.pallas_call(
         functools.partial(join_kernel, rounds, late, own.shape[0] - TILE, other.shape[0] - TILE),
-        out_shape=held(size * (2 if late else 1), cols),
+        out_shape=held(size, cols),
         in_specs=[whole(VMEM)] * 4,
         out_specs=whole(VMEM),
         compiler_params=pltpu.CompilerParams(vmem_limit_bytes=8 * MIB),
@@ -639,8 +641,8 @@
 
 def finish_kernel(rounds, swapped, known, response, joined, *rest):
     late, results = rounds == 2, 4 if rounds == 2 else 2
-    table, tend, far, near = rest[:4] if late else (None,) * 4
-    rest = rest[(4 if late else 0) + (results if swapped else results - 2) :]
+    flux_in, table, tend, far, near = rest[:5] if late else (None,) * 5
+    rest = rest[(5 if late else 0) + (results if swapped else results - 2) :]
     outs, (result, rim, sems) = rest[:results], rest[results:]
     _, levels, rows, cols = known.shape
     width, half = 2 * TILE, rows // 2
@@ -665,7 +667,7 @@
                 for diff in diffs
             )
             edge = jnp.where(row_at == 0, head, jnp.where(row_at == rows - 1, tail, 0.0))
-            flux = joined[pl.ds((2 + field) * half, half), :]
+            flux = flux_in[pl.ds(field * half, half), :]
             rim[field] = tend[field, level, pl.ds(start, half), :] + gain * flux + edge
             copies.append(
                 pltpu.make_async_copy(
@@ -742,15 +744,15 @@
         temp, u_vel, w_vel, v_vel, temp_prev, w_prev, lower, upper, metric
     )
     other = lax.ppermute(fluxes, "gz", cores)
+    near = lax.ppermute(near, "gx", both_ways([(i, i + 1) for i in range(0, across, 2)]))
     far = lax.ppermute(far, "gx", both_ways([(i, (i + 1) % across) for i in range(1, across, 2)]))
-    near = lax.ppermute(near, "gx", both_ways([(i, i + 1) for i in range(0, across, 2)]))
     outer = ()
     if rounds > 2:
         seams = both_ways([(i, i + 1) for i in range(1, stacked - 1, 2)])
         outer = (lax.ppermute(outward, "gz", seams),)
     forward, tend, first = bulk(other, table, temp, u_vel, v_vel, w_vel, temp_prev, w_prev)
     entries, changes, *late = fix(
-        rounds, other, far, near, fluxes, outward, forward, first, table, outer
+        rounds, other, near, far, fluxes, outward, forward, first, table, outer
     )
     message, seam = late if late else (entries, fluxes)
     bases, gains, own, other_own = [], [], fluxes, other
@@ -768,16 +770,20 @@
     partners = [(i, i ^ (stacked // 2)) for i in range(stacked)]
     theirs = lax.ppermute(message, "gz", partners)
     other_own = lax.ppermute(own, "gz", partners)
-    known, response = prepare(
-        rounds, temp, w_vel, forward, table, changes, fluxes, other, outer, bases, gains
+    known, response, *passed = prepare(
+        rounds, temp, w_vel, forward, table, changes, fluxes, other, *(outer or (other_own,)),
+        bases, gains,
     )
     tendencies = tends(rounds, table, tend, far, near, other, outer)
     joined = join(rounds, bool(late), message, theirs, own, other_own)
     swapped = lax.ppermute(joined, "gz", cores)
-    late = (table, tend, far, near) if late else ()
-    written = finish(rounds, known, response, joined, late, tendencies if late else ())
-    written = finish(rounds, known, response, swapped, late, written)
-    return tuple(written) if late else (*written, *tendencies)
+    if not late:
+        written = finish(rounds, known, response, joined, (), ())
+        return *finish(rounds, known, response, swapped, (), written), *tendencies
+    crossed = lax.ppermute(passed[0], "gz", cores)
+    late = (table, tend, far, near)
+    written = finish(rounds, known, response, joined, (other_own, *late), tendencies)
+    return tuple(finish(rounds, known, response, swapped, (crossed, *late), written))
 
 
 def solution(mesh):

time: 21.4 us -> 20.9 us (0.977)
  waiting for transfers between devices: 2.21 us -> 1.17 us
  starting transfers between devices: 9.27 us -> 9.88 us
    ppermute x1, starting transfers between devices: 0.01 us -> 2.59 us  [local(): lax.ppermute(near, 'gx', both_ways([(i, i + 1) for i in range(0, across,...]
    ppermute x1, starting transfers between devices: 5.63 us -> 3.54 us  [local(): lax.ppermute(far, 'gx', both_ways([(i, (i + 1) % across) for i in range(1...]
    ppermute x1, waiting for transfers between devices: 0.96 us -> 0.01 us  [local(): lax.ppermute(near, 'gx', both_ways([(i, i + 1) for i in range(0, across,...]
    ppermute x2, waiting for transfers between devices: 1.01 us -> 0.46 us  [local(): theirs = lax.ppermute(message, 'gz', partners)]
    ppermute x1, waiting for transfers between devices: 0.01 us -> 0.44 us  [local(): other_own = lax.ppermute(own, 'gz', partners)]
  transfers between devices with their start and end apart: 7 -> 8, of which waited for: 3 -> 4; matrix products, arithmetic and copies ran while one was open for 0% -> 0% of each run, Pallas kernels for 28% -> 29%
where the time goes in v7:
time: 20.9 us; the launch traced here: 20.8 us
  starting transfers between devices  9.88 us (47%)
  Pallas kernels  8.91 us (43%)
  waiting for transfers between devices  1.17 us (6%)
  between operations  0.8 us (4%)
    ppermute x1, starting transfers between devices, local(): lax.ppermute(far, 'gx', both_ways([(i, (i + 1) % across) for i in range(1...  3.54 us
    pallas_call x1, Pallas kernels, bulk(): pl.pallas_call(bulk_kernel, out_shape=(held(2, levels + 1, rows, cols), h...  2.86 us
    ppermute x1, starting transfers between devices, local(): lax.ppermute(near, 'gx', both_ways([(i, i + 1) for i in range(0, across,...  2.59 us
    pallas_call x2, Pallas kernels, finish(): pl.pallas_call(functools.partial(finish_kernel, rounds, swapped), out_sha...  2.16 us
    pallas_call x1, Pallas kernels, edges(): pl.pallas_call(edges_kernel, out_shape=(held(2 * levels, cols), held(2 *...  1.59 us
    ppermute x1, starting transfers between devices, local(): other_own = lax.ppermute(own, 'gz', partners)  1.56 us
    ppermute x2, starting transfers between devices, local(): theirs = lax.ppermute(message, 'gz', partners)  1.5 us
    pallas_call x1, Pallas kernels, tends(): pl.pallas_call(functools.partial(tends_kernel, rounds), out_shape=(jax.Sh...  1.38 us
  transfers between devices with their start and end apart: 8, of which 4 were waited for; matrix products, arithmetic and copies ran while one was open for 0% of the time, Pallas kernels for 29%

profile of v7, /device:TPU:0, one launch (start us, length us, event | category | flops | bytes accessed | tf_op | source)
XLA Modules:
  0.0 20.8 jit_solution(646484338560561720)
XLA Ops:
  0.7 1.6 %edges.1 = (f32[32,256]{1,0:T(8,128)S(1)}, f32[32,256]{1,0:T(8,128)S(1)}, f32[200,256]{1,0:T(8,128)S(1)}, f32[128,256]{1,0:T(8,128)S(1)}, f32[16,8,256]{2,1,0:T(8,128)S(1)}) custom-call(f32[16,64,256]{2,1,0:T(8,128)} %temp.5, f32[16,64,256]{2,1,0:T(8,128)} %u_vel.3, f32[16,64,256]{2,1,0:T(8,128)} %w_vel.5, f32[16,64,256]{2,1,0:T(8,128)} %v_vel.3, ...), custom_call_target="tpu_custom_call" | custom-call | tf_op jit(solution)/shard_map/edges/pallas_call | solution.py:108
  2.3 0.5 %collective-permute-start = (f32[200,256]{1,0:T(8,128)S(1)}, f32[200,256]{1,0:T(8,128)S(1)}, u32[]{:S(2)}, u32[]{:S(2)}) collective-permute-start(f32[200,256]{1,0:T(8,128)S(1)} %get-tuple-element.28.fluxes.own), channel_id=1, source_target_pairs={{0,1},{2,3},{1,0},{3,2},{4,5},{6,7},{5,4},{7,6},{8,9},{10,11},{9,8... | collective-permute-start | bytes 614408 | tf_op jit(solution)/shard_map/ppermute | solution.py:746
  2.8 2.6 %collective-permute-start.1 = (f32[32,256]{1,0:T(8,128)S(1)}, f32[32,256]{1,0:T(8,128)S(1)}, u32[]{:S(2)}, u32[]{:S(2)}) collective-permute-start(f32[32,256]{1,0:T(8,128)S(1)} %get-tuple-element.31), channel_id=1, source_target_pairs={{0,4},{8,12},{16,20},{24,28},{4,0},{12,8},{20,16},{28,24},{1,5},{9... | collective-permute-start | bytes 98312 | tf_op jit(solution)/shard_map/ppermute | solution.py:747
  5.4 3.5 %collective-permute-start.2 = (f32[32,256]{1,0:T(8,128)S(1)}, f32[32,256]{1,0:T(8,128)S(1)}, u32[]{:S(2)}, u32[]{:S(2)}) collective-permute-start(f32[32,256]{1,0:T(8,128)S(1)} %get-tuple-element.32), channel_id=1, source_target_pairs={{4,8},{12,16},{20,24},{28,0},{8,4},{16,12},{24,20},{0,28},{5,9},{1... | collective-permute-start | bytes 98312 | tf_op jit(solution)/shard_map/ppermute | solution.py:748
  8.9 0.0 collective-permute-done.arrived.other
  9.0 2.9 %bulk.1 = (f32[2,17,64,256]{3,2,1,0:T(8,128)S(1)}, f32[2,16,64,256]{3,2,1,0:T(8,128)S(1)}, f32[2,64,256]{2,1,0:T(8,128)S(1)}) custom-call(f32[200,256]{1,0:T(8,128)S(1)} %collective-permute-done.arrived.other, f32[16,8,256]{2,1,0:T(8,128)S(1)} %get-tuple-element.29.table.rest_1_, f32[16,64,256]{2,1,0:T(8,128)S(1)} %copy-done, f32[16,64,256]{2,1,0:T(8,128)S(1)} %copy-done.2, ...), custom_call_target="tpu_custom_call" | custom-call | flops 26214400000 | bytes 6291456 | tf_op jit(solution)/shard_map/bulk/pallas_call | solution.py:246
  11.9 0.0 collective-permute-done.1.near.rest_4_
  11.9 0.1 collective-permute-done.2.far.rest_3_
  12.0 0.2 fix.1
  12.2 0.1 collective-permute-start.4
  12.2 1.6 %collective-permute-start.3 = (f32[72,256]{1,0:T(8,128)S(1)}, f32[72,256]{1,0:T(8,128)S(1)}, u32[]{:S(2)}, u32[]{:S(2)}) collective-permute-start(f32[72,256]{1,0:T(8,128)S(1)} %get-tuple-element.36.own), channel_id=1, source_target_pairs={{0,2},{1,3},{2,0},{3,1},{4,6},{5,7},{6,4},{7,5},{8,10},{9,11},{10,... | collective-permute-start | bytes 221192 | tf_op jit(solution)/shard_map/ppermute | solution.py:772
  13.8 0.0 collective-permute-done.4.theirs
  13.8 0.1 merge.1
  13.9 1.4 %collective-permute-start.5 = (f32[64,256]{1,0:T(8,128)S(1)}, f32[64,256]{1,0:T(8,128)S(1)}, u32[]{:S(2)}, u32[]{:S(2)}) collective-permute-start(f32[64,256]{1,0:T(8,128)S(1)} %get-tuple-element.43.mine), channel_id=1, source_target_pairs={{0,2},{1,3},{2,0},{3,1},{4,6},{5,7},{6,4},{7,5},{8,10},{9,11},{10,... | collective-permute-start | bytes 196616 | tf_op jit(solution)/shard_map/ppermute | solution.py:771
  15.3 1.4 %tends.1 = (f32[16,64,256]{2,1,0:T(8,128)}, f32[16,64,256]{2,1,0:T(8,128)}) custom-call(f32[16,8,256]{2,1,0:T(8,128)S(1)} %get-tuple-element.29.table.rest_1_, f32[2,16,64,256]{3,2,1,0:T(8,128)S(1)} %get-tuple-element.45.tend.rest_2_, f32[32,256]{1,0:T(8,128)S(1)} %collective-permute-done.2.far.rest_3_, f32[32,256]{1,0:T(8,128)S(1)} %collective-permute-done.1.near.rest_4_, ...), custom_call_target="tpu_custom_call" | custom-call | flops 262144 | bytes 2097152 | tf_op jit(solution)/shard_map/tends/pallas_call | solution.py:428
  16.7 0.4 %collective-permute-done.3.crossing.other.rest_0_ = f32[72,256]{1,0:T(8,128)S(1)} collective-permute-done((f32[72,256]{1,0:T(8,128)S(1)}, f32[72,256]{1,0:T(8,128)S(1)}, u32[]{:S(2)}, u32[]{:S(2)}) %collective-permute-start.3) | collective-permute-done | bytes 73760 | tf_op jit(solution)/shard_map/ppermute | solution.py:772
  17.2 0.6 %prepare.1 = (f32[2,16,64,256]{3,2,1,0:T(8,128)S(1)}, f32[16,8,256]{2,1,0:T(8,128)S(1)}, f32[64,256]{1,0:T(8,128)S(1)}) custom-call(f32[16,64,256]{2,1,0:T(8,128)S(1)} %copy-done, f32[16,64,256]{2,1,0:T(8,128)S(1)} %copy-done.1, f32[2,17,64,256]{3,2,1,0:T(8,128)S(1)} %get-tuple-element.30.forward, f32[16,8,256]{2,1,0:T(8,128)S(1)} %get-tuple-element.29.table.rest_1_, ...), custom_call_target="tpu_custom_call" | custom-call | flops 262144 | bytes 6291456 | tf_op jit(solution)/shard_map/prepare/pallas_call | solution.py:593
  17.8 0.1 collective-permute-start.7
  17.9 0.5 %collective-permute-done.5.theirs = f32[64,256]{1,0:T(8,128)S(1)} collective-permute-done((f32[64,256]{1,0:T(8,128)S(1)}, f32[64,256]{1,0:T(8,128)S(1)}, u32[]{:S(2)}, u32[]{:S(2)}) %collective-permute-start.5) | collective-permute-done | bytes 65568 | tf_op jit(solution)/shard_map/ppermute | solution.py:771
  18.4 0.1 collective-permute-start.6
  18.5 1.1 %finish.2 = (f32[16,64,256]{2,1,0:T(8,128)}, f32[16,64,256]{2,1,0:T(8,128)}, f32[16,64,256]{2,1,0:T(8,128)}, f32[16,64,256]{2,1,0:T(8,128)}) custom-call(f32[2,16,64,256]{3,2,1,0:T(8,128)S(1)} %get-tuple-element.41.known, f32[16,8,256]{2,1,0:T(8,128)S(1)} %get-tuple-element.42.response, ...), custom_call_target="tpu_custom_call", output_to_operand_aliasing={{2}: (8, {}), {3}: (9, {})} | custom-call | flops 5242880000 | bytes 2097152 | tf_op jit(solution)/shard_map/finish/pallas_call | solution.py:711
  19.6 0.0 collective-permute-done.7.rest_0_
  19.6 0.1 collective-permute-done.6.joined
  19.7 1.1 %finish.3 = (f32[16,64,256]{2,1,0:T(8,128)}, f32[16,64,256]{2,1,0:T(8,128)}, f32[16,64,256]{2,1,0:T(8,128)}, f32[16,64,256]{2,1,0:T(8,128)}) custom-call(f32[2,16,64,256]{3,2,1,0:T(8,128)S(1)} %get-tuple-element.41.known, f32[16,8,256]{2,1,0:T(8,128)S(1)} %get-tuple-element.42.response, ...), custom_call_target="tpu_custom_call", output_to_operand_aliasing={{0}: (8, {}), {1}: (9, {}), {2}: (10, {}), {3}: (11, {})} | custom-call | flops 5242880000 | bytes 2097152 | tf_op jit(solution)/shard_map/finish/pallas_call | solution.py:711
  (13 shorter events, 0.1 us)
Async XLA Ops:
  0.6 8.3 %copy-start.1 = (f32[16,64,256]{2,1,0:T(8,128)S(1)}, f32[16,64,256]{2,1,0:T(8,128)}, u32[]{:S(2)}) copy-start(f32[16,64,256]{2,1,0:T(8,128)} %w_vel.5) | copy-start | bytes 3145732
  0.6 8.3 %copy-start = (f32[16,64,256]{2,1,0:T(8,128)S(1)}, f32[16,64,256]{2,1,0:T(8,128)}, u32[]{:S(2)}) copy-start(f32[16,64,256]{2,1,0:T(8,128)} %temp.5) | copy-start | bytes 3145732
  0.7 8.3 %copy-start.5 = (f32[16,64,256]{2,1,0:T(8,128)S(1)}, f32[16,64,256]{2,1,0:T(8,128)}, u32[]{:S(2)}) copy-start(f32[16,64,256]{2,1,0:T(8,128)} %w_prev.3) | copy-start | bytes 3145732
  0.7 8.3 %copy-start.4 = (f32[16,64,256]{2,1,0:T(8,128)S(1)}, f32[16,64,256]{2,1,0:T(8,128)}, u32[]{:S(2)}) copy-start(f32[16,64,256]{2,1,0:T(8,128)} %temp_prev.3) | copy-start | bytes 3145732
  0.7 8.3 %copy-start.3 = (f32[16,64,256]{2,1,0:T(8,128)S(1)}, f32[16,64,256]{2,1,0:T(8,128)}, u32[]{:S(2)}) copy-start(f32[16,64,256]{2,1,0:T(8,128)} %v_vel.3) | copy-start | bytes 3145732
  0.7 8.3 %copy-start.2 = (f32[16,64,256]{2,1,0:T(8,128)S(1)}, f32[16,64,256]{2,1,0:T(8,128)}, u32[]{:S(2)}) copy-start(f32[16,64,256]{2,1,0:T(8,128)} %u_vel.3) | copy-start | bytes 3145732
  2.3 6.7 %collective-permute-start = (f32[200,256]{1,0:T(8,128)S(1)}, f32[200,256]{1,0:T(8,128)S(1)}, u32[]{:S(2)}, u32[]{:S(2)}) collective-permute-start(f32[200,256]{1,0:T(8,128)S(1)} %get-tuple-element.28.fluxes.own), channel_id=1, source_target_pairs={{0,1},{2,3},{1,0},{3,2},{4,5},{6,7},{5,4},{7,6},{8,9},{10,11},{9,8... | collective-permute-start | bytes 614408 | tf_op jit(solution)/shard_map/ppermute | solution.py:746
  2.8 9.1 %collective-permute-start.1 = (f32[32,256]{1,0:T(8,128)S(1)}, f32[32,256]{1,0:T(8,128)S(1)}, u32[]{:S(2)}, u32[]{:S(2)}) collective-permute-start(f32[32,256]{1,0:T(8,128)S(1)} %get-tuple-element.31), channel_id=1, source_target_pairs={{0,4},{8,12},{16,20},{24,28},{4,0},{12,8},{20,16},{28,24},{1,5},{9... | collective-permute-start | bytes 98312 | tf_op jit(solution)/shard_map/ppermute | solution.py:747
  5.4 6.6 %collective-permute-start.2 = (f32[32,256]{1,0:T(8,128)S(1)}, f32[32,256]{1,0:T(8,128)S(1)}, u32[]{:S(2)}, u32[]{:S(2)}) collective-permute-start(f32[32,256]{1,0:T(8,128)S(1)} %get-tuple-element.32), channel_id=1, source_target_pairs={{4,8},{12,16},{20,24},{28,0},{8,4},{16,12},{24,20},{0,28},{5,9},{1... | collective-permute-start | bytes 98312 | tf_op jit(solution)/shard_map/ppermute | solution.py:748
  12.2 1.6 %collective-permute-start.4 = (f32[192,256]{1,0:T(8,128)S(1)}, f32[192,256]{1,0:T(8,128)S(1)}, u32[]{:S(2)}, u32[]{:S(2)}) collective-permute-start(f32[192,256]{1,0:T(8,128)S(1)} %get-tuple-element.38), channel_id=1, source_target_pairs={{0,1},{1,0},{2,3},{3,2},{4,5},{5,4},{6,7},{7,6},{8,9},{9,8},{10,11... | collective-permute-start | bytes 589832 | tf_op jit(solution)/shard_map/ppermute | solution.py:761
  12.2 4.9 %collective-permute-start.3 = (f32[72,256]{1,0:T(8,128)S(1)}, f32[72,256]{1,0:T(8,128)S(1)}, u32[]{:S(2)}, u32[]{:S(2)}) collective-permute-start(f32[72,256]{1,0:T(8,128)S(1)} %get-tuple-element.36.own), channel_id=1, source_target_pairs={{0,2},{1,3},{2,0},{3,1},{4,6},{5,7},{6,4},{7,5},{8,10},{9,11},{10,... | collective-permute-start | bytes 221192 | tf_op jit(solution)/shard_map/ppermute | solution.py:772
  13.9 4.4 %collective-permute-start.5 = (f32[64,256]{1,0:T(8,128)S(1)}, f32[64,256]{1,0:T(8,128)S(1)}, u32[]{:S(2)}, u32[]{:S(2)}) collective-permute-start(f32[64,256]{1,0:T(8,128)S(1)} %get-tuple-element.43.mine), channel_id=1, source_target_pairs={{0,2},{1,3},{2,0},{3,1},{4,6},{5,7},{6,4},{7,5},{8,10},{9,11},{10,... | collective-permute-start | bytes 196616 | tf_op jit(solution)/shard_map/ppermute | solution.py:771
  17.8 1.8 %collective-permute-start.7 = (f32[64,256]{1,0:T(8,128)S(1)}, f32[64,256]{1,0:T(8,128)S(1)}, u32[]{:S(2)}, u32[]{:S(2)}) collective-permute-start(f32[64,256]{1,0:T(8,128)S(1)} %get-tuple-element.44), channel_id=1, source_target_pairs={{0,1},{2,3},{1,0},{3,2},{4,5},{6,7},{5,4},{7,6},{8,9},{10,11},{9,8... | collective-permute-start | bytes 196616 | tf_op jit(solution)/shard_map/ppermute | solution.py:783
  18.4 1.3 %collective-permute-start.6 = (f32[64,256]{1,0:T(8,128)S(1)}, f32[64,256]{1,0:T(8,128)S(1)}, u32[]{:S(2)}, u32[]{:S(2)}) collective-permute-start(f32[64,256]{1,0:T(8,128)S(1)} %join.1.joined), channel_id=1, source_target_pairs={{0,1},{2,3},{1,0},{3,2},{4,5},{6,7},{5,4},{7,6},{8,9},{10,11},{9,8... | collective-permute-start | bytes 196616 | tf_op jit(solution)/shard_map/ppermute | solution.py:779

commit v8 on v7

--- a/solution.py
+++ b/solution.py
@@ -67,8 +67,8 @@
     levels, rows, cols = temp.shape
     copies = [(lower, lower_at), (upper, upper_at), (metric, metric_at)]
     for at, array in enumerate((temp, w_vel, u_vel)):
-        for side, first in enumerate((0, rows - TILE)):
-            copies.append((array.at[:, pl.ds(first, TILE), :], strips.at[at, side]))
+        for side, row in enumerate((0, rows - 1)):
+            copies.append((array.at[:, row, :], strips.at[at, side]))
     for at, array in enumerate((temp, w_vel)):
         for side, level in enumerate((0, levels - 1)):
             copies.append((array.at[level], layers.at[at, side]))
@@ -81,11 +81,10 @@
     for copy in copies[3:]:
         copy.wait()
     odd = bit_of("gx", 0) == 1
-    last = TILE - 1
     for field in range(2):
         at = pl.ds(field * levels, levels)
-        to_left = (HORIZ_DIFF - 0.5 * strips[2, 0, :, 0, :]) * strips[field, 0, :, 0, :]
-        to_right = (HORIZ_DIFF + 0.5 * strips[2, 1, :, last, :]) * strips[field, 1, :, last, :]
+        to_left = (HORIZ_DIFF - 0.5 * strips[2, 0]) * strips[field, 0]
+        to_right = (HORIZ_DIFF + 0.5 * strips[2, 1]) * strips[field, 1]
         near[at, :] = jnp.where(odd, to_left, to_right)
         far[at, :] = jnp.where(odd, to_right, to_left)
     position = lax.axis_index("gz")
@@ -117,7 +116,7 @@
         in_specs=[whole(pl.ANY)] * 9,
         out_specs=[whole(VMEM)] * 5,
         scratch_shapes=[
-            pltpu.VMEM((3, 2, levels, TILE, cols), F32),
+            pltpu.VMEM((3, 2, levels, cols), F32),
             pltpu.VMEM((2, 2, rows, cols), F32),
             pltpu.SMEM((levels,), F32),
             pltpu.SMEM((levels,), F32),
@@ -190,55 +189,67 @@
     row_at = lax.broadcasted_iota(jnp.int32, (TILE, cols), 0)
     zero = jnp.zeros((TILE, cols), F32)
 
-    def level_step(level, carry):
-        def spread(at):
+    def sides(level, strip):
+        at = pl.ds(strip * TILE, TILE)
+        half = 0.5 * u_vel[level, at, :]
+        back, ahead = HORIZ_DIFF - half, HORIZ_DIFF + half
+        here = [values[level, at, :] for values in fields]
+        return (
+            here,
+            [pltpu.roll(back * value, TILE - 1, 0) for value in here],
+            [pltpu.roll(ahead * value, 1, 0) for value in here],
+        )
+
+    def pair_step(pair, carry):
+        both = (2 * pair, 2 * pair + 1)
+        under, over = jnp.maximum(both[0] - 1, 0), jnp.minimum(both[1] + 1, levels - 1)
+
+        def spread(level, at):
             return jnp.broadcast_to(table[level, pl.ds(at, 1), :], (TILE, cols))
 
-        pivot, lower_pivot, green = spread(PIVOT_NEW), spread(LOWER_PIVOT), spread(FIRST_GREEN)
-        rise, fall = spread(RISE), spread(FALL)
-        over = jnp.minimum(level + 1, levels - 1)
-        under = jnp.maximum(level - 1, 0)
-
-        def sides(strip):
+        factors = [
+            [spread(level, at) for at in (PIVOT_NEW, LOWER_PIVOT, FIRST_GREEN, RISE, FALL)]
+            for level in both
+        ]
+        before = [[zero, zero], [zero, zero]]
+        now = [sides(level, 0) for level in both]
+        for strip in range(strips):
+            none = (None, [zero, zero], None)
+            later = [sides(level, strip + 1) if strip + 1 < strips else none for level in both]
             at = pl.ds(strip * TILE, TILE)
-            half = 0.5 * u_vel[level, at, :]
-            back, ahead = HORIZ_DIFF - half, HORIZ_DIFF + half
-            here = [values[level, at, :] for values in fields]
-            return (
-                here,
-                [pltpu.roll(back * value, TILE - 1, 0) for value in here],
-                [pltpu.roll(ahead * value, 1, 0) for value in here],
-            )
-
-        before = [zero, zero]
-        here, back, ahead = sides(0)
-        for strip in range(strips):
-            after = sides(strip + 1) if strip + 1 < strips else (None, [zero, zero], None)
-            at = pl.ds(strip * TILE, TILE)
-            half = 0.5 * v_vel[level, at, :]
-            v_back, v_ahead = HORIZ_DIFF - half, HORIZ_DIFF + half
-            w_over = rise * w_vel[over, at, :]
-            w_under = fall * w_vel[under, at, :]
+            beneath = [values[under, at, :] for values in fields]
+            above = [values[over, at, :] for values in fields]
+            solved = [forward[field, both[0], at, :] for field in range(2)]
+            total = [first[field, at, :] for field in range(2)]
+            for i, level in enumerate(both):
+                here, back, ahead = now[i]
+                pivot, lower_pivot, green, rise, fall = factors[i]
+                upward = above if i else now[1][0]
+                downward = now[0][0] if i else beneath
+                half = 0.5 * v_vel[level, at, :]
+                v_back, v_ahead = HORIZ_DIFF - half, HORIZ_DIFF + half
+                w_over, w_under = rise * upward[1], fall * downward[1]
+                for field in range(2):
+                    value = here[field]
+                    change = jnp.where(row_at == TILE - 1, later[i][1][field], back[field])
+                    change = change + jnp.where(row_at == 0, before[i][field], ahead[field])
+                    change = change + pltpu.roll(v_back * value, cols - 1, 1)
+                    change = change + pltpu.roll(v_ahead * value, 1, 1)
+                    change = change - w_over * upward[field] + w_under * downward[field]
+                    change = change + (here[1 - field] - (4.0 * HORIZ_DIFF) * value)
+                    tend[field, level, at, :] = change
+                    old = prevs[field][level, at, :]
+                    right = change + (FIELD_WEIGHT * value - PREV_WEIGHT * old)
+                    solved[field] = pivot * right + lower_pivot * solved[field]
+                    forward[field, level + 1, at, :] = solved[field]
+                    total[field] = total[field] + green * right
             for field in range(2):
-                value = here[field]
-                change = jnp.where(row_at == TILE - 1, after[1][field], back[field])
-                change = change + jnp.where(row_at == 0, before[field], ahead[field])
-                change = change + pltpu.roll(v_back * value, cols - 1, 1)
-                change = change + pltpu.roll(v_ahead * value, 1, 1)
-                change = change - w_over * fields[field][over, at, :]
-                change = change + w_under * fields[field][under, at, :]
-                change = change + (here[1 - field] - (4.0 * HORIZ_DIFF) * value)
-                tend[field, level, at, :] = change
-                right = change + (FIELD_WEIGHT * value - PREV_WEIGHT * prevs[field][level, at, :])
-                forward[field, level + 1, at, :] = (
-                    pivot * right + lower_pivot * forward[field, level, at, :]
-                )
-                first[field, at, :] = first[field, at, :] + green * right
-            before = ahead
-            here, back, ahead = after
+                first[field, at, :] = total[field]
+            before = [now[0][2], now[1][2]]
+            now = later
         return carry
 
-    lax.fori_loop(0, levels, level_step, 0)
+    lax.fori_loop(0, levels // 2, pair_step, 0)
 
 
 def bulk(arrived, table, *arrays):
@@ -690,7 +701,7 @@
                     result[field, level, pl.ds(at, TILE), :] = value
                 return carry
 
-            lax.fori_loop(0, levels, step, 0, unroll=4)
+            lax.fori_loop(0, levels, step, 0, unroll=True)
             copies.append(
                 pltpu.make_async_copy(
                     result.at[field, :, pl.ds(begin, width), :],

time: 20.9 us -> 20.6 us (0.986)
  Pallas kernels: 8.91 us -> 8.51 us
    pallas_call x1, Pallas kernels: 1.59 us -> 1.31 us  [edges(): pl.pallas_call(edges_kernel, out_shape=(held(2 * levels, cols), held(2 *...]
where the time goes in v8:
time: 20.6 us; the launch traced here: 20.5 us
  starting transfers between devices  9.88 us (48%)
  Pallas kernels  8.51 us (41%)
  waiting for transfers between devices  1.27 us (6%)
  between operations  0.8 us (4%)
    ppermute x1, starting transfers between devices, local(): lax.ppermute(far, 'gx', both_ways([(i, (i + 1) % across) for i in range(1...  3.54 us
    pallas_call x1, Pallas kernels, bulk(): pl.pallas_call(bulk_kernel, out_shape=(held(2, levels + 1, rows, cols), h...  2.76 us
    ppermute x1, starting transfers between devices, local(): lax.ppermute(near, 'gx', both_ways([(i, i + 1) for i in range(0, across,...  2.59 us
    pallas_call x2, Pallas kernels, finish(): pl.pallas_call(functools.partial(finish_kernel, rounds, swapped), out_sha...  2.14 us
    ppermute x1, starting transfers between devices, local(): other_own = lax.ppermute(own, 'gz', partners)  1.56 us
    ppermute x2, starting transfers between devices, local(): theirs = lax.ppermute(message, 'gz', partners)  1.5 us
    pallas_call x1, Pallas kernels, tends(): pl.pallas_call(functools.partial(tends_kernel, rounds), out_shape=(jax.Sh...  1.38 us
    pallas_call x1, Pallas kernels, edges(): pl.pallas_call(edges_kernel, out_shape=(held(2 * levels, cols), held(2 *...  1.31 us
  transfers between devices with their start and end apart: 8, of which 4 were waited for; matrix products, arithmetic and copies ran while one was open for 0% of the time, Pallas kernels for 29%

profile of v8, /device:TPU:0, one launch (start us, length us, event | category | flops | bytes accessed | tf_op | source)
XLA Modules:
  0.0 20.5 jit_solution(15301711863388118741)
XLA Ops:
  0.7 1.3 %edges.1 = (f32[32,256]{1,0:T(8,128)S(1)}, f32[32,256]{1,0:T(8,128)S(1)}, f32[200,256]{1,0:T(8,128)S(1)}, f32[128,256]{1,0:T(8,128)S(1)}, f32[16,8,256]{2,1,0:T(8,128)S(1)}) custom-call(f32[16,64,256]{2,1,0:T(8,128)} %temp.5, f32[16,64,256]{2,1,0:T(8,128)} %u_vel.3, f32[16,64,256]{2,1,0:T(8,128)} %w_vel.5, f32[16,64,256]{2,1,0:T(8,128)} %v_vel.3, ...), custom_call_target="tpu_custom_call" | custom-call | tf_op jit(solution)/shard_map/edges/pallas_call | solution.py:107
  2.0 0.5 %collective-permute-start = (f32[200,256]{1,0:T(8,128)S(1)}, f32[200,256]{1,0:T(8,128)S(1)}, u32[]{:S(2)}, u32[]{:S(2)}) collective-permute-start(f32[200,256]{1,0:T(8,128)S(1)} %get-tuple-element.28.fluxes.own), channel_id=1, source_target_pairs={{0,1},{2,3},{1,0},{3,2},{4,5},{6,7},{5,4},{7,6},{8,9},{10,11},{9,8... | collective-permute-start | bytes 614408 | tf_op jit(solution)/shard_map/ppermute | solution.py:757
  2.5 2.6 %collective-permute-start.1 = (f32[32,256]{1,0:T(8,128)S(1)}, f32[32,256]{1,0:T(8,128)S(1)}, u32[]{:S(2)}, u32[]{:S(2)}) collective-permute-start(f32[32,256]{1,0:T(8,128)S(1)} %get-tuple-element.31), channel_id=1, source_target_pairs={{0,4},{8,12},{16,20},{24,28},{4,0},{12,8},{20,16},{28,24},{1,5},{9... | collective-permute-start | bytes 98312 | tf_op jit(solution)/shard_map/ppermute | solution.py:758
  5.1 3.5 %collective-permute-start.2 = (f32[32,256]{1,0:T(8,128)S(1)}, f32[32,256]{1,0:T(8,128)S(1)}, u32[]{:S(2)}, u32[]{:S(2)}) collective-permute-start(f32[32,256]{1,0:T(8,128)S(1)} %get-tuple-element.32), channel_id=1, source_target_pairs={{4,8},{12,16},{20,24},{28,0},{8,4},{16,12},{24,20},{0,28},{5,9},{1... | collective-permute-start | bytes 98312 | tf_op jit(solution)/shard_map/ppermute | solution.py:759
  8.7 0.0 collective-permute-done.arrived.other
  8.7 2.8 %bulk.1 = (f32[2,17,64,256]{3,2,1,0:T(8,128)S(1)}, f32[2,16,64,256]{3,2,1,0:T(8,128)S(1)}, f32[2,64,256]{2,1,0:T(8,128)S(1)}) custom-call(f32[200,256]{1,0:T(8,128)S(1)} %collective-permute-done.arrived.other, f32[16,8,256]{2,1,0:T(8,128)S(1)} %get-tuple-element.29.table.rest_1_, f32[16,64,256]{2,1,0:T(8,128)S(1)} %copy-done, f32[16,64,256]{2,1,0:T(8,128)S(1)} %copy-done.2, ...), custom_call_target="tpu_custom_call" | custom-call | flops 26214400000 | bytes 6291456 | tf_op jit(solution)/shard_map/bulk/pallas_call | solution.py:257
  11.5 0.0 collective-permute-done.1.near.rest_4_
  11.5 0.2 %collective-permute-done.2.far.rest_3_ = f32[32,256]{1,0:T(8,128)S(1)} collective-permute-done((f32[32,256]{1,0:T(8,128)S(1)}, f32[32,256]{1,0:T(8,128)S(1)}, u32[]{:S(2)}, u32[]{:S(2)}) %collective-permute-start.2) | collective-permute-done | bytes 32800 | tf_op jit(solution)/shard_map/ppermute | solution.py:759
  11.7 0.2 fix.1
  11.9 0.1 collective-permute-start.4
  12.0 1.6 %collective-permute-start.3 = (f32[72,256]{1,0:T(8,128)S(1)}, f32[72,256]{1,0:T(8,128)S(1)}, u32[]{:S(2)}, u32[]{:S(2)}) collective-permute-start(f32[72,256]{1,0:T(8,128)S(1)} %get-tuple-element.36.own), channel_id=1, source_target_pairs={{0,2},{1,3},{2,0},{3,1},{4,6},{5,7},{6,4},{7,5},{8,10},{9,11},{10,... | collective-permute-start | bytes 221192 | tf_op jit(solution)/shard_map/ppermute | solution.py:783
  13.5 0.0 collective-permute-done.4.theirs
  13.5 0.1 merge.1
  13.6 1.4 %collective-permute-start.5 = (f32[64,256]{1,0:T(8,128)S(1)}, f32[64,256]{1,0:T(8,128)S(1)}, u32[]{:S(2)}, u32[]{:S(2)}) collective-permute-start(f32[64,256]{1,0:T(8,128)S(1)} %get-tuple-element.43.mine), channel_id=1, source_target_pairs={{0,2},{1,3},{2,0},{3,1},{4,6},{5,7},{6,4},{7,5},{8,10},{9,11},{10,... | collective-permute-start | bytes 196616 | tf_op jit(solution)/shard_map/ppermute | solution.py:782
  15.0 1.4 %tends.1 = (f32[16,64,256]{2,1,0:T(8,128)}, f32[16,64,256]{2,1,0:T(8,128)}) custom-call(f32[16,8,256]{2,1,0:T(8,128)S(1)} %get-tuple-element.29.table.rest_1_, f32[2,16,64,256]{3,2,1,0:T(8,128)S(1)} %get-tuple-element.45.tend.rest_2_, f32[32,256]{1,0:T(8,128)S(1)} %collective-permute-done.2.far.rest_3_, f32[32,256]{1,0:T(8,128)S(1)} %collective-permute-done.1.near.rest_4_, ...), custom_call_target="tpu_custom_call" | custom-call | flops 262144 | bytes 2097152 | tf_op jit(solution)/shard_map/tends/pallas_call | solution.py:439
  16.4 0.4 %collective-permute-done.3.crossing.other.rest_0_ = f32[72,256]{1,0:T(8,128)S(1)} collective-permute-done((f32[72,256]{1,0:T(8,128)S(1)}, f32[72,256]{1,0:T(8,128)S(1)}, u32[]{:S(2)}, u32[]{:S(2)}) %collective-permute-start.3) | collective-permute-done | bytes 73760 | tf_op jit(solution)/shard_map/ppermute | solution.py:783
  16.9 0.6 %prepare.1 = (f32[2,16,64,256]{3,2,1,0:T(8,128)S(1)}, f32[16,8,256]{2,1,0:T(8,128)S(1)}, f32[64,256]{1,0:T(8,128)S(1)}) custom-call(f32[16,64,256]{2,1,0:T(8,128)S(1)} %copy-done, f32[16,64,256]{2,1,0:T(8,128)S(1)} %copy-done.1, f32[2,17,64,256]{3,2,1,0:T(8,128)S(1)} %get-tuple-element.30.forward, f32[16,8,256]{2,1,0:T(8,128)S(1)} %get-tuple-element.29.table.rest_1_, ...), custom_call_target="tpu_custom_call" | custom-call | flops 262144 | bytes 6291456 | tf_op jit(solution)/shard_map/prepare/pallas_call | solution.py:604
  17.5 0.1 collective-permute-start.7
  17.6 0.5 %collective-permute-done.5.theirs = f32[64,256]{1,0:T(8,128)S(1)} collective-permute-done((f32[64,256]{1,0:T(8,128)S(1)}, f32[64,256]{1,0:T(8,128)S(1)}, u32[]{:S(2)}, u32[]{:S(2)}) %collective-permute-start.5) | collective-permute-done | bytes 65568 | tf_op jit(solution)/shard_map/ppermute | solution.py:782
  18.1 0.1 collective-permute-start.6
  18.2 1.1 %finish.2 = (f32[16,64,256]{2,1,0:T(8,128)}, f32[16,64,256]{2,1,0:T(8,128)}, f32[16,64,256]{2,1,0:T(8,128)}, f32[16,64,256]{2,1,0:T(8,128)}) custom-call(f32[2,16,64,256]{3,2,1,0:T(8,128)S(1)} %get-tuple-element.41.known, f32[16,8,256]{2,1,0:T(8,128)S(1)} %get-tuple-element.42.response, ...), custom_call_target="tpu_custom_call", output_to_operand_aliasing={{2}: (8, {}), {3}: (9, {})} | custom-call | flops 5242880000 | bytes 2097152 | tf_op jit(solution)/shard_map/finish/pallas_call | solution.py:722
  19.3 0.0 collective-permute-done.7.rest_0_
  19.3 0.1 collective-permute-done.6.joined
  19.4 1.1 %finish.3 = (f32[16,64,256]{2,1,0:T(8,128)}, f32[16,64,256]{2,1,0:T(8,128)}, f32[16,64,256]{2,1,0:T(8,128)}, f32[16,64,256]{2,1,0:T(8,128)}) custom-call(f32[2,16,64,256]{3,2,1,0:T(8,128)S(1)} %get-tuple-element.41.known, f32[16,8,256]{2,1,0:T(8,128)S(1)} %get-tuple-element.42.response, ...), custom_call_target="tpu_custom_call", output_to_operand_aliasing={{0}: (8, {}), {1}: (9, {}), {2}: (10, {}), {3}: (11, {})} | custom-call | flops 5242880000 | bytes 2097152 | tf_op jit(solution)/shard_map/finish/pallas_call | solution.py:722
  (13 shorter events, 0.1 us)
Async XLA Ops:
  0.6 8.0 %copy-start.1 = (f32[16,64,256]{2,1,0:T(8,128)S(1)}, f32[16,64,256]{2,1,0:T(8,128)}, u32[]{:S(2)}) copy-start(f32[16,64,256]{2,1,0:T(8,128)} %w_vel.5) | copy-start | bytes 3145732
  0.6 8.0 %copy-start = (f32[16,64,256]{2,1,0:T(8,128)S(1)}, f32[16,64,256]{2,1,0:T(8,128)}, u32[]{:S(2)}) copy-start(f32[16,64,256]{2,1,0:T(8,128)} %temp.5) | copy-start | bytes 3145732
  0.7 8.0 %copy-start.5 = (f32[16,64,256]{2,1,0:T(8,128)S(1)}, f32[16,64,256]{2,1,0:T(8,128)}, u32[]{:S(2)}) copy-start(f32[16,64,256]{2,1,0:T(8,128)} %w_prev.3) | copy-start | bytes 3145732
  0.7 8.0 %copy-start.4 = (f32[16,64,256]{2,1,0:T(8,128)S(1)}, f32[16,64,256]{2,1,0:T(8,128)}, u32[]{:S(2)}) copy-start(f32[16,64,256]{2,1,0:T(8,128)} %temp_prev.3) | copy-start | bytes 3145732
  0.7 8.0 %copy-start.3 = (f32[16,64,256]{2,1,0:T(8,128)S(1)}, f32[16,64,256]{2,1,0:T(8,128)}, u32[]{:S(2)}) copy-start(f32[16,64,256]{2,1,0:T(8,128)} %v_vel.3) | copy-start | bytes 3145732
  0.7 8.0 %copy-start.2 = (f32[16,64,256]{2,1,0:T(8,128)S(1)}, f32[16,64,256]{2,1,0:T(8,128)}, u32[]{:S(2)}) copy-start(f32[16,64,256]{2,1,0:T(8,128)} %u_vel.3) | copy-start | bytes 3145732
  2.0 6.7 %collective-permute-start = (f32[200,256]{1,0:T(8,128)S(1)}, f32[200,256]{1,0:T(8,128)S(1)}, u32[]{:S(2)}, u32[]{:S(2)}) collective-permute-start(f32[200,256]{1,0:T(8,128)S(1)} %get-tuple-element.28.fluxes.own), channel_id=1, source_target_pairs={{0,1},{2,3},{1,0},{3,2},{4,5},{6,7},{5,4},{7,6},{8,9},{10,11},{9,8... | collective-permute-start | bytes 614408 | tf_op jit(solution)/shard_map/ppermute | solution.py:757
  2.5 9.0 %collective-permute-start.1 = (f32[32,256]{1,0:T(8,128)S(1)}, f32[32,256]{1,0:T(8,128)S(1)}, u32[]{:S(2)}, u32[]{:S(2)}) collective-permute-start(f32[32,256]{1,0:T(8,128)S(1)} %get-tuple-element.31), channel_id=1, source_target_pairs={{0,4},{8,12},{16,20},{24,28},{4,0},{12,8},{20,16},{28,24},{1,5},{9... | collective-permute-start | bytes 98312 | tf_op jit(solution)/shard_map/ppermute | solution.py:758
  5.1 6.6 %collective-permute-start.2 = (f32[32,256]{1,0:T(8,128)S(1)}, f32[32,256]{1,0:T(8,128)S(1)}, u32[]{:S(2)}, u32[]{:S(2)}) collective-permute-start(f32[32,256]{1,0:T(8,128)S(1)} %get-tuple-element.32), channel_id=1, source_target_pairs={{4,8},{12,16},{20,24},{28,0},{8,4},{16,12},{24,20},{0,28},{5,9},{1... | collective-permute-start | bytes 98312 | tf_op jit(solution)/shard_map/ppermute | solution.py:759
  11.9 1.6 %collective-permute-start.4 = (f32[192,256]{1,0:T(8,128)S(1)}, f32[192,256]{1,0:T(8,128)S(1)}, u32[]{:S(2)}, u32[]{:S(2)}) collective-permute-start(f32[192,256]{1,0:T(8,128)S(1)} %get-tuple-element.38), channel_id=1, source_target_pairs={{0,1},{1,0},{2,3},{3,2},{4,5},{5,4},{6,7},{7,6},{8,9},{9,8},{10,11... | collective-permute-start | bytes 589832 | tf_op jit(solution)/shard_map/ppermute | solution.py:772
  12.0 4.9 %collective-permute-start.3 = (f32[72,256]{1,0:T(8,128)S(1)}, f32[72,256]{1,0:T(8,128)S(1)}, u32[]{:S(2)}, u32[]{:S(2)}) collective-permute-start(f32[72,256]{1,0:T(8,128)S(1)} %get-tuple-element.36.own), channel_id=1, source_target_pairs={{0,2},{1,3},{2,0},{3,1},{4,6},{5,7},{6,4},{7,5},{8,10},{9,11},{10,... | collective-permute-start | bytes 221192 | tf_op jit(solution)/shard_map/ppermute | solution.py:783
  13.6 4.4 %collective-permute-start.5 = (f32[64,256]{1,0:T(8,128)S(1)}, f32[64,256]{1,0:T(8,128)S(1)}, u32[]{:S(2)}, u32[]{:S(2)}) collective-permute-start(f32[64,256]{1,0:T(8,128)S(1)} %get-tuple-element.43.mine), channel_id=1, source_target_pairs={{0,2},{1,3},{2,0},{3,1},{4,6},{5,7},{6,4},{7,5},{8,10},{9,11},{10,... | collective-permute-start | bytes 196616 | tf_op jit(solution)/shard_map/ppermute | solution.py:782
  17.5 1.8 %collective-permute-start.7 = (f32[64,256]{1,0:T(8,128)S(1)}, f32[64,256]{1,0:T(8,128)S(1)}, u32[]{:S(2)}, u32[]{:S(2)}) collective-permute-start(f32[64,256]{1,0:T(8,128)S(1)} %get-tuple-element.44), channel_id=1, source_target_pairs={{0,1},{2,3},{1,0},{3,2},{4,5},{6,7},{5,4},{7,6},{8,9},{10,11},{9,8... | collective-permute-start | bytes 196616 | tf_op jit(solution)/shard_map/ppermute | solution.py:794
  18.1 1.3 %collective-permute-start.6 = (f32[64,256]{1,0:T(8,128)S(1)}, f32[64,256]{1,0:T(8,128)S(1)}, u32[]{:S(2)}, u32[]{:S(2)}) collective-permute-start(f32[64,256]{1,0:T(8,128)S(1)} %join.1.joined), channel_id=1, source_target_pairs={{0,1},{2,3},{1,0},{3,2},{4,5},{6,7},{5,4},{7,6},{8,9},{10,11},{9,8... | collective-permute-start | bytes 196616 | tf_op jit(solution)/shard_map/ppermute | solution.py:790

commit v9 on v8

--- a/solution.py
+++ b/solution.py
@@ -134,32 +134,36 @@
     def row(value):
         return jnp.full((1, cols), value, F32)
 
-    ratio = jnp.zeros((1, cols), F32)
-    forward = jnp.ones((1, cols), F32)
+    low = [row(lower[level]) for level in range(levels)]
+    high = [row(upper[level]) for level in range(levels)]
+    scale = [1.0 / (1.0 + a + b) for a, b in zip(low, high)]
+    minors = [jnp.ones((1, cols), F32)] * 2
+    for level in range(1, levels):
+        product = (low[level] * scale[level]) * (high[level - 1] * scale[level - 1])
+        minors.append(minors[-1] - product * minors[-2])
+    pivots = [scale[level] * minors[level] * (1.0 / minors[level + 1]) for level in range(levels)]
+    ratios = [a * b for a, b in zip(high, pivots)]
+    forward = [pivots[0]]
+    for level in range(1, levels):
+        forward.append(low[level] * pivots[level] * forward[-1])
+    green = [forward[-1]]
+    for level in range(levels - 2, -1, -1):
+        green.insert(0, forward[level] + ratios[level] * green[0])
     for level in range(levels):
-        low, high = row(lower[level]), row(upper[level])
-        pivot = 1.0 / (1.0 + low + high - low * ratio)
-        ratio = high * pivot
-        lower_pivot = low * pivot
-        forward = pivot if level == 0 else lower_pivot * forward
-        table[level, pl.ds(PIVOT_NEW, 1), :] = NEW_WEIGHT * pivot
-        table[level, pl.ds(LOWER_PIVOT, 1), :] = lower_pivot
-        table[level, pl.ds(UPPER_PIVOT, 1), :] = ratio
-        table[level, pl.ds(BELOW_FORWARD, 1), :] = forward
-        table[level, pl.ds(PIVOT, 1), :] = pivot
-        table[level, pl.ds(RISE, 1), :] = row(metric[level] if level < levels - 1 else 0.0)
-        table[level, pl.ds(FALL, 1), :] = row(metric[level] if level > 0 else 0.0)
-    green = forward
-    table[levels - 1, pl.ds(FIRST_GREEN, 1), :] = NEW_WEIGHT * green
-    for level in range(levels - 2, -1, -1):
-        green = (
-            table[level, pl.ds(BELOW_FORWARD, 1), :]
-            + table[level, pl.ds(UPPER_PIVOT, 1), :] * green
-        )
-        table[level, pl.ds(FIRST_GREEN, 1), :] = NEW_WEIGHT * green
-    scalars[pl.ds(FIRST, 1), :] = green
-    scalars[pl.ds(CORNER, 1), :] = forward
-    scalars[pl.ds(LAST, 1), :] = pivot
+        for at, value in (
+            (PIVOT_NEW, NEW_WEIGHT * pivots[level]),
+            (LOWER_PIVOT, low[level] * pivots[level]),
+            (UPPER_PIVOT, ratios[level]),
+            (FIRST_GREEN, NEW_WEIGHT * green[level]),
+            (BELOW_FORWARD, forward[level]),
+            (PIVOT, pivots[level]),
+            (RISE, row(metric[level] if level < levels - 1 else 0.0)),
+            (FALL, row(metric[level] if level > 0 else 0.0)),
+        ):
+            table[level, pl.ds(at, 1), :] = value
+    scalars[pl.ds(FIRST, 1), :] = green[0]
+    scalars[pl.ds(CORNER, 1), :] = forward[-1]
+    scalars[pl.ds(LAST, 1), :] = pivots[-1]
     scalars[pl.ds(BELOW, 1), :] = row(lower[0])
     scalars[pl.ds(ABOVE, 1), :] = row(upper[levels - 1])
     scalars[pl.ds(METRIC_BELOW, 1), :] = row(NEW_WEIGHT * metric[0])
@@ -660,6 +664,28 @@
     core = bit_of("gz", 0)
     start = pl.multiple_of((1 - core if swapped else core) * half, half)
     copies = []
+    for field in range(2):
+        for part, begin in enumerate(range(0, half, width)):
+            into = joined[pl.ds(field * half + begin, width), :]
+            tiles = [into[i : i + TILE] for i in range(0, width, TILE)]
+
+            def step(level, carry, field=field, begin=begin, tiles=tiles):
+                gain = response[level]
+                for i, tile in enumerate(tiles):
+                    at = begin + i * TILE
+                    value = known[field, level, pl.ds(start + at, TILE), :] + gain * tile
+                    result[field, level, pl.ds(at, TILE), :] = value
+                return carry
+
+            lax.fori_loop(0, levels, step, 0, unroll=True)
+            copies.append(
+                pltpu.make_async_copy(
+                    result.at[field, :, pl.ds(begin, width), :],
+                    outs[field].at[:, pl.ds(start + begin, width), :],
+                    sems.at[2 + 2 * field + part],
+                )
+            )
+            copies[-1].start()
     if late:
         diffs = side_changes(far, near)
         level = core * (levels - 1)
@@ -685,28 +711,6 @@
                     rim.at[field],
                     outs[2 + field].at[level, pl.ds(start, half), :],
                     sems.at[field],
-                )
-            )
-            copies[-1].start()
-    for field in range(2):
-        for part, begin in enumerate(range(0, half, width)):
-            into = joined[pl.ds(field * half + begin, width), :]
-            tiles = [into[i : i + TILE] for i in range(0, width, TILE)]
-
-            def step(level, carry, field=field, begin=begin, tiles=tiles):
-                gain = response[level]
-                for i, tile in enumerate(tiles):
-                    at = begin + i * TILE
-                    value = known[field, level, pl.ds(start + at, TILE), :] + gain * tile
-                    result[field, level, pl.ds(at, TILE), :] = value
-                return carry
-
-            lax.fori_loop(0, levels, step, 0, unroll=True)
-            copies.append(
-                pltpu.make_async_copy(
-                    result.at[field, :, pl.ds(begin, width), :],
-                    outs[field].at[:, pl.ds(start + begin, width), :],
-                    sems.at[2 + 2 * field + part],
                 )
             )
             copies[-1].start()

time: 20.6 us -> 20.6 us (level)
  no operation moved by 1% of the time
where the time goes in v9:
time: 20.6 us; the launch traced here: 20.5 us
  starting transfers between devices  9.88 us (48%)
  Pallas kernels  8.5 us (41%)
  waiting for transfers between devices  1.28 us (6%)
  between operations  0.8 us (4%)
    ppermute x1, starting transfers between devices, local(): lax.ppermute(far, 'gx', both_ways([(i, (i + 1) % across) for i in range(1...  3.54 us
    pallas_call x1, Pallas kernels, bulk(): pl.pallas_call(bulk_kernel, out_shape=(held(2, levels + 1, rows, cols), h...  2.76 us
    ppermute x1, starting transfers between devices, local(): lax.ppermute(near, 'gx', both_ways([(i, i + 1) for i in range(0, across,...  2.59 us
    pallas_call x2, Pallas kernels, finish(): pl.pallas_call(functools.partial(finish_kernel, rounds, swapped), out_sha...  2.13 us
    ppermute x1, starting transfers between devices, local(): other_own = lax.ppermute(own, 'gz', partners)  1.56 us
    ppermute x2, starting transfers between devices, local(): theirs = lax.ppermute(message, 'gz', partners)  1.5 us
    pallas_call x1, Pallas kernels, tends(): pl.pallas_call(functools.partial(tends_kernel, rounds), out_shape=(jax.Sh...  1.38 us
    pallas_call x1, Pallas kernels, edges(): pl.pallas_call(edges_kernel, out_shape=(held(2 * levels, cols), held(2 *...  1.31 us
  transfers between devices with their start and end apart: 8, of which 4 were waited for; matrix products, arithmetic and copies ran while one was open for 0% of the time, Pallas kernels for 29%

profile of v9, /device:TPU:0, one launch (start us, length us, event | category | flops | bytes accessed | tf_op | source)
XLA Modules:
  0.0 20.5 jit_solution(13524500271521995117)
XLA Ops:
  0.7 1.3 %edges.1 = (f32[32,256]{1,0:T(8,128)S(1)}, f32[32,256]{1,0:T(8,128)S(1)}, f32[200,256]{1,0:T(8,128)S(1)}, f32[128,256]{1,0:T(8,128)S(1)}, f32[16,8,256]{2,1,0:T(8,128)S(1)}) custom-call(f32[16,64,256]{2,1,0:T(8,128)} %temp.5, f32[16,64,256]{2,1,0:T(8,128)} %u_vel.3, f32[16,64,256]{2,1,0:T(8,128)} %w_vel.5, f32[16,64,256]{2,1,0:T(8,128)} %v_vel.3, ...), custom_call_target="tpu_custom_call" | custom-call | tf_op jit(solution)/shard_map/edges/pallas_call | solution.py:107
  2.0 0.5 %collective-permute-start = (f32[200,256]{1,0:T(8,128)S(1)}, f32[200,256]{1,0:T(8,128)S(1)}, u32[]{:S(2)}, u32[]{:S(2)}) collective-permute-start(f32[200,256]{1,0:T(8,128)S(1)} %get-tuple-element.28.fluxes.own), channel_id=1, source_target_pairs={{0,1},{2,3},{1,0},{3,2},{4,5},{6,7},{5,4},{7,6},{8,9},{10,11},{9,8... | collective-permute-start | bytes 614408 | tf_op jit(solution)/shard_map/ppermute | solution.py:761
  2.5 2.6 %collective-permute-start.1 = (f32[32,256]{1,0:T(8,128)S(1)}, f32[32,256]{1,0:T(8,128)S(1)}, u32[]{:S(2)}, u32[]{:S(2)}) collective-permute-start(f32[32,256]{1,0:T(8,128)S(1)} %get-tuple-element.31), channel_id=1, source_target_pairs={{0,4},{8,12},{16,20},{24,28},{4,0},{12,8},{20,16},{28,24},{1,5},{9... | collective-permute-start | bytes 98312 | tf_op jit(solution)/shard_map/ppermute | solution.py:762
  5.1 3.5 %collective-permute-start.2 = (f32[32,256]{1,0:T(8,128)S(1)}, f32[32,256]{1,0:T(8,128)S(1)}, u32[]{:S(2)}, u32[]{:S(2)}) collective-permute-start(f32[32,256]{1,0:T(8,128)S(1)} %get-tuple-element.32), channel_id=1, source_target_pairs={{4,8},{12,16},{20,24},{28,0},{8,4},{16,12},{24,20},{0,28},{5,9},{1... | collective-permute-start | bytes 98312 | tf_op jit(solution)/shard_map/ppermute | solution.py:763
  8.7 0.0 collective-permute-done.arrived.other
  8.7 2.8 %bulk.1 = (f32[2,17,64,256]{3,2,1,0:T(8,128)S(1)}, f32[2,16,64,256]{3,2,1,0:T(8,128)S(1)}, f32[2,64,256]{2,1,0:T(8,128)S(1)}) custom-call(f32[200,256]{1,0:T(8,128)S(1)} %collective-permute-done.arrived.other, f32[16,8,256]{2,1,0:T(8,128)S(1)} %get-tuple-element.29.table.rest_1_, f32[16,64,256]{2,1,0:T(8,128)S(1)} %copy-done, f32[16,64,256]{2,1,0:T(8,128)S(1)} %copy-done.2, ...), custom_call_target="tpu_custom_call" | custom-call | flops 26214400000 | bytes 6291456 | tf_op jit(solution)/shard_map/bulk/pallas_call | solution.py:261
  11.5 0.0 collective-permute-done.1.near.rest_4_
  11.5 0.2 %collective-permute-done.2.far.rest_3_ = f32[32,256]{1,0:T(8,128)S(1)} collective-permute-done((f32[32,256]{1,0:T(8,128)S(1)}, f32[32,256]{1,0:T(8,128)S(1)}, u32[]{:S(2)}, u32[]{:S(2)}) %collective-permute-start.2) | collective-permute-done | bytes 32800 | tf_op jit(solution)/shard_map/ppermute | solution.py:763
  11.7 0.2 fix.1
  11.9 0.1 collective-permute-start.4
  12.0 1.6 %collective-permute-start.3 = (f32[72,256]{1,0:T(8,128)S(1)}, f32[72,256]{1,0:T(8,128)S(1)}, u32[]{:S(2)}, u32[]{:S(2)}) collective-permute-start(f32[72,256]{1,0:T(8,128)S(1)} %get-tuple-element.36.own), channel_id=1, source_target_pairs={{0,2},{1,3},{2,0},{3,1},{4,6},{5,7},{6,4},{7,5},{8,10},{9,11},{10,... | collective-permute-start | bytes 221192 | tf_op jit(solution)/shard_map/ppermute | solution.py:787
  13.5 0.0 collective-permute-done.4.theirs
  13.5 0.1 merge.1
  13.6 1.4 %collective-permute-start.5 = (f32[64,256]{1,0:T(8,128)S(1)}, f32[64,256]{1,0:T(8,128)S(1)}, u32[]{:S(2)}, u32[]{:S(2)}) collective-permute-start(f32[64,256]{1,0:T(8,128)S(1)} %get-tuple-element.43.mine), channel_id=1, source_target_pairs={{0,2},{1,3},{2,0},{3,1},{4,6},{5,7},{6,4},{7,5},{8,10},{9,11},{10,... | collective-permute-start | bytes 196616 | tf_op jit(solution)/shard_map/ppermute | solution.py:786
  15.0 1.4 %tends.1 = (f32[16,64,256]{2,1,0:T(8,128)}, f32[16,64,256]{2,1,0:T(8,128)}) custom-call(f32[16,8,256]{2,1,0:T(8,128)S(1)} %get-tuple-element.29.table.rest_1_, f32[2,16,64,256]{3,2,1,0:T(8,128)S(1)} %get-tuple-element.45.tend.rest_2_, f32[32,256]{1,0:T(8,128)S(1)} %collective-permute-done.2.far.rest_3_, f32[32,256]{1,0:T(8,128)S(1)} %collective-permute-done.1.near.rest_4_, ...), custom_call_target="tpu_custom_call" | custom-call | flops 262144 | bytes 2097152 | tf_op jit(solution)/shard_map/tends/pallas_call | solution.py:443
  16.4 0.4 %collective-permute-done.3.crossing.other.rest_0_ = f32[72,256]{1,0:T(8,128)S(1)} collective-permute-done((f32[72,256]{1,0:T(8,128)S(1)}, f32[72,256]{1,0:T(8,128)S(1)}, u32[]{:S(2)}, u32[]{:S(2)}) %collective-permute-start.3) | collective-permute-done | bytes 73760 | tf_op jit(solution)/shard_map/ppermute | solution.py:787
  16.9 0.6 %prepare.1 = (f32[2,16,64,256]{3,2,1,0:T(8,128)S(1)}, f32[16,8,256]{2,1,0:T(8,128)S(1)}, f32[64,256]{1,0:T(8,128)S(1)}) custom-call(f32[16,64,256]{2,1,0:T(8,128)S(1)} %copy-done, f32[16,64,256]{2,1,0:T(8,128)S(1)} %copy-done.1, f32[2,17,64,256]{3,2,1,0:T(8,128)S(1)} %get-tuple-element.30.forward, f32[16,8,256]{2,1,0:T(8,128)S(1)} %get-tuple-element.29.table.rest_1_, ...), custom_call_target="tpu_custom_call" | custom-call | flops 262144 | bytes 6291456 | tf_op jit(solution)/shard_map/prepare/pallas_call | solution.py:608
  17.5 0.1 collective-permute-start.7
  17.6 0.5 %collective-permute-done.5.theirs = f32[64,256]{1,0:T(8,128)S(1)} collective-permute-done((f32[64,256]{1,0:T(8,128)S(1)}, f32[64,256]{1,0:T(8,128)S(1)}, u32[]{:S(2)}, u32[]{:S(2)}) %collective-permute-start.5) | collective-permute-done | bytes 65568 | tf_op jit(solution)/shard_map/ppermute | solution.py:786
  18.1 0.1 collective-permute-start.6
  18.2 1.1 %finish.2 = (f32[16,64,256]{2,1,0:T(8,128)}, f32[16,64,256]{2,1,0:T(8,128)}, f32[16,64,256]{2,1,0:T(8,128)}, f32[16,64,256]{2,1,0:T(8,128)}) custom-call(f32[2,16,64,256]{3,2,1,0:T(8,128)S(1)} %get-tuple-element.41.known, f32[16,8,256]{2,1,0:T(8,128)S(1)} %get-tuple-element.42.response, ...), custom_call_target="tpu_custom_call", output_to_operand_aliasing={{2}: (8, {}), {3}: (9, {})} | custom-call | flops 5242880000 | bytes 2097152 | tf_op jit(solution)/shard_map/finish/pallas_call | solution.py:726
  19.3 0.0 collective-permute-done.7.rest_0_
  19.3 0.1 collective-permute-done.6.joined
  19.4 1.1 %finish.3 = (f32[16,64,256]{2,1,0:T(8,128)}, f32[16,64,256]{2,1,0:T(8,128)}, f32[16,64,256]{2,1,0:T(8,128)}, f32[16,64,256]{2,1,0:T(8,128)}) custom-call(f32[2,16,64,256]{3,2,1,0:T(8,128)S(1)} %get-tuple-element.41.known, f32[16,8,256]{2,1,0:T(8,128)S(1)} %get-tuple-element.42.response, ...), custom_call_target="tpu_custom_call", output_to_operand_aliasing={{0}: (8, {}), {1}: (9, {}), {2}: (10, {}), {3}: (11, {})} | custom-call | flops 5242880000 | bytes 2097152 | tf_op jit(solution)/shard_map/finish/pallas_call | solution.py:726
  (13 shorter events, 0.1 us)
Async XLA Ops:
  0.6 8.0 %copy-start.1 = (f32[16,64,256]{2,1,0:T(8,128)S(1)}, f32[16,64,256]{2,1,0:T(8,128)}, u32[]{:S(2)}) copy-start(f32[16,64,256]{2,1,0:T(8,128)} %w_vel.5) | copy-start | bytes 3145732
  0.6 8.0 %copy-start = (f32[16,64,256]{2,1,0:T(8,128)S(1)}, f32[16,64,256]{2,1,0:T(8,128)}, u32[]{:S(2)}) copy-start(f32[16,64,256]{2,1,0:T(8,128)} %temp.5) | copy-start | bytes 3145732
  0.7 8.0 %copy-start.5 = (f32[16,64,256]{2,1,0:T(8,128)S(1)}, f32[16,64,256]{2,1,0:T(8,128)}, u32[]{:S(2)}) copy-start(f32[16,64,256]{2,1,0:T(8,128)} %w_prev.3) | copy-start | bytes 3145732
  0.7 8.0 %copy-start.4 = (f32[16,64,256]{2,1,0:T(8,128)S(1)}, f32[16,64,256]{2,1,0:T(8,128)}, u32[]{:S(2)}) copy-start(f32[16,64,256]{2,1,0:T(8,128)} %temp_prev.3) | copy-start | bytes 3145732
  0.7 8.0 %copy-start.3 = (f32[16,64,256]{2,1,0:T(8,128)S(1)}, f32[16,64,256]{2,1,0:T(8,128)}, u32[]{:S(2)}) copy-start(f32[16,64,256]{2,1,0:T(8,128)} %v_vel.3) | copy-start | bytes 3145732
  0.7 8.0 %copy-start.2 = (f32[16,64,256]{2,1,0:T(8,128)S(1)}, f32[16,64,256]{2,1,0:T(8,128)}, u32[]{:S(2)}) copy-start(f32[16,64,256]{2,1,0:T(8,128)} %u_vel.3) | copy-start | bytes 3145732
  2.0 6.7 %collective-permute-start = (f32[200,256]{1,0:T(8,128)S(1)}, f32[200,256]{1,0:T(8,128)S(1)}, u32[]{:S(2)}, u32[]{:S(2)}) collective-permute-start(f32[200,256]{1,0:T(8,128)S(1)} %get-tuple-element.28.fluxes.own), channel_id=1, source_target_pairs={{0,1},{2,3},{1,0},{3,2},{4,5},{6,7},{5,4},{7,6},{8,9},{10,11},{9,8... | collective-permute-start | bytes 614408 | tf_op jit(solution)/shard_map/ppermute | solution.py:761
  2.5 9.0 %collective-permute-start.1 = (f32[32,256]{1,0:T(8,128)S(1)}, f32[32,256]{1,0:T(8,128)S(1)}, u32[]{:S(2)}, u32[]{:S(2)}) collective-permute-start(f32[32,256]{1,0:T(8,128)S(1)} %get-tuple-element.31), channel_id=1, source_target_pairs={{0,4},{8,12},{16,20},{24,28},{4,0},{12,8},{20,16},{28,24},{1,5},{9... | collective-permute-start | bytes 98312 | tf_op jit(solution)/shard_map/ppermute | solution.py:762
  5.1 6.6 %collective-permute-start.2 = (f32[32,256]{1,0:T(8,128)S(1)}, f32[32,256]{1,0:T(8,128)S(1)}, u32[]{:S(2)}, u32[]{:S(2)}) collective-permute-start(f32[32,256]{1,0:T(8,128)S(1)} %get-tuple-element.32), channel_id=1, source_target_pairs={{4,8},{12,16},{20,24},{28,0},{8,4},{16,12},{24,20},{0,28},{5,9},{1... | collective-permute-start | bytes 98312 | tf_op jit(solution)/shard_map/ppermute | solution.py:763
  11.9 1.6 %collective-permute-start.4 = (f32[192,256]{1,0:T(8,128)S(1)}, f32[192,256]{1,0:T(8,128)S(1)}, u32[]{:S(2)}, u32[]{:S(2)}) collective-permute-start(f32[192,256]{1,0:T(8,128)S(1)} %get-tuple-element.38), channel_id=1, source_target_pairs={{0,1},{1,0},{2,3},{3,2},{4,5},{5,4},{6,7},{7,6},{8,9},{9,8},{10,11... | collective-permute-start | bytes 589832 | tf_op jit(solution)/shard_map/ppermute | solution.py:776
  12.0 4.9 %collective-permute-start.3 = (f32[72,256]{1,0:T(8,128)S(1)}, f32[72,256]{1,0:T(8,128)S(1)}, u32[]{:S(2)}, u32[]{:S(2)}) collective-permute-start(f32[72,256]{1,0:T(8,128)S(1)} %get-tuple-element.36.own), channel_id=1, source_target_pairs={{0,2},{1,3},{2,0},{3,1},{4,6},{5,7},{6,4},{7,5},{8,10},{9,11},{10,... | collective-permute-start | bytes 221192 | tf_op jit(solution)/shard_map/ppermute | solution.py:787
  13.6 4.4 %collective-permute-start.5 = (f32[64,256]{1,0:T(8,128)S(1)}, f32[64,256]{1,0:T(8,128)S(1)}, u32[]{:S(2)}, u32[]{:S(2)}) collective-permute-start(f32[64,256]{1,0:T(8,128)S(1)} %get-tuple-element.43.mine), channel_id=1, source_target_pairs={{0,2},{1,3},{2,0},{3,1},{4,6},{5,7},{6,4},{7,5},{8,10},{9,11},{10,... | collective-permute-start | bytes 196616 | tf_op jit(solution)/shard_map/ppermute | solution.py:786
  17.5 1.8 %collective-permute-start.7 = (f32[64,256]{1,0:T(8,128)S(1)}, f32[64,256]{1,0:T(8,128)S(1)}, u32[]{:S(2)}, u32[]{:S(2)}) collective-permute-start(f32[64,256]{1,0:T(8,128)S(1)} %get-tuple-element.44), channel_id=1, source_target_pairs={{0,1},{2,3},{1,0},{3,2},{4,5},{6,7},{5,4},{7,6},{8,9},{10,11},{9,8... | collective-permute-start | bytes 196616 | tf_op jit(solution)/shard_map/ppermute | solution.py:798
  18.1 1.3 %collective-permute-start.6 = (f32[64,256]{1,0:T(8,128)S(1)}, f32[64,256]{1,0:T(8,128)S(1)}, u32[]{:S(2)}, u32[]{:S(2)}) collective-permute-start(f32[64,256]{1,0:T(8,128)S(1)} %join.1.joined), channel_id=1, source_target_pairs={{0,1},{2,3},{1,0},{3,2},{4,5},{6,7},{5,4},{7,6},{8,9},{10,11},{9,8... | collective-permute-start | bytes 196616 | tf_op jit(solution)/shard_map/ppermute | solution.py:794

commit v10 on v9

--- a/solution.py
+++ b/solution.py
@@ -134,36 +134,32 @@
     def row(value):
         return jnp.full((1, cols), value, F32)
 
-    low = [row(lower[level]) for level in range(levels)]
-    high = [row(upper[level]) for level in range(levels)]
-    scale = [1.0 / (1.0 + a + b) for a, b in zip(low, high)]
-    minors = [jnp.ones((1, cols), F32)] * 2
-    for level in range(1, levels):
-        product = (low[level] * scale[level]) * (high[level - 1] * scale[level - 1])
-        minors.append(minors[-1] - product * minors[-2])
-    pivots = [scale[level] * minors[level] * (1.0 / minors[level + 1]) for level in range(levels)]
-    ratios = [a * b for a, b in zip(high, pivots)]
-    forward = [pivots[0]]
-    for level in range(1, levels):
-        forward.append(low[level] * pivots[level] * forward[-1])
-    green = [forward[-1]]
+    ratio = jnp.zeros((1, cols), F32)
+    forward = jnp.ones((1, cols), F32)
+    for level in range(levels):
+        low, high = row(lower[level]), row(upper[level])
+        pivot = 1.0 / (1.0 + low + high - low * ratio)
+        ratio = high * pivot
+        lower_pivot = low * pivot
+        forward = pivot if level == 0 else lower_pivot * forward
+        table[level, pl.ds(PIVOT_NEW, 1), :] = NEW_WEIGHT * pivot
+        table[level, pl.ds(LOWER_PIVOT, 1), :] = lower_pivot
+        table[level, pl.ds(UPPER_PIVOT, 1), :] = ratio
+        table[level, pl.ds(BELOW_FORWARD, 1), :] = forward
+        table[level, pl.ds(PIVOT, 1), :] = pivot
+        table[level, pl.ds(RISE, 1), :] = row(metric[level] if level < levels - 1 else 0.0)
+        table[level, pl.ds(FALL, 1), :] = row(metric[level] if level > 0 else 0.0)
+    green = forward
+    table[levels - 1, pl.ds(FIRST_GREEN, 1), :] = NEW_WEIGHT * green
     for level in range(levels - 2, -1, -1):
-        green.insert(0, forward[level] + ratios[level] * green[0])
-    for level in range(levels):
-        for at, value in (
-            (PIVOT_NEW, NEW_WEIGHT * pivots[level]),
-            (LOWER_PIVOT, low[level] * pivots[level]),
-            (UPPER_PIVOT, ratios[level]),
-            (FIRST_GREEN, NEW_WEIGHT * green[level]),
-            (BELOW_FORWARD, forward[level]),
-            (PIVOT, pivots[level]),
-            (RISE, row(metric[level] if level < levels - 1 else 0.0)),
-            (FALL, row(metric[level] if level > 0 else 0.0)),
-        ):
-            table[level, pl.ds(at, 1), :] = value
-    scalars[pl.ds(FIRST, 1), :] = green[0]
-    scalars[pl.ds(CORNER, 1), :] = forward[-1]
-    scalars[pl.ds(LAST, 1), :] = pivots[-1]
+        green = (
+            table[level, pl.ds(BELOW_FORWARD, 1), :]
+            + table[level, pl.ds(UPPER_PIVOT, 1), :] * green
+        )
+        table[level, pl.ds(FIRST_GREEN, 1), :] = NEW_WEIGHT * green
+    scalars[pl.ds(FIRST, 1), :] = green
+    scalars[pl.ds(CORNER, 1), :] = forward
+    scalars[pl.ds(LAST, 1), :] = pivot
     scalars[pl.ds(BELOW, 1), :] = row(lower[0])
     scalars[pl.ds(ABOVE, 1), :] = row(upper[levels - 1])
     scalars[pl.ds(METRIC_BELOW, 1), :] = row(NEW_WEIGHT * metric[0])
@@ -298,6 +294,18 @@
 
 def scalar_rows(ref, begin=0):
     return [ref[pl.ds(begin + at, 1), :] for at in range(7)]
+
+
+def put_seam(ref, field, value):
+    size, cols = value.shape
+    for part in range(2):
+        at = pl.ds((2 * part + field) * size, size)
+        ref[at, :] = value[:, part * cols // 2 : (part + 1) * cols // 2]
+
+
+def get_seam(ref, field, size):
+    parts = [ref[pl.ds((2 * part + field) * size, size), :] for part in range(2)]
+    return jnp.concatenate(parts, axis=1)
 
 
 def in_order(upper, own, other):
@@ -374,13 +382,11 @@
             message[there, :] = jnp.where(core, last_entry[:size], first_entry[size:])
             value = outward[at, :]
             value = jnp.where(core, value[size:], value[:size])
-            seam[pl.ds(field * size, size), :] = jnp.where(
-                beside_seam(rounds), value, other[there, :]
-            )
+            put_seam(seam, field, jnp.where(beside_seam(rounds), value, other[there, :]))
     if late:
         far_scalars = scalar_rows(other, 3 * rows)
         for at, value in enumerate(joint_scalars(*in_order(core, scalars, far_scalars))):
-            seam[pl.ds(rows + at, 1), :] = value
+            seam[pl.ds(2 * rows + at, 1), :] = value[:, : cols // 2]
 
 
 def fix(rounds, other, near, far, fluxes, outward, forward, first, table, outer):
@@ -388,7 +394,7 @@
     _, rows, cols = first.shape
     shapes = [held(4 * rows, cols), held(4 * levels, cols)]
     if rounds == 2:
-        shapes += [held(3 * rows, cols), held(rows + TILE, cols)]
+        shapes += [held(3 * rows, cols), held(2 * rows + TILE, cols // 2)]
     return pl.pallas_call(
         functools.partial(fix_kernel, rounds, levels),
         out_shape=tuple(shapes),
@@ -604,7 +610,7 @@
 def prepare(rounds, temp, w_vel, forward, table, changes, fluxes, other, crossing, bases, gains):
     levels, rows, cols = temp.shape
     shapes = (held(2, levels, rows, cols), held(levels, TILE, cols))
-    shapes += (held(rows, cols),) * (rounds == 2)
+    shapes += (held(2 * rows, cols // 2),) * (rounds == 2)
     return pl.pallas_call(
         functools.partial(prepare_kernel, rounds),
         out_shape=shapes,
@@ -628,6 +634,8 @@
     size = theirs.shape[0] // 2
     upper = bit_of("gz", rounds - 1) == 1
     low, high = in_order(upper, scalar_rows(own, own_at), scalar_rows(other, other_at))
+    if late:
+        low, high = ([jnp.concatenate([a, a], axis=1) for a in rows] for rows in (low, high))
     coupling, inverse = interface(low, high)
     scale = coupling * inverse
     to_other = scale * coupling * jnp.where(upper, low[LAST], high[FIRST])
@@ -638,7 +646,8 @@
         at = pl.ds(field * size, size)
         into = scale * theirs[at, :] + to_other * mine[at, :]
         if late:
-            into = into + (own_gain * own[at, :] + other_gain * other[at, :])
+            into = into + own_gain * get_seam(own, field, size)
+            into = into + other_gain * get_seam(other, field, size)
         joined[at, :] = into
 
 
@@ -704,7 +713,7 @@
                 for diff in diffs
             )
             edge = jnp.where(row_at == 0, head, jnp.where(row_at == rows - 1, tail, 0.0))
-            flux = flux_in[pl.ds(field * half, half), :]
+            flux = get_seam(flux_in, field, half)
             rim[field] = tend[field, level, pl.ds(start, half), :] + gain * flux + edge
             copies.append(
                 pltpu.make_async_copy(

time: 20.6 us -> 20.6 us (level)
  transfers between devices with their start and end apart: 8 -> 8, of which waited for: 4 -> 4; matrix products, arithmetic and copies ran while one was open for 0% -> 0% of each run, Pallas kernels for 29% -> 30%
where the time goes in v10:
time: 20.6 us; the launch traced here: 20.4 us
  starting transfers between devices  9.85 us (48%)
  Pallas kernels  8.65 us (42%)
  waiting for transfers between devices  1.08 us (5%)
  between operations  0.8 us (4%)
    ppermute x1, starting transfers between devices, local(): lax.ppermute(far, 'gx', both_ways([(i, (i + 1) % across) for i in range(1...  3.54 us
    pallas_call x1, Pallas kernels, bulk(): pl.pallas_call(bulk_kernel, out_shape=(held(2, levels + 1, rows, cols), h...  2.89 us
    ppermute x1, starting transfers between devices, local(): lax.ppermute(near, 'gx', both_ways([(i, i + 1) for i in range(0, across,...  2.59 us
    pallas_call x2, Pallas kernels, finish(): pl.pallas_call(functools.partial(finish_kernel, rounds, swapped), out_sha...  2.14 us
    ppermute x1, starting transfers between devices, local(): other_own = lax.ppermute(own, 'gz', partners)  1.56 us
    ppermute x2, starting transfers between devices, local(): theirs = lax.ppermute(message, 'gz', partners)  1.5 us
    pallas_call x1, Pallas kernels, tends(): pl.pallas_call(functools.partial(tends_kernel, rounds), out_shape=(jax.Sh...  1.38 us
    pallas_call x1, Pallas kernels, edges(): pl.pallas_call(edges_kernel, out_shape=(held(2 * levels, cols), held(2 *...  1.31 us
  transfers between devices with their start and end apart: 8, of which 4 were waited for; matrix products, arithmetic and copies ran while one was open for 0% of the time, Pallas kernels for 30%

profile of v10, /device:TPU:0, one launch (start us, length us, event | category | flops | bytes accessed | tf_op | source)
XLA Modules:
  0.0 20.4 jit_solution(8799229024682109644)
XLA Ops:
  0.7 1.3 %edges.1 = (f32[32,256]{1,0:T(8,128)S(1)}, f32[32,256]{1,0:T(8,128)S(1)}, f32[200,256]{1,0:T(8,128)S(1)}, f32[128,256]{1,0:T(8,128)S(1)}, f32[16,8,256]{2,1,0:T(8,128)S(1)}) custom-call(f32[16,64,256]{2,1,0:T(8,128)} %temp.5, f32[16,64,256]{2,1,0:T(8,128)} %u_vel.3, f32[16,64,256]{2,1,0:T(8,128)} %w_vel.5, f32[16,64,256]{2,1,0:T(8,128)} %v_vel.3, ...), custom_call_target="tpu_custom_call" | custom-call | tf_op jit(solution)/shard_map/edges/pallas_call | solution.py:107
  2.0 0.5 %collective-permute-start = (f32[200,256]{1,0:T(8,128)S(1)}, f32[200,256]{1,0:T(8,128)S(1)}, u32[]{:S(2)}, u32[]{:S(2)}) collective-permute-start(f32[200,256]{1,0:T(8,128)S(1)} %get-tuple-element.28.fluxes.own), channel_id=1, source_target_pairs={{0,1},{2,3},{1,0},{3,2},{4,5},{6,7},{5,4},{7,6},{8,9},{10,11},{9,8... | collective-permute-start | bytes 614408 | tf_op jit(solution)/shard_map/ppermute | solution.py:770
  2.5 2.6 %collective-permute-start.1 = (f32[32,256]{1,0:T(8,128)S(1)}, f32[32,256]{1,0:T(8,128)S(1)}, u32[]{:S(2)}, u32[]{:S(2)}) collective-permute-start(f32[32,256]{1,0:T(8,128)S(1)} %get-tuple-element.31), channel_id=1, source_target_pairs={{0,4},{8,12},{16,20},{24,28},{4,0},{12,8},{20,16},{28,24},{1,5},{9... | collective-permute-start | bytes 98312 | tf_op jit(solution)/shard_map/ppermute | solution.py:771
  5.1 3.5 %collective-permute-start.2 = (f32[32,256]{1,0:T(8,128)S(1)}, f32[32,256]{1,0:T(8,128)S(1)}, u32[]{:S(2)}, u32[]{:S(2)}) collective-permute-start(f32[32,256]{1,0:T(8,128)S(1)} %get-tuple-element.32), channel_id=1, source_target_pairs={{4,8},{12,16},{20,24},{28,0},{8,4},{16,12},{24,20},{0,28},{5,9},{1... | collective-permute-start | bytes 98312 | tf_op jit(solution)/shard_map/ppermute | solution.py:772
  8.7 0.0 collective-permute-done.arrived.other
  8.7 2.9 %bulk.1 = (f32[2,17,64,256]{3,2,1,0:T(8,128)S(1)}, f32[2,16,64,256]{3,2,1,0:T(8,128)S(1)}, f32[2,64,256]{2,1,0:T(8,128)S(1)}) custom-call(f32[200,256]{1,0:T(8,128)S(1)} %collective-permute-done.arrived.other, f32[16,8,256]{2,1,0:T(8,128)S(1)} %get-tuple-element.29.table.rest_1_, f32[16,64,256]{2,1,0:T(8,128)S(1)} %copy-done, f32[16,64,256]{2,1,0:T(8,128)S(1)} %copy-done.2, ...), custom_call_target="tpu_custom_call" | custom-call | flops 26214400000 | bytes 6291456 | tf_op jit(solution)/shard_map/bulk/pallas_call | solution.py:257
  11.6 0.0 collective-permute-done.1.near.rest_4_
  11.6 0.1 collective-permute-done.2.far.rest_3_
  11.7 0.2 fix.1
  11.9 0.1 collective-permute-start.4
  12.0 1.6 %collective-permute-start.3 = (f32[136,128]{1,0:T(8,128)S(1)}, f32[136,128]{1,0:T(8,128)S(1)}, u32[]{:S(2)}, u32[]{:S(2)}) collective-permute-start(f32[136,128]{1,0:T(8,128)S(1)} %get-tuple-element.36.own), channel_id=1, source_target_pairs={{0,2},{1,3},{2,0},{3,1},{4,6},{5,7},{6,4},{7,5},{8,10},{9,11},{10,... | collective-permute-start | bytes 208904 | tf_op jit(solution)/shard_map/ppermute | solution.py:796
  13.5 0.0 collective-permute-done.4.theirs
  13.5 0.1 merge.1
  13.6 1.4 %collective-permute-start.5 = (f32[64,256]{1,0:T(8,128)S(1)}, f32[64,256]{1,0:T(8,128)S(1)}, u32[]{:S(2)}, u32[]{:S(2)}) collective-permute-start(f32[64,256]{1,0:T(8,128)S(1)} %get-tuple-element.43.mine), channel_id=1, source_target_pairs={{0,2},{1,3},{2,0},{3,1},{4,6},{5,7},{6,4},{7,5},{8,10},{9,11},{10,... | collective-permute-start | bytes 196616 | tf_op jit(solution)/shard_map/ppermute | solution.py:795
  15.0 1.4 %tends.1 = (f32[16,64,256]{2,1,0:T(8,128)}, f32[16,64,256]{2,1,0:T(8,128)}) custom-call(f32[16,8,256]{2,1,0:T(8,128)S(1)} %get-tuple-element.29.table.rest_1_, f32[2,16,64,256]{3,2,1,0:T(8,128)S(1)} %get-tuple-element.45.tend.rest_2_, f32[32,256]{1,0:T(8,128)S(1)} %collective-permute-done.2.far.rest_3_, f32[32,256]{1,0:T(8,128)S(1)} %collective-permute-done.1.near.rest_4_, ...), custom_call_target="tpu_custom_call" | custom-call | flops 262144 | bytes 2097152 | tf_op jit(solution)/shard_map/tends/pallas_call | solution.py:449
  16.4 0.3 %collective-permute-done.3.crossing.other.rest_0_ = f32[136,128]{1,0:T(8,128)S(1)} collective-permute-done((f32[136,128]{1,0:T(8,128)S(1)}, f32[136,128]{1,0:T(8,128)S(1)}, u32[]{:S(2)}, u32[]{:S(2)}) %collective-permute-start.3) | collective-permute-done | bytes 69664 | tf_op jit(solution)/shard_map/ppermute | solution.py:796
  16.7 0.6 %prepare.1 = (f32[2,16,64,256]{3,2,1,0:T(8,128)S(1)}, f32[16,8,256]{2,1,0:T(8,128)S(1)}, f32[128,128]{1,0:T(8,128)S(1)}) custom-call(f32[16,64,256]{2,1,0:T(8,128)S(1)} %copy-done, f32[16,64,256]{2,1,0:T(8,128)S(1)} %copy-done.1, f32[2,17,64,256]{3,2,1,0:T(8,128)S(1)} %get-tuple-element.30.forward, f32[16,8,256]{2,1,0:T(8,128)S(1)} %get-tuple-element.29.table.rest_1_, ...), custom_call_target="tpu_custom_call" | custom-call | flops 262144 | bytes 6291456 | tf_op jit(solution)/shard_map/prepare/pallas_call | solution.py:614
  17.3 0.1 collective-permute-start.7
  17.4 0.5 %collective-permute-done.5.theirs = f32[64,256]{1,0:T(8,128)S(1)} collective-permute-done((f32[64,256]{1,0:T(8,128)S(1)}, f32[64,256]{1,0:T(8,128)S(1)}, u32[]{:S(2)}, u32[]{:S(2)}) %collective-permute-start.5) | collective-permute-done | bytes 65568 | tf_op jit(solution)/shard_map/ppermute | solution.py:795
  18.0 0.1 collective-permute-start.6
  18.1 1.1 %finish.2 = (f32[16,64,256]{2,1,0:T(8,128)}, f32[16,64,256]{2,1,0:T(8,128)}, f32[16,64,256]{2,1,0:T(8,128)}, f32[16,64,256]{2,1,0:T(8,128)}) custom-call(f32[2,16,64,256]{3,2,1,0:T(8,128)S(1)} %get-tuple-element.41.known, f32[16,8,256]{2,1,0:T(8,128)S(1)} %get-tuple-element.42.response, ...), custom_call_target="tpu_custom_call", output_to_operand_aliasing={{2}: (8, {}), {3}: (9, {})} | custom-call | flops 5242880000 | bytes 2097152 | tf_op jit(solution)/shard_map/finish/pallas_call | solution.py:735
  19.2 0.0 collective-permute-done.7.rest_0_
  19.2 0.2 collective-permute-done.6.joined
  19.3 1.1 %finish.3 = (f32[16,64,256]{2,1,0:T(8,128)}, f32[16,64,256]{2,1,0:T(8,128)}, f32[16,64,256]{2,1,0:T(8,128)}, f32[16,64,256]{2,1,0:T(8,128)}) custom-call(f32[2,16,64,256]{3,2,1,0:T(8,128)S(1)} %get-tuple-element.41.known, f32[16,8,256]{2,1,0:T(8,128)S(1)} %get-tuple-element.42.response, ...), custom_call_target="tpu_custom_call", output_to_operand_aliasing={{0}: (8, {}), {1}: (9, {}), {2}: (10, {}), {3}: (11, {})} | custom-call | flops 5242880000 | bytes 2097152 | tf_op jit(solution)/shard_map/finish/pallas_call | solution.py:735
  (13 shorter events, 0.1 us)
Async XLA Ops:
  0.6 8.0 %copy-start.1 = (f32[16,64,256]{2,1,0:T(8,128)S(1)}, f32[16,64,256]{2,1,0:T(8,128)}, u32[]{:S(2)}) copy-start(f32[16,64,256]{2,1,0:T(8,128)} %w_vel.5) | copy-start | bytes 3145732
  0.6 8.0 %copy-start = (f32[16,64,256]{2,1,0:T(8,128)S(1)}, f32[16,64,256]{2,1,0:T(8,128)}, u32[]{:S(2)}) copy-start(f32[16,64,256]{2,1,0:T(8,128)} %temp.5) | copy-start | bytes 3145732
  0.7 8.0 %copy-start.5 = (f32[16,64,256]{2,1,0:T(8,128)S(1)}, f32[16,64,256]{2,1,0:T(8,128)}, u32[]{:S(2)}) copy-start(f32[16,64,256]{2,1,0:T(8,128)} %w_prev.3) | copy-start | bytes 3145732
  0.7 8.0 %copy-start.4 = (f32[16,64,256]{2,1,0:T(8,128)S(1)}, f32[16,64,256]{2,1,0:T(8,128)}, u32[]{:S(2)}) copy-start(f32[16,64,256]{2,1,0:T(8,128)} %temp_prev.3) | copy-start | bytes 3145732
  0.7 8.0 %copy-start.3 = (f32[16,64,256]{2,1,0:T(8,128)S(1)}, f32[16,64,256]{2,1,0:T(8,128)}, u32[]{:S(2)}) copy-start(f32[16,64,256]{2,1,0:T(8,128)} %v_vel.3) | copy-start | bytes 3145732
  0.7 8.0 %copy-start.2 = (f32[16,64,256]{2,1,0:T(8,128)S(1)}, f32[16,64,256]{2,1,0:T(8,128)}, u32[]{:S(2)}) copy-start(f32[16,64,256]{2,1,0:T(8,128)} %u_vel.3) | copy-start | bytes 3145732
  2.0 6.7 %collective-permute-start = (f32[200,256]{1,0:T(8,128)S(1)}, f32[200,256]{1,0:T(8,128)S(1)}, u32[]{:S(2)}, u32[]{:S(2)}) collective-permute-start(f32[200,256]{1,0:T(8,128)S(1)} %get-tuple-element.28.fluxes.own), channel_id=1, source_target_pairs={{0,1},{2,3},{1,0},{3,2},{4,5},{6,7},{5,4},{7,6},{8,9},{10,11},{9,8... | collective-permute-start | bytes 614408 | tf_op jit(solution)/shard_map/ppermute | solution.py:770
  2.5 9.1 %collective-permute-start.1 = (f32[32,256]{1,0:T(8,128)S(1)}, f32[32,256]{1,0:T(8,128)S(1)}, u32[]{:S(2)}, u32[]{:S(2)}) collective-permute-start(f32[32,256]{1,0:T(8,128)S(1)} %get-tuple-element.31), channel_id=1, source_target_pairs={{0,4},{8,12},{16,20},{24,28},{4,0},{12,8},{20,16},{28,24},{1,5},{9... | collective-permute-start | bytes 98312 | tf_op jit(solution)/shard_map/ppermute | solution.py:771
  5.1 6.6 %collective-permute-start.2 = (f32[32,256]{1,0:T(8,128)S(1)}, f32[32,256]{1,0:T(8,128)S(1)}, u32[]{:S(2)}, u32[]{:S(2)}) collective-permute-start(f32[32,256]{1,0:T(8,128)S(1)} %get-tuple-element.32), channel_id=1, source_target_pairs={{4,8},{12,16},{20,24},{28,0},{8,4},{16,12},{24,20},{0,28},{5,9},{1... | collective-permute-start | bytes 98312 | tf_op jit(solution)/shard_map/ppermute | solution.py:772
  11.9 1.6 %collective-permute-start.4 = (f32[192,256]{1,0:T(8,128)S(1)}, f32[192,256]{1,0:T(8,128)S(1)}, u32[]{:S(2)}, u32[]{:S(2)}) collective-permute-start(f32[192,256]{1,0:T(8,128)S(1)} %get-tuple-element.38), channel_id=1, source_target_pairs={{0,1},{1,0},{2,3},{3,2},{4,5},{5,4},{6,7},{7,6},{8,9},{9,8},{10,11... | collective-permute-start | bytes 589832 | tf_op jit(solution)/shard_map/ppermute | solution.py:785
  12.0 4.7 %collective-permute-start.3 = (f32[136,128]{1,0:T(8,128)S(1)}, f32[136,128]{1,0:T(8,128)S(1)}, u32[]{:S(2)}, u32[]{:S(2)}) collective-permute-start(f32[136,128]{1,0:T(8,128)S(1)} %get-tuple-element.36.own), channel_id=1, source_target_pairs={{0,2},{1,3},{2,0},{3,1},{4,6},{5,7},{6,4},{7,5},{8,10},{9,11},{10,... | collective-permute-start | bytes 208904 | tf_op jit(solution)/shard_map/ppermute | solution.py:796
  13.6 4.3 %collective-permute-start.5 = (f32[64,256]{1,0:T(8,128)S(1)}, f32[64,256]{1,0:T(8,128)S(1)}, u32[]{:S(2)}, u32[]{:S(2)}) collective-permute-start(f32[64,256]{1,0:T(8,128)S(1)} %get-tuple-element.43.mine), channel_id=1, source_target_pairs={{0,2},{1,3},{2,0},{3,1},{4,6},{5,7},{6,4},{7,5},{8,10},{9,11},{10,... | collective-permute-start | bytes 196616 | tf_op jit(solution)/shard_map/ppermute | solution.py:795
  17.3 1.8 %collective-permute-start.7 = (f32[128,128]{1,0:T(8,128)S(1)}, f32[128,128]{1,0:T(8,128)S(1)}, u32[]{:S(2)}, u32[]{:S(2)}) collective-permute-start(f32[128,128]{1,0:T(8,128)S(1)} %get-tuple-element.44), channel_id=1, source_target_pairs={{0,1},{2,3},{1,0},{3,2},{4,5},{6,7},{5,4},{7,6},{8,9},{10,11},{9,8... | collective-permute-start | bytes 196616 | tf_op jit(solution)/shard_map/ppermute | solution.py:807
  18.0 1.3 %collective-permute-start.6 = (f32[64,256]{1,0:T(8,128)S(1)}, f32[64,256]{1,0:T(8,128)S(1)}, u32[]{:S(2)}, u32[]{:S(2)}) collective-permute-start(f32[64,256]{1,0:T(8,128)S(1)} %join.1.joined), channel_id=1, source_target_pairs={{0,1},{2,3},{1,0},{3,2},{4,5},{6,7},{5,4},{7,6},{8,9},{10,11},{9,8... | collective-permute-start | bytes 196616 | tf_op jit(solution)/shard_map/ppermute | solution.py:803

commit v11 on v10

--- a/solution.py
+++ b/solution.py
@@ -205,7 +205,8 @@
         under, over = jnp.maximum(both[0] - 1, 0), jnp.minimum(both[1] + 1, levels - 1)
 
         def spread(level, at):
-            return jnp.broadcast_to(table[level, pl.ds(at, 1), :], (TILE, cols))
+            tile = jnp.broadcast_to(table[level, pl.ds(at, 1), : cols // 2], (TILE, cols // 2))
+            return jnp.concatenate([tile, tile], axis=1)
 
         factors = [
             [spread(level, at) for at in (PIVOT_NEW, LOWER_PIVOT, FIRST_GREEN, RISE, FALL)]

time: 20.6 us -> 20.6 us (level)
  transfers between devices with their start and end apart: 8 -> 8, of which waited for: 4 -> 4; matrix products, arithmetic and copies ran while one was open for 0% -> 0% of each run, Pallas kernels for 30% -> 29%
where the time goes in v11:
time: 20.6 us; the launch traced here: 20.4 us
  starting transfers between devices  9.85 us (48%)
  Pallas kernels  8.52 us (41%)
  waiting for transfers between devices  1.21 us (6%)
  between operations  0.8 us (4%)
    ppermute x1, starting transfers between devices, local(): lax.ppermute(far, 'gx', both_ways([(i, (i + 1) % across) for i in range(1...  3.54 us
    pallas_call x1, Pallas kernels, bulk(): pl.pallas_call(bulk_kernel, out_shape=(held(2, levels + 1, rows, cols), h...  2.77 us
    ppermute x1, starting transfers between devices, local(): lax.ppermute(near, 'gx', both_ways([(i, i + 1) for i in range(0, across,...  2.59 us
    pallas_call x2, Pallas kernels, finish(): pl.pallas_call(functools.partial(finish_kernel, rounds, swapped), out_sha...  2.14 us
    ppermute x1, starting transfers between devices, local(): other_own = lax.ppermute(own, 'gz', partners)  1.56 us
    ppermute x2, starting transfers between devices, local(): theirs = lax.ppermute(message, 'gz', partners)  1.5 us
    pallas_call x1, Pallas kernels, tends(): pl.pallas_call(functools.partial(tends_kernel, rounds), out_shape=(jax.Sh...  1.38 us
    pallas_call x1, Pallas kernels, edges(): pl.pallas_call(edges_kernel, out_shape=(held(2 * levels, cols), held(2 *...  1.31 us
  transfers between devices with their start and end apart: 8, of which 4 were waited for; matrix products, arithmetic and copies ran while one was open for 0% of the time, Pallas kernels for 29%

profile of v11, /device:TPU:0, one launch (start us, length us, event | category | flops | bytes accessed | tf_op | source)
XLA Modules:
  0.0 20.4 jit_solution(6606590969823873536)
XLA Ops:
  0.7 1.3 %edges.1 = (f32[32,256]{1,0:T(8,128)S(1)}, f32[32,256]{1,0:T(8,128)S(1)}, f32[200,256]{1,0:T(8,128)S(1)}, f32[128,256]{1,0:T(8,128)S(1)}, f32[16,8,256]{2,1,0:T(8,128)S(1)}) custom-call(f32[16,64,256]{2,1,0:T(8,128)} %temp.5, f32[16,64,256]{2,1,0:T(8,128)} %u_vel.3, f32[16,64,256]{2,1,0:T(8,128)} %w_vel.5, f32[16,64,256]{2,1,0:T(8,128)} %v_vel.3, ...), custom_call_target="tpu_custom_call" | custom-call | tf_op jit(solution)/shard_map/edges/pallas_call | solution.py:107
  2.0 0.5 %collective-permute-start = (f32[200,256]{1,0:T(8,128)S(1)}, f32[200,256]{1,0:T(8,128)S(1)}, u32[]{:S(2)}, u32[]{:S(2)}) collective-permute-start(f32[200,256]{1,0:T(8,128)S(1)} %get-tuple-element.28.fluxes.own), channel_id=1, source_target_pairs={{0,1},{2,3},{1,0},{3,2},{4,5},{6,7},{5,4},{7,6},{8,9},{10,11},{9,8... | collective-permute-start | bytes 614408 | tf_op jit(solution)/shard_map/ppermute | solution.py:771
  2.5 2.6 %collective-permute-start.1 = (f32[32,256]{1,0:T(8,128)S(1)}, f32[32,256]{1,0:T(8,128)S(1)}, u32[]{:S(2)}, u32[]{:S(2)}) collective-permute-start(f32[32,256]{1,0:T(8,128)S(1)} %get-tuple-element.31), channel_id=1, source_target_pairs={{0,4},{8,12},{16,20},{24,28},{4,0},{12,8},{20,16},{28,24},{1,5},{9... | collective-permute-start | bytes 98312 | tf_op jit(solution)/shard_map/ppermute | solution.py:772
  5.1 3.5 %collective-permute-start.2 = (f32[32,256]{1,0:T(8,128)S(1)}, f32[32,256]{1,0:T(8,128)S(1)}, u32[]{:S(2)}, u32[]{:S(2)}) collective-permute-start(f32[32,256]{1,0:T(8,128)S(1)} %get-tuple-element.32), channel_id=1, source_target_pairs={{4,8},{12,16},{20,24},{28,0},{8,4},{16,12},{24,20},{0,28},{5,9},{1... | collective-permute-start | bytes 98312 | tf_op jit(solution)/shard_map/ppermute | solution.py:773
  8.7 0.0 collective-permute-done.arrived.other
  8.7 2.8 %bulk.1 = (f32[2,17,64,256]{3,2,1,0:T(8,128)S(1)}, f32[2,16,64,256]{3,2,1,0:T(8,128)S(1)}, f32[2,64,256]{2,1,0:T(8,128)S(1)}) custom-call(f32[200,256]{1,0:T(8,128)S(1)} %collective-permute-done.arrived.other, f32[16,8,256]{2,1,0:T(8,128)S(1)} %get-tuple-element.29.table.rest_1_, f32[16,64,256]{2,1,0:T(8,128)S(1)} %copy-done, f32[16,64,256]{2,1,0:T(8,128)S(1)} %copy-done.2, ...), custom_call_target="tpu_custom_call" | custom-call | flops 26214400000 | bytes 6291456 | tf_op jit(solution)/shard_map/bulk/pallas_call | solution.py:258
  11.5 0.0 collective-permute-done.1.near.rest_4_
  11.5 0.2 %collective-permute-done.2.far.rest_3_ = f32[32,256]{1,0:T(8,128)S(1)} collective-permute-done((f32[32,256]{1,0:T(8,128)S(1)}, f32[32,256]{1,0:T(8,128)S(1)}, u32[]{:S(2)}, u32[]{:S(2)}) %collective-permute-start.2) | collective-permute-done | bytes 32800 | tf_op jit(solution)/shard_map/ppermute | solution.py:773
  11.7 0.2 fix.1
  11.9 0.1 collective-permute-start.4
  12.0 1.6 %collective-permute-start.3 = (f32[136,128]{1,0:T(8,128)S(1)}, f32[136,128]{1,0:T(8,128)S(1)}, u32[]{:S(2)}, u32[]{:S(2)}) collective-permute-start(f32[136,128]{1,0:T(8,128)S(1)} %get-tuple-element.36.own), channel_id=1, source_target_pairs={{0,2},{1,3},{2,0},{3,1},{4,6},{5,7},{6,4},{7,5},{8,10},{9,11},{10,... | collective-permute-start | bytes 208904 | tf_op jit(solution)/shard_map/ppermute | solution.py:797
  13.5 0.0 collective-permute-done.4.theirs
  13.5 0.1 merge.1
  13.6 1.4 %collective-permute-start.5 = (f32[64,256]{1,0:T(8,128)S(1)}, f32[64,256]{1,0:T(8,128)S(1)}, u32[]{:S(2)}, u32[]{:S(2)}) collective-permute-start(f32[64,256]{1,0:T(8,128)S(1)} %get-tuple-element.43.mine), channel_id=1, source_target_pairs={{0,2},{1,3},{2,0},{3,1},{4,6},{5,7},{6,4},{7,5},{8,10},{9,11},{10,... | collective-permute-start | bytes 196616 | tf_op jit(solution)/shard_map/ppermute | solution.py:796
  15.0 1.4 %tends.1 = (f32[16,64,256]{2,1,0:T(8,128)}, f32[16,64,256]{2,1,0:T(8,128)}) custom-call(f32[16,8,256]{2,1,0:T(8,128)S(1)} %get-tuple-element.29.table.rest_1_, f32[2,16,64,256]{3,2,1,0:T(8,128)S(1)} %get-tuple-element.45.tend.rest_2_, f32[32,256]{1,0:T(8,128)S(1)} %collective-permute-done.2.far.rest_3_, f32[32,256]{1,0:T(8,128)S(1)} %collective-permute-done.1.near.rest_4_, ...), custom_call_target="tpu_custom_call" | custom-call | flops 262144 | bytes 2097152 | tf_op jit(solution)/shard_map/tends/pallas_call | solution.py:450
  16.4 0.3 %collective-permute-done.3.crossing.other.rest_0_ = f32[136,128]{1,0:T(8,128)S(1)} collective-permute-done((f32[136,128]{1,0:T(8,128)S(1)}, f32[136,128]{1,0:T(8,128)S(1)}, u32[]{:S(2)}, u32[]{:S(2)}) %collective-permute-start.3) | collective-permute-done | bytes 69664 | tf_op jit(solution)/shard_map/ppermute | solution.py:797
  16.7 0.6 %prepare.1 = (f32[2,16,64,256]{3,2,1,0:T(8,128)S(1)}, f32[16,8,256]{2,1,0:T(8,128)S(1)}, f32[128,128]{1,0:T(8,128)S(1)}) custom-call(f32[16,64,256]{2,1,0:T(8,128)S(1)} %copy-done, f32[16,64,256]{2,1,0:T(8,128)S(1)} %copy-done.1, f32[2,17,64,256]{3,2,1,0:T(8,128)S(1)} %get-tuple-element.30.forward, f32[16,8,256]{2,1,0:T(8,128)S(1)} %get-tuple-element.29.table.rest_1_, ...), custom_call_target="tpu_custom_call" | custom-call | flops 262144 | bytes 6291456 | tf_op jit(solution)/shard_map/prepare/pallas_call | solution.py:615
  17.3 0.1 collective-permute-start.7
  17.4 0.5 %collective-permute-done.5.theirs = f32[64,256]{1,0:T(8,128)S(1)} collective-permute-done((f32[64,256]{1,0:T(8,128)S(1)}, f32[64,256]{1,0:T(8,128)S(1)}, u32[]{:S(2)}, u32[]{:S(2)}) %collective-permute-start.5) | collective-permute-done | bytes 65568 | tf_op jit(solution)/shard_map/ppermute | solution.py:796
  18.0 0.1 collective-permute-start.6
  18.1 1.1 %finish.2 = (f32[16,64,256]{2,1,0:T(8,128)}, f32[16,64,256]{2,1,0:T(8,128)}, f32[16,64,256]{2,1,0:T(8,128)}, f32[16,64,256]{2,1,0:T(8,128)}) custom-call(f32[2,16,64,256]{3,2,1,0:T(8,128)S(1)} %get-tuple-element.41.known, f32[16,8,256]{2,1,0:T(8,128)S(1)} %get-tuple-element.42.response, ...), custom_call_target="tpu_custom_call", output_to_operand_aliasing={{2}: (8, {}), {3}: (9, {})} | custom-call | flops 5242880000 | bytes 2097152 | tf_op jit(solution)/shard_map/finish/pallas_call | solution.py:736
  19.2 0.0 collective-permute-done.7.rest_0_
  19.2 0.2 collective-permute-done.6.joined
  19.3 1.1 %finish.3 = (f32[16,64,256]{2,1,0:T(8,128)}, f32[16,64,256]{2,1,0:T(8,128)}, f32[16,64,256]{2,1,0:T(8,128)}, f32[16,64,256]{2,1,0:T(8,128)}) custom-call(f32[2,16,64,256]{3,2,1,0:T(8,128)S(1)} %get-tuple-element.41.known, f32[16,8,256]{2,1,0:T(8,128)S(1)} %get-tuple-element.42.response, ...), custom_call_target="tpu_custom_call", output_to_operand_aliasing={{0}: (8, {}), {1}: (9, {}), {2}: (10, {}), {3}: (11, {})} | custom-call | flops 5242880000 | bytes 2097152 | tf_op jit(solution)/shard_map/finish/pallas_call | solution.py:736
  (13 shorter events, 0.1 us)
Async XLA Ops:
  0.6 8.0 %copy-start.1 = (f32[16,64,256]{2,1,0:T(8,128)S(1)}, f32[16,64,256]{2,1,0:T(8,128)}, u32[]{:S(2)}) copy-start(f32[16,64,256]{2,1,0:T(8,128)} %w_vel.5) | copy-start | bytes 3145732
  0.6 8.0 %copy-start = (f32[16,64,256]{2,1,0:T(8,128)S(1)}, f32[16,64,256]{2,1,0:T(8,128)}, u32[]{:S(2)}) copy-start(f32[16,64,256]{2,1,0:T(8,128)} %temp.5) | copy-start | bytes 3145732
  0.7 8.0 %copy-start.5 = (f32[16,64,256]{2,1,0:T(8,128)S(1)}, f32[16,64,256]{2,1,0:T(8,128)}, u32[]{:S(2)}) copy-start(f32[16,64,256]{2,1,0:T(8,128)} %w_prev.3) | copy-start | bytes 3145732
  0.7 8.0 %copy-start.4 = (f32[16,64,256]{2,1,0:T(8,128)S(1)}, f32[16,64,256]{2,1,0:T(8,128)}, u32[]{:S(2)}) copy-start(f32[16,64,256]{2,1,0:T(8,128)} %temp_prev.3) | copy-start | bytes 3145732
  0.7 8.0 %copy-start.3 = (f32[16,64,256]{2,1,0:T(8,128)S(1)}, f32[16,64,256]{2,1,0:T(8,128)}, u32[]{:S(2)}) copy-start(f32[16,64,256]{2,1,0:T(8,128)} %v_vel.3) | copy-start | bytes 3145732
  0.7 8.0 %copy-start.2 = (f32[16,64,256]{2,1,0:T(8,128)S(1)}, f32[16,64,256]{2,1,0:T(8,128)}, u32[]{:S(2)}) copy-start(f32[16,64,256]{2,1,0:T(8,128)} %u_vel.3) | copy-start | bytes 3145732
  2.0 6.7 %collective-permute-start = (f32[200,256]{1,0:T(8,128)S(1)}, f32[200,256]{1,0:T(8,128)S(1)}, u32[]{:S(2)}, u32[]{:S(2)}) collective-permute-start(f32[200,256]{1,0:T(8,128)S(1)} %get-tuple-element.28.fluxes.own), channel_id=1, source_target_pairs={{0,1},{2,3},{1,0},{3,2},{4,5},{6,7},{5,4},{7,6},{8,9},{10,11},{9,8... | collective-permute-start | bytes 614408 | tf_op jit(solution)/shard_map/ppermute | solution.py:771
  2.5 9.0 %collective-permute-start.1 = (f32[32,256]{1,0:T(8,128)S(1)}, f32[32,256]{1,0:T(8,128)S(1)}, u32[]{:S(2)}, u32[]{:S(2)}) collective-permute-start(f32[32,256]{1,0:T(8,128)S(1)} %get-tuple-element.31), channel_id=1, source_target_pairs={{0,4},{8,12},{16,20},{24,28},{4,0},{12,8},{20,16},{28,24},{1,5},{9... | collective-permute-start | bytes 98312 | tf_op jit(solution)/shard_map/ppermute | solution.py:772
  5.1 6.6 %collective-permute-start.2 = (f32[32,256]{1,0:T(8,128)S(1)}, f32[32,256]{1,0:T(8,128)S(1)}, u32[]{:S(2)}, u32[]{:S(2)}) collective-permute-start(f32[32,256]{1,0:T(8,128)S(1)} %get-tuple-element.32), channel_id=1, source_target_pairs={{4,8},{12,16},{20,24},{28,0},{8,4},{16,12},{24,20},{0,28},{5,9},{1... | collective-permute-start | bytes 98312 | tf_op jit(solution)/shard_map/ppermute | solution.py:773
  11.9 1.6 %collective-permute-start.4 = (f32[192,256]{1,0:T(8,128)S(1)}, f32[192,256]{1,0:T(8,128)S(1)}, u32[]{:S(2)}, u32[]{:S(2)}) collective-permute-start(f32[192,256]{1,0:T(8,128)S(1)} %get-tuple-element.38), channel_id=1, source_target_pairs={{0,1},{1,0},{2,3},{3,2},{4,5},{5,4},{6,7},{7,6},{8,9},{9,8},{10,11... | collective-permute-start | bytes 589832 | tf_op jit(solution)/shard_map/ppermute | solution.py:786
  12.0 4.7 %collective-permute-start.3 = (f32[136,128]{1,0:T(8,128)S(1)}, f32[136,128]{1,0:T(8,128)S(1)}, u32[]{:S(2)}, u32[]{:S(2)}) collective-permute-start(f32[136,128]{1,0:T(8,128)S(1)} %get-tuple-element.36.own), channel_id=1, source_target_pairs={{0,2},{1,3},{2,0},{3,1},{4,6},{5,7},{6,4},{7,5},{8,10},{9,11},{10,... | collective-permute-start | bytes 208904 | tf_op jit(solution)/shard_map/ppermute | solution.py:797
  13.6 4.3 %collective-permute-start.5 = (f32[64,256]{1,0:T(8,128)S(1)}, f32[64,256]{1,0:T(8,128)S(1)}, u32[]{:S(2)}, u32[]{:S(2)}) collective-permute-start(f32[64,256]{1,0:T(8,128)S(1)} %get-tuple-element.43.mine), channel_id=1, source_target_pairs={{0,2},{1,3},{2,0},{3,1},{4,6},{5,7},{6,4},{7,5},{8,10},{9,11},{10,... | collective-permute-start | bytes 196616 | tf_op jit(solution)/shard_map/ppermute | solution.py:796
  17.3 1.8 %collective-permute-start.7 = (f32[128,128]{1,0:T(8,128)S(1)}, f32[128,128]{1,0:T(8,128)S(1)}, u32[]{:S(2)}, u32[]{:S(2)}) collective-permute-start(f32[128,128]{1,0:T(8,128)S(1)} %get-tuple-element.44), channel_id=1, source_target_pairs={{0,1},{2,3},{1,0},{3,2},{4,5},{6,7},{5,4},{7,6},{8,9},{10,11},{9,8... | collective-permute-start | bytes 196616 | tf_op jit(solution)/shard_map/ppermute | solution.py:808
  18.0 1.3 %collective-permute-start.6 = (f32[64,256]{1,0:T(8,128)S(1)}, f32[64,256]{1,0:T(8,128)S(1)}, u32[]{:S(2)}, u32[]{:S(2)}) collective-permute-start(f32[64,256]{1,0:T(8,128)S(1)} %join.1.joined), channel_id=1, source_target_pairs={{0,1},{2,3},{1,0},{3,2},{4,5},{6,7},{5,4},{7,6},{8,9},{10,11},{9,8... | collective-permute-start | bytes 196616 | tf_op jit(solution)/shard_map/ppermute | solution.py:804

commit v12 on v11

--- a/solution.py
+++ b/solution.py
@@ -168,7 +168,6 @@
 
 
 def bulk_kernel(
-    arrived,
     table,
     temp,
     u_vel,
@@ -253,7 +252,7 @@
     lax.fori_loop(0, levels // 2, pair_step, 0)
 
 
-def bulk(arrived, table, *arrays):
+def bulk(table, *arrays):
     levels, rows, cols = arrays[0].shape
     return pl.pallas_call(
         bulk_kernel,
@@ -262,7 +261,7 @@
             held(2, levels, rows, cols),
             held(2, rows, cols),
         ),
-        in_specs=[whole(pl.ANY)] + [whole(VMEM)] * 7,
+        in_specs=[whole(VMEM)] * 7,
         out_specs=[whole(VMEM)] * 3,
         compiler_params=pltpu.CompilerParams(vmem_limit_bytes=8 * MIB),
         cost_estimate=pl.CostEstimate(
@@ -271,7 +270,7 @@
             transcendentals=0,
         ),
         name="bulk",
-    )(arrived, *map(in_vmem, (table, *arrays)))
+    )(*map(in_vmem, (table, *arrays)))
 
 
 def side_changes(far, near):
@@ -336,7 +335,7 @@
 
 
 def fix_kernel(
-    rounds, levels, other, near, far, fluxes, outward, forward, first, table, *rest
+    rounds, levels, near, far, other, fluxes, outward, forward, first, table, *rest
 ):
     outer, rest = (rest[0], rest[1:]) if rounds > 2 else (None, rest)
     entries, changes, *late = rest
@@ -390,7 +389,7 @@
             seam[pl.ds(2 * rows + at, 1), :] = value[:, : cols // 2]
 
 
-def fix(rounds, other, near, far, fluxes, outward, forward, first, table, outer):
+def fix(rounds, near, far, other, fluxes, outward, forward, first, table, outer):
     levels = table.shape[0]
     _, rows, cols = first.shape
     shapes = [held(4 * rows, cols), held(4 * levels, cols)]
@@ -404,7 +403,7 @@
         compiler_params=pltpu.CompilerParams(vmem_limit_bytes=8 * MIB),
         name="fix",
     )(
-        other, near, far, fluxes, outward, in_vmem(forward), in_vmem(first), in_vmem(table), *outer
+        near, far, other, fluxes, outward, in_vmem(forward), in_vmem(first), in_vmem(table), *outer
     )
 
 
@@ -768,16 +767,16 @@
     far, near, fluxes, outward, table = edges(
         temp, u_vel, w_vel, v_vel, temp_prev, w_prev, lower, upper, metric
     )
-    other = lax.ppermute(fluxes, "gz", cores)
     near = lax.ppermute(near, "gx", both_ways([(i, i + 1) for i in range(0, across, 2)]))
     far = lax.ppermute(far, "gx", both_ways([(i, (i + 1) % across) for i in range(1, across, 2)]))
+    other = lax.ppermute(fluxes, "gz", cores)
     outer = ()
     if rounds > 2:
         seams = both_ways([(i, i + 1) for i in range(1, stacked - 1, 2)])
         outer = (lax.ppermute(outward, "gz", seams),)
-    forward, tend, first = bulk(other, table, temp, u_vel, v_vel, w_vel, temp_prev, w_prev)
+    forward, tend, first = bulk(table, temp, u_vel, v_vel, w_vel, temp_prev, w_prev)
     entries, changes, *late = fix(
-        rounds, other, near, far, fluxes, outward, forward, first, table, outer
+        rounds, near, far, other, fluxes, outward, forward, first, table, outer
     )
     message, seam = late if late else (entries, fluxes)
     bases, gains, own, other_own = [], [], fluxes, other

time: 20.6 us -> 20.5 us (level)
  waiting for transfers between devices: 1.21 us -> 1.44 us
    ppermute x1, starting transfers between devices: 0.52 us -> 0.01 us  [local(): other = lax.ppermute(fluxes, 'gz', cores)]
    ppermute x1, starting transfers between devices: 2.59 us -> 3.03 us  [local(): lax.ppermute(near, 'gx', both_ways([(i, i + 1) for i in range(0, across,...]
  transfers between devices with their start and end apart: 8 -> 8, of which waited for: 4 -> 4; matrix products, arithmetic and copies ran while one was open for 0% -> 0% of each run, Pallas kernels for 29% -> 28%
where the time goes in v12:
time: 20.5 us; the launch traced here: 20.4 us
  starting transfers between devices  9.78 us (48%)
  Pallas kernels  8.34 us (41%)
  waiting for transfers between devices  1.44 us (7%)
  between operations  0.8 us (4%)
    ppermute x1, starting transfers between devices, local(): lax.ppermute(far, 'gx', both_ways([(i, (i + 1) % across) for i in range(1...  3.54 us
    ppermute x1, starting transfers between devices, local(): lax.ppermute(near, 'gx', both_ways([(i, i + 1) for i in range(0, across,...  3.03 us
    pallas_call x1, Pallas kernels, bulk(): pl.pallas_call(bulk_kernel, out_shape=(held(2, levels + 1, rows, cols), h...  2.6 us
    pallas_call x2, Pallas kernels, finish(): pl.pallas_call(functools.partial(finish_kernel, rounds, swapped), out_sha...  2.14 us
    ppermute x2, starting transfers between devices, local(): theirs = lax.ppermute(message, 'gz', partners)  1.54 us
    ppermute x1, starting transfers between devices, local(): other_own = lax.ppermute(own, 'gz', partners)  1.52 us
    pallas_call x1, Pallas kernels, tends(): pl.pallas_call(functools.partial(tends_kernel, rounds), out_shape=(jax.Sh...  1.38 us
    pallas_call x1, Pallas kernels, edges(): pl.pallas_call(edges_kernel, out_shape=(held(2 * levels, cols), held(2 *...  1.31 us
  transfers between devices with their start and end apart: 8, of which 4 were waited for; matrix products, arithmetic and copies ran while one was open for 0% of the time, Pallas kernels for 28%

profile of v12, /device:TPU:0, one launch (start us, length us, event | category | flops | bytes accessed | tf_op | source)
XLA Modules:
  0.0 20.4 jit_solution(16967825622730485814)
XLA Ops:
  0.7 1.3 %edges.1 = (f32[32,256]{1,0:T(8,128)S(1)}, f32[32,256]{1,0:T(8,128)S(1)}, f32[200,256]{1,0:T(8,128)S(1)}, f32[128,256]{1,0:T(8,128)S(1)}, f32[16,8,256]{2,1,0:T(8,128)S(1)}) custom-call(f32[16,64,256]{2,1,0:T(8,128)} %temp.5, f32[16,64,256]{2,1,0:T(8,128)} %u_vel.3, f32[16,64,256]{2,1,0:T(8,128)} %w_vel.5, f32[16,64,256]{2,1,0:T(8,128)} %v_vel.3, ...), custom_call_target="tpu_custom_call" | custom-call | tf_op jit(solution)/shard_map/edges/pallas_call | solution.py:107
  2.0 3.0 %collective-permute-start = (f32[32,256]{1,0:T(8,128)S(1)}, f32[32,256]{1,0:T(8,128)S(1)}, u32[]{:S(2)}, u32[]{:S(2)}) collective-permute-start(f32[32,256]{1,0:T(8,128)S(1)} %get-tuple-element.30), channel_id=1, source_target_pairs={{0,4},{8,12},{16,20},{24,28},{4,0},{12,8},{20,16},{28,24},{1,5},{9... | collective-permute-start | bytes 98312 | tf_op jit(solution)/shard_map/ppermute | solution.py:770
  5.0 3.5 %collective-permute-start.1 = (f32[32,256]{1,0:T(8,128)S(1)}, f32[32,256]{1,0:T(8,128)S(1)}, u32[]{:S(2)}, u32[]{:S(2)}) collective-permute-start(f32[32,256]{1,0:T(8,128)S(1)} %get-tuple-element.31), channel_id=1, source_target_pairs={{4,8},{12,16},{20,24},{28,0},{8,4},{16,12},{24,20},{0,28},{5,9},{1... | collective-permute-start | bytes 98312 | tf_op jit(solution)/shard_map/ppermute | solution.py:771
  8.6 0.0 collective-permute-start.2
  8.6 2.6 %bulk.1 = (f32[2,17,64,256]{3,2,1,0:T(8,128)S(1)}, f32[2,16,64,256]{3,2,1,0:T(8,128)S(1)}, f32[2,64,256]{2,1,0:T(8,128)S(1)}) custom-call(f32[16,8,256]{2,1,0:T(8,128)S(1)} %get-tuple-element.28.table.rest_1_, f32[16,64,256]{2,1,0:T(8,128)S(1)} %copy-done, f32[16,64,256]{2,1,0:T(8,128)S(1)} %copy-done.2, f32[16,64,256]{2,1,0:T(8,128)S(1)} %copy-done.3, ...), custom_call_target="tpu_custom_call" | custom-call | flops 26214400000 | bytes 6291456 | tf_op jit(solution)/shard_map/bulk/pallas_call | solution.py:257
  11.2 0.0 collective-permute-done.near.rest_4_
  11.3 0.4 %collective-permute-done.1.far.rest_3_ = f32[32,256]{1,0:T(8,128)S(1)} collective-permute-done((f32[32,256]{1,0:T(8,128)S(1)}, f32[32,256]{1,0:T(8,128)S(1)}, u32[]{:S(2)}, u32[]{:S(2)}) %collective-permute-start.1) | collective-permute-done | bytes 32800 | tf_op jit(solution)/shard_map/ppermute | solution.py:771
  11.7 0.0 collective-permute-done.2.other
  11.7 0.2 fix.1
  11.8 0.2 collective-permute-start.4
  12.0 1.5 %collective-permute-start.3 = (f32[136,128]{1,0:T(8,128)S(1)}, f32[136,128]{1,0:T(8,128)S(1)}, u32[]{:S(2)}, u32[]{:S(2)}) collective-permute-start(f32[136,128]{1,0:T(8,128)S(1)} %get-tuple-element.36.own), channel_id=1, source_target_pairs={{0,2},{1,3},{2,0},{3,1},{4,6},{5,7},{6,4},{7,5},{8,10},{9,11},{10,... | collective-permute-start | bytes 208904 | tf_op jit(solution)/shard_map/ppermute | solution.py:796
  13.5 0.0 collective-permute-done.4.theirs
  13.5 0.1 merge.1
  13.6 1.4 %collective-permute-start.5 = (f32[64,256]{1,0:T(8,128)S(1)}, f32[64,256]{1,0:T(8,128)S(1)}, u32[]{:S(2)}, u32[]{:S(2)}) collective-permute-start(f32[64,256]{1,0:T(8,128)S(1)} %get-tuple-element.43.mine), channel_id=1, source_target_pairs={{0,2},{1,3},{2,0},{3,1},{4,6},{5,7},{6,4},{7,5},{8,10},{9,11},{10,... | collective-permute-start | bytes 196616 | tf_op jit(solution)/shard_map/ppermute | solution.py:795
  15.0 1.4 %tends.1 = (f32[16,64,256]{2,1,0:T(8,128)}, f32[16,64,256]{2,1,0:T(8,128)}) custom-call(f32[16,8,256]{2,1,0:T(8,128)S(1)} %get-tuple-element.28.table.rest_1_, f32[2,16,64,256]{3,2,1,0:T(8,128)S(1)} %get-tuple-element.45.tend.rest_2_, f32[32,256]{1,0:T(8,128)S(1)} %collective-permute-done.1.far.rest_3_, f32[32,256]{1,0:T(8,128)S(1)} %collective-permute-done.near.rest_4_, ...), custom_call_target="tpu_custom_call" | custom-call | flops 262144 | bytes 2097152 | tf_op jit(solution)/shard_map/tends/pallas_call | solution.py:449
  16.4 0.3 %collective-permute-done.3.crossing.other.rest_0_ = f32[136,128]{1,0:T(8,128)S(1)} collective-permute-done((f32[136,128]{1,0:T(8,128)S(1)}, f32[136,128]{1,0:T(8,128)S(1)}, u32[]{:S(2)}, u32[]{:S(2)}) %collective-permute-start.3) | collective-permute-done | bytes 69664 | tf_op jit(solution)/shard_map/ppermute | solution.py:796
  16.6 0.6 %prepare.1 = (f32[2,16,64,256]{3,2,1,0:T(8,128)S(1)}, f32[16,8,256]{2,1,0:T(8,128)S(1)}, f32[128,128]{1,0:T(8,128)S(1)}) custom-call(f32[16,64,256]{2,1,0:T(8,128)S(1)} %copy-done, f32[16,64,256]{2,1,0:T(8,128)S(1)} %copy-done.1, f32[2,17,64,256]{3,2,1,0:T(8,128)S(1)} %get-tuple-element.29.forward, f32[16,8,256]{2,1,0:T(8,128)S(1)} %get-tuple-element.28.table.rest_1_, ...), custom_call_target="tpu_custom_call" | custom-call | flops 262144 | bytes 6291456 | tf_op jit(solution)/shard_map/prepare/pallas_call | solution.py:614
  17.3 0.1 collective-permute-start.7
  17.3 0.6 %collective-permute-done.5.theirs = f32[64,256]{1,0:T(8,128)S(1)} collective-permute-done((f32[64,256]{1,0:T(8,128)S(1)}, f32[64,256]{1,0:T(8,128)S(1)}, u32[]{:S(2)}, u32[]{:S(2)}) %collective-permute-start.5) | collective-permute-done | bytes 65568 | tf_op jit(solution)/shard_map/ppermute | solution.py:795
  18.0 0.1 collective-permute-start.6
  18.1 1.1 %finish.2 = (f32[16,64,256]{2,1,0:T(8,128)}, f32[16,64,256]{2,1,0:T(8,128)}, f32[16,64,256]{2,1,0:T(8,128)}, f32[16,64,256]{2,1,0:T(8,128)}) custom-call(f32[2,16,64,256]{3,2,1,0:T(8,128)S(1)} %get-tuple-element.41.known, f32[16,8,256]{2,1,0:T(8,128)S(1)} %get-tuple-element.42.response, ...), custom_call_target="tpu_custom_call", output_to_operand_aliasing={{2}: (8, {}), {3}: (9, {})} | custom-call | flops 5242880000 | bytes 2097152 | tf_op jit(solution)/shard_map/finish/pallas_call | solution.py:735
  19.2 0.0 collective-permute-done.7.rest_0_
  19.2 0.2 collective-permute-done.6.joined
  19.3 1.1 %finish.3 = (f32[16,64,256]{2,1,0:T(8,128)}, f32[16,64,256]{2,1,0:T(8,128)}, f32[16,64,256]{2,1,0:T(8,128)}, f32[16,64,256]{2,1,0:T(8,128)}) custom-call(f32[2,16,64,256]{3,2,1,0:T(8,128)S(1)} %get-tuple-element.41.known, f32[16,8,256]{2,1,0:T(8,128)S(1)} %get-tuple-element.42.response, ...), custom_call_target="tpu_custom_call", output_to_operand_aliasing={{0}: (8, {}), {1}: (9, {}), {2}: (10, {}), {3}: (11, {})} | custom-call | flops 5242880000 | bytes 2097152 | tf_op jit(solution)/shard_map/finish/pallas_call | solution.py:735
  (13 shorter events, 0.1 us)
Async XLA Ops:
  0.6 8.0 %copy-start.1 = (f32[16,64,256]{2,1,0:T(8,128)S(1)}, f32[16,64,256]{2,1,0:T(8,128)}, u32[]{:S(2)}) copy-start(f32[16,64,256]{2,1,0:T(8,128)} %w_vel.5) | copy-start | bytes 3145732
  0.6 8.0 %copy-start = (f32[16,64,256]{2,1,0:T(8,128)S(1)}, f32[16,64,256]{2,1,0:T(8,128)}, u32[]{:S(2)}) copy-start(f32[16,64,256]{2,1,0:T(8,128)} %temp.5) | copy-start | bytes 3145732
  0.7 7.9 %copy-start.5 = (f32[16,64,256]{2,1,0:T(8,128)S(1)}, f32[16,64,256]{2,1,0:T(8,128)}, u32[]{:S(2)}) copy-start(f32[16,64,256]{2,1,0:T(8,128)} %w_prev.3) | copy-start | bytes 3145732
  0.7 7.9 %copy-start.4 = (f32[16,64,256]{2,1,0:T(8,128)S(1)}, f32[16,64,256]{2,1,0:T(8,128)}, u32[]{:S(2)}) copy-start(f32[16,64,256]{2,1,0:T(8,128)} %temp_prev.3) | copy-start | bytes 3145732
  0.7 7.9 %copy-start.3 = (f32[16,64,256]{2,1,0:T(8,128)S(1)}, f32[16,64,256]{2,1,0:T(8,128)}, u32[]{:S(2)}) copy-start(f32[16,64,256]{2,1,0:T(8,128)} %v_vel.3) | copy-start | bytes 3145732
  0.7 7.9 %copy-start.2 = (f32[16,64,256]{2,1,0:T(8,128)S(1)}, f32[16,64,256]{2,1,0:T(8,128)}, u32[]{:S(2)}) copy-start(f32[16,64,256]{2,1,0:T(8,128)} %u_vel.3) | copy-start | bytes 3145732
  2.0 9.2 %collective-permute-start = (f32[32,256]{1,0:T(8,128)S(1)}, f32[32,256]{1,0:T(8,128)S(1)}, u32[]{:S(2)}, u32[]{:S(2)}) collective-permute-start(f32[32,256]{1,0:T(8,128)S(1)} %get-tuple-element.30), channel_id=1, source_target_pairs={{0,4},{8,12},{16,20},{24,28},{4,0},{12,8},{20,16},{28,24},{1,5},{9... | collective-permute-start | bytes 98312 | tf_op jit(solution)/shard_map/ppermute | solution.py:770
  5.0 6.6 %collective-permute-start.1 = (f32[32,256]{1,0:T(8,128)S(1)}, f32[32,256]{1,0:T(8,128)S(1)}, u32[]{:S(2)}, u32[]{:S(2)}) collective-permute-start(f32[32,256]{1,0:T(8,128)S(1)} %get-tuple-element.31), channel_id=1, source_target_pairs={{4,8},{12,16},{20,24},{28,0},{8,4},{16,12},{24,20},{0,28},{5,9},{1... | collective-permute-start | bytes 98312 | tf_op jit(solution)/shard_map/ppermute | solution.py:771
  8.6 3.1 %collective-permute-start.2 = (f32[200,256]{1,0:T(8,128)S(1)}, f32[200,256]{1,0:T(8,128)S(1)}, u32[]{:S(2)}, u32[]{:S(2)}) collective-permute-start(f32[200,256]{1,0:T(8,128)S(1)} %get-tuple-element.32.fluxes.own), channel_id=1, source_target_pairs={{0,1},{2,3},{1,0},{3,2},{4,5},{6,7},{5,4},{7,6},{8,9},{10,11},{9,8... | collective-permute-start | bytes 614408 | tf_op jit(solution)/shard_map/ppermute | solution.py:772
  11.8 1.7 %collective-permute-start.4 = (f32[192,256]{1,0:T(8,128)S(1)}, f32[192,256]{1,0:T(8,128)S(1)}, u32[]{:S(2)}, u32[]{:S(2)}) collective-permute-start(f32[192,256]{1,0:T(8,128)S(1)} %get-tuple-element.38), channel_id=1, source_target_pairs={{0,1},{1,0},{2,3},{3,2},{4,5},{5,4},{6,7},{7,6},{8,9},{9,8},{10,11... | collective-permute-start | bytes 589832 | tf_op jit(solution)/shard_map/ppermute | solution.py:785
  12.0 4.6 %collective-permute-start.3 = (f32[136,128]{1,0:T(8,128)S(1)}, f32[136,128]{1,0:T(8,128)S(1)}, u32[]{:S(2)}, u32[]{:S(2)}) collective-permute-start(f32[136,128]{1,0:T(8,128)S(1)} %get-tuple-element.36.own), channel_id=1, source_target_pairs={{0,2},{1,3},{2,0},{3,1},{4,6},{5,7},{6,4},{7,5},{8,10},{9,11},{10,... | collective-permute-start | bytes 208904 | tf_op jit(solution)/shard_map/ppermute | solution.py:796
  13.6 4.3 %collective-permute-start.5 = (f32[64,256]{1,0:T(8,128)S(1)}, f32[64,256]{1,0:T(8,128)S(1)}, u32[]{:S(2)}, u32[]{:S(2)}) collective-permute-start(f32[64,256]{1,0:T(8,128)S(1)} %get-tuple-element.43.mine), channel_id=1, source_target_pairs={{0,2},{1,3},{2,0},{3,1},{4,6},{5,7},{6,4},{7,5},{8,10},{9,11},{10,... | collective-permute-start | bytes 196616 | tf_op jit(solution)/shard_map/ppermute | solution.py:795
  17.3 1.9 %collective-permute-start.7 = (f32[128,128]{1,0:T(8,128)S(1)}, f32[128,128]{1,0:T(8,128)S(1)}, u32[]{:S(2)}, u32[]{:S(2)}) collective-permute-start(f32[128,128]{1,0:T(8,128)S(1)} %get-tuple-element.44), channel_id=1, source_target_pairs={{0,1},{2,3},{1,0},{3,2},{4,5},{6,7},{5,4},{7,6},{8,9},{10,11},{9,8... | collective-permute-start | bytes 196616 | tf_op jit(solution)/shard_map/ppermute | solution.py:807
  18.0 1.3 %collective-permute-start.6 = (f32[64,256]{1,0:T(8,128)S(1)}, f32[64,256]{1,0:T(8,128)S(1)}, u32[]{:S(2)}, u32[]{:S(2)}) collective-permute-start(f32[64,256]{1,0:T(8,128)S(1)} %join.1.joined), channel_id=1, source_target_pairs={{0,1},{2,3},{1,0},{3,2},{4,5},{6,7},{5,4},{7,6},{8,9},{10,11},{9,8... | collective-permute-start | bytes 196616 | tf_op jit(solution)/shard_map/ppermute | solution.py:803

commit v13 on v12

--- a/solution.py
+++ b/solution.py
@@ -65,21 +65,24 @@
     sems,
 ):
     levels, rows, cols = temp.shape
-    copies = [(lower, lower_at), (upper, upper_at), (metric, metric_at)]
+    copies = []
     for at, array in enumerate((temp, w_vel, u_vel)):
         for side, row in enumerate((0, rows - 1)):
             copies.append((array.at[:, row, :], strips.at[at, side]))
+    needed = range(len(copies), len(copies) + 3)
+    copies += [(lower, lower_at), (upper, upper_at), (metric, metric_at)]
     for at, array in enumerate((temp, w_vel)):
         for side, level in enumerate((0, levels - 1)):
             copies.append((array.at[level], layers.at[at, side]))
     copies = [pltpu.make_async_copy(src, dst, sems.at[i]) for i, (src, dst) in enumerate(copies)]
     for copy in copies:
         copy.start()
-    for copy in copies[:3]:
-        copy.wait()
+    for i in needed:
+        copies[i].wait()
     coefficients(lower_at, upper_at, metric_at, table, fluxes.at[pl.ds(3 * rows, TILE)])
-    for copy in copies[3:]:
-        copy.wait()
+    for i, copy in enumerate(copies):
+        if i not in needed:
+            copy.wait()
     odd = bit_of("gx", 0) == 1
     for field in range(2):
         at = pl.ds(field * levels, levels)

time: 20.5 us -> 20.5 us (level)
  no operation moved by 1% of the time
where the time goes in v13:
time: 20.5 us; the launch traced here: 20.4 us
  starting transfers between devices  9.78 us (48%)
  Pallas kernels  8.34 us (41%)
  waiting for transfers between devices  1.44 us (7%)
  between operations  0.8 us (4%)
    ppermute x1, starting transfers between devices, local(): lax.ppermute(far, 'gx', both_ways([(i, (i + 1) % across) for i in range(1...  3.54 us
    ppermute x1, starting transfers between devices, local(): lax.ppermute(near, 'gx', both_ways([(i, i + 1) for i in range(0, across,...  3.03 us
    pallas_call x1, Pallas kernels, bulk(): pl.pallas_call(bulk_kernel, out_shape=(held(2, levels + 1, rows, cols), h...  2.6 us
    pallas_call x2, Pallas kernels, finish(): pl.pallas_call(functools.partial(finish_kernel, rounds, swapped), out_sha...  2.14 us
    ppermute x2, starting transfers between devices, local(): theirs = lax.ppermute(message, 'gz', partners)  1.54 us
    ppermute x1, starting transfers between devices, local(): other_own = lax.ppermute(own, 'gz', partners)  1.52 us
    pallas_call x1, Pallas kernels, tends(): pl.pallas_call(functools.partial(tends_kernel, rounds), out_shape=(jax.Sh...  1.38 us
    pallas_call x1, Pallas kernels, edges(): pl.pallas_call(edges_kernel, out_shape=(held(2 * levels, cols), held(2 *...  1.31 us
  transfers between devices with their start and end apart: 8, of which 4 were waited for; matrix products, arithmetic and copies ran while one was open for 0% of the time, Pallas kernels for 28%

profile of v13, /device:TPU:0, one launch (start us, length us, event | category | flops | bytes accessed | tf_op | source)
XLA Modules:
  0.0 20.4 jit_solution(6284293190077890659)
XLA Ops:
  0.7 1.3 %edges.1 = (f32[32,256]{1,0:T(8,128)S(1)}, f32[32,256]{1,0:T(8,128)S(1)}, f32[200,256]{1,0:T(8,128)S(1)}, f32[128,256]{1,0:T(8,128)S(1)}, f32[16,8,256]{2,1,0:T(8,128)S(1)}) custom-call(f32[16,64,256]{2,1,0:T(8,128)} %temp.5, f32[16,64,256]{2,1,0:T(8,128)} %u_vel.3, f32[16,64,256]{2,1,0:T(8,128)} %w_vel.5, f32[16,64,256]{2,1,0:T(8,128)} %v_vel.3, ...), custom_call_target="tpu_custom_call" | custom-call | tf_op jit(solution)/shard_map/edges/pallas_call | solution.py:110
  2.0 3.0 %collective-permute-start = (f32[32,256]{1,0:T(8,128)S(1)}, f32[32,256]{1,0:T(8,128)S(1)}, u32[]{:S(2)}, u32[]{:S(2)}) collective-permute-start(f32[32,256]{1,0:T(8,128)S(1)} %get-tuple-element.30), channel_id=1, source_target_pairs={{0,4},{8,12},{16,20},{24,28},{4,0},{12,8},{20,16},{28,24},{1,5},{9... | collective-permute-start | bytes 98312 | tf_op jit(solution)/shard_map/ppermute | solution.py:773
  5.0 3.5 %collective-permute-start.1 = (f32[32,256]{1,0:T(8,128)S(1)}, f32[32,256]{1,0:T(8,128)S(1)}, u32[]{:S(2)}, u32[]{:S(2)}) collective-permute-start(f32[32,256]{1,0:T(8,128)S(1)} %get-tuple-element.31), channel_id=1, source_target_pairs={{4,8},{12,16},{20,24},{28,0},{8,4},{16,12},{24,20},{0,28},{5,9},{1... | collective-permute-start | bytes 98312 | tf_op jit(solution)/shard_map/ppermute | solution.py:774
  8.6 0.0 collective-permute-start.2
  8.6 2.6 %bulk.1 = (f32[2,17,64,256]{3,2,1,0:T(8,128)S(1)}, f32[2,16,64,256]{3,2,1,0:T(8,128)S(1)}, f32[2,64,256]{2,1,0:T(8,128)S(1)}) custom-call(f32[16,8,256]{2,1,0:T(8,128)S(1)} %get-tuple-element.28.table.rest_1_, f32[16,64,256]{2,1,0:T(8,128)S(1)} %copy-done, f32[16,64,256]{2,1,0:T(8,128)S(1)} %copy-done.2, f32[16,64,256]{2,1,0:T(8,128)S(1)} %copy-done.3, ...), custom_call_target="tpu_custom_call" | custom-call | flops 26214400000 | bytes 6291456 | tf_op jit(solution)/shard_map/bulk/pallas_call | solution.py:260
  11.2 0.0 collective-permute-done.near.rest_4_
  11.3 0.4 %collective-permute-done.1.far.rest_3_ = f32[32,256]{1,0:T(8,128)S(1)} collective-permute-done((f32[32,256]{1,0:T(8,128)S(1)}, f32[32,256]{1,0:T(8,128)S(1)}, u32[]{:S(2)}, u32[]{:S(2)}) %collective-permute-start.1) | collective-permute-done | bytes 32800 | tf_op jit(solution)/shard_map/ppermute | solution.py:774
  11.7 0.0 collective-permute-done.2.other
  11.7 0.2 fix.1
  11.8 0.2 collective-permute-start.4
  12.0 1.5 %collective-permute-start.3 = (f32[136,128]{1,0:T(8,128)S(1)}, f32[136,128]{1,0:T(8,128)S(1)}, u32[]{:S(2)}, u32[]{:S(2)}) collective-permute-start(f32[136,128]{1,0:T(8,128)S(1)} %get-tuple-element.36.own), channel_id=1, source_target_pairs={{0,2},{1,3},{2,0},{3,1},{4,6},{5,7},{6,4},{7,5},{8,10},{9,11},{10,... | collective-permute-start | bytes 208904 | tf_op jit(solution)/shard_map/ppermute | solution.py:799
  13.5 0.0 collective-permute-done.4.theirs
  13.5 0.1 merge.1
  13.6 1.4 %collective-permute-start.5 = (f32[64,256]{1,0:T(8,128)S(1)}, f32[64,256]{1,0:T(8,128)S(1)}, u32[]{:S(2)}, u32[]{:S(2)}) collective-permute-start(f32[64,256]{1,0:T(8,128)S(1)} %get-tuple-element.43.mine), channel_id=1, source_target_pairs={{0,2},{1,3},{2,0},{3,1},{4,6},{5,7},{6,4},{7,5},{8,10},{9,11},{10,... | collective-permute-start | bytes 196616 | tf_op jit(solution)/shard_map/ppermute | solution.py:798
  15.0 1.4 %tends.1 = (f32[16,64,256]{2,1,0:T(8,128)}, f32[16,64,256]{2,1,0:T(8,128)}) custom-call(f32[16,8,256]{2,1,0:T(8,128)S(1)} %get-tuple-element.28.table.rest_1_, f32[2,16,64,256]{3,2,1,0:T(8,128)S(1)} %get-tuple-element.45.tend.rest_2_, f32[32,256]{1,0:T(8,128)S(1)} %collective-permute-done.1.far.rest_3_, f32[32,256]{1,0:T(8,128)S(1)} %collective-permute-done.near.rest_4_, ...), custom_call_target="tpu_custom_call" | custom-call | flops 262144 | bytes 2097152 | tf_op jit(solution)/shard_map/tends/pallas_call | solution.py:452
  16.4 0.3 %collective-permute-done.3.crossing.other.rest_0_ = f32[136,128]{1,0:T(8,128)S(1)} collective-permute-done((f32[136,128]{1,0:T(8,128)S(1)}, f32[136,128]{1,0:T(8,128)S(1)}, u32[]{:S(2)}, u32[]{:S(2)}) %collective-permute-start.3) | collective-permute-done | bytes 69664 | tf_op jit(solution)/shard_map/ppermute | solution.py:799
  16.6 0.6 %prepare.1 = (f32[2,16,64,256]{3,2,1,0:T(8,128)S(1)}, f32[16,8,256]{2,1,0:T(8,128)S(1)}, f32[128,128]{1,0:T(8,128)S(1)}) custom-call(f32[16,64,256]{2,1,0:T(8,128)S(1)} %copy-done, f32[16,64,256]{2,1,0:T(8,128)S(1)} %copy-done.1, f32[2,17,64,256]{3,2,1,0:T(8,128)S(1)} %get-tuple-element.29.forward, f32[16,8,256]{2,1,0:T(8,128)S(1)} %get-tuple-element.28.table.rest_1_, ...), custom_call_target="tpu_custom_call" | custom-call | flops 262144 | bytes 6291456 | tf_op jit(solution)/shard_map/prepare/pallas_call | solution.py:617
  17.3 0.1 collective-permute-start.7
  17.3 0.6 %collective-permute-done.5.theirs = f32[64,256]{1,0:T(8,128)S(1)} collective-permute-done((f32[64,256]{1,0:T(8,128)S(1)}, f32[64,256]{1,0:T(8,128)S(1)}, u32[]{:S(2)}, u32[]{:S(2)}) %collective-permute-start.5) | collective-permute-done | bytes 65568 | tf_op jit(solution)/shard_map/ppermute | solution.py:798
  18.0 0.1 collective-permute-start.6
  18.1 1.1 %finish.2 = (f32[16,64,256]{2,1,0:T(8,128)}, f32[16,64,256]{2,1,0:T(8,128)}, f32[16,64,256]{2,1,0:T(8,128)}, f32[16,64,256]{2,1,0:T(8,128)}) custom-call(f32[2,16,64,256]{3,2,1,0:T(8,128)S(1)} %get-tuple-element.41.known, f32[16,8,256]{2,1,0:T(8,128)S(1)} %get-tuple-element.42.response, ...), custom_call_target="tpu_custom_call", output_to_operand_aliasing={{2}: (8, {}), {3}: (9, {})} | custom-call | flops 5242880000 | bytes 2097152 | tf_op jit(solution)/shard_map/finish/pallas_call | solution.py:738
  19.2 0.0 collective-permute-done.7.rest_0_
  19.2 0.2 collective-permute-done.6.joined
  19.3 1.1 %finish.3 = (f32[16,64,256]{2,1,0:T(8,128)}, f32[16,64,256]{2,1,0:T(8,128)}, f32[16,64,256]{2,1,0:T(8,128)}, f32[16,64,256]{2,1,0:T(8,128)}) custom-call(f32[2,16,64,256]{3,2,1,0:T(8,128)S(1)} %get-tuple-element.41.known, f32[16,8,256]{2,1,0:T(8,128)S(1)} %get-tuple-element.42.response, ...), custom_call_target="tpu_custom_call", output_to_operand_aliasing={{0}: (8, {}), {1}: (9, {}), {2}: (10, {}), {3}: (11, {})} | custom-call | flops 5242880000 | bytes 2097152 | tf_op jit(solution)/shard_map/finish/pallas_call | solution.py:738
  (13 shorter events, 0.1 us)
Async XLA Ops:
  0.6 8.0 %copy-start.1 = (f32[16,64,256]{2,1,0:T(8,128)S(1)}, f32[16,64,256]{2,1,0:T(8,128)}, u32[]{:S(2)}) copy-start(f32[16,64,256]{2,1,0:T(8,128)} %w_vel.5) | copy-start | bytes 3145732
  0.6 8.0 %copy-start = (f32[16,64,256]{2,1,0:T(8,128)S(1)}, f32[16,64,256]{2,1,0:T(8,128)}, u32[]{:S(2)}) copy-start(f32[16,64,256]{2,1,0:T(8,128)} %temp.5) | copy-start | bytes 3145732
  0.7 7.9 %copy-start.5 = (f32[16,64,256]{2,1,0:T(8,128)S(1)}, f32[16,64,256]{2,1,0:T(8,128)}, u32[]{:S(2)}) copy-start(f32[16,64,256]{2,1,0:T(8,128)} %w_prev.3) | copy-start | bytes 3145732
  0.7 7.9 %copy-start.4 = (f32[16,64,256]{2,1,0:T(8,128)S(1)}, f32[16,64,256]{2,1,0:T(8,128)}, u32[]{:S(2)}) copy-start(f32[16,64,256]{2,1,0:T(8,128)} %temp_prev.3) | copy-start | bytes 3145732
  0.7 7.9 %copy-start.3 = (f32[16,64,256]{2,1,0:T(8,128)S(1)}, f32[16,64,256]{2,1,0:T(8,128)}, u32[]{:S(2)}) copy-start(f32[16,64,256]{2,1,0:T(8,128)} %v_vel.3) | copy-start | bytes 3145732
  0.7 7.9 %copy-start.2 = (f32[16,64,256]{2,1,0:T(8,128)S(1)}, f32[16,64,256]{2,1,0:T(8,128)}, u32[]{:S(2)}) copy-start(f32[16,64,256]{2,1,0:T(8,128)} %u_vel.3) | copy-start | bytes 3145732
  2.0 9.2 %collective-permute-start = (f32[32,256]{1,0:T(8,128)S(1)}, f32[32,256]{1,0:T(8,128)S(1)}, u32[]{:S(2)}, u32[]{:S(2)}) collective-permute-start(f32[32,256]{1,0:T(8,128)S(1)} %get-tuple-element.30), channel_id=1, source_target_pairs={{0,4},{8,12},{16,20},{24,28},{4,0},{12,8},{20,16},{28,24},{1,5},{9... | collective-permute-start | bytes 98312 | tf_op jit(solution)/shard_map/ppermute | solution.py:773
  5.0 6.6 %collective-permute-start.1 = (f32[32,256]{1,0:T(8,128)S(1)}, f32[32,256]{1,0:T(8,128)S(1)}, u32[]{:S(2)}, u32[]{:S(2)}) collective-permute-start(f32[32,256]{1,0:T(8,128)S(1)} %get-tuple-element.31), channel_id=1, source_target_pairs={{4,8},{12,16},{20,24},{28,0},{8,4},{16,12},{24,20},{0,28},{5,9},{1... | collective-permute-start | bytes 98312 | tf_op jit(solution)/shard_map/ppermute | solution.py:774
  8.6 3.1 %collective-permute-start.2 = (f32[200,256]{1,0:T(8,128)S(1)}, f32[200,256]{1,0:T(8,128)S(1)}, u32[]{:S(2)}, u32[]{:S(2)}) collective-permute-start(f32[200,256]{1,0:T(8,128)S(1)} %get-tuple-element.32.fluxes.own), channel_id=1, source_target_pairs={{0,1},{2,3},{1,0},{3,2},{4,5},{6,7},{5,4},{7,6},{8,9},{10,11},{9,8... | collective-permute-start | bytes 614408 | tf_op jit(solution)/shard_map/ppermute | solution.py:775
  11.8 1.7 %collective-permute-start.4 = (f32[192,256]{1,0:T(8,128)S(1)}, f32[192,256]{1,0:T(8,128)S(1)}, u32[]{:S(2)}, u32[]{:S(2)}) collective-permute-start(f32[192,256]{1,0:T(8,128)S(1)} %get-tuple-element.38), channel_id=1, source_target_pairs={{0,1},{1,0},{2,3},{3,2},{4,5},{5,4},{6,7},{7,6},{8,9},{9,8},{10,11... | collective-permute-start | bytes 589832 | tf_op jit(solution)/shard_map/ppermute | solution.py:788
  12.0 4.6 %collective-permute-start.3 = (f32[136,128]{1,0:T(8,128)S(1)}, f32[136,128]{1,0:T(8,128)S(1)}, u32[]{:S(2)}, u32[]{:S(2)}) collective-permute-start(f32[136,128]{1,0:T(8,128)S(1)} %get-tuple-element.36.own), channel_id=1, source_target_pairs={{0,2},{1,3},{2,0},{3,1},{4,6},{5,7},{6,4},{7,5},{8,10},{9,11},{10,... | collective-permute-start | bytes 208904 | tf_op jit(solution)/shard_map/ppermute | solution.py:799
  13.6 4.3 %collective-permute-start.5 = (f32[64,256]{1,0:T(8,128)S(1)}, f32[64,256]{1,0:T(8,128)S(1)}, u32[]{:S(2)}, u32[]{:S(2)}) collective-permute-start(f32[64,256]{1,0:T(8,128)S(1)} %get-tuple-element.43.mine), channel_id=1, source_target_pairs={{0,2},{1,3},{2,0},{3,1},{4,6},{5,7},{6,4},{7,5},{8,10},{9,11},{10,... | collective-permute-start | bytes 196616 | tf_op jit(solution)/shard_map/ppermute | solution.py:798
  17.3 1.9 %collective-permute-start.7 = (f32[128,128]{1,0:T(8,128)S(1)}, f32[128,128]{1,0:T(8,128)S(1)}, u32[]{:S(2)}, u32[]{:S(2)}) collective-permute-start(f32[128,128]{1,0:T(8,128)S(1)} %get-tuple-element.44), channel_id=1, source_target_pairs={{0,1},{2,3},{1,0},{3,2},{4,5},{6,7},{5,4},{7,6},{8,9},{10,11},{9,8... | collective-permute-start | bytes 196616 | tf_op jit(solution)/shard_map/ppermute | solution.py:810
  18.0 1.3 %collective-permute-start.6 = (f32[64,256]{1,0:T(8,128)S(1)}, f32[64,256]{1,0:T(8,128)S(1)}, u32[]{:S(2)}, u32[]{:S(2)}) collective-permute-start(f32[64,256]{1,0:T(8,128)S(1)} %join.1.joined), channel_id=1, source_target_pairs={{0,1},{2,3},{1,0},{3,2},{4,5},{6,7},{5,4},{7,6},{8,9},{10,11},{9,8... | collective-permute-start | bytes 196616 | tf_op jit(solution)/shard_map/ppermute | solution.py:806

commit v14 on v13

--- a/solution.py
+++ b/solution.py
@@ -252,7 +252,7 @@
             now = later
         return carry
 
-    lax.fori_loop(0, levels // 2, pair_step, 0)
+    lax.fori_loop(0, levels // 2, pair_step, 0, unroll=2)
 
 
 def bulk(table, *arrays):

time: 20.5 us -> 20.5 us (level)
  no operation moved by 1% of the time
where the time goes in v14:
time: 20.5 us; the launch traced here: 20.3 us
  starting transfers between devices  9.78 us (48%)
  Pallas kernels  8.31 us (41%)
  waiting for transfers between devices  1.41 us (7%)
  between operations  0.8 us (4%)
    ppermute x1, starting transfers between devices, local(): lax.ppermute(far, 'gx', both_ways([(i, (i + 1) % across) for i in range(1...  3.54 us
    ppermute x1, starting transfers between devices, local(): lax.ppermute(near, 'gx', both_ways([(i, i + 1) for i in range(0, across,...  3.03 us
    pallas_call x1, Pallas kernels, bulk(): pl.pallas_call(bulk_kernel, out_shape=(held(2, levels + 1, rows, cols), h...  2.57 us
    pallas_call x2, Pallas kernels, finish(): pl.pallas_call(functools.partial(finish_kernel, rounds, swapped), out_sha...  2.14 us
    ppermute x2, starting transfers between devices, local(): theirs = lax.ppermute(message, 'gz', partners)  1.57 us
    ppermute x1, starting transfers between devices, local(): other_own = lax.ppermute(own, 'gz', partners)  1.49 us
    pallas_call x1, Pallas kernels, tends(): pl.pallas_call(functools.partial(tends_kernel, rounds), out_shape=(jax.Sh...  1.38 us
    pallas_call x1, Pallas kernels, edges(): pl.pallas_call(edges_kernel, out_shape=(held(2 * levels, cols), held(2 *...  1.31 us
  transfers between devices with their start and end apart: 8, of which 4 were waited for; matrix products, arithmetic and copies ran while one was open for 0% of the time, Pallas kernels for 28%

profile of v14, /device:TPU:0, one launch (start us, length us, event | category | flops | bytes accessed | tf_op | source)
XLA Modules:
  0.0 20.3 jit_solution(13338914753918800437)
XLA Ops:
  0.7 1.3 %edges.1 = (f32[32,256]{1,0:T(8,128)S(1)}, f32[32,256]{1,0:T(8,128)S(1)}, f32[200,256]{1,0:T(8,128)S(1)}, f32[128,256]{1,0:T(8,128)S(1)}, f32[16,8,256]{2,1,0:T(8,128)S(1)}) custom-call(f32[16,64,256]{2,1,0:T(8,128)} %temp.5, f32[16,64,256]{2,1,0:T(8,128)} %u_vel.3, f32[16,64,256]{2,1,0:T(8,128)} %w_vel.5, f32[16,64,256]{2,1,0:T(8,128)} %v_vel.3, ...), custom_call_target="tpu_custom_call" | custom-call | tf_op jit(solution)/shard_map/edges/pallas_call | solution.py:110
  2.0 3.0 %collective-permute-start = (f32[32,256]{1,0:T(8,128)S(1)}, f32[32,256]{1,0:T(8,128)S(1)}, u32[]{:S(2)}, u32[]{:S(2)}) collective-permute-start(f32[32,256]{1,0:T(8,128)S(1)} %get-tuple-element.30), channel_id=1, source_target_pairs={{0,4},{8,12},{16,20},{24,28},{4,0},{12,8},{20,16},{28,24},{1,5},{9... | collective-permute-start | bytes 98312 | tf_op jit(solution)/shard_map/ppermute | solution.py:773
  5.0 3.5 %collective-permute-start.1 = (f32[32,256]{1,0:T(8,128)S(1)}, f32[32,256]{1,0:T(8,128)S(1)}, u32[]{:S(2)}, u32[]{:S(2)}) collective-permute-start(f32[32,256]{1,0:T(8,128)S(1)} %get-tuple-element.31), channel_id=1, source_target_pairs={{4,8},{12,16},{20,24},{28,0},{8,4},{16,12},{24,20},{0,28},{5,9},{1... | collective-permute-start | bytes 98312 | tf_op jit(solution)/shard_map/ppermute | solution.py:774
  8.6 0.0 collective-permute-start.2
  8.6 2.6 %bulk.1 = (f32[2,17,64,256]{3,2,1,0:T(8,128)S(1)}, f32[2,16,64,256]{3,2,1,0:T(8,128)S(1)}, f32[2,64,256]{2,1,0:T(8,128)S(1)}) custom-call(f32[16,8,256]{2,1,0:T(8,128)S(1)} %get-tuple-element.28.table.rest_1_, f32[16,64,256]{2,1,0:T(8,128)S(1)} %copy-done, f32[16,64,256]{2,1,0:T(8,128)S(1)} %copy-done.2, f32[16,64,256]{2,1,0:T(8,128)S(1)} %copy-done.3, ...), custom_call_target="tpu_custom_call" | custom-call | flops 26214400000 | bytes 6291456 | tf_op jit(solution)/shard_map/bulk/pallas_call | solution.py:260
  11.2 0.0 collective-permute-done.near.rest_4_
  11.2 0.4 %collective-permute-done.1.far.rest_3_ = f32[32,256]{1,0:T(8,128)S(1)} collective-permute-done((f32[32,256]{1,0:T(8,128)S(1)}, f32[32,256]{1,0:T(8,128)S(1)}, u32[]{:S(2)}, u32[]{:S(2)}) %collective-permute-start.1) | collective-permute-done | bytes 32800 | tf_op jit(solution)/shard_map/ppermute | solution.py:774
  11.7 0.0 collective-permute-done.2.other
  11.7 0.2 fix.1
  11.8 0.1 collective-permute-start.4
  12.0 1.5 %collective-permute-start.3 = (f32[136,128]{1,0:T(8,128)S(1)}, f32[136,128]{1,0:T(8,128)S(1)}, u32[]{:S(2)}, u32[]{:S(2)}) collective-permute-start(f32[136,128]{1,0:T(8,128)S(1)} %get-tuple-element.36.own), channel_id=1, source_target_pairs={{0,2},{1,3},{2,0},{3,1},{4,6},{5,7},{6,4},{7,5},{8,10},{9,11},{10,... | collective-permute-start | bytes 208904 | tf_op jit(solution)/shard_map/ppermute | solution.py:799
  13.5 0.0 collective-permute-done.4.theirs
  13.5 0.1 merge.1
  13.6 1.4 %collective-permute-start.5 = (f32[64,256]{1,0:T(8,128)S(1)}, f32[64,256]{1,0:T(8,128)S(1)}, u32[]{:S(2)}, u32[]{:S(2)}) collective-permute-start(f32[64,256]{1,0:T(8,128)S(1)} %get-tuple-element.43.mine), channel_id=1, source_target_pairs={{0,2},{1,3},{2,0},{3,1},{4,6},{5,7},{6,4},{7,5},{8,10},{9,11},{10,... | collective-permute-start | bytes 196616 | tf_op jit(solution)/shard_map/ppermute | solution.py:798
  15.0 1.4 %tends.1 = (f32[16,64,256]{2,1,0:T(8,128)}, f32[16,64,256]{2,1,0:T(8,128)}) custom-call(f32[16,8,256]{2,1,0:T(8,128)S(1)} %get-tuple-element.28.table.rest_1_, f32[2,16,64,256]{3,2,1,0:T(8,128)S(1)} %get-tuple-element.45.tend.rest_2_, f32[32,256]{1,0:T(8,128)S(1)} %collective-permute-done.1.far.rest_3_, f32[32,256]{1,0:T(8,128)S(1)} %collective-permute-done.near.rest_4_, ...), custom_call_target="tpu_custom_call" | custom-call | flops 262144 | bytes 2097152 | tf_op jit(solution)/shard_map/tends/pallas_call | solution.py:452
  16.4 0.3 %collective-permute-done.3.crossing.other.rest_0_ = f32[136,128]{1,0:T(8,128)S(1)} collective-permute-done((f32[136,128]{1,0:T(8,128)S(1)}, f32[136,128]{1,0:T(8,128)S(1)}, u32[]{:S(2)}, u32[]{:S(2)}) %collective-permute-start.3) | collective-permute-done | bytes 69664 | tf_op jit(solution)/shard_map/ppermute | solution.py:799
  16.6 0.6 %prepare.1 = (f32[2,16,64,256]{3,2,1,0:T(8,128)S(1)}, f32[16,8,256]{2,1,0:T(8,128)S(1)}, f32[128,128]{1,0:T(8,128)S(1)}) custom-call(f32[16,64,256]{2,1,0:T(8,128)S(1)} %copy-done, f32[16,64,256]{2,1,0:T(8,128)S(1)} %copy-done.1, f32[2,17,64,256]{3,2,1,0:T(8,128)S(1)} %get-tuple-element.29.forward, f32[16,8,256]{2,1,0:T(8,128)S(1)} %get-tuple-element.28.table.rest_1_, ...), custom_call_target="tpu_custom_call" | custom-call | flops 262144 | bytes 6291456 | tf_op jit(solution)/shard_map/prepare/pallas_call | solution.py:617
  17.3 0.1 collective-permute-start.7
  17.3 0.6 %collective-permute-done.5.theirs = f32[64,256]{1,0:T(8,128)S(1)} collective-permute-done((f32[64,256]{1,0:T(8,128)S(1)}, f32[64,256]{1,0:T(8,128)S(1)}, u32[]{:S(2)}, u32[]{:S(2)}) %collective-permute-start.5) | collective-permute-done | bytes 65568 | tf_op jit(solution)/shard_map/ppermute | solution.py:798
  17.9 0.1 collective-permute-start.6
  18.0 1.1 %finish.2 = (f32[16,64,256]{2,1,0:T(8,128)}, f32[16,64,256]{2,1,0:T(8,128)}, f32[16,64,256]{2,1,0:T(8,128)}, f32[16,64,256]{2,1,0:T(8,128)}) custom-call(f32[2,16,64,256]{3,2,1,0:T(8,128)S(1)} %get-tuple-element.41.known, f32[16,8,256]{2,1,0:T(8,128)S(1)} %get-tuple-element.42.response, ...), custom_call_target="tpu_custom_call", output_to_operand_aliasing={{2}: (8, {}), {3}: (9, {})} | custom-call | flops 5242880000 | bytes 2097152 | tf_op jit(solution)/shard_map/finish/pallas_call | solution.py:738
  19.1 0.0 collective-permute-done.7.rest_0_
  19.1 0.2 collective-permute-done.6.joined
  19.3 1.1 %finish.3 = (f32[16,64,256]{2,1,0:T(8,128)}, f32[16,64,256]{2,1,0:T(8,128)}, f32[16,64,256]{2,1,0:T(8,128)}, f32[16,64,256]{2,1,0:T(8,128)}) custom-call(f32[2,16,64,256]{3,2,1,0:T(8,128)S(1)} %get-tuple-element.41.known, f32[16,8,256]{2,1,0:T(8,128)S(1)} %get-tuple-element.42.response, ...), custom_call_target="tpu_custom_call", output_to_operand_aliasing={{0}: (8, {}), {1}: (9, {}), {2}: (10, {}), {3}: (11, {})} | custom-call | flops 5242880000 | bytes 2097152 | tf_op jit(solution)/shard_map/finish/pallas_call | solution.py:738
  (13 shorter events, 0.1 us)
Async XLA Ops:
  0.6 8.0 %copy-start.1 = (f32[16,64,256]{2,1,0:T(8,128)S(1)}, f32[16,64,256]{2,1,0:T(8,128)}, u32[]{:S(2)}) copy-start(f32[16,64,256]{2,1,0:T(8,128)} %w_vel.5) | copy-start | bytes 3145732
  0.6 8.0 %copy-start = (f32[16,64,256]{2,1,0:T(8,128)S(1)}, f32[16,64,256]{2,1,0:T(8,128)}, u32[]{:S(2)}) copy-start(f32[16,64,256]{2,1,0:T(8,128)} %temp.5) | copy-start | bytes 3145732
  0.7 7.9 %copy-start.5 = (f32[16,64,256]{2,1,0:T(8,128)S(1)}, f32[16,64,256]{2,1,0:T(8,128)}, u32[]{:S(2)}) copy-start(f32[16,64,256]{2,1,0:T(8,128)} %w_prev.3) | copy-start | bytes 3145732
  0.7 7.9 %copy-start.4 = (f32[16,64,256]{2,1,0:T(8,128)S(1)}, f32[16,64,256]{2,1,0:T(8,128)}, u32[]{:S(2)}) copy-start(f32[16,64,256]{2,1,0:T(8,128)} %temp_prev.3) | copy-start | bytes 3145732
  0.7 7.9 %copy-start.3 = (f32[16,64,256]{2,1,0:T(8,128)S(1)}, f32[16,64,256]{2,1,0:T(8,128)}, u32[]{:S(2)}) copy-start(f32[16,64,256]{2,1,0:T(8,128)} %v_vel.3) | copy-start | bytes 3145732
  0.7 7.9 %copy-start.2 = (f32[16,64,256]{2,1,0:T(8,128)S(1)}, f32[16,64,256]{2,1,0:T(8,128)}, u32[]{:S(2)}) copy-start(f32[16,64,256]{2,1,0:T(8,128)} %u_vel.3) | copy-start | bytes 3145732
  2.0 9.2 %collective-permute-start = (f32[32,256]{1,0:T(8,128)S(1)}, f32[32,256]{1,0:T(8,128)S(1)}, u32[]{:S(2)}, u32[]{:S(2)}) collective-permute-start(f32[32,256]{1,0:T(8,128)S(1)} %get-tuple-element.30), channel_id=1, source_target_pairs={{0,4},{8,12},{16,20},{24,28},{4,0},{12,8},{20,16},{28,24},{1,5},{9... | collective-permute-start | bytes 98312 | tf_op jit(solution)/shard_map/ppermute | solution.py:773
  5.0 6.6 %collective-permute-start.1 = (f32[32,256]{1,0:T(8,128)S(1)}, f32[32,256]{1,0:T(8,128)S(1)}, u32[]{:S(2)}, u32[]{:S(2)}) collective-permute-start(f32[32,256]{1,0:T(8,128)S(1)} %get-tuple-element.31), channel_id=1, source_target_pairs={{4,8},{12,16},{20,24},{28,0},{8,4},{16,12},{24,20},{0,28},{5,9},{1... | collective-permute-start | bytes 98312 | tf_op jit(solution)/shard_map/ppermute | solution.py:774
  8.6 3.1 %collective-permute-start.2 = (f32[200,256]{1,0:T(8,128)S(1)}, f32[200,256]{1,0:T(8,128)S(1)}, u32[]{:S(2)}, u32[]{:S(2)}) collective-permute-start(f32[200,256]{1,0:T(8,128)S(1)} %get-tuple-element.32.fluxes.own), channel_id=1, source_target_pairs={{0,1},{2,3},{1,0},{3,2},{4,5},{6,7},{5,4},{7,6},{8,9},{10,11},{9,8... | collective-permute-start | bytes 614408 | tf_op jit(solution)/shard_map/ppermute | solution.py:775
  11.8 1.6 %collective-permute-start.4 = (f32[192,256]{1,0:T(8,128)S(1)}, f32[192,256]{1,0:T(8,128)S(1)}, u32[]{:S(2)}, u32[]{:S(2)}) collective-permute-start(f32[192,256]{1,0:T(8,128)S(1)} %get-tuple-element.38), channel_id=1, source_target_pairs={{0,1},{1,0},{2,3},{3,2},{4,5},{5,4},{6,7},{7,6},{8,9},{9,8},{10,11... | collective-permute-start | bytes 589832 | tf_op jit(solution)/shard_map/ppermute | solution.py:788
  12.0 4.7 %collective-permute-start.3 = (f32[136,128]{1,0:T(8,128)S(1)}, f32[136,128]{1,0:T(8,128)S(1)}, u32[]{:S(2)}, u32[]{:S(2)}) collective-permute-start(f32[136,128]{1,0:T(8,128)S(1)} %get-tuple-element.36.own), channel_id=1, source_target_pairs={{0,2},{1,3},{2,0},{3,1},{4,6},{5,7},{6,4},{7,5},{8,10},{9,11},{10,... | collective-permute-start | bytes 208904 | tf_op jit(solution)/shard_map/ppermute | solution.py:799
  13.6 4.3 %collective-permute-start.5 = (f32[64,256]{1,0:T(8,128)S(1)}, f32[64,256]{1,0:T(8,128)S(1)}, u32[]{:S(2)}, u32[]{:S(2)}) collective-permute-start(f32[64,256]{1,0:T(8,128)S(1)} %get-tuple-element.43.mine), channel_id=1, source_target_pairs={{0,2},{1,3},{2,0},{3,1},{4,6},{5,7},{6,4},{7,5},{8,10},{9,11},{10,... | collective-permute-start | bytes 196616 | tf_op jit(solution)/shard_map/ppermute | solution.py:798
  17.3 1.8 %collective-permute-start.7 = (f32[128,128]{1,0:T(8,128)S(1)}, f32[128,128]{1,0:T(8,128)S(1)}, u32[]{:S(2)}, u32[]{:S(2)}) collective-permute-start(f32[128,128]{1,0:T(8,128)S(1)} %get-tuple-element.44), channel_id=1, source_target_pairs={{0,1},{2,3},{1,0},{3,2},{4,5},{6,7},{5,4},{7,6},{8,9},{10,11},{9,8... | collective-permute-start | bytes 196616 | tf_op jit(solution)/shard_map/ppermute | solution.py:810
  17.9 1.3 %collective-permute-start.6 = (f32[64,256]{1,0:T(8,128)S(1)}, f32[64,256]{1,0:T(8,128)S(1)}, u32[]{:S(2)}, u32[]{:S(2)}) collective-permute-start(f32[64,256]{1,0:T(8,128)S(1)} %join.1.joined), channel_id=1, source_target_pairs={{0,1},{2,3},{1,0},{3,2},{4,5},{6,7},{5,4},{7,6},{8,9},{10,11},{9,8... | collective-permute-start | bytes 196616 | tf_op jit(solution)/shard_map/ppermute | solution.py:806
